TPU v7x, 32 devices: a whole 2x2x4 slice. The times are simulated.
32 devices in a mesh: tile: 8 (over z, core), mem: 4 (over y, x).
Axes of the slice: x: 2, y: 2, z: 4, core: 2. Of those that a mesh axis runs over, the one named last changes fastest.
Arguments:
- right_side: float32 [8, 64, 16, 256], P('tile', 'mem'), may hold values from -6 to 6
- perturbations: bfloat16 [8, 64, 6, 16, 256], P('tile', 'mem'), may hold values from -0.75 to 0.75
- precision: float32 [8, 6, 16, 256], P('tile'), may hold values from 5 to 40
- covered: int32 [8, 2, 16], P('tile'), may hold values 0 or 1
Outputs:
- weights: float32 [8, 64, 16, 256], P('tile', 'mem')
- residual: float32 [8, 64, 16, 256], P('tile', 'mem')
All inputs are finite; a program needn't handle non-finite values. No bound on the sum of `covered` on one device may be relied on, other than what follows from the above.
Results may differ from a plain program's by a relative error of at most 0.006.
Values sent between devices are 32-bit elements; how exact they have to be, the bound alone decides.
No kernel may reach another device: no remote copies, remote signals or barrier semaphores. Data moves between devices by JAX's collectives and lax.ppermute only.
A program may use at most 64 MiB of HBM per device.

v0:
```python
import jax
import jax.numpy as jnp
from jax import lax
from jax.sharding import PartitionSpec as P

ITERS = 2


def passed_along(value, axis, steps):
    count = lax.axis_size(axis)
    first, last = (max(0, -steps), min(count, count - steps))
    return lax.ppermute(value, axis, [(source, source + steps) for source in range(first, last)])


def padded_2(cells, sides, width):
    for axis, dim in sides:
        count = lax.axis_size(axis)
        head = lax.slice_in_dim(cells, 0, width, axis=dim)
        tail = lax.slice_in_dim(cells, cells.shape[dim] - width, cells.shape[dim], axis=dim)
        cells = jnp.concatenate(
            [
                lax.ppermute(tail, axis, [(i, (i + 1) % count) for i in range(count)]),
                cells,
                lax.ppermute(head, axis, [((i + 1) % count, i) for i in range(count)]),
            ],
            axis=dim,
        )
    return cells


def filter_taps():
    offsets = jnp.arange(-8, 9).astype(jnp.float32)
    raw = jnp.exp(-offsets * offsets / 32.0)
    return raw / jnp.sqrt(jnp.sum(jnp.exp(-offsets * offsets / 16.0)))


def smooth(field):
    taps = filter_taps()
    height = field.shape[1]
    width = field.shape[2]
    above = passed_along(field[:, height - 8 :, :], "tile", 8)
    below = passed_along(field[:, :8, :], "tile", -8)
    padded = jnp.concatenate([above, field, below], axis=1)
    along = jnp.zeros_like(field)
    for j in range(17):
        along = along + taps[j] * padded[:, j : j + height, :]
    sided = padded_2(along, (("tile", 2),), 8)
    result = jnp.zeros_like(field)
    for j in range(17):
        result = result + taps[j] * sided[:, :, j : j + width]
    return result


def apply_operator(direction, members_data, obs_weight):
    smoothed = smooth(direction)
    partial_terms = jnp.einsum("kvyx,kyx->vyx", members_data.astype(jnp.float32), smoothed)
    increment = lax.psum(partial_terms, "mem")
    weighted = obs_weight * increment
    back = jnp.einsum("kvyx,vyx->kyx", members_data.astype(jnp.float32), weighted)
    return direction + smooth(back)


def two_products(residual, image):
    return lax.psum((jnp.sum(residual * residual), jnp.sum(residual * image)), ("tile", "mem"))


def local(right_side, perturbations, precision, covered):
    members_data = perturbations[0]
    mask = covered[0].astype(jnp.float32)
    levels = precision.shape[1]
    height = precision.shape[2]
    width = precision.shape[3]
    obs_weight = (
        precision[0].reshape(levels, height // 8, 8, width // 16, 16) * mask[None, :, None, :, None]
    ).reshape(levels, height, width)
    source = right_side[0]
    weights = jnp.zeros_like(source)
    residual = source
    image = apply_operator(residual, members_data, obs_weight)
    norm_now, product = two_products(residual, image)
    length = norm_now / product
    direction, along = (residual, image)
    for step in range(ITERS):
        weights = weights + length * direction
        residual = residual - length * along
        if step + 1 < ITERS:
            image = apply_operator(residual, members_data, obs_weight)
            norm_next, product = two_products(residual, image)
            ratio = norm_next / norm_now
            length = norm_next / (product - ratio * norm_next / length)
            direction = residual + ratio * direction
            along = image + ratio * along
            norm_now = norm_next
    return (weights[None], residual[None])


def solution(mesh):
    return jax.shard_map(
        local,
        mesh=mesh,
        in_specs=(
            P("tile", "mem", None, None),
            P("tile", "mem", None, None, None),
            P("tile", None, None, None),
            P("tile", None, None),
        ),
        out_specs=(P("tile", "mem", None, None), P("tile", "mem", None, None)),
        check_vma=False,
    )
```

profile of v0, /device:TPU:0, one launch (start us, length us, event | category | flops | bytes accessed | tf_op | source)
XLA Modules:
  0.0 320.9 jit_solution(6059782007022575567)
XLA Ops:
  7.2 1.0 fusion.385
  11.7 11.3 %fusion.319 = f32[16,16,256]{2,1,0:T(8,128)S(1)} fusion(f32[16,16,256]{2,1,0:T(8,128)S(1)} %bitcast.64, f32[16,8,256]{2,1,0:T(8,128)S(1)} %collective-permute-done.1, f32[16,8,256]{2,1,0:T(8,128)S(1)} %collective-permute-done, f32[]{:T(128)} %bitcast.27, f32[]{:T(128)} %bitcast.26, f32[]{:T(128)} %bitcast.25, f32[]{:T(128)} %bitcast.24, f32[]{:T(128)} %bitcast.23, ...), kind=kLoop, calls=%fused_computation.547 | loop fusion | flops 3211264 | bytes 786500 | tf_op jit(solution)/shard_map/add | solution.py:46
  23.5 4.1 %collective-permute-start.3 = (f32[16,16,8]{2,1,0:T(8,128)S(1)}, f32[16,16,8]{2,1,0:T(8,128)S(1)}, u32[]{:S(2)}, u32[]{:S(2)}) collective-permute-start(f32[16,16,8]{2,1,0:T(8,128)S(1)} %get-tuple-element.27), channel_id=1, source_target_pairs={{4,0},{8,4},{12,8},{16,12},{20,16},{24,20},{28,24},{0,28},{5,1},{9... | collective-permute-start | bytes 24584 | tf_op jit(solution)/shard_map/ppermute | solution.py:24
  27.6 2.7 collective-permute-done.2
  30.3 12.2 %fusion.275 = f32[16,256,16]{1,0,2:T(8,128)S(1)} fusion(f32[16,16,256]{2,1,0:T(8,128)S(1)} %fusion.319, f32[16,16,8]{2,1,0:T(8,128)S(1)} %collective-permute-done.3, f32[16,16,8]{2,1,0:T(8,128)S(1)} %collective-permute-done.2, f32[]{:T(128)} %bitcast.27, f32[]{:T(128)} %bitcast.26, f32[]{:T(128)} %bitcast.25, f32[]{:T(128)} %bitcast.24, f32[]{:T(128)} %bitcast.23, ...), kind=kLoop, calls=%fused_computation.503 | loop fusion | flops 3211264 | bytes 540740
  43.7 43.4 %all-reduce.5.cloned.1.call-done = f32[6,16,256]{2,1,0:T(8,128)} async-done(((f32[6,16,256]{2,1,0:T(8,128)}), f32[6,16,256]{2,1,0:T(8,128)}) %all-reduce.5.cloned.1.call-update) | async-done | bytes 98320 | tf_op jit(solution)/shard_map/psum | solution.py:57
  87.1 0.9 multiply_bitcast_fusion.1
  89.5 11.3 %fusion.230 = f32[16,16,256]{2,1,0:T(8,128)S(1)} fusion(f32[16,16,256]{2,1,0:T(8,128)S(1)} %bitcast.66, f32[16,8,256]{2,1,0:T(8,128)S(1)} %collective-permute-done.5, f32[16,8,256]{2,1,0:T(8,128)S(1)} %collective-permute-done.4, f32[]{:T(128)} %bitcast.27, f32[]{:T(128)} %bitcast.26, f32[]{:T(128)} %bitcast.25, f32[]{:T(128)} %bitcast.24, f32[]{:T(128)} %bitcast.23, ...), kind=kLoop, calls=%fused_computation.458 | loop fusion | flops 3211264 | bytes 786500 | tf_op jit(solution)/shard_map/add | solution.py:46
  101.0 3.5 %collective-permute-start.7 = (f32[16,16,8]{2,1,0:T(8,128)S(1)}, f32[16,16,8]{2,1,0:T(8,128)S(1)}, u32[]{:S(2)}, u32[]{:S(2)}) collective-permute-start(f32[16,16,8]{2,1,0:T(8,128)S(1)} %get-tuple-element.23), channel_id=1, source_target_pairs={{4,0},{8,4},{12,8},{16,12},{20,16},{24,20},{28,24},{0,28},{5,1},{9... | collective-permute-start | bytes 24584 | tf_op jit(solution)/shard_map/ppermute | solution.py:24
  104.5 2.8 collective-permute-done.6
  107.3 12.8 %multiply_reduce_fusion.2 = (f32[]{:T(128)}, f32[]{:T(128)}, f32[16,16,256]{2,1,0:T(8,128)S(1)}) fusion(f32[1,16,16,256]{3,2,1,0:T(8,128)S(1)} %copy-done.1, f32[16,16,8]{2,1,0:T(8,128)S(1)} %collective-permute-done.7, f32[16,16,256]{2,1,0:T(8,128)S(1)} %fusion.230, f32[]{:T(128)} %bitcast.27, f32[]{:T(128)} %bitcast.26, f32[]{:T(128)} %bitcast.25, ...), kind=kLoop, calls=%fused_computation.625 | loop fusion | flops 3538942 | bytes 802892 | tf_op jit(solution)/shard_map/reduce_sum | solution.py:64
  120.1 39.0 %all-reduce.1 = (f32[]{:T(128)}, f32[]{:T(128)}) all-reduce(f32[]{:T(128)} %get-tuple-element.5, f32[]{:T(128)} %get-tuple-element.4), channel_id=1, replica_groups=mesh['tile'=8,'mem'=4] {'tile','mem'}, use_global_device_ids=true, to_apply=%region_1.0 | all-reduce | flops 2 | bytes 16 | tf_op jit(solution)/shard_map/psum | solution.py:64
  161.9 11.3 %fusion.141 = f32[16,16,256]{2,1,0:T(8,128)S(1)} fusion(f32[16,16,256]{2,1,0:T(8,128)S(1)} %multiply_subtract_fusion, f32[16,8,256]{2,1,0:T(8,128)S(1)} %collective-permute-done.9, f32[16,8,256]{2,1,0:T(8,128)S(1)} %collective-permute-done.8, f32[]{:T(128)} %bitcast.27, f32[]{:T(128)} %bitcast.26, f32[]{:T(128)} %bitcast.25, f32[]{:T(128)} %bitcast.24, ...), kind=kLoop, calls=%fused_computation.369 | loop fusion | flops 3211264 | bytes 786500 | tf_op jit(solution)/shard_map/add | solution.py:46
  173.3 3.5 %collective-permute-start.11 = (f32[16,16,8]{2,1,0:T(8,128)S(1)}, f32[16,16,8]{2,1,0:T(8,128)S(1)}, u32[]{:S(2)}, u32[]{:S(2)}) collective-permute-start(f32[16,16,8]{2,1,0:T(8,128)S(1)} %get-tuple-element.19), channel_id=1, source_target_pairs={{4,0},{8,4},{12,8},{16,12},{20,16},{24,20},{28,24},{0,28},{5,1},{9... | collective-permute-start | bytes 24584 | tf_op jit(solution)/shard_map/ppermute | solution.py:24
  176.8 3.8 %collective-permute-done.10 = f32[16,16,8]{2,1,0:T(8,128)S(1)} collective-permute-done((f32[16,16,8]{2,1,0:T(8,128)S(1)}, f32[16,16,8]{2,1,0:T(8,128)S(1)}, u32[]{:S(2)}, u32[]{:S(2)}) %collective-permute-start.10) | collective-permute-done | bytes 8224 | tf_op jit(solution)/shard_map/ppermute | solution.py:22
  180.6 12.2 %fusion.97 = f32[16,256,16]{1,0,2:T(8,128)S(1)} fusion(f32[16,16,256]{2,1,0:T(8,128)S(1)} %fusion.141, f32[16,16,8]{2,1,0:T(8,128)S(1)} %collective-permute-done.11, f32[16,16,8]{2,1,0:T(8,128)S(1)} %collective-permute-done.10, f32[]{:T(128)} %bitcast.27, f32[]{:T(128)} %bitcast.26, f32[]{:T(128)} %bitcast.25, f32[]{:T(128)} %bitcast.24, f32[]{:T(128)} %bitcast.23, ...), kind=kLoop, calls=%fused_computation.325 | loop fusion | flops 3211264 | bytes 540740
  193.7 42.8 %all-reduce.7.cloned.1.call-done = f32[6,16,256]{2,1,0:T(8,128)} async-done(((f32[6,16,256]{2,1,0:T(8,128)}), f32[6,16,256]{2,1,0:T(8,128)}) %all-reduce.7.cloned.1.call-update) | async-done | bytes 98320 | tf_op jit(solution)/shard_map/psum | solution.py:57
  236.5 0.9 multiply_bitcast_fusion
  239.0 11.3 %fusion.52 = f32[16,16,256]{2,1,0:T(8,128)S(1)} fusion(f32[16,16,256]{2,1,0:T(8,128)S(1)} %bitcast.68, f32[16,8,256]{2,1,0:T(8,128)S(1)} %collective-permute-done.13, f32[16,8,256]{2,1,0:T(8,128)S(1)} %collective-permute-done.12, f32[]{:T(128)} %bitcast.27, f32[]{:T(128)} %bitcast.26, f32[]{:T(128)} %bitcast.25, f32[]{:T(128)} %bitcast.24, f32[]{:T(128)} %bitcast.23, ...), kind=kLoop, calls=%fused_computation.280 | loop fusion | flops 3211264 | bytes 786500 | tf_op jit(solution)/shard_map/add | solution.py:46
  250.4 3.5 %collective-permute-start.15 = (f32[16,16,8]{2,1,0:T(8,128)S(1)}, f32[16,16,8]{2,1,0:T(8,128)S(1)}, u32[]{:S(2)}, u32[]{:S(2)}) collective-permute-start(f32[16,16,8]{2,1,0:T(8,128)S(1)} %get-tuple-element.15), channel_id=1, source_target_pairs={{4,0},{8,4},{12,8},{16,12},{20,16},{24,20},{28,24},{0,28},{5,1},{9... | collective-permute-start | bytes 24584 | tf_op jit(solution)/shard_map/ppermute | solution.py:24
  253.9 2.8 collective-permute-done.14
  256.7 12.8 %multiply_reduce_fusion = (f32[]{:T(128)}, f32[]{:T(128)}, f32[16,16,256]{2,1,0:T(8,128)S(1)}) fusion(f32[16,16,256]{2,1,0:T(8,128)S(1)} %multiply_subtract_fusion, f32[16,16,8]{2,1,0:T(8,128)S(1)} %collective-permute-done.15, f32[16,16,256]{2,1,0:T(8,128)S(1)} %fusion.52, f32[]{:T(128)} %bitcast.27, f32[]{:T(128)} %bitcast.26, f32[]{:T(128)} %bitcast.25, ...), kind=kLoop, calls=%fused_computation.622 | loop fusion | flops 3538942 | bytes 802892 | tf_op jit(solution)/shard_map/reduce_sum | solution.py:64
  269.6 39.0 %all-reduce = (f32[]{:T(128)}, f32[]{:T(128)}) all-reduce(f32[]{:T(128)} %get-tuple-element.3, f32[]{:T(128)} %get-tuple-element.2), channel_id=1, replica_groups=mesh['tile'=8,'mem'=4] {'tile','mem'}, use_global_device_ids=true, to_apply=%region_7.0 | all-reduce | flops 2 | bytes 16 | tf_op jit(solution)/shard_map/psum | solution.py:64
  313.1 0.9 subtract_bitcast_fusion
  (54 shorter events, 10.1 us)
Async XLA Ops:
  7.2 4.5 %copy-start.1 = (f32[1,16,16,256]{3,2,1,0:T(8,128)S(1)}, f32[1,16,16,256]{3,2,1,0:T(8,128)}, u32[]{:S(2)}) copy-start(f32[1,16,16,256]{3,2,1,0:T(8,128)} %param.4) | copy-start | bytes 786436
  7.2 79.9 %all-reduce.5.cloned.1.call-start = ((), (), s32[]{:S(2)}) async-start(), calls=%async_computation | async-start | bytes 196608 | tf_op jit(solution)/shard_map/psum | solution.py:57
  8.2 3.4 %collective-permute-start = (f32[16,8,256]{2,1,0:T(8,128)S(1)}, f32[16,8,256]{2,1,0:T(8,128)S(1)}, u32[]{:S(2)}, u32[]{:S(2)}) collective-permute-start(f32[16,8,256]{2,1,0:T(8,128)S(1)} %get-tuple-element.28), channel_id=1, source_target_pairs={} | collective-permute-start | bytes 393224 | tf_op jit(solution)/shard_map/ppermute | solution.py:12
  8.9 2.7 collective-permute-start.1
  22.9 19.6 %copy-start = (bf16[1,16,6,16,256]{4,3,2,1,0:T(8,128)(2,1)S(1)}, bf16[1,16,6,16,256]{4,3,2,1,0:T(8,128)(2,1)}, u32[]{:S(2)}) copy-start(bf16[1,16,6,16,256]{4,3,2,1,0:T(8,128)(2,1)} %param.5) | copy-start | bytes 2359300
  23.0 7.3 %collective-permute-start.2 = (f32[16,16,8]{2,1,0:T(8,128)S(1)}, f32[16,16,8]{2,1,0:T(8,128)S(1)}, u32[]{:S(2)}, u32[]{:S(2)}) collective-permute-start(f32[16,16,8]{2,1,0:T(8,128)S(1)} %get-tuple-element.26), channel_id=1, source_target_pairs={{0,4},{4,8},{8,12},{12,16},{16,20},{20,24},{24,28},{28,0},{1,5},{5... | collective-permute-start | bytes 24584 | tf_op jit(solution)/shard_map/ppermute | solution.py:22
  23.5 6.8 %collective-permute-start.3 = (f32[16,16,8]{2,1,0:T(8,128)S(1)}, f32[16,16,8]{2,1,0:T(8,128)S(1)}, u32[]{:S(2)}, u32[]{:S(2)}) collective-permute-start(f32[16,16,8]{2,1,0:T(8,128)S(1)} %get-tuple-element.27), channel_id=1, source_target_pairs={{4,0},{8,4},{12,8},{16,12},{20,16},{24,20},{28,24},{0,28},{5,1},{9... | collective-permute-start | bytes 24584 | tf_op jit(solution)/shard_map/ppermute | solution.py:24
  42.5 0.9 copy-start.3
  42.6 44.5 %copy-start.2 = (f32[1,6,16,256]{3,2,1,0:T(8,128)S(1)}, f32[1,6,16,256]{3,2,1,0:T(8,128)}, u32[]{:S(2)}) copy-start(f32[1,6,16,256]{3,2,1,0:T(8,128)} %param.6) | copy-start | bytes 294916
  43.4 193.1 %all-reduce.7.cloned.1.call-start = ((), (), s32[]{:S(2)}) async-start(), calls=%async_computation.1 | async-start | bytes 196608 | tf_op jit(solution)/shard_map/psum | solution.py:57
  88.2 1.3 collective-permute-start.4
  88.8 0.7 collective-permute-start.5
  100.9 6.4 %collective-permute-start.6 = (f32[16,16,8]{2,1,0:T(8,128)S(1)}, f32[16,16,8]{2,1,0:T(8,128)S(1)}, u32[]{:S(2)}, u32[]{:S(2)}) collective-permute-start(f32[16,16,8]{2,1,0:T(8,128)S(1)} %get-tuple-element.22), channel_id=1, source_target_pairs={{0,4},{4,8},{8,12},{12,16},{16,20},{20,24},{24,28},{28,0},{1,5},{5... | collective-permute-start | bytes 24584 | tf_op jit(solution)/shard_map/ppermute | solution.py:22
  101.0 6.3 %collective-permute-start.7 = (f32[16,16,8]{2,1,0:T(8,128)S(1)}, f32[16,16,8]{2,1,0:T(8,128)S(1)}, u32[]{:S(2)}, u32[]{:S(2)}) collective-permute-start(f32[16,16,8]{2,1,0:T(8,128)S(1)} %get-tuple-element.23), channel_id=1, source_target_pairs={{4,0},{8,4},{12,8},{16,12},{20,16},{24,20},{28,24},{0,28},{5,1},{9... | collective-permute-start | bytes 24584 | tf_op jit(solution)/shard_map/ppermute | solution.py:24
  160.5 1.3 collective-permute-start.8
  161.2 0.7 collective-permute-start.9
  173.2 7.4 %collective-permute-start.10 = (f32[16,16,8]{2,1,0:T(8,128)S(1)}, f32[16,16,8]{2,1,0:T(8,128)S(1)}, u32[]{:S(2)}, u32[]{:S(2)}) collective-permute-start(f32[16,16,8]{2,1,0:T(8,128)S(1)} %get-tuple-element.18), channel_id=1, source_target_pairs={{0,4},{4,8},{8,12},{12,16},{16,20},{20,24},{24,28},{28,0},{1,5},{5... | collective-permute-start | bytes 24584 | tf_op jit(solution)/shard_map/ppermute | solution.py:22
  173.3 7.3 %collective-permute-start.11 = (f32[16,16,8]{2,1,0:T(8,128)S(1)}, f32[16,16,8]{2,1,0:T(8,128)S(1)}, u32[]{:S(2)}, u32[]{:S(2)}) collective-permute-start(f32[16,16,8]{2,1,0:T(8,128)S(1)} %get-tuple-element.19), channel_id=1, source_target_pairs={{4,0},{8,4},{12,8},{16,12},{20,16},{24,20},{28,24},{0,28},{5,1},{9... | collective-permute-start | bytes 24584 | tf_op jit(solution)/shard_map/ppermute | solution.py:24
  237.6 1.3 collective-permute-start.12
  238.3 0.7 collective-permute-start.13
  250.3 6.4 %collective-permute-start.14 = (f32[16,16,8]{2,1,0:T(8,128)S(1)}, f32[16,16,8]{2,1,0:T(8,128)S(1)}, u32[]{:S(2)}, u32[]{:S(2)}) collective-permute-start(f32[16,16,8]{2,1,0:T(8,128)S(1)} %get-tuple-element.14), channel_id=1, source_target_pairs={{0,4},{4,8},{8,12},{12,16},{16,20},{20,24},{24,28},{28,0},{1,5},{5... | collective-permute-start | bytes 24584 | tf_op jit(solution)/shard_map/ppermute | solution.py:22
  250.4 6.3 %collective-permute-start.15 = (f32[16,16,8]{2,1,0:T(8,128)S(1)}, f32[16,16,8]{2,1,0:T(8,128)S(1)}, u32[]{:S(2)}, u32[]{:S(2)}) collective-permute-start(f32[16,16,8]{2,1,0:T(8,128)S(1)} %get-tuple-element.15), channel_id=1, source_target_pairs={{4,0},{8,4},{12,8},{16,12},{20,16},{24,20},{28,24},{0,28},{5,1},{9... | collective-permute-start | bytes 24584 | tf_op jit(solution)/shard_map/ppermute | solution.py:24
Sparse Core Ops, SparseCore 0:
  43.5 43.4 all-reduce.4
  193.8 42.6 all-reduce.6
where the time goes:
time: 323 us; the launch traced here: 321 us
  other arithmetic  101 us (31%)
  waiting for transfers between devices  98.3 us (30%)
  blocking collectives  78 us (24%)
  between operations  20.9 us (6%)
  starting transfers between devices  20.7 us (6%)
    psum x2, waiting for transfers between devices, apply_operator(): increment = lax.psum(partial_terms, 'mem')  86.2 us
    psum x2, blocking collectives, two_products(): lax.psum((jnp.sum(residual * residual), jnp.sum(residual * image)), ('til...  78 us
    add x4, other arithmetic, smooth(): along = along + taps[j] * padded[:, j:j + height, :]  45.1 us
    unnamed x4, other arithmetic  26.2 us
    reduce_sum x2, other arithmetic, two_products(): jnp.sum(residual * image)  25.7 us
    ppermute x4, starting transfers between devices, padded_2(): lax.ppermute(head, axis, [((i + 1) % count, i) for i in range(count)])  14.7 us
    ppermute x4, waiting for transfers between devices, padded_2(): lax.ppermute(tail, axis, [(i, (i + 1) % count) for i in range(count)])  12 us
  transfers between devices with their start and end apart: 18, of which 6 were waited for; matrix products, arithmetic and copies ran while one was open for 0% of the time, Pallas kernels for 0%

commit v1 on v0

v1 whole, which is shorter than its diff:
```python
import functools

import jax
import jax.numpy as jnp
import ml_dtypes
import numpy as np
from jax import lax
from jax.experimental import pallas as pl
from jax.experimental.pallas import tpu as pltpu
from jax.sharding import PartitionSpec as P

ITERS = 2
TCOLS = 8
REACH = 8
LANES = 128
F32 = jnp.float32
BF16 = jnp.bfloat16


def taps_np():
    offsets = np.arange(-REACH, REACH + 1, dtype=np.float64)
    raw = np.exp(-offsets * offsets / 32.0)
    return raw / np.sqrt(np.sum(np.exp(-offsets * offsets / 16.0)))


def band(taps, source, target):
    reach = (len(taps) - 1) // 2
    gap = source[:, None] - target[None, :]
    inside = np.abs(gap) <= reach
    return np.where(inside, taps[np.clip(gap + reach, 0, 2 * reach)], 0.0)


def halves(matrix):
    whole = matrix.astype(np.float32)
    high = whole.astype(ml_dtypes.bfloat16)
    low = (whole - high.astype(np.float32)).astype(ml_dtypes.bfloat16)
    return np.stack([high, low])


def column_matrix(taps, width, edge):
    target = np.arange(width)
    slots = LANES // edge
    left = np.tile(np.arange(edge) - edge, slots)
    right = np.tile(np.arange(edge) + width, slots)
    return np.concatenate([band(taps, s, target) for s in (np.arange(width), left, right)])


def row_matrix(taps, height, members, times):
    one = band(taps, np.arange(height), np.arange(height))
    return np.kron(np.eye(members), np.linalg.matrix_power(one, times))


def split(x):
    high = x.astype(BF16)
    return high, (x - high.astype(F32)).astype(BF16)


def dot3(left, right):
    mul = functools.partial(jnp.dot, preferred_element_type=F32)
    return mul(left[0], right[0]) + (mul(left[1], right[0]) + mul(left[0], right[1]))


def both(ref):
    return ref[0], ref[1]


def lane_of(shape):
    return lax.broadcasted_iota(jnp.int32, shape, len(shape) - 1)


def pack_edges(field, edge, first):
    members, rows, width = field.shape
    slots = LANES // edge
    groups = members // slots
    lane = lane_of((rows, LANES))
    out = []
    for g in range(groups):
        total = jnp.zeros((rows, LANES), F32)
        for j in range(slots):
            member = field[j * groups + g]
            block = member[:, :LANES] if first else member[:, width - LANES :]
            start = 0 if first else LANES - edge
            shift = (j * edge - start) % LANES
            moved = pltpu.roll(block, shift, 1) if shift else block
            total = jnp.where((lane >= j * edge) & (lane < (j + 1) * edge), moved, total)
        out.append(total)
    return jnp.stack(out)


def spread_edges(packed, edge):
    groups, rows, _ = packed.shape
    slots = LANES // edge
    lane = lane_of((groups, rows, LANES))
    parts = [jnp.where((lane >= j * edge) & (lane < (j + 1) * edge), packed, 0.0) for j in range(slots)]
    return jnp.concatenate(parts, axis=0).reshape(slots * groups * rows, LANES)


def beside(field, left, right, edge):
    members, rows, width = field.shape
    return jnp.concatenate(
        [field.reshape(members * rows, width), spread_edges(left, edge), spread_edges(right, edge)], axis=1
    )


def increments(members_ref, smoothed):
    members, levels = members_ref.shape[:2]
    totals = []
    for v in range(levels):
        total = members_ref[0, v].astype(F32) * smoothed[0]
        for k in range(1, members):
            total = total + members_ref[k, v].astype(F32) * smoothed[k]
        totals.append(total)
    return jnp.stack(totals)


def adjoint(members_ref, weighted):
    members, levels = members_ref.shape[:2]
    back = []
    for k in range(members):
        total = members_ref[k, 0].astype(F32) * weighted[0]
        for v in range(1, levels):
            total = total + members_ref[k, v].astype(F32) * weighted[v]
        back.append(total)
    return jnp.stack(back)


def folded(x):
    width = x.shape[-1]
    x = x.reshape(-1, 8, width).sum(axis=0)
    return sum(x[:, i : i + LANES] for i in range(0, width, LANES))


def prepare_kernel(source, precision, covered, to_next, to_previous, obs_weight):
    levels, height, width = precision.shape
    rows, blocks = covered.shape
    to_next[...] = pack_edges(source, REACH, False)
    to_previous[...] = pack_edges(source, REACH, True)
    spread = lax.broadcasted_iota(jnp.int32, (blocks, width), 1) // (width // blocks)
    spread = (spread == lax.broadcasted_iota(jnp.int32, (blocks, width), 0)).astype(BF16)
    mask = jnp.dot(covered[...].astype(F32).astype(BF16), spread, preferred_element_type=F32)
    for v in range(levels):
        for i in range(rows):
            part = pl.ds(i * (height // rows), height // rows)
            obs_weight[v, part] = precision[v, part] * mask[i : i + 1]


def forward_kernel(source, left, right, members_ref, column, row, increment, norm):
    lhs = split(beside(source[...], left[...], right[...], REACH))
    smoothed = dot3(both(row), split(dot3(lhs, both(column))))
    increment[...] = increments(members_ref, smoothed.reshape(source.shape))
    norm[...] = folded(source[...] * source[...])


def adjoint_kernel(i0, i1, i2, i3, obs_weight, members_ref, back, to_next, to_previous, norm):
    increment = (i0[...] + i1[...]) + (i2[...] + i3[...])
    weighted = obs_weight[...] * increment
    norm[...] = folded(weighted * increment)
    back[...] = adjoint(members_ref, weighted)
    to_next[...] = pack_edges(back, 2 * REACH, False)
    to_previous[...] = pack_edges(back, 2 * REACH, True)


def middle_kernel(back, left, right, members_ref, norm_source, column, row, row_twice, first, second):
    members, height, width = back.shape
    levels = members_ref.shape[1]
    lhs = split(beside(back[...], left[...], right[...], 2 * REACH))
    both_filters = dot3(lhs, both(column))
    z = dot3(both(row), split(both_filters[:, :width]))
    smoothed = dot3(both(row_twice), split(both_filters[:, width:]))
    first[...] = z.reshape(first.shape)
    second[: levels * height] = increments(members_ref, smoothed.reshape(back.shape)).reshape(levels * height, width)
    second[levels * height :] = jnp.concatenate([norm_source[...], folded(z * z)], axis=1)


def last_kernel(i0, i1, i2, i3, obs_weight, members_ref, norm_mixed, back, to_next, to_previous, norms):
    levels, height, width = obs_weight.shape
    total = (i0[...] + i1[...]) + (i2[...] + i3[...])
    increment = total[: levels * height].reshape(levels, height, width)
    sums = total[levels * height :]
    weighted = obs_weight[...] * increment
    four = [sums[:, :LANES], norm_mixed[...], sums[:, LANES:], folded(weighted * increment)]
    row = lax.broadcasted_iota(jnp.int32, (8, LANES), 0)
    stacked = jnp.zeros((8, LANES), F32)
    for i, part in enumerate(four):
        stacked = jnp.where(row == i, jnp.sum(part, axis=0, keepdims=True), stacked)
    norms[...] = stacked
    back[...] = adjoint(members_ref, weighted)
    to_next[...] = pack_edges(back, REACH, False)
    to_previous[...] = pack_edges(back, REACH, True)


def filter_kernel(back, left, right, column, row, out):
    lhs = split(beside(back[...], left[...], right[...], REACH))
    out[...] = dot3(both(row), split(dot3(lhs, both(column)))).reshape(out.shape)


def combine_kernel(norms, source, first, second, weights, residual):
    total = jnp.sum(norms[...], axis=1, keepdims=True)
    bb, bg, gg, gh = (total[i : i + 1] for i in range(4))
    bg, gg, gh = bg / bb, gg / bb, gh / bb
    q = 1.0 / (1.0 + bg)
    p = bg * q
    ratio = (gg - bg * bg) * q * q
    d = p + ratio
    square = d * d - 2.0 * d * q * bg + q * q * gg
    image = d * d * bg - 2.0 * d * q * gg + q * q * gh
    step = ratio / (square + image)
    b, g, h = source[...], first[...], second[...]
    weights[...] = (q + step * d) * b - (step * q) * g
    residual[...] = (p - step * d) * b + (step * q - q - step * d) * g + (step * q) * h


def call(kernel, outs, *operands, cost=None):
    shapes = [jax.ShapeDtypeStruct(shape, F32) for shape in outs]
    vmem = pl.BlockSpec(memory_space=pltpu.VMEM)
    return pl.pallas_call(
        kernel,
        out_shape=shapes,
        in_specs=[vmem] * len(operands),
        out_specs=[vmem] * len(outs),
        compiler_params=pltpu.CompilerParams(vmem_limit_bytes=24 * 1024 * 1024),
        cost_estimate=cost,
    )(*operands)


def from_both_sides(to_next, to_previous, axis):
    count = lax.axis_size(axis)
    left = lax.ppermute(to_next, axis, [(i, (i + 1) % count) for i in range(count)])
    right = lax.ppermute(to_previous, axis, [((i + 1) % count, i) for i in range(count)])
    return left, right


def from_all(value, axis):
    count = lax.axis_size(axis)
    return [value] + [lax.ppermute(value, axis, [(i, i ^ k) for i in range(count)]) for k in range(1, count)]


def summed(value, axis):
    count = lax.axis_size(axis)
    step = 1
    while step < count:
        value = value + lax.ppermute(value, axis, [(i, i ^ step) for i in range(count)])
        step *= 2
    return value


def one_tile_row(right_side, perturbations, precision, covered):
    source, members_data = right_side[0], perturbations[0]
    members, levels, height, width = members_data.shape
    taps = taps_np()
    twice = np.convolve(taps, taps)
    field = (members, height, width)
    near = (members * REACH // LANES, height, LANES)
    far = (2 * members * REACH // LANES, height, LANES)
    small = (8, LANES)
    column = halves(column_matrix(taps, width, REACH))
    column_wide = halves(
        np.concatenate(
            [column_matrix(taps, width, 2 * REACH), column_matrix(twice, width, 2 * REACH)], axis=1
        )
    )
    row = halves(row_matrix(taps, height, members, 1))
    row_twice = halves(row_matrix(taps, height, members, 2))

    to_next, to_previous, obs_weight = call(
        prepare_kernel, [near, near, precision.shape[1:]], source, precision[0], covered[0]
    )
    left, right = from_both_sides(to_next, to_previous, "tile")
    increment, norm_source = call(
        forward_kernel, [(levels, height, width), small], source, left, right, members_data, column, row
    )
    parts = from_all(increment, "mem")
    back, to_next, to_previous, norm_mixed = call(
        adjoint_kernel, [field, far, far, small], *parts, obs_weight, members_data
    )
    left, right = from_both_sides(to_next, to_previous, "tile")
    first, second = call(
        middle_kernel,
        [field, (levels * height + 8, width)],
        back, left, right, members_data, norm_source, column_wide, row, row_twice,
    )
    parts = from_all(second, "mem")
    back, to_next, to_previous, norms = call(
        last_kernel, [field, near, near, small], *parts, obs_weight, members_data, norm_mixed
    )
    left, right = from_both_sides(to_next, to_previous, "tile")
    (second,) = call(filter_kernel, [field], back, left, right, column, row)
    norms = summed(norms, "tile")
    weights, residual = call(combine_kernel, [field, field], norms, source, first, second)
    return weights[None], residual[None]


def passed_along(value, axis, steps):
    count = lax.axis_size(axis)
    first, last = (max(0, -steps), min(count, count - steps))
    return lax.ppermute(value, axis, [(source, source + steps) for source in range(first, last)])


def smooth(field):
    taps = taps_np().astype(np.float32)
    height, width = field.shape[1:]
    above = passed_along(field[:, height - REACH :, :], "tile", TCOLS)
    below = passed_along(field[:, :REACH, :], "tile", -TCOLS)
    padded = jnp.concatenate([above, field, below], axis=1)
    along = sum(taps[j] * padded[:, j : j + height, :] for j in range(2 * REACH + 1))
    left, right = from_both_sides(along[:, :, width - REACH :], along[:, :, :REACH], "tile")
    sided = jnp.concatenate([left, along, right], axis=2)
    return sum(taps[j] * sided[:, :, j : j + width] for j in range(2 * REACH + 1))


def several_tile_rows(right_side, perturbations, precision, covered):
    source = right_side[0]
    members_data = perturbations[0].astype(F32)
    levels, height, width = precision.shape[1:]
    rows, blocks = covered.shape[1:]
    mask = covered[0].astype(F32)
    obs_weight = (
        precision[0].reshape(levels, rows, height // rows, blocks, width // blocks) * mask[None, :, None, :, None]
    ).reshape(levels, height, width)

    def operator(direction):
        partial_terms = jnp.einsum("kvyx,kyx->vyx", members_data, smooth(direction))
        weighted = obs_weight * lax.psum(partial_terms, "mem")
        return direction + smooth(jnp.einsum("kvyx,vyx->kyx", members_data, weighted))

    weights = jnp.zeros_like(source)
    residual = direction = source
    norm_now = lax.psum(jnp.sum(source * source), ("tile", "mem"))
    for step in range(ITERS):
        image = operator(direction)
        length = norm_now / lax.psum(jnp.sum(direction * image), ("tile", "mem"))
        weights = weights + length * direction
        residual = residual - length * image
        if step + 1 < ITERS:
            norm_next = lax.psum(jnp.sum(residual * residual), ("tile", "mem"))
            direction = residual + norm_next / norm_now * direction
            norm_now = norm_next
    return weights[None], residual[None]


def solution(mesh):
    single = mesh.shape["tile"] == TCOLS and mesh.shape["mem"] == 4
    local = one_tile_row if single else several_tile_rows
    return jax.shard_map(
        local,
        mesh=mesh,
        in_specs=(
            P("tile", "mem", None, None),
            P("tile", "mem", None, None, None),
            P("tile", None, None, None),
            P("tile", None, None),
        ),
        out_specs=(P("tile", "mem", None, None), P("tile", "mem", None, None)),
        check_vma=False,
    )
```

time: 323 us -> 48.2 us (0.15)
  other arithmetic: 101 us -> 0.01 us
  waiting for transfers between devices: 98.3 us -> 19.1 us
  blocking collectives: 78 us -> 0 us
  between operations: 20.9 us -> 0.76 us
  Pallas kernels: 0 us -> 4.33 us
    psum x2 -> x0, waiting for transfers between devices: 86.2 us -> none  [apply_operator(): increment = lax.psum(partial_terms, 'mem')]
    psum x2 -> x0, blocking collectives: 78 us -> none  [two_products(): lax.psum((jnp.sum(residual * residual), jnp.sum(residual * image)), ('til...]
    add x4 -> x3, other arithmetic: 45.1 us -> 0.01 us  [summed(): value + lax.ppermute(value, axis, [(i, i ^ step) for i in range(count)])]
    reduce_sum x3 -> x0, other arithmetic: 26.3 us -> none  [the longest x2 25.7 us: two_products(): jnp.sum(residual * image)]
    unnamed x4 -> x0, other arithmetic: 26.2 us -> none
    ppermute x16 -> x15, waiting for transfers between devices: 12 us -> 19.1 us  [the longest x6 8.96 us: from_all(): lax.ppermute(value, axis, [(i, i ^ k) for i in range(count)])]
    unnamed x8 -> x22, local copies, waits for them, and re-layouts: 0.02 us -> 4.72 us
    pallas_call x0 -> x7, Pallas kernels: none -> 4.33 us  [call(): pl.pallas_call(kernel, out_shape=shapes, in_specs=[vmem] * len(operands),...]
  transfers between devices with their start and end apart: 18 -> 15, of which waited for: 6 -> 11; matrix products, arithmetic and copies ran while one was open for 0% -> 0% of each run, Pallas kernels for 0% -> 2%
where the time goes in v1:
time: 48.2 us; the launch traced here: 47.9 us
  waiting for transfers between devices  19.1 us (40%)
  starting transfers between devices  19 us (39%)
  local copies, waits for them, and re-layouts  4.72 us (10%)
  Pallas kernels  4.33 us (9%)
  between operations  0.76 us (2%)
    ppermute x3, starting transfers between devices, from_both_sides(): lax.ppermute(to_previous, axis, [((i + 1) % count, i) for i in range(coun...  10.7 us
    ppermute x6, waiting for transfers between devices, from_all(): lax.ppermute(value, axis, [(i, i ^ k) for i in range(count)])  8.96 us
    ppermute x3, waiting for transfers between devices, summed(): lax.ppermute(value, axis, [(i, i ^ step) for i in range(count)])  7.28 us
    ppermute x6, starting transfers between devices, from_all(): lax.ppermute(value, axis, [(i, i ^ k) for i in range(count)])  7.15 us
    unnamed x22, local copies, waits for them, and re-layouts  4.72 us
    pallas_call x7, Pallas kernels, call(): pl.pallas_call(kernel, out_shape=shapes, in_specs=[vmem] * len(operands),...  4.33 us
    ppermute x3, waiting for transfers between devices, from_both_sides(): lax.ppermute(to_next, axis, [(i, (i + 1) % count) for i in range(count)])  2.69 us
    ppermute x3, starting transfers between devices, from_both_sides(): lax.ppermute(to_next, axis, [(i, (i + 1) % count) for i in range(count)])  1.06 us
  transfers between devices with their start and end apart: 15, of which 11 were waited for; matrix products, arithmetic and copies ran while one was open for 0% of the time, Pallas kernels for 2%

profile of v1, /device:TPU:0, one launch (start us, length us, event | category | flops | bytes accessed | tf_op | source)
XLA Modules:
  0.0 47.9 jit_solution(9630720710201775171)
XLA Ops:
  0.6 0.7 %copy-done.10 = s32[1,2,16]{2,1,0:T(2,128)S(1)} copy-done((s32[1,2,16]{2,1,0:T(2,128)S(1)}, s32[1,2,16]{2,1,0:T(2,128)}, u32[]{:S(2)}) %copy-start.10) | copy-done | bytes 152
  1.3 0.9 %copy-done.2 = f32[1,16,16,256]{3,2,1,0:T(8,128)S(1)} copy-done((f32[1,16,16,256]{3,2,1,0:T(8,128)S(1)}, f32[1,16,16,256]{3,2,1,0:T(8,128)}, u32[]{:S(2)}) %copy-start.2) | copy-done | bytes 262168
  2.3 0.9 %copy-done.9 = f32[1,6,16,256]{3,2,1,0:T(8,128)S(1)} copy-done((f32[1,6,16,256]{3,2,1,0:T(8,128)S(1)}, f32[1,6,16,256]{3,2,1,0:T(8,128)}, u32[]{:S(2)}) %copy-start.9) | copy-done | bytes 98328
  3.3 0.5 %collective-permute-start = (f32[1,16,128]{2,1,0:T(8,128)S(1)}, f32[1,16,128]{2,1,0:T(8,128)S(1)}, u32[]{:S(2)}, u32[]{:S(2)}) collective-permute-start(f32[1,16,128]{2,1,0:T(8,128)S(1)} %get-tuple-element.19), channel_id=1, source_target_pairs={{0,4},{4,8},{8,12},{12,16},{16,20},{20,24},{24,28},{28,0},{1,5},{5... | collective-permute-start | bytes 24584 | tf_op jit(solution)/shard_map/ppermute | solution.py:228
  3.8 4.1 %collective-permute-start.1 = (f32[1,16,128]{2,1,0:T(8,128)S(1)}, f32[1,16,128]{2,1,0:T(8,128)S(1)}, u32[]{:S(2)}, u32[]{:S(2)}) collective-permute-start(f32[1,16,128]{2,1,0:T(8,128)S(1)} %get-tuple-element.20), channel_id=1, source_target_pairs={{4,0},{8,4},{12,8},{16,12},{20,16},{24,20},{28,24},{0,28},{5,1},{9... | collective-permute-start | bytes 24584 | tf_op jit(solution)/shard_map/ppermute | solution.py:229
  7.9 1.3 %collective-permute-done.left = f32[1,16,128]{2,1,0:T(8,128)S(1)} collective-permute-done((f32[1,16,128]{2,1,0:T(8,128)S(1)}, f32[1,16,128]{2,1,0:T(8,128)S(1)}, u32[]{:S(2)}, u32[]{:S(2)}) %collective-permute-start) | collective-permute-done | bytes 8224 | tf_op jit(solution)/shard_map/ppermute | solution.py:228
  9.3 1.1 %copy-done = bf16[1,16,6,16,256]{4,3,2,1,0:T(8,128)(2,1)S(1)} copy-done((bf16[1,16,6,16,256]{4,3,2,1,0:T(8,128)(2,1)S(1)}, bf16[1,16,6,16,256]{4,3,2,1,0:T(8,128)(2,1)}, u32[]{:S(2)}) %copy-start) | copy-done | bytes 786456
  10.4 1.0 %copy-done.5 = bf16[2,512,256]{2,1,0:T(8,128)(2,1)S(1)} copy-done((bf16[2,512,256]{2,1,0:T(8,128)(2,1)S(1)}, bf16[2,512,256]{2,1,0:T(8,128)(2,1)}, u32[]{:S(2)}) %copy-start.5) | copy-done | bytes 524312
  11.5 0.9 %shard_map.96 = (f32[6,16,256]{2,1,0:T(8,128)S(1)}, f32[8,128]{1,0:T(8,128)S(1)}) custom-call(f32[16,16,256]{2,1,0:T(8,128)S(1)} %bitcast.11, f32[1,16,128]{2,1,0:T(8,128)S(1)} %collective-permute-done.left, f32[1,16,128]{2,1,0:T(8,128)S(1)} %collective-permute-done.1.right, bf16[16,6,16,256]{3,2,1,0:T(8,128)(2,1)S(1)} %bitcast.6, ...), custom_call_target="tpu_custom_call" | custom-call | tf_op jit(solution)/shard_map/pallas_call | solution.py:216
  12.4 2.9 %collective-permute-start.4 = (f32[6,16,256]{2,1,0:T(8,128)S(1)}, f32[6,16,256]{2,1,0:T(8,128)S(1)}, u32[]{:S(2)}, u32[]{:S(2)}) collective-permute-start(f32[6,16,256]{2,1,0:T(8,128)S(1)} %get-tuple-element.21.i0), channel_id=1, source_target_pairs={{0,3},{1,2},{2,1},{3,0},{4,7},{5,6},{6,5},{7,4},{8,11},{9,10},{10,... | collective-permute-start | bytes 294920 | tf_op jit(solution)/shard_map/ppermute | solution.py:235
  15.3 0.5 %collective-permute-start.3 = (f32[6,16,256]{2,1,0:T(8,128)S(1)}, f32[6,16,256]{2,1,0:T(8,128)S(1)}, u32[]{:S(2)}, u32[]{:S(2)}) collective-permute-start(f32[6,16,256]{2,1,0:T(8,128)S(1)} %get-tuple-element.21.i0), channel_id=1, source_target_pairs={{0,2},{1,3},{2,0},{3,1},{4,6},{5,7},{6,4},{7,5},{8,10},{9,11},{10,... | collective-permute-start | bytes 294920 | tf_op jit(solution)/shard_map/ppermute | solution.py:235
  16.0 2.6 %collective-permute-done.4.i3 = f32[6,16,256]{2,1,0:T(8,128)S(1)} collective-permute-done((f32[6,16,256]{2,1,0:T(8,128)S(1)}, f32[6,16,256]{2,1,0:T(8,128)S(1)}, u32[]{:S(2)}, u32[]{:S(2)}) %collective-permute-start.4) | collective-permute-done | bytes 98336 | tf_op jit(solution)/shard_map/ppermute | solution.py:235
  18.5 1.9 %collective-permute-done.3.i2 = f32[6,16,256]{2,1,0:T(8,128)S(1)} collective-permute-done((f32[6,16,256]{2,1,0:T(8,128)S(1)}, f32[6,16,256]{2,1,0:T(8,128)S(1)}, u32[]{:S(2)}, u32[]{:S(2)}) %collective-permute-start.3) | collective-permute-done | bytes 98336 | tf_op jit(solution)/shard_map/ppermute | solution.py:235
  21.0 3.5 %collective-permute-start.6 = (f32[2,16,128]{2,1,0:T(8,128)S(1)}, f32[2,16,128]{2,1,0:T(8,128)S(1)}, u32[]{:S(2)}, u32[]{:S(2)}) collective-permute-start(f32[2,16,128]{2,1,0:T(8,128)S(1)} %get-tuple-element.25), channel_id=1, source_target_pairs={{4,0},{8,4},{12,8},{16,12},{20,16},{24,20},{28,24},{0,28},{5,1},{9... | collective-permute-start | bytes 49160 | tf_op jit(solution)/shard_map/ppermute | solution.py:229
  24.6 1.4 %collective-permute-done.5.left = f32[2,16,128]{2,1,0:T(8,128)S(1)} collective-permute-done((f32[2,16,128]{2,1,0:T(8,128)S(1)}, f32[2,16,128]{2,1,0:T(8,128)S(1)}, u32[]{:S(2)}, u32[]{:S(2)}) %collective-permute-start.5) | collective-permute-done | bytes 16416 | tf_op jit(solution)/shard_map/ppermute | solution.py:228
  26.0 1.0 %shard_map.98 = (f32[16,16,256]{2,1,0:T(8,128)S(1)}, f32[104,256]{1,0:T(8,128)S(1)}) custom-call(f32[16,16,256]{2,1,0:T(8,128)S(1)} %get-tuple-element.23.back, f32[2,16,128]{2,1,0:T(8,128)S(1)} %collective-permute-done.5.left, f32[2,16,128]{2,1,0:T(8,128)S(1)} %collective-permute-done.6.right, bf16[16,6,16,256]{3,2,1,0:T(8,128)(2,1)S(1)} %bitcast.8, ...), custom_call_target="tpu_custom_call" | custom-call | tf_op jit(solution)/shard_map/pallas_call | solution.py:216
  27.0 1.6 %collective-permute-start.9 = (f32[104,256]{1,0:T(8,128)S(1)}, f32[104,256]{1,0:T(8,128)S(1)}, u32[]{:S(2)}, u32[]{:S(2)}) collective-permute-start(f32[104,256]{1,0:T(8,128)S(1)} %get-tuple-element.27.i0), channel_id=1, source_target_pairs={{0,3},{1,2},{2,1},{3,0},{4,7},{5,6},{6,5},{7,4},{8,11},{9,10},{10,... | collective-permute-start | bytes 319496 | tf_op jit(solution)/shard_map/ppermute | solution.py:235
  28.7 1.4 %collective-permute-start.8 = (f32[104,256]{1,0:T(8,128)S(1)}, f32[104,256]{1,0:T(8,128)S(1)}, u32[]{:S(2)}, u32[]{:S(2)}) collective-permute-start(f32[104,256]{1,0:T(8,128)S(1)} %get-tuple-element.27.i0), channel_id=1, source_target_pairs={{0,2},{1,3},{2,0},{3,1},{4,6},{5,7},{6,4},{7,5},{8,10},{9,11},{10,... | collective-permute-start | bytes 319496 | tf_op jit(solution)/shard_map/ppermute | solution.py:235
  30.6 3.3 %collective-permute-done.9.i3 = f32[104,256]{1,0:T(8,128)S(1)} collective-permute-done((f32[104,256]{1,0:T(8,128)S(1)}, f32[104,256]{1,0:T(8,128)S(1)}, u32[]{:S(2)}, u32[]{:S(2)}) %collective-permute-start.9) | collective-permute-done | bytes 106528 | tf_op jit(solution)/shard_map/ppermute | solution.py:235
  35.6 3.1 %collective-permute-start.14 = (f32[1,16,128]{2,1,0:T(8,128)S(1)}, f32[1,16,128]{2,1,0:T(8,128)S(1)}, u32[]{:S(2)}, u32[]{:S(2)}) collective-permute-start(f32[1,16,128]{2,1,0:T(8,128)S(1)} %get-tuple-element.33), channel_id=1, source_target_pairs={{4,0},{8,4},{12,8},{16,12},{20,16},{24,20},{28,24},{0,28},{5,1},{9... | collective-permute-start | bytes 24584 | tf_op jit(solution)/shard_map/ppermute | solution.py:229
  38.8 3.6 %collective-permute-done.11 = f32[8,128]{1,0:T(8,128)S(1)} collective-permute-done((f32[8,128]{1,0:T(8,128)S(1)}, f32[8,128]{1,0:T(8,128)S(1)}, u32[]{:S(2)}, u32[]{:S(2)}) %collective-permute-start.11) | collective-permute-done | bytes 4128 | tf_op jit(solution)/shard_map/ppermute | solution.py:242
  42.4 0.8 %shard_map.100.second = f32[16,16,256]{2,1,0:T(8,128)S(1)} custom-call(f32[16,16,256]{2,1,0:T(8,128)S(1)} %get-tuple-element.31.back, f32[1,16,128]{2,1,0:T(8,128)S(1)} %collective-permute-done.13.left, f32[1,16,128]{2,1,0:T(8,128)S(1)} %collective-permute-done.14.right, bf16[2,512,256]{2,1,0:T(8,128)(2,1)S(1)} %copy-done.6, bf16[2,256,256]{2,1,0:T(8,128)(2,1)S(1)} %copy-done.4), custom_call_target="tpu_custom_call" | custom-call | tf_op jit(solution)/shard_map/pallas_call | solution.py:216
  43.2 3.7 %collective-permute-done.12 = f32[8,128]{1,0:T(8,128)S(1)} collective-permute-done((f32[8,128]{1,0:T(8,128)S(1)}, f32[8,128]{1,0:T(8,128)S(1)}, u32[]{:S(2)}, u32[]{:S(2)}) %collective-permute-start.12) | collective-permute-done | bytes 4128 | tf_op jit(solution)/shard_map/ppermute | solution.py:242
  46.9 1.0 %shard_map.101 = (f32[16,16,256]{2,1,0:T(8,128)}, f32[16,16,256]{2,1,0:T(8,128)}) custom-call(f32[8,128]{1,0:T(8,128)S(1)} %add.11.norms, f32[16,16,256]{2,1,0:T(8,128)S(1)} %bitcast.12, f32[16,16,256]{2,1,0:T(8,128)S(1)} %get-tuple-element.30.first, f32[16,16,256]{2,1,0:T(8,128)S(1)} %shard_map.100.second), custom_call_target="tpu_custom_call" | custom-call | tf_op jit(solution)/shard_map/pallas_call | solution.py:216
  (38 shorter events, 3.2 us)
Async XLA Ops:
  1.3 0.9 %copy-start.2 = (f32[1,16,16,256]{3,2,1,0:T(8,128)S(1)}, f32[1,16,16,256]{3,2,1,0:T(8,128)}, u32[]{:S(2)}) copy-start(f32[1,16,16,256]{3,2,1,0:T(8,128)} %param.8) | copy-start | bytes 786436
  3.2 6.1 %copy-start.4 = (bf16[2,256,256]{2,1,0:T(8,128)(2,1)S(1)}, bf16[2,256,256]{2,1,0:T(8,128)(2,1)}, u32[]{:S(2)}) copy-start(bf16[2,256,256]{2,1,0:T(8,128)(2,1)} %constant.9.clone.row) | copy-start | bytes 786436
  3.3 5.9 %collective-permute-start = (f32[1,16,128]{2,1,0:T(8,128)S(1)}, f32[1,16,128]{2,1,0:T(8,128)S(1)}, u32[]{:S(2)}, u32[]{:S(2)}) collective-permute-start(f32[1,16,128]{2,1,0:T(8,128)S(1)} %get-tuple-element.19), channel_id=1, source_target_pairs={{0,4},{4,8},{8,12},{12,16},{16,20},{20,24},{24,28},{28,0},{1,5},{5... | collective-permute-start | bytes 24584 | tf_op jit(solution)/shard_map/ppermute | solution.py:228
  3.8 5.5 %collective-permute-start.1 = (f32[1,16,128]{2,1,0:T(8,128)S(1)}, f32[1,16,128]{2,1,0:T(8,128)S(1)}, u32[]{:S(2)}, u32[]{:S(2)}) collective-permute-start(f32[1,16,128]{2,1,0:T(8,128)S(1)} %get-tuple-element.20), channel_id=1, source_target_pairs={{4,0},{8,4},{12,8},{16,12},{20,16},{24,20},{28,24},{0,28},{5,1},{9... | collective-permute-start | bytes 24584 | tf_op jit(solution)/shard_map/ppermute | solution.py:229
  9.3 1.1 %copy-start = (bf16[1,16,6,16,256]{4,3,2,1,0:T(8,128)(2,1)S(1)}, bf16[1,16,6,16,256]{4,3,2,1,0:T(8,128)(2,1)}, u32[]{:S(2)}) copy-start(bf16[1,16,6,16,256]{4,3,2,1,0:T(8,128)(2,1)} %param.9) | copy-start | bytes 2359300
  10.4 1.0 %copy-start.5 = (bf16[2,512,256]{2,1,0:T(8,128)(2,1)S(1)}, bf16[2,512,256]{2,1,0:T(8,128)(2,1)}, u32[]{:S(2)}) copy-start(bf16[2,512,256]{2,1,0:T(8,128)(2,1)} %constant.8.clone.column) | copy-start | bytes 1572868
  11.4 9.3 %copy-start.1 = (bf16[1,16,6,16,256]{4,3,2,1,0:T(8,128)(2,1)S(1)}, bf16[1,16,6,16,256]{4,3,2,1,0:T(8,128)(2,1)}, u32[]{:S(2)}) copy-start(bf16[1,16,6,16,256]{4,3,2,1,0:T(8,128)(2,1)} %param.9) | copy-start | bytes 2359300
  11.4 14.6 %copy-start.8 = (bf16[2,256,256]{2,1,0:T(8,128)(2,1)S(1)}, bf16[2,256,256]{2,1,0:T(8,128)(2,1)}, u32[]{:S(2)}) copy-start(bf16[2,256,256]{2,1,0:T(8,128)(2,1)} %constant.11.clone.row_twice) | copy-start | bytes 786436
  12.4 13.7 %copy-start.7 = (bf16[2,512,512]{2,1,0:T(8,128)(2,1)S(1)}, bf16[2,512,512]{2,1,0:T(8,128)(2,1)}, u32[]{:S(2)}) copy-start(bf16[2,512,512]{2,1,0:T(8,128)(2,1)} %constant.10.clone.column) | copy-start | bytes 3145732
  12.4 6.2 %collective-permute-start.4 = (f32[6,16,256]{2,1,0:T(8,128)S(1)}, f32[6,16,256]{2,1,0:T(8,128)S(1)}, u32[]{:S(2)}, u32[]{:S(2)}) collective-permute-start(f32[6,16,256]{2,1,0:T(8,128)S(1)} %get-tuple-element.21.i0), channel_id=1, source_target_pairs={{0,3},{1,2},{2,1},{3,0},{4,7},{5,6},{6,5},{7,4},{8,11},{9,10},{10,... | collective-permute-start | bytes 294920 | tf_op jit(solution)/shard_map/ppermute | solution.py:235
  15.3 5.1 %collective-permute-start.3 = (f32[6,16,256]{2,1,0:T(8,128)S(1)}, f32[6,16,256]{2,1,0:T(8,128)S(1)}, u32[]{:S(2)}, u32[]{:S(2)}) collective-permute-start(f32[6,16,256]{2,1,0:T(8,128)S(1)} %get-tuple-element.21.i0), channel_id=1, source_target_pairs={{0,2},{1,3},{2,0},{3,1},{4,6},{5,7},{6,4},{7,5},{8,10},{9,11},{10,... | collective-permute-start | bytes 294920 | tf_op jit(solution)/shard_map/ppermute | solution.py:235
  15.8 4.9 %collective-permute-start.2 = (f32[6,16,256]{2,1,0:T(8,128)S(1)}, f32[6,16,256]{2,1,0:T(8,128)S(1)}, u32[]{:S(2)}, u32[]{:S(2)}) collective-permute-start(f32[6,16,256]{2,1,0:T(8,128)S(1)} %get-tuple-element.21.i0), channel_id=1, source_target_pairs={{0,1},{1,0},{2,3},{3,2},{4,5},{5,4},{6,7},{7,6},{8,9},{9,8},{10,11... | collective-permute-start | bytes 294920 | tf_op jit(solution)/shard_map/ppermute | solution.py:235
  21.0 5.0 %collective-permute-start.5 = (f32[2,16,128]{2,1,0:T(8,128)S(1)}, f32[2,16,128]{2,1,0:T(8,128)S(1)}, u32[]{:S(2)}, u32[]{:S(2)}) collective-permute-start(f32[2,16,128]{2,1,0:T(8,128)S(1)} %get-tuple-element.24), channel_id=1, source_target_pairs={{0,4},{4,8},{8,12},{12,16},{16,20},{20,24},{24,28},{28,0},{1,5},{5... | collective-permute-start | bytes 49160 | tf_op jit(solution)/shard_map/ppermute | solution.py:228
  21.0 5.0 %collective-permute-start.6 = (f32[2,16,128]{2,1,0:T(8,128)S(1)}, f32[2,16,128]{2,1,0:T(8,128)S(1)}, u32[]{:S(2)}, u32[]{:S(2)}) collective-permute-start(f32[2,16,128]{2,1,0:T(8,128)S(1)} %get-tuple-element.25), channel_id=1, source_target_pairs={{4,0},{8,4},{12,8},{16,12},{20,16},{24,20},{28,24},{0,28},{5,1},{9... | collective-permute-start | bytes 49160 | tf_op jit(solution)/shard_map/ppermute | solution.py:229
  27.0 6.9 %collective-permute-start.9 = (f32[104,256]{1,0:T(8,128)S(1)}, f32[104,256]{1,0:T(8,128)S(1)}, u32[]{:S(2)}, u32[]{:S(2)}) collective-permute-start(f32[104,256]{1,0:T(8,128)S(1)} %get-tuple-element.27.i0), channel_id=1, source_target_pairs={{0,3},{1,2},{2,1},{3,0},{4,7},{5,6},{6,5},{7,4},{8,11},{9,10},{10,... | collective-permute-start | bytes 319496 | tf_op jit(solution)/shard_map/ppermute | solution.py:235
  28.7 5.7 %collective-permute-start.8 = (f32[104,256]{1,0:T(8,128)S(1)}, f32[104,256]{1,0:T(8,128)S(1)}, u32[]{:S(2)}, u32[]{:S(2)}) collective-permute-start(f32[104,256]{1,0:T(8,128)S(1)} %get-tuple-element.27.i0), channel_id=1, source_target_pairs={{0,2},{1,3},{2,0},{3,1},{4,6},{5,7},{6,4},{7,5},{8,10},{9,11},{10,... | collective-permute-start | bytes 319496 | tf_op jit(solution)/shard_map/ppermute | solution.py:235
  30.1 4.7 %collective-permute-start.7 = (f32[104,256]{1,0:T(8,128)S(1)}, f32[104,256]{1,0:T(8,128)S(1)}, u32[]{:S(2)}, u32[]{:S(2)}) collective-permute-start(f32[104,256]{1,0:T(8,128)S(1)} %get-tuple-element.27.i0), channel_id=1, source_target_pairs={{0,1},{1,0},{2,3},{3,2},{4,5},{5,4},{6,7},{7,6},{8,9},{9,8},{10,11... | collective-permute-start | bytes 319496 | tf_op jit(solution)/shard_map/ppermute | solution.py:235
  34.8 7.6 %copy-start.6 = (bf16[2,512,256]{2,1,0:T(8,128)(2,1)S(1)}, bf16[2,512,256]{2,1,0:T(8,128)(2,1)}, u32[]{:S(2)}) copy-start(bf16[2,512,256]{2,1,0:T(8,128)(2,1)} %constant.8.clone.column) | copy-start | bytes 1572868
  35.1 3.7 %collective-permute-start.10 = (f32[8,128]{1,0:T(8,128)S(1)}, f32[8,128]{1,0:T(8,128)S(1)}, u32[]{:S(2)}, u32[]{:S(2)}) collective-permute-start(f32[8,128]{1,0:T(8,128)S(1)} %get-tuple-element.29), channel_id=1, source_target_pairs={{0,4},{4,0},{8,12},{12,8},{16,20},{20,16},{24,28},{28,24},{1,5},{5... | collective-permute-start | bytes 12296 | tf_op jit(solution)/shard_map/ppermute | solution.py:242
  35.1 7.2 %collective-permute-start.13 = (f32[1,16,128]{2,1,0:T(8,128)S(1)}, f32[1,16,128]{2,1,0:T(8,128)S(1)}, u32[]{:S(2)}, u32[]{:S(2)}) collective-permute-start(f32[1,16,128]{2,1,0:T(8,128)S(1)} %get-tuple-element.32), channel_id=1, source_target_pairs={{0,4},{4,8},{8,12},{12,16},{16,20},{20,24},{24,28},{28,0},{1,5},{5... | collective-permute-start | bytes 24584 | tf_op jit(solution)/shard_map/ppermute | solution.py:228
  35.6 6.7 %collective-permute-start.14 = (f32[1,16,128]{2,1,0:T(8,128)S(1)}, f32[1,16,128]{2,1,0:T(8,128)S(1)}, u32[]{:S(2)}, u32[]{:S(2)}) collective-permute-start(f32[1,16,128]{2,1,0:T(8,128)S(1)} %get-tuple-element.33), channel_id=1, source_target_pairs={{4,0},{8,4},{12,8},{16,12},{20,16},{24,20},{28,24},{0,28},{5,1},{9... | collective-permute-start | bytes 24584 | tf_op jit(solution)/shard_map/ppermute | solution.py:229
  38.7 3.6 %collective-permute-start.11 = (f32[8,128]{1,0:T(8,128)S(1)}, f32[8,128]{1,0:T(8,128)S(1)}, u32[]{:S(2)}, u32[]{:S(2)}) collective-permute-start(f32[8,128]{1,0:T(8,128)S(1)} %add.9), channel_id=1, source_target_pairs={{0,8},{4,12},{8,0},{12,4},{16,24},{20,28},{24,16},{28,20},{1,9},{5... | collective-permute-start | bytes 12296 | tf_op jit(solution)/shard_map/ppermute | solution.py:242
  42.4 4.5 %collective-permute-start.12 = (f32[8,128]{1,0:T(8,128)S(1)}, f32[8,128]{1,0:T(8,128)S(1)}, u32[]{:S(2)}, u32[]{:S(2)}) collective-permute-start(f32[8,128]{1,0:T(8,128)S(1)} %add.10), channel_id=1, source_target_pairs={{0,16},{4,20},{8,24},{12,28},{16,0},{20,4},{24,8},{28,12},{1,17},{... | collective-permute-start | bytes 12296 | tf_op jit(solution)/shard_map/ppermute | solution.py:242
  42.4 4.5 %copy-start.3 = (f32[1,16,16,256]{3,2,1,0:T(8,128)S(1)}, f32[1,16,16,256]{3,2,1,0:T(8,128)}, u32[]{:S(2)}) copy-start(f32[1,16,16,256]{3,2,1,0:T(8,128)} %param.8) | copy-start | bytes 786436
  (2 other events, 1.6 us)

commit v2 on v1

--- a/solution.py
+++ b/solution.py
@@ -87,6 +87,17 @@
     return jnp.stack(out)
 
 
+def edges_for_partners(field, edge):
+    odd = lax.axis_index("tile") % 2 == 1
+    first, last = pack_edges(field, edge, True), pack_edges(field, edge, False)
+    return jnp.where(odd, first, last), jnp.where(odd, last, first)
+
+
+def sides_of(core, chip):
+    odd = lax.axis_index("tile") % 2 == 1
+    return jnp.where(odd, core, chip), jnp.where(odd, chip, core)
+
+
 def spread_edges(packed, edge):
     groups, rows, _ = packed.shape
     slots = LANES // edge
@@ -95,8 +106,9 @@
     return jnp.concatenate(parts, axis=0).reshape(slots * groups * rows, LANES)
 
 
-def beside(field, left, right, edge):
+def beside(field, core, chip, edge):
     members, rows, width = field.shape
+    left, right = sides_of(core, chip)
     return jnp.concatenate(
         [field.reshape(members * rows, width), spread_edges(left, edge), spread_edges(right, edge)], axis=1
     )
@@ -130,72 +142,91 @@
     return sum(x[:, i : i + LANES] for i in range(0, width, LANES))
 
 
-def prepare_kernel(source, precision, covered, to_next, to_previous, obs_weight):
+def edges_kernel(source, held, to_core, to_chip, sem):
+    copy = pltpu.make_async_copy(source, held, sem)
+    copy.start()
+    copy.wait()
+    to_core[...], to_chip[...] = edges_for_partners(held, REACH)
+
+
+def fetch_kernel(*refs):
+    count = (len(refs) - 2) // 2
+    copies = [pltpu.make_async_copy(refs[1 + i], refs[1 + count + i], refs[-1].at[i]) for i in range(count)]
+    for copy in copies:
+        copy.start()
+    for copy in copies:
+        copy.wait()
+
+
+def forward_kernel(source, core, chip, members_ref, column, row, increment):
+    members, levels, height, width = members_ref.shape
+    lhs = split(beside(source[...], core[...], chip[...], REACH))
+    smoothed = dot3(both(row), split(dot3(lhs, both(column)))).reshape(source.shape)
+    increment[: levels * height] = increments(members_ref, smoothed).reshape(levels * height, width)
+    increment[levels * height :] = (source[...] * source[...]).reshape(-1, 8, width).sum(axis=0)
+
+
+def weight_of(precision, covered):
     levels, height, width = precision.shape
     rows, blocks = covered.shape
-    to_next[...] = pack_edges(source, REACH, False)
-    to_previous[...] = pack_edges(source, REACH, True)
     spread = lax.broadcasted_iota(jnp.int32, (blocks, width), 1) // (width // blocks)
     spread = (spread == lax.broadcasted_iota(jnp.int32, (blocks, width), 0)).astype(BF16)
     mask = jnp.dot(covered[...].astype(F32).astype(BF16), spread, preferred_element_type=F32)
-    for v in range(levels):
-        for i in range(rows):
-            part = pl.ds(i * (height // rows), height // rows)
-            obs_weight[v, part] = precision[v, part] * mask[i : i + 1]
-
-
-def forward_kernel(source, left, right, members_ref, column, row, increment, norm):
-    lhs = split(beside(source[...], left[...], right[...], REACH))
-    smoothed = dot3(both(row), split(dot3(lhs, both(column))))
-    increment[...] = increments(members_ref, smoothed.reshape(source.shape))
-    norm[...] = folded(source[...] * source[...])
-
-
-def adjoint_kernel(i0, i1, i2, i3, obs_weight, members_ref, back, to_next, to_previous, norm):
+    tall = height // rows
+    mask = jnp.concatenate([jnp.broadcast_to(mask[i : i + 1], (tall, width)) for i in range(rows)], axis=0)
+    return precision[...] * mask
+
+
+def adjoint_kernel(
+    i0, i1, i2, i3, precision, covered, members_ref, back, to_core, to_chip, obs_weight, weighted, sums
+):
+    levels, height, width = precision.shape
+    total = (i0[...] + i1[...]) + (i2[...] + i3[...])
+    increment = total[: levels * height].reshape(levels, height, width)
+    obs_weight[...] = weight_of(precision, covered)
+    weighted[...] = obs_weight[...] * increment
+    sums[0] = folded(total[levels * height :])
+    sums[1] = folded(weighted[...] * increment)
+    back[...] = adjoint(members_ref, weighted)
+    to_core[...], to_chip[...] = edges_for_partners(back, 2 * REACH)
+
+
+def filtered(field, core, chip, edge, column, row):
+    lhs = split(beside(field[...], core[...], chip[...], edge))
+    return dot3(both(row), split(dot3(lhs, both(column)))).reshape(field.shape)
+
+
+def middle_kernel(back, core, chip, members_ref, column_twice, row_twice, increment):
+    smoothed = filtered(back, core, chip, 2 * REACH, column_twice, row_twice)
+    increment[...] = increments(members_ref, smoothed)
+
+
+def wide_filter_kernel(back, core, chip, column, row, out):
+    out[...] = filtered(back, core, chip, 2 * REACH, column, row)
+
+
+def filter_kernel(back, core, chip, column, row, out):
+    rows = back.shape[1]
+    out[...] = filtered(back, core[:, :rows], chip[:, :rows], REACH, column, row)
+
+
+def last_kernel(i0, i1, i2, i3, obs_weight, before, sums, members_ref, back, to_core, to_chip):
+    rows = back.shape[1]
     increment = (i0[...] + i1[...]) + (i2[...] + i3[...])
     weighted = obs_weight[...] * increment
-    norm[...] = folded(weighted * increment)
-    back[...] = adjoint(members_ref, weighted)
-    to_next[...] = pack_edges(back, 2 * REACH, False)
-    to_previous[...] = pack_edges(back, 2 * REACH, True)
-
-
-def middle_kernel(back, left, right, members_ref, norm_source, column, row, row_twice, first, second):
-    members, height, width = back.shape
-    levels = members_ref.shape[1]
-    lhs = split(beside(back[...], left[...], right[...], 2 * REACH))
-    both_filters = dot3(lhs, both(column))
-    z = dot3(both(row), split(both_filters[:, :width]))
-    smoothed = dot3(both(row_twice), split(both_filters[:, width:]))
-    first[...] = z.reshape(first.shape)
-    second[: levels * height] = increments(members_ref, smoothed.reshape(back.shape)).reshape(levels * height, width)
-    second[levels * height :] = jnp.concatenate([norm_source[...], folded(z * z)], axis=1)
-
-
-def last_kernel(i0, i1, i2, i3, obs_weight, members_ref, norm_mixed, back, to_next, to_previous, norms):
-    levels, height, width = obs_weight.shape
-    total = (i0[...] + i1[...]) + (i2[...] + i3[...])
-    increment = total[: levels * height].reshape(levels, height, width)
-    sums = total[levels * height :]
-    weighted = obs_weight[...] * increment
-    four = [sums[:, :LANES], norm_mixed[...], sums[:, LANES:], folded(weighted * increment)]
+    four = [sums[0], sums[1], folded(before[...] * increment), folded(weighted * increment)]
     row = lax.broadcasted_iota(jnp.int32, (8, LANES), 0)
     stacked = jnp.zeros((8, LANES), F32)
     for i, part in enumerate(four):
         stacked = jnp.where(row == i, jnp.sum(part, axis=0, keepdims=True), stacked)
-    norms[...] = stacked
     back[...] = adjoint(members_ref, weighted)
-    to_next[...] = pack_edges(back, REACH, False)
-    to_previous[...] = pack_edges(back, REACH, True)
-
-
-def filter_kernel(back, left, right, column, row, out):
-    lhs = split(beside(back[...], left[...], right[...], REACH))
-    out[...] = dot3(both(row), split(dot3(lhs, both(column)))).reshape(out.shape)
-
-
-def combine_kernel(norms, source, first, second, weights, residual):
-    total = jnp.sum(norms[...], axis=1, keepdims=True)
+    to_core[:, :rows], to_chip[:, :rows] = edges_for_partners(back, REACH)
+    to_core[0, rows:] = stacked
+    to_chip[0, rows:] = stacked
+
+
+def combine_kernel(own, other, source, first, second, weights, residual, held_weights, held_residual, sems):
+    total = jnp.sum(own[...] + other[...], axis=1, keepdims=True)
     bb, bg, gg, gh = (total[i : i + 1] for i in range(4))
     bg, gg, gh = bg / bb, gg / bb, gh / bb
     q = 1.0 / (1.0 + bg)
@@ -205,9 +236,19 @@
     square = d * d - 2.0 * d * q * bg + q * q * gg
     image = d * d * bg - 2.0 * d * q * gg + q * q * gh
     step = ratio / (square + image)
-    b, g, h = source[...], first[...], second[...]
-    weights[...] = (q + step * d) * b - (step * q) * g
-    residual[...] = (p - step * d) * b + (step * q - q - step * d) * g + (step * q) * h
+    members = source.shape[0]
+    pieces = sems.shape[1]
+    copies = []
+    for i in range(pieces):
+        part = pl.ds(i * (members // pieces), members // pieces)
+        b, g, h = source[part], first[part], second[part]
+        held_weights[part] = (q + step * d) * b - (step * q) * g
+        held_residual[part] = (p - step * d) * b + (step * q - q - step * d) * g + (step * q) * h
+        for k, (held, out) in enumerate(((held_weights, weights), (held_residual, residual))):
+            copies.append(pltpu.make_async_copy(held.at[part], out.at[part], sems.at[k, i]))
+            copies[-1].start()
+    for copy in copies:
+        copy.wait()
 
 
 def call(kernel, outs, *operands, cost=None):
@@ -223,6 +264,52 @@
     )(*operands)
 
 
+def in_hbm(array):
+    return pltpu.with_memory_space_constraint(array, pltpu.HBM)
+
+
+def held_edges(source):
+    members, height, width = source.shape
+    near = (members * REACH // LANES, height, LANES)
+    vmem = pl.BlockSpec(memory_space=pltpu.VMEM)
+    return pl.pallas_call(
+        edges_kernel,
+        out_shape=[pltpu.VMEM(source.shape, F32), pltpu.VMEM(near, F32), pltpu.VMEM(near, F32)],
+        in_specs=[pl.BlockSpec(memory_space=pltpu.HBM)],
+        out_specs=[vmem] * 3,
+        scratch_shapes=[pltpu.SemaphoreType.DMA],
+        compiler_params=pltpu.CompilerParams(vmem_limit_bytes=24 * 1024 * 1024),
+    )(in_hbm(source))
+
+
+def fetched(after, *arrays):
+    vmem = pl.BlockSpec(memory_space=pltpu.VMEM)
+    hbm = pl.BlockSpec(memory_space=pltpu.HBM)
+    size = sum(a.size * a.dtype.itemsize for a in arrays)
+    return pl.pallas_call(
+        fetch_kernel,
+        out_shape=[pltpu.VMEM(a.shape, a.dtype) for a in arrays],
+        in_specs=[vmem] + [hbm] * len(arrays),
+        out_specs=[vmem] * len(arrays),
+        scratch_shapes=[pltpu.SemaphoreType.DMA((len(arrays),))],
+        compiler_params=pltpu.CompilerParams(vmem_limit_bytes=24 * 1024 * 1024),
+        cost_estimate=pl.CostEstimate(flops=0, bytes_accessed=2 * size, transcendentals=0),
+    )(after, *map(in_hbm, arrays))
+
+
+def combined(own, other, source, first, second):
+    vmem = pl.BlockSpec(memory_space=pltpu.VMEM)
+    hbm = pl.BlockSpec(memory_space=pltpu.HBM)
+    return pl.pallas_call(
+        combine_kernel,
+        out_shape=[jax.ShapeDtypeStruct(source.shape, F32)] * 2,
+        in_specs=[vmem] * 5,
+        out_specs=[hbm] * 2,
+        scratch_shapes=[pltpu.VMEM(source.shape, F32)] * 2 + [pltpu.SemaphoreType.DMA((2, 4))],
+        compiler_params=pltpu.CompilerParams(vmem_limit_bytes=24 * 1024 * 1024),
+    )(own, other, source, first, second)
+
+
 def from_both_sides(to_next, to_previous, axis):
     count = lax.axis_size(axis)
     left = lax.ppermute(to_next, axis, [(i, (i + 1) % count) for i in range(count)])
@@ -230,18 +317,19 @@
     return left, right
 
 
+def from_core(value):
+    count = lax.axis_size("tile")
+    return lax.ppermute(value, "tile", [(i, i ^ 1) for i in range(count)])
+
+
+def from_chip(value):
+    count = lax.axis_size("tile")
+    return lax.ppermute(value, "tile", [(i, (i + 1) % count if i % 2 else (i - 1) % count) for i in range(count)])
+
+
 def from_all(value, axis):
     count = lax.axis_size(axis)
     return [value] + [lax.ppermute(value, axis, [(i, i ^ k) for i in range(count)]) for k in range(1, count)]
-
-
-def summed(value, axis):
-    count = lax.axis_size(axis)
-    step = 1
-    while step < count:
-        value = value + lax.ppermute(value, axis, [(i, i ^ step) for i in range(count)])
-        step *= 2
-    return value
 
 
 def one_tile_row(right_side, perturbations, precision, covered):
@@ -252,41 +340,42 @@
     field = (members, height, width)
     near = (members * REACH // LANES, height, LANES)
     far = (2 * members * REACH // LANES, height, LANES)
-    small = (8, LANES)
-    column = halves(column_matrix(taps, width, REACH))
-    column_wide = halves(
-        np.concatenate(
-            [column_matrix(taps, width, 2 * REACH), column_matrix(twice, width, 2 * REACH)], axis=1
-        )
-    )
-    row = halves(row_matrix(taps, height, members, 1))
-    row_twice = halves(row_matrix(taps, height, members, 2))
-
-    to_next, to_previous, obs_weight = call(
-        prepare_kernel, [near, near, precision.shape[1:]], source, precision[0], covered[0]
-    )
-    left, right = from_both_sides(to_next, to_previous, "tile")
-    increment, norm_source = call(
-        forward_kernel, [(levels, height, width), small], source, left, right, members_data, column, row
+    plane = (levels, height, width)
+    constants = [
+        halves(column_matrix(taps, width, REACH)),
+        halves(row_matrix(taps, height, members, 1)),
+        halves(column_matrix(taps, width, 2 * REACH)),
+        halves(column_matrix(twice, width, 2 * REACH)),
+        halves(row_matrix(taps, height, members, 2)),
+    ]
+
+    source, to_core, to_chip = held_edges(source)
+    core, chip = from_core(to_core), from_chip(to_chip)
+    members_data, column, row = fetched(to_core, members_data, *constants[:2])
+    (increment,) = call(
+        forward_kernel, [(levels * height + 8, width)], source, core, chip, members_data, column, row
     )
     parts = from_all(increment, "mem")
-    back, to_next, to_previous, norm_mixed = call(
-        adjoint_kernel, [field, far, far, small], *parts, obs_weight, members_data
+    precision, covered, column_far, column_twice, row_twice = fetched(increment, precision[0], covered[0], *constants[2:])
+    back, to_core, to_chip, obs_weight, weighted, sums = call(
+        adjoint_kernel, [field, far, far, plane, plane, (2, 8, LANES)], *parts, precision, covered, members_data
     )
-    left, right = from_both_sides(to_next, to_previous, "tile")
-    first, second = call(
-        middle_kernel,
-        [field, (levels * height + 8, width)],
-        back, left, right, members_data, norm_source, column_wide, row, row_twice,
+    core, chip = from_core(to_core), from_chip(to_chip)
+    (increment,) = call(middle_kernel, [plane], back, core, chip, members_data, column_twice, row_twice)
+    parts = from_all(increment, "mem")
+    (first,) = call(wide_filter_kernel, [field], back, core, chip, column_far, row)
+    ended = (1, height + 8, LANES)
+    back, to_core, to_chip = call(
+        last_kernel, [field, ended, ended], *parts, obs_weight, weighted, sums, members_data
     )
-    parts = from_all(second, "mem")
-    back, to_next, to_previous, norms = call(
-        last_kernel, [field, near, near, small], *parts, obs_weight, members_data, norm_mixed
-    )
-    left, right = from_both_sides(to_next, to_previous, "tile")
-    (second,) = call(filter_kernel, [field], back, left, right, column, row)
-    norms = summed(norms, "tile")
-    weights, residual = call(combine_kernel, [field, field], norms, source, first, second)
+    core = from_core(to_core)
+    to_chip = jnp.concatenate([to_chip[:, :height], to_chip[:, height:] + core[:, height:]], axis=1)
+    chip = from_chip(to_chip)
+    norms = to_chip[0, height:] + chip[0, height:]
+    count = lax.axis_size("tile")
+    others = lax.ppermute(norms, "tile", [(i, (i + count // 2) % count) for i in range(count)])
+    (second,) = call(filter_kernel, [field], back, core, chip, column, row)
+    weights, residual = combined(norms, others, source, first, second)
     return weights[None], residual[None]
 
 

time: 48.2 us -> 43.4 us (0.900)
  local copies, waits for them, and re-layouts: 4.72 us -> 0.01 us
  Pallas kernels: 4.33 us -> 8.73 us
  starting transfers between devices: 19 us -> 16.1 us
  waiting for transfers between devices: 19.1 us -> 17.6 us
    pallas_call x0 -> x4, Pallas kernels: none -> 4.85 us  [the longest x2 2.75 us: fetched(): pl.pallas_call(fetch_kernel, out_shape=[pltpu.VMEM(a.shape, a.dtype) for...]
    unnamed x22 -> x0, local copies, waits for them, and re-layouts: 4.72 us -> none
    ppermute x9 -> x7, starting transfers between devices: 11.9 us -> 8.99 us  [the longest x3 8.84 us: from_chip(): lax.ppermute(value, 'tile', [(i, (i + 1) % count if i % 2 else (i - 1) %...]
    ppermute x6, waiting for transfers between devices: 8.96 us -> 7.83 us  [from_all(): lax.ppermute(value, axis, [(i, i ^ k) for i in range(count)])]
    pallas_call x7 -> x6, Pallas kernels: 4.33 us -> 3.88 us  [call(): pl.pallas_call(kernel, out_shape=shapes, in_specs=[vmem] * len(operands),...]
    ppermute x9 -> x7, waiting for transfers between devices: 10.1 us -> 9.75 us  [the longest x3 5.66 us: from_chip(): lax.ppermute(value, 'tile', [(i, (i + 1) % count if i % 2 else (i - 1) %...]
  transfers between devices with their start and end apart: 15 -> 13, of which waited for: 11 -> 10; matrix products, arithmetic and copies ran while one was open for 0% -> 0% of each run, Pallas kernels for 2% -> 10%
where the time goes in v2:
time: 43.4 us; the launch traced here: 43.2 us
  waiting for transfers between devices  17.6 us (41%)
  starting transfers between devices  16.1 us (37%)
  Pallas kernels  8.73 us (20%)
  between operations  0.74 us (2%)
    ppermute x3, starting transfers between devices, from_chip(): lax.ppermute(value, 'tile', [(i, (i + 1) % count if i % 2 else (i - 1) %...  8.84 us
    ppermute x6, waiting for transfers between devices, from_all(): lax.ppermute(value, axis, [(i, i ^ k) for i in range(count)])  7.83 us
    ppermute x6, starting transfers between devices, from_all(): lax.ppermute(value, axis, [(i, i ^ k) for i in range(count)])  7.14 us
    ppermute x3, waiting for transfers between devices, from_chip(): lax.ppermute(value, 'tile', [(i, (i + 1) % count if i % 2 else (i - 1) %...  5.66 us
    pallas_call x6, Pallas kernels, call(): pl.pallas_call(kernel, out_shape=shapes, in_specs=[vmem] * len(operands),...  3.88 us
    ppermute x1, waiting for transfers between devices, one_tile_row(): lax.ppermute(norms, 'tile', [(i, (i + count // 2) % count) for i in range...  2.94 us
    pallas_call x2, Pallas kernels, fetched(): pl.pallas_call(fetch_kernel, out_shape=[pltpu.VMEM(a.shape, a.dtype) for...  2.75 us
    ppermute x3, waiting for transfers between devices, from_core(): return lax.ppermute(value, 'tile', [(i, i ^ 1) for i in range(count)])  1.16 us
  transfers between devices with their start and end apart: 13, of which 10 were waited for; matrix products, arithmetic and copies ran while one was open for 0% of the time, Pallas kernels for 10%

profile of v2, /device:TPU:0, one launch (start us, length us, event | category | flops | bytes accessed | tf_op | source)
XLA Modules:
  0.0 43.2 jit_solution(6897961695560154828)
XLA Ops:
  0.6 1.1 %shard_map.104 = (f32[16,16,256]{2,1,0:T(8,128)S(1)}, f32[1,16,128]{2,1,0:T(8,128)S(1)}, f32[1,16,128]{2,1,0:T(8,128)S(1)}) custom-call(f32[16,16,256]{2,1,0:T(8,128)} %bitcast.9), custom_call_target="tpu_custom_call" | custom-call | tf_op jit(solution)/shard_map/pallas_call | solution.py:275
  1.7 4.6 %collective-permute-start.1 = (f32[1,16,128]{2,1,0:T(8,128)S(1)}, f32[1,16,128]{2,1,0:T(8,128)S(1)}, u32[]{:S(2)}, u32[]{:S(2)}) collective-permute-start(f32[1,16,128]{2,1,0:T(8,128)S(1)} %get-tuple-element.26), channel_id=1, source_target_pairs={{0,28},{4,8},{8,4},{12,16},{16,12},{20,24},{24,20},{28,0},{1,29},{... | collective-permute-start | bytes 24584 | tf_op jit(solution)/shard_map/ppermute | solution.py:327
  6.3 1.4 %shard_map.105 = (bf16[16,6,16,256]{3,2,1,0:T(8,128)(2,1)S(1)}, bf16[2,512,256]{2,1,0:T(8,128)(2,1)S(1)}, bf16[2,256,256]{2,1,0:T(8,128)(2,1)S(1)}) custom-call(f32[1,16,128]{2,1,0:T(8,128)S(1)} %get-tuple-element.25.refs_0_, bf16[16,6,16,256]{3,2,1,0:T(8,128)(2,1)} %bitcast.8, bf16[2,512,256]{2,1,0:T(8,128)(2,1)} %constant.10.clone.refs_2_, ...), custom_call_target="tpu_custom_call" | custom-call | bytes 3145728 | tf_op jit(solution)/shard_map/pallas_call | solution.py:289
  7.7 0.9 %shard_map.106.refs_0_.i0 = f32[104,256]{1,0:T(8,128)S(1)} custom-call(f32[16,16,256]{2,1,0:T(8,128)S(1)} %get-tuple-element.24.source, f32[1,16,128]{2,1,0:T(8,128)S(1)} %collective-permute-done.core, f32[1,16,128]{2,1,0:T(8,128)S(1)} %collective-permute-done.1.chip, bf16[16,6,16,256]{3,2,1,0:T(8,128)(2,1)S(1)} %get-tuple-element.27.members_ref, ...), custom_call_target="tpu_custom_call" | custom-call | tf_op jit(solution)/shard_map/pallas_call | solution.py:257
  8.6 2.9 %collective-permute-start.4 = (f32[104,256]{1,0:T(8,128)S(1)}, f32[104,256]{1,0:T(8,128)S(1)}, u32[]{:S(2)}, u32[]{:S(2)}) collective-permute-start(f32[104,256]{1,0:T(8,128)S(1)} %shard_map.106.refs_0_.i0), channel_id=1, source_target_pairs={{0,3},{1,2},{2,1},{3,0},{4,7},{5,6},{6,5},{7,4},{8,11},{9,10},{10,... | collective-permute-start | bytes 319496 | tf_op jit(solution)/shard_map/ppermute | solution.py:332
  11.5 0.5 %collective-permute-start.3 = (f32[104,256]{1,0:T(8,128)S(1)}, f32[104,256]{1,0:T(8,128)S(1)}, u32[]{:S(2)}, u32[]{:S(2)}) collective-permute-start(f32[104,256]{1,0:T(8,128)S(1)} %shard_map.106.refs_0_.i0), channel_id=1, source_target_pairs={{0,2},{1,3},{2,0},{3,1},{4,6},{5,7},{6,4},{7,5},{8,10},{9,11},{10,... | collective-permute-start | bytes 319496 | tf_op jit(solution)/shard_map/ppermute | solution.py:332
  12.2 1.4 %shard_map.107 = (f32[6,16,256]{2,1,0:T(8,128)S(1)}, s32[2,16]{1,0:T(2,128)S(1)}, bf16[2,512,256]{2,1,0:T(8,128)(2,1)S(1)}, bf16[2,512,256]{2,1,0:T(8,128)(2,1)S(1)}, bf16[2,256,256]{2,1,0:T(8,128)(2,1)S(1)}) custom-call(f32[104,256]{1,0:T(8,128)S(1)} %shard_map.106.refs_0_.i0, f32[6,16,256]{2,1,0:T(8,128)} %bitcast.10, s32[2,16]{1,0:T(2,128)} %bitcast.11, ...), custom_call_target="tpu_custom_call" | custom-call | bytes 2818304 | tf_op jit(solution)/shard_map/pallas_call | solution.py:289
  13.5 1.5 %collective-permute-done.4.i3 = f32[104,256]{1,0:T(8,128)S(1)} collective-permute-done((f32[104,256]{1,0:T(8,128)S(1)}, f32[104,256]{1,0:T(8,128)S(1)}, u32[]{:S(2)}, u32[]{:S(2)}) %collective-permute-start.4) | collective-permute-done | bytes 106528 | tf_op jit(solution)/shard_map/ppermute | solution.py:332
  15.0 2.2 %collective-permute-done.3.i2 = f32[104,256]{1,0:T(8,128)S(1)} collective-permute-done((f32[104,256]{1,0:T(8,128)S(1)}, f32[104,256]{1,0:T(8,128)S(1)}, u32[]{:S(2)}, u32[]{:S(2)}) %collective-permute-start.3) | collective-permute-done | bytes 106528 | tf_op jit(solution)/shard_map/ppermute | solution.py:332
  17.7 2.7 %collective-permute-start.6 = (f32[2,16,128]{2,1,0:T(8,128)S(1)}, f32[2,16,128]{2,1,0:T(8,128)S(1)}, u32[]{:S(2)}, u32[]{:S(2)}) collective-permute-start(f32[2,16,128]{2,1,0:T(8,128)S(1)} %get-tuple-element.34), channel_id=1, source_target_pairs={{0,28},{4,8},{8,4},{12,16},{16,12},{20,24},{24,20},{28,0},{1,29},{... | collective-permute-start | bytes 49160 | tf_op jit(solution)/shard_map/ppermute | solution.py:327
  20.4 2.3 %collective-permute-done.6.chip = f32[2,16,128]{2,1,0:T(8,128)S(1)} collective-permute-done((f32[2,16,128]{2,1,0:T(8,128)S(1)}, f32[2,16,128]{2,1,0:T(8,128)S(1)}, u32[]{:S(2)}, u32[]{:S(2)}) %collective-permute-start.6) | collective-permute-done | bytes 16416 | tf_op jit(solution)/shard_map/ppermute | solution.py:327
  22.7 0.9 %shard_map.109.i0 = f32[6,16,256]{2,1,0:T(8,128)S(1)} custom-call(f32[16,16,256]{2,1,0:T(8,128)S(1)} %get-tuple-element.32.back, f32[2,16,128]{2,1,0:T(8,128)S(1)} %collective-permute-done.5.core, f32[2,16,128]{2,1,0:T(8,128)S(1)} %collective-permute-done.6.chip, bf16[16,6,16,256]{3,2,1,0:T(8,128)(2,1)S(1)} %get-tuple-element.27.members_ref, ...), custom_call_target="tpu_custom_call" | custom-call | tf_op jit(solution)/shard_map/pallas_call | solution.py:257
  23.6 1.8 %collective-permute-start.9 = (f32[6,16,256]{2,1,0:T(8,128)S(1)}, f32[6,16,256]{2,1,0:T(8,128)S(1)}, u32[]{:S(2)}, u32[]{:S(2)}) collective-permute-start(f32[6,16,256]{2,1,0:T(8,128)S(1)} %shard_map.109.i0), channel_id=1, source_target_pairs={{0,3},{1,2},{2,1},{3,0},{4,7},{5,6},{6,5},{7,4},{8,11},{9,10},{10,... | collective-permute-start | bytes 294920 | tf_op jit(solution)/shard_map/ppermute | solution.py:332
  25.3 1.3 %collective-permute-start.8 = (f32[6,16,256]{2,1,0:T(8,128)S(1)}, f32[6,16,256]{2,1,0:T(8,128)S(1)}, u32[]{:S(2)}, u32[]{:S(2)}) collective-permute-start(f32[6,16,256]{2,1,0:T(8,128)S(1)} %shard_map.109.i0), channel_id=1, source_target_pairs={{0,2},{1,3},{2,0},{3,1},{4,6},{5,7},{6,4},{7,5},{8,10},{9,11},{10,... | collective-permute-start | bytes 294920 | tf_op jit(solution)/shard_map/ppermute | solution.py:332
  27.1 2.5 %collective-permute-done.9.i3 = f32[6,16,256]{2,1,0:T(8,128)S(1)} collective-permute-done((f32[6,16,256]{2,1,0:T(8,128)S(1)}, f32[6,16,256]{2,1,0:T(8,128)S(1)}, u32[]{:S(2)}, u32[]{:S(2)}) %collective-permute-start.9) | collective-permute-done | bytes 98336 | tf_op jit(solution)/shard_map/ppermute | solution.py:332
  29.7 0.9 %collective-permute-done.8.i2 = f32[6,16,256]{2,1,0:T(8,128)S(1)} collective-permute-done((f32[6,16,256]{2,1,0:T(8,128)S(1)}, f32[6,16,256]{2,1,0:T(8,128)S(1)}, u32[]{:S(2)}, u32[]{:S(2)}) %collective-permute-start.8) | collective-permute-done | bytes 98336 | tf_op jit(solution)/shard_map/ppermute | solution.py:332
  30.6 0.7 %collective-permute-done.7.i1 = f32[6,16,256]{2,1,0:T(8,128)S(1)} collective-permute-done((f32[6,16,256]{2,1,0:T(8,128)S(1)}, f32[6,16,256]{2,1,0:T(8,128)S(1)}, u32[]{:S(2)}, u32[]{:S(2)}) %collective-permute-start.7) | collective-permute-done | bytes 98336 | tf_op jit(solution)/shard_map/ppermute | solution.py:332
  31.6 1.2 %collective-permute-done.10.core = f32[1,24,128]{2,1,0:T(8,128)S(1)} collective-permute-done((f32[1,24,128]{2,1,0:T(8,128)S(1)}, f32[1,24,128]{2,1,0:T(8,128)S(1)}, u32[]{:S(2)}, u32[]{:S(2)}) %collective-permute-start.10) | collective-permute-done | bytes 12320 | tf_op jit(solution)/shard_map/ppermute | solution.py:322
  32.8 1.6 %collective-permute-start.11 = (f32[1,24,128]{2,1,0:T(8,128)S(1)}, f32[1,24,128]{2,1,0:T(8,128)S(1)}, u32[]{:S(2)}, u32[]{:S(2)}) collective-permute-start(f32[1,24,128]{2,1,0:T(8,128)S(1)} %pad_maximum_fusion), channel_id=1, source_target_pairs={{0,28},{4,8},{8,4},{12,16},{16,12},{20,24},{24,20},{28,0},{1,29},{... | collective-permute-start | bytes 36872 | tf_op jit(solution)/shard_map/ppermute | solution.py:327
  34.3 3.3 %collective-permute-done.11.chip = f32[1,24,128]{2,1,0:T(8,128)S(1)} collective-permute-done((f32[1,24,128]{2,1,0:T(8,128)S(1)}, f32[1,24,128]{2,1,0:T(8,128)S(1)}, u32[]{:S(2)}, u32[]{:S(2)}) %collective-permute-start.11) | collective-permute-done | bytes 12320 | tf_op jit(solution)/shard_map/ppermute | solution.py:327
  37.7 0.8 %shard_map.111.first = f32[16,16,256]{2,1,0:T(8,128)S(1)} custom-call(f32[16,16,256]{2,1,0:T(8,128)S(1)} %get-tuple-element.32.back, f32[2,16,128]{2,1,0:T(8,128)S(1)} %collective-permute-done.5.core, f32[2,16,128]{2,1,0:T(8,128)S(1)} %collective-permute-done.6.chip, bf16[2,512,256]{2,1,0:T(8,128)(2,1)S(1)} %get-tuple-element.42.column, ...), custom_call_target="tpu_custom_call" | custom-call | tf_op jit(solution)/shard_map/pallas_call | solution.py:257
  38.5 0.8 %shard_map.112.second = f32[16,16,256]{2,1,0:T(8,128)S(1)} custom-call(f32[16,16,256]{2,1,0:T(8,128)S(1)} %get-tuple-element.43.back, f32[1,24,128]{2,1,0:T(8,128)S(1)} %collective-permute-done.10.core, f32[1,24,128]{2,1,0:T(8,128)S(1)} %collective-permute-done.11.chip, bf16[2,512,256]{2,1,0:T(8,128)(2,1)S(1)} %get-tuple-element.28.column, ...), custom_call_target="tpu_custom_call" | custom-call | tf_op jit(solution)/shard_map/pallas_call | solution.py:257
  39.2 2.9 %collective-permute-done.12.other = f32[8,128]{1,0:T(8,128)S(1)} collective-permute-done((f32[8,128]{1,0:T(8,128)S(1)}, f32[8,128]{1,0:T(8,128)S(1)}, u32[]{:S(2)}, u32[]{:S(2)}) %collective-permute-start.12) | collective-permute-done | bytes 4128 | tf_op jit(solution)/shard_map/ppermute | solution.py:376
  42.2 1.0 %shard_map.113 = (f32[16,16,256]{2,1,0:T(8,128)}, f32[16,16,256]{2,1,0:T(8,128)}) custom-call(f32[8,128]{1,0:T(8,128)S(1)} %fusion.own, f32[8,128]{1,0:T(8,128)S(1)} %collective-permute-done.12.other, f32[16,16,256]{2,1,0:T(8,128)S(1)} %get-tuple-element.24.source, f32[16,16,256]{2,1,0:T(8,128)S(1)} %shard_map.111.first, f32[16,16,256]{2,1,0:T(8,128)S(1)} %shard_map.112.second), custom_call_target="tpu_custom_call" | custom-call | tf_op jit(solution)/shard_map/pallas_call | solution.py:303
  (16 shorter events, 1.4 us)
Async XLA Ops:
  1.7 5.9 %collective-permute-start.1 = (f32[1,16,128]{2,1,0:T(8,128)S(1)}, f32[1,16,128]{2,1,0:T(8,128)S(1)}, u32[]{:S(2)}, u32[]{:S(2)}) collective-permute-start(f32[1,16,128]{2,1,0:T(8,128)S(1)} %get-tuple-element.26), channel_id=1, source_target_pairs={{0,28},{4,8},{8,4},{12,16},{16,12},{20,24},{24,20},{28,0},{1,29},{... | collective-permute-start | bytes 24584 | tf_op jit(solution)/shard_map/ppermute | solution.py:327
  6.3 1.4 %collective-permute-start = (f32[1,16,128]{2,1,0:T(8,128)S(1)}, f32[1,16,128]{2,1,0:T(8,128)S(1)}, u32[]{:S(2)}, u32[]{:S(2)}) collective-permute-start(f32[1,16,128]{2,1,0:T(8,128)S(1)} %get-tuple-element.25.refs_0_), channel_id=1, source_target_pairs={{0,4},{4,0},{8,12},{12,8},{16,20},{20,16},{24,28},{28,24},{1,5},{5... | collective-permute-start | bytes 24584 | tf_op jit(solution)/shard_map/ppermute | solution.py:322
  8.6 6.5 %collective-permute-start.4 = (f32[104,256]{1,0:T(8,128)S(1)}, f32[104,256]{1,0:T(8,128)S(1)}, u32[]{:S(2)}, u32[]{:S(2)}) collective-permute-start(f32[104,256]{1,0:T(8,128)S(1)} %shard_map.106.refs_0_.i0), channel_id=1, source_target_pairs={{0,3},{1,2},{2,1},{3,0},{4,7},{5,6},{6,5},{7,4},{8,11},{9,10},{10,... | collective-permute-start | bytes 319496 | tf_op jit(solution)/shard_map/ppermute | solution.py:332
  11.5 5.7 %collective-permute-start.3 = (f32[104,256]{1,0:T(8,128)S(1)}, f32[104,256]{1,0:T(8,128)S(1)}, u32[]{:S(2)}, u32[]{:S(2)}) collective-permute-start(f32[104,256]{1,0:T(8,128)S(1)} %shard_map.106.refs_0_.i0), channel_id=1, source_target_pairs={{0,2},{1,3},{2,0},{3,1},{4,6},{5,7},{6,4},{7,5},{8,10},{9,11},{10,... | collective-permute-start | bytes 319496 | tf_op jit(solution)/shard_map/ppermute | solution.py:332
  12.0 5.2 %collective-permute-start.2 = (f32[104,256]{1,0:T(8,128)S(1)}, f32[104,256]{1,0:T(8,128)S(1)}, u32[]{:S(2)}, u32[]{:S(2)}) collective-permute-start(f32[104,256]{1,0:T(8,128)S(1)} %shard_map.106.refs_0_.i0), channel_id=1, source_target_pairs={{0,1},{1,0},{2,3},{3,2},{4,5},{5,4},{6,7},{7,6},{8,9},{9,8},{10,11... | collective-permute-start | bytes 319496 | tf_op jit(solution)/shard_map/ppermute | solution.py:332
  17.6 2.8 %collective-permute-start.5 = (f32[2,16,128]{2,1,0:T(8,128)S(1)}, f32[2,16,128]{2,1,0:T(8,128)S(1)}, u32[]{:S(2)}, u32[]{:S(2)}) collective-permute-start(f32[2,16,128]{2,1,0:T(8,128)S(1)} %get-tuple-element.33), channel_id=1, source_target_pairs={{0,4},{4,0},{8,12},{12,8},{16,20},{20,16},{24,28},{28,24},{1,5},{5... | collective-permute-start | bytes 49160 | tf_op jit(solution)/shard_map/ppermute | solution.py:322
  17.7 5.0 %collective-permute-start.6 = (f32[2,16,128]{2,1,0:T(8,128)S(1)}, f32[2,16,128]{2,1,0:T(8,128)S(1)}, u32[]{:S(2)}, u32[]{:S(2)}) collective-permute-start(f32[2,16,128]{2,1,0:T(8,128)S(1)} %get-tuple-element.34), channel_id=1, source_target_pairs={{0,28},{4,8},{8,4},{12,16},{16,12},{20,24},{24,20},{28,0},{1,29},{... | collective-permute-start | bytes 49160 | tf_op jit(solution)/shard_map/ppermute | solution.py:327
  23.6 6.1 %collective-permute-start.9 = (f32[6,16,256]{2,1,0:T(8,128)S(1)}, f32[6,16,256]{2,1,0:T(8,128)S(1)}, u32[]{:S(2)}, u32[]{:S(2)}) collective-permute-start(f32[6,16,256]{2,1,0:T(8,128)S(1)} %shard_map.109.i0), channel_id=1, source_target_pairs={{0,3},{1,2},{2,1},{3,0},{4,7},{5,6},{6,5},{7,4},{8,11},{9,10},{10,... | collective-permute-start | bytes 294920 | tf_op jit(solution)/shard_map/ppermute | solution.py:332
  25.3 5.2 %collective-permute-start.8 = (f32[6,16,256]{2,1,0:T(8,128)S(1)}, f32[6,16,256]{2,1,0:T(8,128)S(1)}, u32[]{:S(2)}, u32[]{:S(2)}) collective-permute-start(f32[6,16,256]{2,1,0:T(8,128)S(1)} %shard_map.109.i0), channel_id=1, source_target_pairs={{0,2},{1,3},{2,0},{3,1},{4,6},{5,7},{6,4},{7,5},{8,10},{9,11},{10,... | collective-permute-start | bytes 294920 | tf_op jit(solution)/shard_map/ppermute | solution.py:332
  26.6 4.6 %collective-permute-start.7 = (f32[6,16,256]{2,1,0:T(8,128)S(1)}, f32[6,16,256]{2,1,0:T(8,128)S(1)}, u32[]{:S(2)}, u32[]{:S(2)}) collective-permute-start(f32[6,16,256]{2,1,0:T(8,128)S(1)} %shard_map.109.i0), channel_id=1, source_target_pairs={{0,1},{1,0},{2,3},{3,2},{4,5},{5,4},{6,7},{7,6},{8,9},{9,8},{10,11... | collective-permute-start | bytes 294920 | tf_op jit(solution)/shard_map/ppermute | solution.py:332
  31.5 1.2 %collective-permute-start.10 = (f32[1,24,128]{2,1,0:T(8,128)S(1)}, f32[1,24,128]{2,1,0:T(8,128)S(1)}, u32[]{:S(2)}, u32[]{:S(2)}) collective-permute-start(f32[1,24,128]{2,1,0:T(8,128)S(1)} %get-tuple-element.41), channel_id=1, source_target_pairs={{0,4},{4,0},{8,12},{12,8},{16,20},{20,16},{24,28},{28,24},{1,5},{5... | collective-permute-start | bytes 36872 | tf_op jit(solution)/shard_map/ppermute | solution.py:322
  32.8 4.9 %collective-permute-start.11 = (f32[1,24,128]{2,1,0:T(8,128)S(1)}, f32[1,24,128]{2,1,0:T(8,128)S(1)}, u32[]{:S(2)}, u32[]{:S(2)}) collective-permute-start(f32[1,24,128]{2,1,0:T(8,128)S(1)} %pad_maximum_fusion), channel_id=1, source_target_pairs={{0,28},{4,8},{8,4},{12,16},{16,12},{20,24},{24,20},{28,0},{1,29},{... | collective-permute-start | bytes 36872 | tf_op jit(solution)/shard_map/ppermute | solution.py:327
  37.7 4.5 %collective-permute-start.12 = (f32[8,128]{1,0:T(8,128)S(1)}, f32[8,128]{1,0:T(8,128)S(1)}, u32[]{:S(2)}, u32[]{:S(2)}) collective-permute-start(f32[8,128]{1,0:T(8,128)S(1)} %fusion.own), channel_id=1, source_target_pairs={{0,16},{4,20},{8,24},{12,28},{16,0},{20,4},{24,8},{28,12},{1,17},{... | collective-permute-start | bytes 12296 | tf_op jit(solution)/shard_map/ppermute | solution.py:376

commit v3 on v2

--- a/solution.py
+++ b/solution.py
@@ -12,6 +12,7 @@
 ITERS = 2
 TCOLS = 8
 REACH = 8
+EDGE = 2 * REACH
 LANES = 128
 F32 = jnp.float32
 BF16 = jnp.bfloat16
@@ -48,6 +49,12 @@
 def row_matrix(taps, height, members, times):
     one = band(taps, np.arange(height), np.arange(height))
     return np.kron(np.eye(members), np.linalg.matrix_power(one, times))
+
+
+def edge_matrix(taps, edge):
+    inner = np.arange(edge)
+    sides = (band(taps, inner - edge, inner), band(taps, inner + edge, inner))
+    return np.stack([halves(np.kron(np.eye(LANES // edge), side)) for side in sides])
 
 
 def split(x):
@@ -146,7 +153,7 @@
     copy = pltpu.make_async_copy(source, held, sem)
     copy.start()
     copy.wait()
-    to_core[...], to_chip[...] = edges_for_partners(held, REACH)
+    to_core[...], to_chip[...] = edges_for_partners(held, EDGE)
 
 
 def fetch_kernel(*refs):
@@ -158,12 +165,80 @@
         copy.wait()
 
 
-def forward_kernel(source, core, chip, members_ref, column, row, increment):
+def own_columns(field, column, row):
+    members, height, width = field.shape
+    lhs = split(field[...].reshape(members * height, width))
+    return dot3(both(row), split(dot3(lhs, both(column)))).reshape(field.shape)
+
+
+def tap_at(gap, inside):
+    scale = 1.0 / np.sqrt(np.sum(np.exp(-(np.arange(-REACH, REACH + 1.0) ** 2) / 16.0)))
+    square = (gap * gap).astype(F32)
+    return jnp.where(inside & (jnp.abs(gap) <= REACH), jnp.exp(square * (-1.0 / 32.0)) * scale, 0.0)
+
+
+def gaps(rows, columns):
+    shape = (rows, columns)
+    down, across = (lax.broadcasted_iota(jnp.int32, shape, i) for i in range(2))
+    return down, across, down - across
+
+
+def kept(ref, matrix):
+    ref[0], ref[1] = split(matrix)
+
+
+def first_kernel(source, after, members_hbm, increment, members_ref, edge_members, edge, thin, sem):
+    copy = pltpu.make_async_copy(members_hbm, members_ref, sem)
+    copy.start()
     members, levels, height, width = members_ref.shape
-    lhs = split(beside(source[...], core[...], chip[...], REACH))
-    smoothed = dot3(both(row), split(dot3(lhs, both(column)))).reshape(source.shape)
+    _, _, gap = gaps(width, width)
+    column = split(tap_at(gap, True))
+    down, across, gap = gaps(members * height, members * height)
+    row = split(tap_at(gap, down // height == across // height))
+    lhs = split(source[...].reshape(members * height, width))
+    smoothed = dot3(row, split(dot3(lhs, column))).reshape(source.shape)
+    increment[levels * height :] = (source[...] * source[...]).reshape(-1, 8, width).sum(axis=0)
+    down, across, gap = gaps(LANES, LANES)
+    same = down // EDGE == across // EDGE
+    kept(edge.at[0], tap_at(gap - EDGE, same))
+    kept(edge.at[1], tap_at(gap + EDGE, same))
+    down, across, gap = gaps(*thin.shape[1:])
+    kept(thin, tap_at(gap, down // height == across // height))
+    copy.wait()
     increment[: levels * height] = increments(members_ref, smoothed).reshape(levels * height, width)
-    increment[levels * height :] = (source[...] * source[...]).reshape(-1, 8, width).sum(axis=0)
+    for v in range(levels):
+        level = members_ref[:, v].astype(F32)
+        edge_members[0, :, v] = pack_edges(level, EDGE, True)
+        edge_members[1, :, v] = pack_edges(level, EDGE, False)
+
+
+def second_kernel(back, column, row, members_ref, increment):
+    increment[...] = increments(members_ref, own_columns(back, column, row))
+
+
+def edge_kernel(inside, core, chip, edge_members, edge, thin, out):
+    groups, height, _ = core.shape
+    levels = edge_members.shape[2]
+    width = out.shape[-1]
+    halo = jnp.concatenate([side.reshape(groups * height, LANES) for side in sides_of(core[...], chip[...])], axis=1)
+    halo = dot3(both(thin), split(halo))
+    lane = lane_of((levels, height, LANES))
+    out[...] = inside[...]
+    for side in range(2):
+        part = halo[:, :LANES] if side == 0 else halo[:, LANES:]
+        part = dot3(split(part), (edge[side, 0], edge[side, 1])).reshape(groups, 1, height, LANES)
+        total = jnp.sum(edge_members[side] * part, axis=0).reshape(levels * height, LANES)
+        step = EDGE
+        while step < LANES:
+            total = total + pltpu.roll(total, step, 1)
+            step *= 2
+        total = total.reshape(levels, height, LANES)
+        if side == 0:
+            span, mask = pl.ds(0, LANES), lane < EDGE
+        else:
+            span, mask = pl.ds(width - LANES, LANES), lane >= LANES - EDGE
+        rows = pl.ds(0, levels * height)
+        out[rows, span] = out[rows, span] + jnp.where(mask, total, 0.0).reshape(levels * height, LANES)
 
 
 def weight_of(precision, covered):
@@ -188,31 +263,19 @@
     sums[0] = folded(total[levels * height :])
     sums[1] = folded(weighted[...] * increment)
     back[...] = adjoint(members_ref, weighted)
-    to_core[...], to_chip[...] = edges_for_partners(back, 2 * REACH)
-
-
-def filtered(field, core, chip, edge, column, row):
-    lhs = split(beside(field[...], core[...], chip[...], edge))
-    return dot3(both(row), split(dot3(lhs, both(column)))).reshape(field.shape)
-
-
-def middle_kernel(back, core, chip, members_ref, column_twice, row_twice, increment):
-    smoothed = filtered(back, core, chip, 2 * REACH, column_twice, row_twice)
-    increment[...] = increments(members_ref, smoothed)
-
-
-def wide_filter_kernel(back, core, chip, column, row, out):
-    out[...] = filtered(back, core, chip, 2 * REACH, column, row)
+    to_core[...], to_chip[...] = edges_for_partners(back, EDGE)
 
 
 def filter_kernel(back, core, chip, column, row, out):
-    rows = back.shape[1]
-    out[...] = filtered(back, core[:, :rows], chip[:, :rows], REACH, column, row)
+    groups, height = back.shape[0] * EDGE // LANES, back.shape[1]
+    core, chip = (x[: groups * height].reshape(groups, height, LANES) for x in (core, chip))
+    lhs = split(beside(back[...], core, chip, EDGE))
+    out[...] = dot3(both(row), split(dot3(lhs, both(column)))).reshape(out.shape)
 
 
 def last_kernel(i0, i1, i2, i3, obs_weight, before, sums, members_ref, back, to_core, to_chip):
-    rows = back.shape[1]
-    increment = (i0[...] + i1[...]) + (i2[...] + i3[...])
+    levels, height, width = obs_weight.shape
+    increment = ((i0[...] + i1[...]) + (i2[...] + i3[...])).reshape(obs_weight.shape)
     weighted = obs_weight[...] * increment
     four = [sums[0], sums[1], folded(before[...] * increment), folded(weighted * increment)]
     row = lax.broadcasted_iota(jnp.int32, (8, LANES), 0)
@@ -220,13 +283,15 @@
     for i, part in enumerate(four):
         stacked = jnp.where(row == i, jnp.sum(part, axis=0, keepdims=True), stacked)
     back[...] = adjoint(members_ref, weighted)
-    to_core[:, :rows], to_chip[:, :rows] = edges_for_partners(back, REACH)
-    to_core[0, rows:] = stacked
-    to_chip[0, rows:] = stacked
-
-
-def combine_kernel(own, other, source, first, second, weights, residual, held_weights, held_residual, sems):
-    total = jnp.sum(own[...] + other[...], axis=1, keepdims=True)
+    core, chip = edges_for_partners(back, EDGE)
+    rows = core.shape[0] * height
+    to_core[:rows] = core.reshape(rows, LANES)
+    to_core[rows:] = stacked
+    to_chip[...] = chip.reshape(rows, LANES)
+
+
+def combine_kernel(norms, source, first, second, weights, residual, held_weights, held_residual, sems):
+    total = jnp.sum(norms[...], axis=1, keepdims=True)
     bb, bg, gg, gh = (total[i : i + 1] for i in range(4))
     bg, gg, gh = bg / bb, gg / bb, gh / bb
     q = 1.0 / (1.0 + bg)
@@ -270,16 +335,37 @@
 
 def held_edges(source):
     members, height, width = source.shape
-    near = (members * REACH // LANES, height, LANES)
+    edges = (members * EDGE // LANES, height, LANES)
     vmem = pl.BlockSpec(memory_space=pltpu.VMEM)
     return pl.pallas_call(
         edges_kernel,
-        out_shape=[pltpu.VMEM(source.shape, F32), pltpu.VMEM(near, F32), pltpu.VMEM(near, F32)],
+        out_shape=[pltpu.VMEM(source.shape, F32), pltpu.VMEM(edges, F32), pltpu.VMEM(edges, F32)],
         in_specs=[pl.BlockSpec(memory_space=pltpu.HBM)],
         out_specs=[vmem] * 3,
         scratch_shapes=[pltpu.SemaphoreType.DMA],
         compiler_params=pltpu.CompilerParams(vmem_limit_bytes=24 * 1024 * 1024),
     )(in_hbm(source))
+
+
+def first_increment(source, after, members_data):
+    members, levels, height, width = members_data.shape
+    groups = members * EDGE // LANES
+    vmem = pl.BlockSpec(memory_space=pltpu.VMEM)
+    return pl.pallas_call(
+        first_kernel,
+        out_shape=[
+            pltpu.VMEM((levels * height + 8, width), F32),
+            pltpu.VMEM(members_data.shape, members_data.dtype),
+            pltpu.VMEM((2, groups, levels, height, LANES), F32),
+            pltpu.VMEM((2, 2, LANES, LANES), BF16),
+            pltpu.VMEM((2, groups * height, groups * height), BF16),
+        ],
+        in_specs=[vmem, vmem, pl.BlockSpec(memory_space=pltpu.HBM)],
+        out_specs=[vmem] * 5,
+        scratch_shapes=[pltpu.SemaphoreType.DMA],
+        compiler_params=pltpu.CompilerParams(vmem_limit_bytes=24 * 1024 * 1024),
+        cost_estimate=pl.CostEstimate(flops=10**8, bytes_accessed=4 * 10**6, transcendentals=0),
+    )(source, after, in_hbm(members_data))
 
 
 def fetched(after, *arrays):
@@ -297,17 +383,17 @@
     )(after, *map(in_hbm, arrays))
 
 
-def combined(own, other, source, first, second):
+def combined(norms, source, first, second):
     vmem = pl.BlockSpec(memory_space=pltpu.VMEM)
     hbm = pl.BlockSpec(memory_space=pltpu.HBM)
     return pl.pallas_call(
         combine_kernel,
         out_shape=[jax.ShapeDtypeStruct(source.shape, F32)] * 2,
-        in_specs=[vmem] * 5,
+        in_specs=[vmem] * 4,
         out_specs=[hbm] * 2,
         scratch_shapes=[pltpu.VMEM(source.shape, F32)] * 2 + [pltpu.SemaphoreType.DMA((2, 4))],
         compiler_params=pltpu.CompilerParams(vmem_limit_bytes=24 * 1024 * 1024),
-    )(own, other, source, first, second)
+    )(norms, source, first, second)
 
 
 def from_both_sides(to_next, to_previous, axis):
@@ -332,50 +418,57 @@
     return [value] + [lax.ppermute(value, axis, [(i, i ^ k) for i in range(count)]) for k in range(1, count)]
 
 
+def total_over_tiles(chip_sums):
+    count = lax.axis_size("tile")
+    step = 2
+    while step < count:
+        chip_sums = chip_sums + lax.ppermute(chip_sums, "tile", [(i, i ^ step) for i in range(count)])
+        step *= 2
+    return chip_sums
+
+
 def one_tile_row(right_side, perturbations, precision, covered):
     source, members_data = right_side[0], perturbations[0]
     members, levels, height, width = members_data.shape
+    groups = members * EDGE // LANES
     taps = taps_np()
     twice = np.convolve(taps, taps)
     field = (members, height, width)
-    near = (members * REACH // LANES, height, LANES)
-    far = (2 * members * REACH // LANES, height, LANES)
+    edges = (groups, height, LANES)
     plane = (levels, height, width)
-    constants = [
-        halves(column_matrix(taps, width, REACH)),
-        halves(row_matrix(taps, height, members, 1)),
-        halves(column_matrix(taps, width, 2 * REACH)),
-        halves(column_matrix(twice, width, 2 * REACH)),
-        halves(row_matrix(taps, height, members, 2)),
-    ]
+    flat = (levels * height, width)
+    row = halves(row_matrix(taps, height, members, 1))
+    own = np.arange(width)
 
     source, to_core, to_chip = held_edges(source)
     core, chip = from_core(to_core), from_chip(to_chip)
-    members_data, column, row = fetched(to_core, members_data, *constants[:2])
-    (increment,) = call(
-        forward_kernel, [(levels * height + 8, width)], source, core, chip, members_data, column, row
+    inside, members_data, edge_members, edge, thin = first_increment(source, to_core, members_data)
+    (increment,) = call(edge_kernel, [inside.shape], inside, core, chip, edge_members, edge, thin)
+    parts = from_all(increment, "mem")
+    precision, covered, column, row, column_twice, row_twice, edge, thin = fetched(
+        increment, precision[0], covered[0], halves(column_matrix(taps, width, EDGE)), row,
+        halves(band(twice, own, own)), halves(row_matrix(taps, height, members, 2)),
+        edge_matrix(twice, EDGE), halves(row_matrix(taps, height, groups, 2)),
     )
-    parts = from_all(increment, "mem")
-    precision, covered, column_far, column_twice, row_twice = fetched(increment, precision[0], covered[0], *constants[2:])
     back, to_core, to_chip, obs_weight, weighted, sums = call(
-        adjoint_kernel, [field, far, far, plane, plane, (2, 8, LANES)], *parts, precision, covered, members_data
+        adjoint_kernel, [field, edges, edges, plane, plane, (2, 8, LANES)], *parts, precision, covered, members_data
     )
     core, chip = from_core(to_core), from_chip(to_chip)
-    (increment,) = call(middle_kernel, [plane], back, core, chip, members_data, column_twice, row_twice)
+    (inside,) = call(second_kernel, [plane], back, column_twice, row_twice, members_data)
+    inside = inside.reshape(flat)
+    (increment,) = call(edge_kernel, [flat], inside, core, chip, edge_members, edge, thin)
     parts = from_all(increment, "mem")
-    (first,) = call(wide_filter_kernel, [field], back, core, chip, column_far, row)
-    ended = (1, height + 8, LANES)
+    core, chip = (x.reshape(groups * height, LANES) for x in (core, chip))
+    (first,) = call(filter_kernel, [field], back, core, chip, column, row)
     back, to_core, to_chip = call(
-        last_kernel, [field, ended, ended], *parts, obs_weight, weighted, sums, members_data
+        last_kernel,
+        [field, (groups * height + 8, LANES), (groups * height, LANES)],
+        *parts, obs_weight, weighted, sums, members_data,
     )
-    core = from_core(to_core)
-    to_chip = jnp.concatenate([to_chip[:, :height], to_chip[:, height:] + core[:, height:]], axis=1)
-    chip = from_chip(to_chip)
-    norms = to_chip[0, height:] + chip[0, height:]
-    count = lax.axis_size("tile")
-    others = lax.ppermute(norms, "tile", [(i, (i + count // 2) % count) for i in range(count)])
+    core, chip = from_core(to_core), from_chip(to_chip)
+    norms = total_over_tiles(to_core[groups * height :] + core[groups * height :])
     (second,) = call(filter_kernel, [field], back, core, chip, column, row)
-    weights, residual = combined(norms, others, source, first, second)
+    weights, residual = combined(norms, source, first, second)
     return weights[None], residual[None]
 
 

time: 43.4 us -> 42.3 us (0.975)
  waiting for transfers between devices: 17.6 us -> 15.7 us
    ppermute x3, waiting for transfers between devices: 5.66 us -> 1.65 us  [from_chip(): lax.ppermute(value, 'tile', [(i, (i + 1) % count if i % 2 else (i - 1) %...]
    ppermute x1 -> x2, waiting for transfers between devices: 2.94 us -> 6.2 us  [total_over_tiles(): lax.ppermute(chip_sums, 'tile', [(i, i ^ step) for i in range(count)])]
    pallas_call x0 -> x1, Pallas kernels: none -> 1.56 us  [first_increment(): pl.pallas_call(first_kernel, out_shape=[pltpu.VMEM((levels * height + 8,...]
    pallas_call x2 -> x1, Pallas kernels: 2.75 us -> 1.44 us  [fetched(): pl.pallas_call(fetch_kernel, out_shape=[pltpu.VMEM(a.shape, a.dtype) for...]
    ppermute x3, waiting for transfers between devices: 1.16 us -> 0.01 us  [from_core(): return lax.ppermute(value, 'tile', [(i, i ^ 1) for i in range(count)])]
    pallas_call x6 -> x7, Pallas kernels: 3.88 us -> 3.99 us  [call(): pl.pallas_call(kernel, out_shape=shapes, in_specs=[vmem] * len(operands),...]
  transfers between devices with their start and end apart: 13 -> 14, of which waited for: 10 -> 9; matrix products, arithmetic and copies ran while one was open for 0% -> 0% of each run, Pallas kernels for 10% -> 13%
where the time goes in v3:
time: 42.3 us; the launch traced here: 42.1 us
  starting transfers between devices  16.5 us (39%)
  waiting for transfers between devices  15.7 us (37%)
  Pallas kernels  9.07 us (21%)
  between operations  0.76 us (2%)
    ppermute x3, starting transfers between devices, from_chip(): lax.ppermute(value, 'tile', [(i, (i + 1) % count if i % 2 else (i - 1) %...  8.97 us
    ppermute x6, waiting for transfers between devices, from_all(): lax.ppermute(value, axis, [(i, i ^ k) for i in range(count)])  7.81 us
    ppermute x6, starting transfers between devices, from_all(): lax.ppermute(value, axis, [(i, i ^ k) for i in range(count)])  7.11 us
    ppermute x2, waiting for transfers between devices, total_over_tiles(): lax.ppermute(chip_sums, 'tile', [(i, i ^ step) for i in range(count)])  6.2 us
    pallas_call x7, Pallas kernels, call(): pl.pallas_call(kernel, out_shape=shapes, in_specs=[vmem] * len(operands),...  3.99 us
    ppermute x3, waiting for transfers between devices, from_chip(): lax.ppermute(value, 'tile', [(i, (i + 1) % count if i % 2 else (i - 1) %...  1.65 us
    pallas_call x1, Pallas kernels, first_increment(): pl.pallas_call(first_kernel, out_shape=[pltpu.VMEM((levels * height + 8,...  1.56 us
    pallas_call x1, Pallas kernels, fetched(): pl.pallas_call(fetch_kernel, out_shape=[pltpu.VMEM(a.shape, a.dtype) for...  1.44 us
  transfers between devices with their start and end apart: 14, of which 9 were waited for; matrix products, arithmetic and copies ran while one was open for 0% of the time, Pallas kernels for 13%

profile of v3, /device:TPU:0, one launch (start us, length us, event | category | flops | bytes accessed | tf_op | source)
XLA Modules:
  0.0 42.1 jit_solution(9388559278786535195)
XLA Ops:
  0.6 1.1 %shard_map.113 = (f32[16,16,256]{2,1,0:T(8,128)S(1)}, f32[2,16,128]{2,1,0:T(8,128)S(1)}, f32[2,16,128]{2,1,0:T(8,128)S(1)}) custom-call(f32[16,16,256]{2,1,0:T(8,128)} %bitcast.13), custom_call_target="tpu_custom_call" | custom-call | tf_op jit(solution)/shard_map/pallas_call | solution.py:340
  1.7 4.6 %collective-permute-start.1 = (f32[2,16,128]{2,1,0:T(8,128)S(1)}, f32[2,16,128]{2,1,0:T(8,128)S(1)}, u32[]{:S(2)}, u32[]{:S(2)}) collective-permute-start(f32[2,16,128]{2,1,0:T(8,128)S(1)} %get-tuple-element.32), channel_id=1, source_target_pairs={{0,28},{4,8},{8,4},{12,16},{16,12},{20,24},{24,20},{28,0},{1,29},{... | collective-permute-start | bytes 49160 | tf_op jit(solution)/shard_map/ppermute | solution.py:413
  6.3 1.6 %shard_map.114 = (f32[104,256]{1,0:T(8,128)S(1)}, bf16[16,6,16,256]{3,2,1,0:T(8,128)(2,1)S(1)}, f32[2,2,6,16,128]{4,3,2,1,0:T(8,128)S(1)}, bf16[2,2,128,128]{3,2,1,0:T(8,128)(2,1)S(1)}, bf16[2,32,32]{2,1,0:T(8,128)(2,1)S(1)}) custom-call(f32[16,16,256]{2,1,0:T(8,128)S(1)} %get-tuple-element.29.source, f32[2,16,128]{2,1,0:T(8,128)S(1)} %get-tuple-element.30.after, ...), custom_call_target="tpu_custom_call" | custom-call | flops 100000000 | bytes 4000000 | tf_op jit(solution)/shard_map/pallas_call | solution.py:354
  7.9 0.6 %shard_map.115.refs_0_.i0 = f32[104,256]{1,0:T(8,128)S(1)} custom-call(f32[104,256]{1,0:T(8,128)S(1)} %get-tuple-element.31.inside, f32[2,16,128]{2,1,0:T(8,128)S(1)} %collective-permute-done.core, f32[2,16,128]{2,1,0:T(8,128)S(1)} %collective-permute-done.1.chip, f32[2,2,6,16,128]{4,3,2,1,0:T(8,128)S(1)} %get-tuple-element.33.edge_members, ...), custom_call_target="tpu_custom_call" | custom-call | tf_op jit(solution)/shard_map/pallas_call | solution.py:322
  8.4 2.8 %collective-permute-start.4 = (f32[104,256]{1,0:T(8,128)S(1)}, f32[104,256]{1,0:T(8,128)S(1)}, u32[]{:S(2)}, u32[]{:S(2)}) collective-permute-start(f32[104,256]{1,0:T(8,128)S(1)} %shard_map.115.refs_0_.i0), channel_id=1, source_target_pairs={{0,3},{1,2},{2,1},{3,0},{4,7},{5,6},{6,5},{7,4},{8,11},{9,10},{10,... | collective-permute-start | bytes 319496 | tf_op jit(solution)/shard_map/ppermute | solution.py:418
  11.3 0.5 %collective-permute-start.3 = (f32[104,256]{1,0:T(8,128)S(1)}, f32[104,256]{1,0:T(8,128)S(1)}, u32[]{:S(2)}, u32[]{:S(2)}) collective-permute-start(f32[104,256]{1,0:T(8,128)S(1)} %shard_map.115.refs_0_.i0), channel_id=1, source_target_pairs={{0,2},{1,3},{2,0},{3,1},{4,6},{5,7},{6,4},{7,5},{8,10},{9,11},{10,... | collective-permute-start | bytes 319496 | tf_op jit(solution)/shard_map/ppermute | solution.py:418
  12.0 1.4 %shard_map.116 = (f32[6,16,256]{2,1,0:T(8,128)S(1)}, s32[2,16]{1,0:T(2,128)S(1)}, bf16[2,512,256]{2,1,0:T(8,128)(2,1)S(1)}, bf16[2,256,256]{2,1,0:T(8,128)(2,1)S...) custom-call(f32[104,256]{1,0:T(8,128)S(1)} %shard_map.115.refs_0_.i0, ...), custom_call_target="tpu_custom_call" | custom-call | bytes 3088640 | tf_op jit(solution)/shard_map/pallas_call | solution.py:375
  13.4 1.5 %collective-permute-done.4.i3 = f32[104,256]{1,0:T(8,128)S(1)} collective-permute-done((f32[104,256]{1,0:T(8,128)S(1)}, f32[104,256]{1,0:T(8,128)S(1)}, u32[]{:S(2)}, u32[]{:S(2)}) %collective-permute-start.4) | collective-permute-done | bytes 106528 | tf_op jit(solution)/shard_map/ppermute | solution.py:418
  14.9 2.2 %collective-permute-done.3.i2 = f32[104,256]{1,0:T(8,128)S(1)} collective-permute-done((f32[104,256]{1,0:T(8,128)S(1)}, f32[104,256]{1,0:T(8,128)S(1)}, u32[]{:S(2)}, u32[]{:S(2)}) %collective-permute-start.3) | collective-permute-done | bytes 106528 | tf_op jit(solution)/shard_map/ppermute | solution.py:418
  17.5 2.6 %collective-permute-start.6 = (f32[2,16,128]{2,1,0:T(8,128)S(1)}, f32[2,16,128]{2,1,0:T(8,128)S(1)}, u32[]{:S(2)}, u32[]{:S(2)}) collective-permute-start(f32[2,16,128]{2,1,0:T(8,128)S(1)} %get-tuple-element.43), channel_id=1, source_target_pairs={{0,28},{4,8},{8,4},{12,16},{16,12},{20,24},{24,20},{28,0},{1,29},{... | collective-permute-start | bytes 49160 | tf_op jit(solution)/shard_map/ppermute | solution.py:413
  20.1 0.8 %shard_map.118 = f32[6,16,256]{2,1,0:T(8,128)S(1)} custom-call(f32[16,16,256]{2,1,0:T(8,128)S(1)} %get-tuple-element.39.back, bf16[2,256,256]{2,1,0:T(8,128)(2,1)S(1)} %get-tuple-element.40.column, bf16[2,256,256]{2,1,0:T(8,128)(2,1)S(1)} %get-tuple-element.41.row, bf16[16,6,16,256]{3,2,1,0:T(8,128)(2,1)S(1)} %get-tuple-element.38.members_ref), custom_call_target="tpu_custom_call" | custom-call | tf_op jit(solution)/shard_map/pallas_call | solution.py:322
  20.9 1.6 %collective-permute-done.6.chip = f32[2,16,128]{2,1,0:T(8,128)S(1)} collective-permute-done((f32[2,16,128]{2,1,0:T(8,128)S(1)}, f32[2,16,128]{2,1,0:T(8,128)S(1)}, u32[]{:S(2)}, u32[]{:S(2)}) %collective-permute-start.6) | collective-permute-done | bytes 16416 | tf_op jit(solution)/shard_map/ppermute | solution.py:413
  22.6 0.5 %shard_map.119.i0 = f32[96,256]{1,0:T(8,128)S(1)} custom-call(f32[96,256]{1,0:T(8,128)S(1)} %bitcast.9, f32[2,16,128]{2,1,0:T(8,128)S(1)} %collective-permute-done.5.core, f32[2,16,128]{2,1,0:T(8,128)S(1)} %collective-permute-done.6.chip, f32[2,2,6,16,128]{4,3,2,1,0:T(8,128)S(1)} %get-tuple-element.33.edge_members, ...), custom_call_target="tpu_custom_call" | custom-call | tf_op jit(solution)/shard_map/pallas_call | solution.py:322
  23.1 1.8 %collective-permute-start.9 = (f32[96,256]{1,0:T(8,128)S(1)}, f32[96,256]{1,0:T(8,128)S(1)}, u32[]{:S(2)}, u32[]{:S(2)}) collective-permute-start(f32[96,256]{1,0:T(8,128)S(1)} %shard_map.119.i0), channel_id=1, source_target_pairs={{0,3},{1,2},{2,1},{3,0},{4,7},{5,6},{6,5},{7,4},{8,11},{9,10},{10,... | collective-permute-start | bytes 294920 | tf_op jit(solution)/shard_map/ppermute | solution.py:418
  24.9 1.3 %collective-permute-start.8 = (f32[96,256]{1,0:T(8,128)S(1)}, f32[96,256]{1,0:T(8,128)S(1)}, u32[]{:S(2)}, u32[]{:S(2)}) collective-permute-start(f32[96,256]{1,0:T(8,128)S(1)} %shard_map.119.i0), channel_id=1, source_target_pairs={{0,2},{1,3},{2,0},{3,1},{4,6},{5,7},{6,4},{7,5},{8,10},{9,11},{10,... | collective-permute-start | bytes 294920 | tf_op jit(solution)/shard_map/ppermute | solution.py:418
  26.7 2.5 %collective-permute-done.9.i3 = f32[96,256]{1,0:T(8,128)S(1)} collective-permute-done((f32[96,256]{1,0:T(8,128)S(1)}, f32[96,256]{1,0:T(8,128)S(1)}, u32[]{:S(2)}, u32[]{:S(2)}) %collective-permute-start.9) | collective-permute-done | bytes 98336 | tf_op jit(solution)/shard_map/ppermute | solution.py:418
  29.2 0.9 %collective-permute-done.8.i2 = f32[96,256]{1,0:T(8,128)S(1)} collective-permute-done((f32[96,256]{1,0:T(8,128)S(1)}, f32[96,256]{1,0:T(8,128)S(1)}, u32[]{:S(2)}, u32[]{:S(2)}) %collective-permute-start.8) | collective-permute-done | bytes 98336 | tf_op jit(solution)/shard_map/ppermute | solution.py:418
  30.1 0.7 %collective-permute-done.7.i1 = f32[96,256]{1,0:T(8,128)S(1)} collective-permute-done((f32[96,256]{1,0:T(8,128)S(1)}, f32[96,256]{1,0:T(8,128)S(1)}, u32[]{:S(2)}, u32[]{:S(2)}) %collective-permute-start.7) | collective-permute-done | bytes 98336 | tf_op jit(solution)/shard_map/ppermute | solution.py:418
  31.1 1.8 %collective-permute-start.13 = (f32[32,128]{1,0:T(8,128)S(1)}, f32[32,128]{1,0:T(8,128)S(1)}, u32[]{:S(2)}, u32[]{:S(2)}) collective-permute-start(f32[32,128]{1,0:T(8,128)S(1)} %get-tuple-element.53), channel_id=1, source_target_pairs={{0,28},{4,8},{8,4},{12,16},{16,12},{20,24},{24,20},{28,0},{1,29},{... | collective-permute-start | bytes 49160 | tf_op jit(solution)/shard_map/ppermute | solution.py:413
  33.3 3.3 %collective-permute-done.11 = f32[8,128]{1,0:T(8,128)S(1)} collective-permute-done((f32[8,128]{1,0:T(8,128)S(1)}, f32[8,128]{1,0:T(8,128)S(1)}, u32[]{:S(2)}, u32[]{:S(2)}) %collective-permute-start.11) | collective-permute-done | bytes 4128 | tf_op jit(solution)/shard_map/ppermute | solution.py:425
  36.5 0.8 %shard_map.121.first = f32[16,16,256]{2,1,0:T(8,128)S(1)} custom-call(f32[16,16,256]{2,1,0:T(8,128)S(1)} %get-tuple-element.39.back, f32[32,128]{1,0:T(8,128)S(1)} %bitcast.10, f32[32,128]{1,0:T(8,128)S(1)} %bitcast.11, bf16[2,512,256]{2,1,0:T(8,128)(2,1)S(1)} %get-tuple-element.50.column, bf16[2,256,256]{2,1,0:T(8,128)(2,1)S(1)} %get-tuple-element.51.row), custom_call_target="tpu_custom_call" | custom-call | tf_op jit(solution)/shard_map/pallas_call | solution.py:322
  37.3 0.8 %shard_map.122.second = f32[16,16,256]{2,1,0:T(8,128)S(1)} custom-call(f32[16,16,256]{2,1,0:T(8,128)S(1)} %get-tuple-element.52.back, f32[40,128]{1,0:T(8,128)S(1)} %collective-permute-done.10.core, f32[32,128]{1,0:T(8,128)S(1)} %collective-permute-done.13.chip, bf16[2,512,256]{2,1,0:T(8,128)(2,1)S(1)} %get-tuple-element.50.column, ...), custom_call_target="tpu_custom_call" | custom-call | tf_op jit(solution)/shard_map/pallas_call | solution.py:322
  38.1 2.9 %collective-permute-done.12 = f32[8,128]{1,0:T(8,128)S(1)} collective-permute-done((f32[8,128]{1,0:T(8,128)S(1)}, f32[8,128]{1,0:T(8,128)S(1)}, u32[]{:S(2)}, u32[]{:S(2)}) %collective-permute-start.12) | collective-permute-done | bytes 4128 | tf_op jit(solution)/shard_map/ppermute | solution.py:425
  41.0 1.0 %shard_map.123 = (f32[16,16,256]{2,1,0:T(8,128)}, f32[16,16,256]{2,1,0:T(8,128)}) custom-call(f32[8,128]{1,0:T(8,128)S(1)} %add.11.norms, f32[16,16,256]{2,1,0:T(8,128)S(1)} %get-tuple-element.29.source, f32[16,16,256]{2,1,0:T(8,128)S(1)} %shard_map.121.first, f32[16,16,256]{2,1,0:T(8,128)S(1)} %shard_map.122.second), custom_call_target="tpu_custom_call" | custom-call | tf_op jit(solution)/shard_map/pallas_call | solution.py:389
  (18 shorter events, 1.8 us)
Async XLA Ops:
  1.7 6.1 %collective-permute-start.1 = (f32[2,16,128]{2,1,0:T(8,128)S(1)}, f32[2,16,128]{2,1,0:T(8,128)S(1)}, u32[]{:S(2)}, u32[]{:S(2)}) collective-permute-start(f32[2,16,128]{2,1,0:T(8,128)S(1)} %get-tuple-element.32), channel_id=1, source_target_pairs={{0,28},{4,8},{8,4},{12,16},{16,12},{20,24},{24,20},{28,0},{1,29},{... | collective-permute-start | bytes 49160 | tf_op jit(solution)/shard_map/ppermute | solution.py:413
  6.3 1.6 %collective-permute-start = (f32[2,16,128]{2,1,0:T(8,128)S(1)}, f32[2,16,128]{2,1,0:T(8,128)S(1)}, u32[]{:S(2)}, u32[]{:S(2)}) collective-permute-start(f32[2,16,128]{2,1,0:T(8,128)S(1)} %get-tuple-element.30.after), channel_id=1, source_target_pairs={{0,4},{4,0},{8,12},{12,8},{16,20},{20,16},{24,28},{28,24},{1,5},{5... | collective-permute-start | bytes 49160 | tf_op jit(solution)/shard_map/ppermute | solution.py:408
  8.4 6.5 %collective-permute-start.4 = (f32[104,256]{1,0:T(8,128)S(1)}, f32[104,256]{1,0:T(8,128)S(1)}, u32[]{:S(2)}, u32[]{:S(2)}) collective-permute-start(f32[104,256]{1,0:T(8,128)S(1)} %shard_map.115.refs_0_.i0), channel_id=1, source_target_pairs={{0,3},{1,2},{2,1},{3,0},{4,7},{5,6},{6,5},{7,4},{8,11},{9,10},{10,... | collective-permute-start | bytes 319496 | tf_op jit(solution)/shard_map/ppermute | solution.py:418
  11.3 5.8 %collective-permute-start.3 = (f32[104,256]{1,0:T(8,128)S(1)}, f32[104,256]{1,0:T(8,128)S(1)}, u32[]{:S(2)}, u32[]{:S(2)}) collective-permute-start(f32[104,256]{1,0:T(8,128)S(1)} %shard_map.115.refs_0_.i0), channel_id=1, source_target_pairs={{0,2},{1,3},{2,0},{3,1},{4,6},{5,7},{6,4},{7,5},{8,10},{9,11},{10,... | collective-permute-start | bytes 319496 | tf_op jit(solution)/shard_map/ppermute | solution.py:418
  11.8 5.3 %collective-permute-start.2 = (f32[104,256]{1,0:T(8,128)S(1)}, f32[104,256]{1,0:T(8,128)S(1)}, u32[]{:S(2)}, u32[]{:S(2)}) collective-permute-start(f32[104,256]{1,0:T(8,128)S(1)} %shard_map.115.refs_0_.i0), channel_id=1, source_target_pairs={{0,1},{1,0},{2,3},{3,2},{4,5},{5,4},{6,7},{7,6},{8,9},{9,8},{10,11... | collective-permute-start | bytes 319496 | tf_op jit(solution)/shard_map/ppermute | solution.py:418
  17.5 3.5 %collective-permute-start.5 = (f32[2,16,128]{2,1,0:T(8,128)S(1)}, f32[2,16,128]{2,1,0:T(8,128)S(1)}, u32[]{:S(2)}, u32[]{:S(2)}) collective-permute-start(f32[2,16,128]{2,1,0:T(8,128)S(1)} %get-tuple-element.42), channel_id=1, source_target_pairs={{0,4},{4,0},{8,12},{12,8},{16,20},{20,16},{24,28},{28,24},{1,5},{5... | collective-permute-start | bytes 49160 | tf_op jit(solution)/shard_map/ppermute | solution.py:408
  17.5 5.0 %collective-permute-start.6 = (f32[2,16,128]{2,1,0:T(8,128)S(1)}, f32[2,16,128]{2,1,0:T(8,128)S(1)}, u32[]{:S(2)}, u32[]{:S(2)}) collective-permute-start(f32[2,16,128]{2,1,0:T(8,128)S(1)} %get-tuple-element.43), channel_id=1, source_target_pairs={{0,28},{4,8},{8,4},{12,16},{16,12},{20,24},{24,20},{28,0},{1,29},{... | collective-permute-start | bytes 49160 | tf_op jit(solution)/shard_map/ppermute | solution.py:413
  23.1 6.1 %collective-permute-start.9 = (f32[96,256]{1,0:T(8,128)S(1)}, f32[96,256]{1,0:T(8,128)S(1)}, u32[]{:S(2)}, u32[]{:S(2)}) collective-permute-start(f32[96,256]{1,0:T(8,128)S(1)} %shard_map.119.i0), channel_id=1, source_target_pairs={{0,3},{1,2},{2,1},{3,0},{4,7},{5,6},{6,5},{7,4},{8,11},{9,10},{10,... | collective-permute-start | bytes 294920 | tf_op jit(solution)/shard_map/ppermute | solution.py:418
  24.9 5.2 %collective-permute-start.8 = (f32[96,256]{1,0:T(8,128)S(1)}, f32[96,256]{1,0:T(8,128)S(1)}, u32[]{:S(2)}, u32[]{:S(2)}) collective-permute-start(f32[96,256]{1,0:T(8,128)S(1)} %shard_map.119.i0), channel_id=1, source_target_pairs={{0,2},{1,3},{2,0},{3,1},{4,6},{5,7},{6,4},{7,5},{8,10},{9,11},{10,... | collective-permute-start | bytes 294920 | tf_op jit(solution)/shard_map/ppermute | solution.py:418
  26.2 4.6 %collective-permute-start.7 = (f32[96,256]{1,0:T(8,128)S(1)}, f32[96,256]{1,0:T(8,128)S(1)}, u32[]{:S(2)}, u32[]{:S(2)}) collective-permute-start(f32[96,256]{1,0:T(8,128)S(1)} %shard_map.119.i0), channel_id=1, source_target_pairs={{0,1},{1,0},{2,3},{3,2},{4,5},{5,4},{6,7},{7,6},{8,9},{9,8},{10,11... | collective-permute-start | bytes 294920 | tf_op jit(solution)/shard_map/ppermute | solution.py:418
  31.0 1.9 %collective-permute-start.10 = (f32[40,128]{1,0:T(8,128)S(1)}, f32[40,128]{1,0:T(8,128)S(1)}, u32[]{:S(2)}, u32[]{:S(2)}) collective-permute-start(f32[40,128]{1,0:T(8,128)S(1)} %get-tuple-element.49), channel_id=1, source_target_pairs={{0,4},{4,0},{8,12},{12,8},{16,20},{20,16},{24,28},{28,24},{1,5},{5... | collective-permute-start | bytes 61448 | tf_op jit(solution)/shard_map/ppermute | solution.py:408
  31.1 6.2 %collective-permute-start.13 = (f32[32,128]{1,0:T(8,128)S(1)}, f32[32,128]{1,0:T(8,128)S(1)}, u32[]{:S(2)}, u32[]{:S(2)}) collective-permute-start(f32[32,128]{1,0:T(8,128)S(1)} %get-tuple-element.53), channel_id=1, source_target_pairs={{0,28},{4,8},{8,4},{12,16},{16,12},{20,24},{24,20},{28,0},{1,29},{... | collective-permute-start | bytes 49160 | tf_op jit(solution)/shard_map/ppermute | solution.py:413
  32.9 3.6 %collective-permute-start.11 = (f32[8,128]{1,0:T(8,128)S(1)}, f32[8,128]{1,0:T(8,128)S(1)}, u32[]{:S(2)}, u32[]{:S(2)}) collective-permute-start(f32[8,128]{1,0:T(8,128)S(1)} %slice_add_fusion), channel_id=1, source_target_pairs={{0,8},{4,12},{8,0},{12,4},{16,24},{20,28},{24,16},{28,20},{1,9},{5... | collective-permute-start | bytes 12296 | tf_op jit(solution)/shard_map/ppermute | solution.py:425
  36.5 4.5 %collective-permute-start.12 = (f32[8,128]{1,0:T(8,128)S(1)}, f32[8,128]{1,0:T(8,128)S(1)}, u32[]{:S(2)}, u32[]{:S(2)}) collective-permute-start(f32[8,128]{1,0:T(8,128)S(1)} %add.10), channel_id=1, source_target_pairs={{0,16},{4,20},{8,24},{12,28},{16,0},{20,4},{24,8},{28,12},{1,17},{... | collective-permute-start | bytes 12296 | tf_op jit(solution)/shard_map/ppermute | solution.py:425

commit v4 on v3

--- a/solution.py
+++ b/solution.py
@@ -16,6 +16,7 @@
 LANES = 128
 F32 = jnp.float32
 BF16 = jnp.bfloat16
+LONG = pl.CostEstimate(flops=10**9, bytes_accessed=10**6, transcendentals=0)
 
 
 def taps_np():
@@ -283,15 +284,20 @@
     for i, part in enumerate(four):
         stacked = jnp.where(row == i, jnp.sum(part, axis=0, keepdims=True), stacked)
     back[...] = adjoint(members_ref, weighted)
-    core, chip = edges_for_partners(back, EDGE)
-    rows = core.shape[0] * height
-    to_core[:rows] = core.reshape(rows, LANES)
+    odd = lax.axis_index("tile") % 2 == 1
+    first, last = pack_edges(back, EDGE, True), pack_edges(back, EDGE, False)
+    rows = first.shape[0] * height
+    to_core[:rows] = jnp.where(odd, first, last).reshape(rows, LANES)
     to_core[rows:] = stacked
-    to_chip[...] = chip.reshape(rows, LANES)
-
-
-def combine_kernel(norms, source, first, second, weights, residual, held_weights, held_residual, sems):
-    total = jnp.sum(norms[...], axis=1, keepdims=True)
+    to_chip[...] = jnp.where(odd, last, first).reshape(rows, LANES)
+
+
+def copy_kernel(value, after, out):
+    out[...] = value[...]
+
+
+def combine_kernel(own, other, source, first, second, weights, residual, held_weights, held_residual, sems):
+    total = jnp.sum(own[...] + other[...], axis=1, keepdims=True)
     bb, bg, gg, gh = (total[i : i + 1] for i in range(4))
     bg, gg, gh = bg / bb, gg / bb, gh / bb
     q = 1.0 / (1.0 + bg)
@@ -383,17 +389,17 @@
     )(after, *map(in_hbm, arrays))
 
 
-def combined(norms, source, first, second):
+def combined(own, other, source, first, second):
     vmem = pl.BlockSpec(memory_space=pltpu.VMEM)
     hbm = pl.BlockSpec(memory_space=pltpu.HBM)
     return pl.pallas_call(
         combine_kernel,
         out_shape=[jax.ShapeDtypeStruct(source.shape, F32)] * 2,
-        in_specs=[vmem] * 4,
+        in_specs=[vmem] * 5,
         out_specs=[hbm] * 2,
         scratch_shapes=[pltpu.VMEM(source.shape, F32)] * 2 + [pltpu.SemaphoreType.DMA((2, 4))],
         compiler_params=pltpu.CompilerParams(vmem_limit_bytes=24 * 1024 * 1024),
-    )(norms, source, first, second)
+    )(own, other, source, first, second)
 
 
 def from_both_sides(to_next, to_previous, axis):
@@ -403,9 +409,13 @@
     return left, right
 
 
+def from_tile(value, bit):
+    count = lax.axis_size("tile")
+    return lax.ppermute(value, "tile", [(i, i ^ bit) for i in range(count)])
+
+
 def from_core(value):
-    count = lax.axis_size("tile")
-    return lax.ppermute(value, "tile", [(i, i ^ 1) for i in range(count)])
+    return from_tile(value, 1)
 
 
 def from_chip(value):
@@ -416,15 +426,6 @@
 def from_all(value, axis):
     count = lax.axis_size(axis)
     return [value] + [lax.ppermute(value, axis, [(i, i ^ k) for i in range(count)]) for k in range(1, count)]
-
-
-def total_over_tiles(chip_sums):
-    count = lax.axis_size("tile")
-    step = 2
-    while step < count:
-        chip_sums = chip_sums + lax.ppermute(chip_sums, "tile", [(i, i ^ step) for i in range(count)])
-        step *= 2
-    return chip_sums
 
 
 def one_tile_row(right_side, perturbations, precision, covered):
@@ -459,16 +460,20 @@
     (increment,) = call(edge_kernel, [flat], inside, core, chip, edge_members, edge, thin)
     parts = from_all(increment, "mem")
     core, chip = (x.reshape(groups * height, LANES) for x in (core, chip))
-    (first,) = call(filter_kernel, [field], back, core, chip, column, row)
+    (first,) = call(filter_kernel, [field], back, core, chip, column, row, cost=LONG)
     back, to_core, to_chip = call(
         last_kernel,
         [field, (groups * height + 8, LANES), (groups * height, LANES)],
         *parts, obs_weight, weighted, sums, members_data,
     )
-    core, chip = from_core(to_core), from_chip(to_chip)
-    norms = total_over_tiles(to_core[groups * height :] + core[groups * height :])
-    (second,) = call(filter_kernel, [field], back, core, chip, column, row)
-    weights, residual = combined(norms, source, first, second)
+    core = from_core(to_core)
+    sums = to_core[groups * height :] + core[groups * height :]
+    (to_chip,) = call(copy_kernel, [to_chip.shape], to_chip, sums)
+    chip = from_chip(to_chip)
+    sums = sums + from_tile(sums, 2)
+    others = from_tile(sums, 4)
+    (second,) = call(filter_kernel, [field], back, core, chip, column, row, cost=LONG)
+    weights, residual = combined(sums, others, source, first, second)
     return weights[None], residual[None]
 
 

time: 42.3 us -> 41.6 us (0.983)
    ppermute x5, waiting for transfers between devices: 6.21 us -> 4.69 us  [from_tile(): return lax.ppermute(value, 'tile', [(i, i ^ bit) for i in range(count)])]
    ppermute x3, waiting for transfers between devices: 1.65 us -> 2.89 us  [from_chip(): lax.ppermute(value, 'tile', [(i, (i + 1) % count if i % 2 else (i - 1) %...]
    pallas_call x7 -> x8, Pallas kernels: 3.99 us -> 3.98 us  [call(): pl.pallas_call(kernel, out_shape=shapes, in_specs=[vmem] * len(operands),...]
  transfers between devices with their start and end apart: 14 -> 14, of which waited for: 9 -> 11; matrix products, arithmetic and copies ran while one was open for 0% -> 0% of each run, Pallas kernels for 13% -> 13%
where the time goes in v4:
time: 41.6 us; the launch traced here: 41.4 us
  starting transfers between devices  16.2 us (39%)
  waiting for transfers between devices  15.4 us (37%)
  Pallas kernels  9.07 us (22%)
  between operations  0.76 us (2%)
    ppermute x3, starting transfers between devices, from_chip(): lax.ppermute(value, 'tile', [(i, (i + 1) % count if i % 2 else (i - 1) %...  8.7 us
    ppermute x6, waiting for transfers between devices, from_all(): lax.ppermute(value, axis, [(i, i ^ k) for i in range(count)])  7.81 us
    ppermute x6, starting transfers between devices, from_all(): lax.ppermute(value, axis, [(i, i ^ k) for i in range(count)])  7.11 us
    ppermute x5, waiting for transfers between devices, from_tile(): return lax.ppermute(value, 'tile', [(i, i ^ bit) for i in range(count)])  4.69 us
    pallas_call x8, Pallas kernels, call(): pl.pallas_call(kernel, out_shape=shapes, in_specs=[vmem] * len(operands),...  3.98 us
    ppermute x3, waiting for transfers between devices, from_chip(): lax.ppermute(value, 'tile', [(i, (i + 1) % count if i % 2 else (i - 1) %...  2.89 us
    pallas_call x1, Pallas kernels, first_increment(): pl.pallas_call(first_kernel, out_shape=[pltpu.VMEM((levels * height + 8,...  1.56 us
    pallas_call x1, Pallas kernels, fetched(): pl.pallas_call(fetch_kernel, out_shape=[pltpu.VMEM(a.shape, a.dtype) for...  1.44 us
  transfers between devices with their start and end apart: 14, of which 11 were waited for; matrix products, arithmetic and copies ran while one was open for 0% of the time, Pallas kernels for 13%

profile of v4, /device:TPU:0, one launch (start us, length us, event | category | flops | bytes accessed | tf_op | source)
XLA Modules:
  0.0 41.4 jit_solution(10652120273595377170)
XLA Ops:
  0.6 1.1 %shard_map.113 = (f32[16,16,256]{2,1,0:T(8,128)S(1)}, f32[2,16,128]{2,1,0:T(8,128)S(1)}, f32[2,16,128]{2,1,0:T(8,128)S(1)}) custom-call(f32[16,16,256]{2,1,0:T(8,128)} %bitcast.13), custom_call_target="tpu_custom_call" | custom-call | tf_op jit(solution)/shard_map/pallas_call | solution.py:346
  1.7 4.6 %collective-permute-start.1 = (f32[2,16,128]{2,1,0:T(8,128)S(1)}, f32[2,16,128]{2,1,0:T(8,128)S(1)}, u32[]{:S(2)}, u32[]{:S(2)}) collective-permute-start(f32[2,16,128]{2,1,0:T(8,128)S(1)} %get-tuple-element.32), channel_id=1, source_target_pairs={{0,28},{4,8},{8,4},{12,16},{16,12},{20,24},{24,20},{28,0},{1,29},{... | collective-permute-start | bytes 49160 | tf_op jit(solution)/shard_map/ppermute | solution.py:423
  6.3 1.6 %shard_map.114 = (f32[104,256]{1,0:T(8,128)S(1)}, bf16[16,6,16,256]{3,2,1,0:T(8,128)(2,1)S(1)}, f32[2,2,6,16,128]{4,3,2,1,0:T(8,128)S(1)}, bf16[2,2,128,128]{3,2,1,0:T(8,128)(2,1)S(1)}, bf16[2,32,32]{2,1,0:T(8,128)(2,1)S(1)}) custom-call(f32[16,16,256]{2,1,0:T(8,128)S(1)} %get-tuple-element.29.source, f32[2,16,128]{2,1,0:T(8,128)S(1)} %get-tuple-element.30.after, ...), custom_call_target="tpu_custom_call" | custom-call | flops 100000000 | bytes 4000000 | tf_op jit(solution)/shard_map/pallas_call | solution.py:360
  7.9 0.6 %shard_map.115.refs_0_.i0 = f32[104,256]{1,0:T(8,128)S(1)} custom-call(f32[104,256]{1,0:T(8,128)S(1)} %get-tuple-element.31.inside, f32[2,16,128]{2,1,0:T(8,128)S(1)} %collective-permute-done.core, f32[2,16,128]{2,1,0:T(8,128)S(1)} %collective-permute-done.1.chip, f32[2,2,6,16,128]{4,3,2,1,0:T(8,128)S(1)} %get-tuple-element.33.edge_members, ...), custom_call_target="tpu_custom_call" | custom-call | tf_op jit(solution)/shard_map/pallas_call | solution.py:328
  8.4 2.8 %collective-permute-start.4 = (f32[104,256]{1,0:T(8,128)S(1)}, f32[104,256]{1,0:T(8,128)S(1)}, u32[]{:S(2)}, u32[]{:S(2)}) collective-permute-start(f32[104,256]{1,0:T(8,128)S(1)} %shard_map.115.refs_0_.i0), channel_id=1, source_target_pairs={{0,3},{1,2},{2,1},{3,0},{4,7},{5,6},{6,5},{7,4},{8,11},{9,10},{10,... | collective-permute-start | bytes 319496 | tf_op jit(solution)/shard_map/ppermute | solution.py:428
  12.0 1.4 %shard_map.116 = (f32[6,16,256]{2,1,0:T(8,128)S(1)}, s32[2,16]{1,0:T(2,128)S(1)}, bf16[2,512,256]{2,1,0:T(8,128)(2,1)S(1)}, bf16[2,256,256]{2,1,0:T(8,128)(2,1)S...) custom-call(f32[104,256]{1,0:T(8,128)S(1)} %shard_map.115.refs_0_.i0, ...), custom_call_target="tpu_custom_call" | custom-call | bytes 3088640 | tf_op jit(solution)/shard_map/pallas_call | solution.py:381
  13.4 1.5 %collective-permute-done.4.i3 = f32[104,256]{1,0:T(8,128)S(1)} collective-permute-done((f32[104,256]{1,0:T(8,128)S(1)}, f32[104,256]{1,0:T(8,128)S(1)}, u32[]{:S(2)}, u32[]{:S(2)}) %collective-permute-start.4) | collective-permute-done | bytes 106528 | tf_op jit(solution)/shard_map/ppermute | solution.py:428
  14.9 2.2 %collective-permute-done.3.i2 = f32[104,256]{1,0:T(8,128)S(1)} collective-permute-done((f32[104,256]{1,0:T(8,128)S(1)}, f32[104,256]{1,0:T(8,128)S(1)}, u32[]{:S(2)}, u32[]{:S(2)}) %collective-permute-start.3) | collective-permute-done | bytes 106528 | tf_op jit(solution)/shard_map/ppermute | solution.py:428
  17.5 2.6 %collective-permute-start.6 = (f32[2,16,128]{2,1,0:T(8,128)S(1)}, f32[2,16,128]{2,1,0:T(8,128)S(1)}, u32[]{:S(2)}, u32[]{:S(2)}) collective-permute-start(f32[2,16,128]{2,1,0:T(8,128)S(1)} %get-tuple-element.43), channel_id=1, source_target_pairs={{0,28},{4,8},{8,4},{12,16},{16,12},{20,24},{24,20},{28,0},{1,29},{... | collective-permute-start | bytes 49160 | tf_op jit(solution)/shard_map/ppermute | solution.py:423
  20.1 0.8 %shard_map.118 = f32[6,16,256]{2,1,0:T(8,128)S(1)} custom-call(f32[16,16,256]{2,1,0:T(8,128)S(1)} %get-tuple-element.39.back, bf16[2,256,256]{2,1,0:T(8,128)(2,1)S(1)} %get-tuple-element.40.column, bf16[2,256,256]{2,1,0:T(8,128)(2,1)S(1)} %get-tuple-element.41.row, bf16[16,6,16,256]{3,2,1,0:T(8,128)(2,1)S(1)} %get-tuple-element.38.members_ref), custom_call_target="tpu_custom_call" | custom-call | tf_op jit(solution)/shard_map/pallas_call | solution.py:328
  20.9 1.6 %collective-permute-done.6.chip = f32[2,16,128]{2,1,0:T(8,128)S(1)} collective-permute-done((f32[2,16,128]{2,1,0:T(8,128)S(1)}, f32[2,16,128]{2,1,0:T(8,128)S(1)}, u32[]{:S(2)}, u32[]{:S(2)}) %collective-permute-start.6) | collective-permute-done | bytes 16416 | tf_op jit(solution)/shard_map/ppermute | solution.py:423
  23.1 1.8 %collective-permute-start.9 = (f32[96,256]{1,0:T(8,128)S(1)}, f32[96,256]{1,0:T(8,128)S(1)}, u32[]{:S(2)}, u32[]{:S(2)}) collective-permute-start(f32[96,256]{1,0:T(8,128)S(1)} %shard_map.119.i0), channel_id=1, source_target_pairs={{0,3},{1,2},{2,1},{3,0},{4,7},{5,6},{6,5},{7,4},{8,11},{9,10},{10,... | collective-permute-start | bytes 294920 | tf_op jit(solution)/shard_map/ppermute | solution.py:428
  24.9 1.3 %collective-permute-start.8 = (f32[96,256]{1,0:T(8,128)S(1)}, f32[96,256]{1,0:T(8,128)S(1)}, u32[]{:S(2)}, u32[]{:S(2)}) collective-permute-start(f32[96,256]{1,0:T(8,128)S(1)} %shard_map.119.i0), channel_id=1, source_target_pairs={{0,2},{1,3},{2,0},{3,1},{4,6},{5,7},{6,4},{7,5},{8,10},{9,11},{10,... | collective-permute-start | bytes 294920 | tf_op jit(solution)/shard_map/ppermute | solution.py:428
  26.7 2.5 %collective-permute-done.9.i3 = f32[96,256]{1,0:T(8,128)S(1)} collective-permute-done((f32[96,256]{1,0:T(8,128)S(1)}, f32[96,256]{1,0:T(8,128)S(1)}, u32[]{:S(2)}, u32[]{:S(2)}) %collective-permute-start.9) | collective-permute-done | bytes 98336 | tf_op jit(solution)/shard_map/ppermute | solution.py:428
  29.2 0.9 %collective-permute-done.8.i2 = f32[96,256]{1,0:T(8,128)S(1)} collective-permute-done((f32[96,256]{1,0:T(8,128)S(1)}, f32[96,256]{1,0:T(8,128)S(1)}, u32[]{:S(2)}, u32[]{:S(2)}) %collective-permute-start.8) | collective-permute-done | bytes 98336 | tf_op jit(solution)/shard_map/ppermute | solution.py:428
  30.1 0.7 %collective-permute-done.7.i1 = f32[96,256]{1,0:T(8,128)S(1)} collective-permute-done((f32[96,256]{1,0:T(8,128)S(1)}, f32[96,256]{1,0:T(8,128)S(1)}, u32[]{:S(2)}, u32[]{:S(2)}) %collective-permute-start.7) | collective-permute-done | bytes 98336 | tf_op jit(solution)/shard_map/ppermute | solution.py:428
  31.1 1.2 %collective-permute-done.10.core = f32[40,128]{1,0:T(8,128)S(1)} collective-permute-done((f32[40,128]{1,0:T(8,128)S(1)}, f32[40,128]{1,0:T(8,128)S(1)}, u32[]{:S(2)}, u32[]{:S(2)}) %collective-permute-start.10) | collective-permute-done | bytes 20512 | tf_op jit(solution)/shard_map/ppermute | solution.py:414
  32.3 1.5 %collective-permute-start.13 = (f32[32,128]{1,0:T(8,128)S(1)}, f32[32,128]{1,0:T(8,128)S(1)}, u32[]{:S(2)}, u32[]{:S(2)}) collective-permute-start(f32[32,128]{1,0:T(8,128)S(1)} %shard_map.122), channel_id=1, source_target_pairs={{0,28},{4,8},{8,4},{12,16},{16,12},{20,24},{24,20},{28,0},{1,29},{... | collective-permute-start | bytes 49160 | tf_op jit(solution)/shard_map/ppermute | solution.py:423
  33.8 0.8 %shard_map.121.first = f32[16,16,256]{2,1,0:T(8,128)S(1)} custom-call(f32[16,16,256]{2,1,0:T(8,128)S(1)} %get-tuple-element.39.back, f32[32,128]{1,0:T(8,128)S(1)} %bitcast.10, f32[32,128]{1,0:T(8,128)S(1)} %bitcast.11, bf16[2,512,256]{2,1,0:T(8,128)(2,1)S(1)} %get-tuple-element.50.column, bf16[2,256,256]{2,1,0:T(8,128)(2,1)S(1)} %get-tuple-element.51.row), custom_call_target="tpu_custom_call" | custom-call | flops 1000000000 | bytes 1000000 | tf_op jit(solution)/shard_map/pallas_call | solution.py:328
  34.6 1.3 %collective-permute-done.11 = f32[8,128]{1,0:T(8,128)S(1)} collective-permute-done((f32[8,128]{1,0:T(8,128)S(1)}, f32[8,128]{1,0:T(8,128)S(1)}, u32[]{:S(2)}, u32[]{:S(2)}) %collective-permute-start.11) | collective-permute-done | bytes 4128 | tf_op jit(solution)/shard_map/ppermute | solution.py:414
  36.2 1.3 %collective-permute-done.13.chip = f32[32,128]{1,0:T(8,128)S(1)} collective-permute-done((f32[32,128]{1,0:T(8,128)S(1)}, f32[32,128]{1,0:T(8,128)S(1)}, u32[]{:S(2)}, u32[]{:S(2)}) %collective-permute-start.13) | collective-permute-done | bytes 16416 | tf_op jit(solution)/shard_map/ppermute | solution.py:423
  37.4 0.8 %shard_map.123.second = f32[16,16,256]{2,1,0:T(8,128)S(1)} custom-call(f32[16,16,256]{2,1,0:T(8,128)S(1)} %get-tuple-element.52.back, f32[40,128]{1,0:T(8,128)S(1)} %collective-permute-done.10.core, f32[32,128]{1,0:T(8,128)S(1)} %collective-permute-done.13.chip, bf16[2,512,256]{2,1,0:T(8,128)(2,1)S(1)} %get-tuple-element.50.column, ...), custom_call_target="tpu_custom_call" | custom-call | flops 1000000000 | bytes 1000000 | tf_op jit(solution)/shard_map/pallas_call | solution.py:328
  38.2 2.2 %collective-permute-done.12.other = f32[8,128]{1,0:T(8,128)S(1)} collective-permute-done((f32[8,128]{1,0:T(8,128)S(1)}, f32[8,128]{1,0:T(8,128)S(1)}, u32[]{:S(2)}, u32[]{:S(2)}) %collective-permute-start.12) | collective-permute-done | bytes 4128 | tf_op jit(solution)/shard_map/ppermute | solution.py:414
  40.4 1.0 %shard_map.124 = (f32[16,16,256]{2,1,0:T(8,128)}, f32[16,16,256]{2,1,0:T(8,128)}) custom-call(f32[8,128]{1,0:T(8,128)S(1)} %add.7.own, f32[8,128]{1,0:T(8,128)S(1)} %collective-permute-done.12.other, f32[16,16,256]{2,1,0:T(8,128)S(1)} %get-tuple-element.29.source, f32[16,16,256]{2,1,0:T(8,128)S(1)} %shard_map.121.first, f32[16,16,256]{2,1,0:T(8,128)S(1)} %shard_map.123.second), custom_call_target="tpu_custom_call" | custom-call | tf_op jit(solution)/shard_map/pallas_call | solution.py:395
  (18 shorter events, 2.8 us)
Async XLA Ops:
  1.7 6.1 %collective-permute-start.1 = (f32[2,16,128]{2,1,0:T(8,128)S(1)}, f32[2,16,128]{2,1,0:T(8,128)S(1)}, u32[]{:S(2)}, u32[]{:S(2)}) collective-permute-start(f32[2,16,128]{2,1,0:T(8,128)S(1)} %get-tuple-element.32), channel_id=1, source_target_pairs={{0,28},{4,8},{8,4},{12,16},{16,12},{20,24},{24,20},{28,0},{1,29},{... | collective-permute-start | bytes 49160 | tf_op jit(solution)/shard_map/ppermute | solution.py:423
  6.3 1.6 %collective-permute-start = (f32[2,16,128]{2,1,0:T(8,128)S(1)}, f32[2,16,128]{2,1,0:T(8,128)S(1)}, u32[]{:S(2)}, u32[]{:S(2)}) collective-permute-start(f32[2,16,128]{2,1,0:T(8,128)S(1)} %get-tuple-element.30.after), channel_id=1, source_target_pairs={{0,4},{4,0},{8,12},{12,8},{16,20},{20,16},{24,28},{28,24},{1,5},{5... | collective-permute-start | bytes 49160 | tf_op jit(solution)/shard_map/ppermute | solution.py:414
  8.4 6.5 %collective-permute-start.4 = (f32[104,256]{1,0:T(8,128)S(1)}, f32[104,256]{1,0:T(8,128)S(1)}, u32[]{:S(2)}, u32[]{:S(2)}) collective-permute-start(f32[104,256]{1,0:T(8,128)S(1)} %shard_map.115.refs_0_.i0), channel_id=1, source_target_pairs={{0,3},{1,2},{2,1},{3,0},{4,7},{5,6},{6,5},{7,4},{8,11},{9,10},{10,... | collective-permute-start | bytes 319496 | tf_op jit(solution)/shard_map/ppermute | solution.py:428
  11.3 5.8 %collective-permute-start.3 = (f32[104,256]{1,0:T(8,128)S(1)}, f32[104,256]{1,0:T(8,128)S(1)}, u32[]{:S(2)}, u32[]{:S(2)}) collective-permute-start(f32[104,256]{1,0:T(8,128)S(1)} %shard_map.115.refs_0_.i0), channel_id=1, source_target_pairs={{0,2},{1,3},{2,0},{3,1},{4,6},{5,7},{6,4},{7,5},{8,10},{9,11},{10,... | collective-permute-start | bytes 319496 | tf_op jit(solution)/shard_map/ppermute | solution.py:428
  11.8 5.3 %collective-permute-start.2 = (f32[104,256]{1,0:T(8,128)S(1)}, f32[104,256]{1,0:T(8,128)S(1)}, u32[]{:S(2)}, u32[]{:S(2)}) collective-permute-start(f32[104,256]{1,0:T(8,128)S(1)} %shard_map.115.refs_0_.i0), channel_id=1, source_target_pairs={{0,1},{1,0},{2,3},{3,2},{4,5},{5,4},{6,7},{7,6},{8,9},{9,8},{10,11... | collective-permute-start | bytes 319496 | tf_op jit(solution)/shard_map/ppermute | solution.py:428
  17.5 3.5 %collective-permute-start.5 = (f32[2,16,128]{2,1,0:T(8,128)S(1)}, f32[2,16,128]{2,1,0:T(8,128)S(1)}, u32[]{:S(2)}, u32[]{:S(2)}) collective-permute-start(f32[2,16,128]{2,1,0:T(8,128)S(1)} %get-tuple-element.42), channel_id=1, source_target_pairs={{0,4},{4,0},{8,12},{12,8},{16,20},{20,16},{24,28},{28,24},{1,5},{5... | collective-permute-start | bytes 49160 | tf_op jit(solution)/shard_map/ppermute | solution.py:414
  17.5 5.0 %collective-permute-start.6 = (f32[2,16,128]{2,1,0:T(8,128)S(1)}, f32[2,16,128]{2,1,0:T(8,128)S(1)}, u32[]{:S(2)}, u32[]{:S(2)}) collective-permute-start(f32[2,16,128]{2,1,0:T(8,128)S(1)} %get-tuple-element.43), channel_id=1, source_target_pairs={{0,28},{4,8},{8,4},{12,16},{16,12},{20,24},{24,20},{28,0},{1,29},{... | collective-permute-start | bytes 49160 | tf_op jit(solution)/shard_map/ppermute | solution.py:423
  23.1 6.1 %collective-permute-start.9 = (f32[96,256]{1,0:T(8,128)S(1)}, f32[96,256]{1,0:T(8,128)S(1)}, u32[]{:S(2)}, u32[]{:S(2)}) collective-permute-start(f32[96,256]{1,0:T(8,128)S(1)} %shard_map.119.i0), channel_id=1, source_target_pairs={{0,3},{1,2},{2,1},{3,0},{4,7},{5,6},{6,5},{7,4},{8,11},{9,10},{10,... | collective-permute-start | bytes 294920 | tf_op jit(solution)/shard_map/ppermute | solution.py:428
  24.9 5.2 %collective-permute-start.8 = (f32[96,256]{1,0:T(8,128)S(1)}, f32[96,256]{1,0:T(8,128)S(1)}, u32[]{:S(2)}, u32[]{:S(2)}) collective-permute-start(f32[96,256]{1,0:T(8,128)S(1)} %shard_map.119.i0), channel_id=1, source_target_pairs={{0,2},{1,3},{2,0},{3,1},{4,6},{5,7},{6,4},{7,5},{8,10},{9,11},{10,... | collective-permute-start | bytes 294920 | tf_op jit(solution)/shard_map/ppermute | solution.py:428
  26.2 4.6 %collective-permute-start.7 = (f32[96,256]{1,0:T(8,128)S(1)}, f32[96,256]{1,0:T(8,128)S(1)}, u32[]{:S(2)}, u32[]{:S(2)}) collective-permute-start(f32[96,256]{1,0:T(8,128)S(1)} %shard_map.119.i0), channel_id=1, source_target_pairs={{0,1},{1,0},{2,3},{3,2},{4,5},{5,4},{6,7},{7,6},{8,9},{9,8},{10,11... | collective-permute-start | bytes 294920 | tf_op jit(solution)/shard_map/ppermute | solution.py:428
  31.0 1.3 %collective-permute-start.10 = (f32[40,128]{1,0:T(8,128)S(1)}, f32[40,128]{1,0:T(8,128)S(1)}, u32[]{:S(2)}, u32[]{:S(2)}) collective-permute-start(f32[40,128]{1,0:T(8,128)S(1)} %get-tuple-element.49), channel_id=1, source_target_pairs={{0,4},{4,0},{8,12},{12,8},{16,20},{20,16},{24,28},{28,24},{1,5},{5... | collective-permute-start | bytes 61448 | tf_op jit(solution)/shard_map/ppermute | solution.py:414
  32.3 3.6 %collective-permute-start.11 = (f32[8,128]{1,0:T(8,128)S(1)}, f32[8,128]{1,0:T(8,128)S(1)}, u32[]{:S(2)}, u32[]{:S(2)}) collective-permute-start(f32[8,128]{1,0:T(8,128)S(1)} %slice_add_fusion.after), channel_id=1, source_target_pairs={{0,8},{4,12},{8,0},{12,4},{16,24},{20,28},{24,16},{28,20},{1,9},{5... | collective-permute-start | bytes 12296 | tf_op jit(solution)/shard_map/ppermute | solution.py:414
  32.3 5.1 %collective-permute-start.13 = (f32[32,128]{1,0:T(8,128)S(1)}, f32[32,128]{1,0:T(8,128)S(1)}, u32[]{:S(2)}, u32[]{:S(2)}) collective-permute-start(f32[32,128]{1,0:T(8,128)S(1)} %shard_map.122), channel_id=1, source_target_pairs={{0,28},{4,8},{8,4},{12,16},{16,12},{20,24},{24,20},{28,0},{1,29},{... | collective-permute-start | bytes 49160 | tf_op jit(solution)/shard_map/ppermute | solution.py:423
  35.9 4.5 %collective-permute-start.12 = (f32[8,128]{1,0:T(8,128)S(1)}, f32[8,128]{1,0:T(8,128)S(1)}, u32[]{:S(2)}, u32[]{:S(2)}) collective-permute-start(f32[8,128]{1,0:T(8,128)S(1)} %add.7.own), channel_id=1, source_target_pairs={{0,16},{4,20},{8,24},{12,28},{16,0},{20,4},{24,8},{28,12},{1,17},{... | collective-permute-start | bytes 12296 | tf_op jit(solution)/shard_map/ppermute | solution.py:414

commit v5 on v4

--- a/solution.py
+++ b/solution.py
@@ -76,29 +76,38 @@
     return lax.broadcasted_iota(jnp.int32, shape, len(shape) - 1)
 
 
-def pack_edges(field, edge, first):
-    members, rows, width = field.shape
+def pack_columns(field, start, edge):
+    members, rows, _ = field.shape
     slots = LANES // edge
     groups = members // slots
     lane = lane_of((rows, LANES))
+    origin = start // LANES * LANES
     out = []
     for g in range(groups):
         total = jnp.zeros((rows, LANES), F32)
         for j in range(slots):
-            member = field[j * groups + g]
-            block = member[:, :LANES] if first else member[:, width - LANES :]
-            start = 0 if first else LANES - edge
-            shift = (j * edge - start) % LANES
+            block = field[j * groups + g][:, origin : origin + LANES]
+            shift = (j * edge - (start - origin)) % LANES
             moved = pltpu.roll(block, shift, 1) if shift else block
             total = jnp.where((lane >= j * edge) & (lane < (j + 1) * edge), moved, total)
         out.append(total)
     return jnp.stack(out)
 
 
-def edges_for_partners(field, edge):
-    odd = lax.axis_index("tile") % 2 == 1
-    first, last = pack_edges(field, edge, True), pack_edges(field, edge, False)
-    return jnp.where(odd, first, last), jnp.where(odd, last, first)
+def pack_edges(field, edge, first):
+    return pack_columns(field, 0 if first else field.shape[-1] - edge, edge)
+
+
+def repeated(x, period):
+    while period < LANES:
+        x = x + pltpu.roll(x, period, len(x.shape) - 1)
+        period *= 2
+    return x
+
+
+def level_lanes(shape, level):
+    lane = lane_of(shape)
+    return (lane >= level * EDGE) & (lane < (level + 1) * EDGE)
 
 
 def sides_of(core, chip):
@@ -114,9 +123,8 @@
     return jnp.concatenate(parts, axis=0).reshape(slots * groups * rows, LANES)
 
 
-def beside(field, core, chip, edge):
+def beside(field, left, right, edge):
     members, rows, width = field.shape
-    left, right = sides_of(core, chip)
     return jnp.concatenate(
         [field.reshape(members * rows, width), spread_edges(left, edge), spread_edges(right, edge)], axis=1
     )
@@ -150,11 +158,47 @@
     return sum(x[:, i : i + LANES] for i in range(0, width, LANES))
 
 
-def edges_kernel(source, held, to_core, to_chip, sem):
-    copy = pltpu.make_async_copy(source, held, sem)
-    copy.start()
-    copy.wait()
-    to_core[...], to_chip[...] = edges_for_partners(held, EDGE)
+def edges_kernel(
+    source_hbm, members_hbm, precision_hbm, covered_hbm,
+    source, members_ref, obs_weight, near, edge_members, to_core, to_chip, precision, covered, sems,
+):
+    pairs = ((source_hbm, source), (precision_hbm, precision), (covered_hbm, covered), (members_hbm, members_ref))
+    copies = [pltpu.make_async_copy(x, y, sems.at[i]) for i, (x, y) in enumerate(pairs)]
+    for copy in copies:
+        copy.start()
+    members, levels, height, width = members_ref.shape
+    groups = members * EDGE // LANES
+    odd = lax.axis_index("tile") % 2 == 1
+    rows = groups * height
+
+    def send(at, first, last):
+        first, last = (x.reshape(-1, LANES) for x in (first, last))
+        part = pl.ds(at, first.shape[0])
+        to_core[part] = jnp.where(odd, first, last)
+        to_chip[part] = jnp.where(odd, last, first)
+
+    copies[0].wait()
+    near[0], near[1] = pack_columns(source, 0, EDGE), pack_columns(source, width - EDGE, EDGE)
+    send(0, near[0], near[1])
+    send(rows, pack_columns(source, EDGE, EDGE), pack_columns(source, width - 2 * EDGE, EDGE))
+    copies[1].wait()
+    copies[2].wait()
+    obs_weight[...] = weight_of(precision, covered)
+    sides = []
+    for start in (0, width - EDGE):
+        total = jnp.zeros((height, LANES), F32)
+        for v in range(levels):
+            origin = start // LANES * LANES
+            shift = (v * EDGE - (start - origin)) % LANES
+            block = obs_weight[v, :, origin : origin + LANES]
+            total = jnp.where(level_lanes(total.shape, v), pltpu.roll(block, shift, 1) if shift else block, total)
+        sides.append(total)
+    send(rows * (2 + levels), *sides)
+    copies[3].wait()
+    for v in range(levels):
+        level = members_ref[:, v].astype(F32)
+        edge_members[0, v], edge_members[1, v] = pack_edges(level, EDGE, True), pack_edges(level, EDGE, False)
+        send(rows * (2 + v), edge_members[0, v], edge_members[1, v])
 
 
 def fetch_kernel(*refs):
@@ -188,9 +232,7 @@
     ref[0], ref[1] = split(matrix)
 
 
-def first_kernel(source, after, members_hbm, increment, members_ref, edge_members, edge, thin, sem):
-    copy = pltpu.make_async_copy(members_hbm, members_ref, sem)
-    copy.start()
+def first_kernel(source, after, members_ref, increment, edge, thin):
     members, levels, height, width = members_ref.shape
     _, _, gap = gaps(width, width)
     column = split(tap_at(gap, True))
@@ -199,47 +241,62 @@
     lhs = split(source[...].reshape(members * height, width))
     smoothed = dot3(row, split(dot3(lhs, column))).reshape(source.shape)
     increment[levels * height :] = (source[...] * source[...]).reshape(-1, 8, width).sum(axis=0)
+    increment[: levels * height] = increments(members_ref, smoothed).reshape(levels * height, width)
     down, across, gap = gaps(LANES, LANES)
     same = down // EDGE == across // EDGE
-    kept(edge.at[0], tap_at(gap - EDGE, same))
-    kept(edge.at[1], tap_at(gap + EDGE, same))
+    for i in range(3):
+        kept(edge.at[i], tap_at(gap + (i - 1) * EDGE, same))
     down, across, gap = gaps(*thin.shape[1:])
     kept(thin, tap_at(gap, down // height == across // height))
-    copy.wait()
-    increment[: levels * height] = increments(members_ref, smoothed).reshape(levels * height, width)
-    for v in range(levels):
-        level = members_ref[:, v].astype(F32)
-        edge_members[0, :, v] = pack_edges(level, EDGE, True)
-        edge_members[1, :, v] = pack_edges(level, EDGE, False)
-
-
-def second_kernel(back, column, row, members_ref, increment):
-    increment[...] = increments(members_ref, own_columns(back, column, row))
-
-
-def edge_kernel(inside, core, chip, edge_members, edge, thin, out):
-    groups, height, _ = core.shape
-    levels = edge_members.shape[2]
+
+
+def edge_sums(edge_members, smoothed):
+    groups, height = edge_members.shape[1:3]
+    return repeated(jnp.sum(edge_members * smoothed.reshape(1, groups, height, LANES), axis=1), EDGE)
+
+
+def add_edges(out, sums, side):
+    levels, height, _ = sums.shape
     width = out.shape[-1]
-    halo = jnp.concatenate([side.reshape(groups * height, LANES) for side in sides_of(core[...], chip[...])], axis=1)
-    halo = dot3(both(thin), split(halo))
-    lane = lane_of((levels, height, LANES))
-    out[...] = inside[...]
-    for side in range(2):
-        part = halo[:, :LANES] if side == 0 else halo[:, LANES:]
-        part = dot3(split(part), (edge[side, 0], edge[side, 1])).reshape(groups, 1, height, LANES)
-        total = jnp.sum(edge_members[side] * part, axis=0).reshape(levels * height, LANES)
-        step = EDGE
-        while step < LANES:
-            total = total + pltpu.roll(total, step, 1)
-            step *= 2
-        total = total.reshape(levels, height, LANES)
-        if side == 0:
-            span, mask = pl.ds(0, LANES), lane < EDGE
-        else:
-            span, mask = pl.ds(width - LANES, LANES), lane >= LANES - EDGE
-        rows = pl.ds(0, levels * height)
-        out[rows, span] = out[rows, span] + jnp.where(mask, total, 0.0).reshape(levels * height, LANES)
+    lane = lane_of(sums.shape)
+    if side == 0:
+        span, mask = pl.ds(0, LANES), lane < EDGE
+    else:
+        span, mask = pl.ds(width - LANES, LANES), lane >= LANES - EDGE
+    rows = pl.ds(0, levels * height)
+    out[rows, span] = out[rows, span] + jnp.where(mask, sums, 0.0).reshape(levels * height, LANES)
+
+
+def halo_members(block, rows, groups, levels):
+    height = rows // groups
+    return block[2 * rows : (2 + levels) * rows].reshape(levels, groups, height, LANES)
+
+
+def edge_kernel(inside, core, chip, near, edge_members, edge, thin, out):
+    levels, groups, height = edge_members.shape[1:4]
+    width = out.shape[-1]
+    rows = groups * height
+    out[: inside.shape[0]] = inside[...]
+    sides = sides_of(core[...], chip[...])
+    parts = []
+    for side, block in enumerate(sides):
+        parts += [block[rows : 2 * rows], block[:rows], near[side].reshape(rows, LANES)]
+    filtered = split(dot3(both(thin), split(jnp.concatenate(parts, axis=1))))
+    outer = []
+    for side, block in enumerate(sides):
+        span = slice(3 * side * LANES, 3 * (side + 1) * LANES)
+        order = (0, 1, 2) if side == 0 else (2, 1, 0)
+        matrix = [jnp.concatenate([edge[i, k] for i in order], axis=0) for k in range(2)]
+        beyond = dot3(tuple(x[:, span] for x in filtered), matrix)
+        middle = slice(span.start + LANES, span.start + 2 * LANES)
+        within = dot3(tuple(x[:, middle] for x in filtered), both(edge.at[order[0]]))
+        add_edges(out, edge_sums(edge_members[side], within), side)
+        sums = edge_sums(halo_members(block, rows, groups, levels), beyond)
+        total = jnp.zeros((height, LANES), F32)
+        for v in range(levels):
+            total = jnp.where(level_lanes(total.shape, v), sums[v], total)
+        outer.append(total)
+    out[inside.shape[0] :] = jnp.concatenate(outer, axis=1)
 
 
 def weight_of(precision, covered):
@@ -253,24 +310,45 @@
     return precision[...] * mask
 
 
-def adjoint_kernel(
-    i0, i1, i2, i3, precision, covered, members_ref, back, to_core, to_chip, obs_weight, weighted, sums
+def middle_kernel(
+    i0, i1, i2, i3, obs_weight, core, chip, members_ref, edge_members, column, row, edge, thin,
+    back, halo, weighted, sums, out,
 ):
-    levels, height, width = precision.shape
+    levels, height, width = obs_weight.shape
+    groups = edge_members.shape[2]
+    rows = groups * height
     total = (i0[...] + i1[...]) + (i2[...] + i3[...])
-    increment = total[: levels * height].reshape(levels, height, width)
-    obs_weight[...] = weight_of(precision, covered)
+    flat = levels * height
+    increment = total[:flat].reshape(levels, height, width)
     weighted[...] = obs_weight[...] * increment
-    sums[0] = folded(total[levels * height :])
+    sums[0] = folded(total[flat : flat + 8])
     sums[1] = folded(weighted[...] * increment)
     back[...] = adjoint(members_ref, weighted)
-    to_core[...], to_chip[...] = edges_for_partners(back, EDGE)
+    smoothed = own_columns(back, column, row)
+    for side, block in enumerate(sides_of(core[...], chip[...])):
+        outer = total[flat + 8 :, side * LANES : (side + 1) * LANES] * block[(2 + levels) * rows :]
+        members = halo_members(block, rows, groups, levels)
+        adjoint_here = jnp.zeros((groups, height, LANES), F32)
+        for v in range(levels):
+            level = repeated(jnp.where(level_lanes(outer.shape, v), outer, 0.0), EDGE)
+            adjoint_here = adjoint_here + members[v] * level
+        halo[side] = adjoint_here
+    filtered = split(dot3(both(thin), split(jnp.concatenate([halo[i].reshape(rows, LANES) for i in range(2)], axis=1))))
+    out[...] = increments(members_ref, smoothed).reshape(flat, width)
+    for side in range(2):
+        part = dot3(tuple(x[:, side * LANES : (side + 1) * LANES] for x in filtered), both(edge.at[side]))
+        add_edges(out, edge_sums(edge_members[side], part), side)
+
+
+def wide_filter_kernel(back, halo, column, row, out):
+    lhs = split(beside(back[...], halo[0], halo[1], EDGE))
+    out[...] = dot3(both(row), split(dot3(lhs, both(column)))).reshape(out.shape)
 
 
 def filter_kernel(back, core, chip, column, row, out):
     groups, height = back.shape[0] * EDGE // LANES, back.shape[1]
-    core, chip = (x[: groups * height].reshape(groups, height, LANES) for x in (core, chip))
-    lhs = split(beside(back[...], core, chip, EDGE))
+    left, right = sides_of(*(x[: groups * height].reshape(groups, height, LANES) for x in (core, chip)))
+    lhs = split(beside(back[...], left, right, EDGE))
     out[...] = dot3(both(row), split(dot3(lhs, both(column)))).reshape(out.shape)
 
 
@@ -339,18 +417,33 @@
     return pltpu.with_memory_space_constraint(array, pltpu.HBM)
 
 
-def held_edges(source):
-    members, height, width = source.shape
-    edges = (members * EDGE // LANES, height, LANES)
+def held_edges(source, members_data, precision, covered):
+    members, levels, height, width = members_data.shape
+    groups = members * EDGE // LANES
+    payload = ((groups * (2 + levels) + 1) * height, LANES)
     vmem = pl.BlockSpec(memory_space=pltpu.VMEM)
+    hbm = pl.BlockSpec(memory_space=pltpu.HBM)
+    arrays = (source, members_data, precision, covered)
     return pl.pallas_call(
         edges_kernel,
-        out_shape=[pltpu.VMEM(source.shape, F32), pltpu.VMEM(edges, F32), pltpu.VMEM(edges, F32)],
-        in_specs=[pl.BlockSpec(memory_space=pltpu.HBM)],
-        out_specs=[vmem] * 3,
-        scratch_shapes=[pltpu.SemaphoreType.DMA],
+        out_shape=[
+            pltpu.VMEM(source.shape, F32),
+            pltpu.VMEM(members_data.shape, members_data.dtype),
+            pltpu.VMEM(precision.shape, F32),
+            pltpu.VMEM((2, groups, height, LANES), F32),
+            pltpu.VMEM((2, levels, groups, height, LANES), F32),
+            pltpu.VMEM(payload, F32),
+            pltpu.VMEM(payload, F32),
+        ],
+        in_specs=[hbm] * 4,
+        out_specs=[vmem] * 7,
+        scratch_shapes=[
+            pltpu.VMEM(precision.shape, F32),
+            pltpu.VMEM(covered.shape, covered.dtype),
+            pltpu.SemaphoreType.DMA((4,)),
+        ],
         compiler_params=pltpu.CompilerParams(vmem_limit_bytes=24 * 1024 * 1024),
-    )(in_hbm(source))
+    )(*map(in_hbm, arrays))
 
 
 def first_increment(source, after, members_data):
@@ -361,17 +454,14 @@
         first_kernel,
         out_shape=[
             pltpu.VMEM((levels * height + 8, width), F32),
-            pltpu.VMEM(members_data.shape, members_data.dtype),
-            pltpu.VMEM((2, groups, levels, height, LANES), F32),
-            pltpu.VMEM((2, 2, LANES, LANES), BF16),
+            pltpu.VMEM((3, 2, LANES, LANES), BF16),
             pltpu.VMEM((2, groups * height, groups * height), BF16),
         ],
-        in_specs=[vmem, vmem, pl.BlockSpec(memory_space=pltpu.HBM)],
-        out_specs=[vmem] * 5,
-        scratch_shapes=[pltpu.SemaphoreType.DMA],
+        in_specs=[vmem] * 3,
+        out_specs=[vmem] * 3,
         compiler_params=pltpu.CompilerParams(vmem_limit_bytes=24 * 1024 * 1024),
-        cost_estimate=pl.CostEstimate(flops=10**8, bytes_accessed=4 * 10**6, transcendentals=0),
-    )(source, after, in_hbm(members_data))
+        cost_estimate=LONG,
+    )(source, after, members_data)
 
 
 def fetched(after, *arrays):
@@ -435,32 +525,32 @@
     taps = taps_np()
     twice = np.convolve(taps, taps)
     field = (members, height, width)
-    edges = (groups, height, LANES)
     plane = (levels, height, width)
     flat = (levels * height, width)
     row = halves(row_matrix(taps, height, members, 1))
     own = np.arange(width)
 
-    source, to_core, to_chip = held_edges(source)
+    source, members_data, obs_weight, near, edge_members, to_core, to_chip = held_edges(
+        source, members_data, precision[0], covered[0]
+    )
     core, chip = from_core(to_core), from_chip(to_chip)
-    inside, members_data, edge_members, edge, thin = first_increment(source, to_core, members_data)
-    (increment,) = call(edge_kernel, [inside.shape], inside, core, chip, edge_members, edge, thin)
+    inside, edge, thin = first_increment(source, to_core, members_data)
+    (increment,) = call(
+        edge_kernel, [((levels + 1) * height + 8, width)], inside, core, chip, near, edge_members, edge, thin
+    )
     parts = from_all(increment, "mem")
-    precision, covered, column, row, column_twice, row_twice, edge, thin = fetched(
-        increment, precision[0], covered[0], halves(column_matrix(taps, width, EDGE)), row,
+    column, row, column_twice, row_twice, edge, thin = fetched(
+        increment, halves(column_matrix(taps, width, EDGE)), row,
         halves(band(twice, own, own)), halves(row_matrix(taps, height, members, 2)),
         edge_matrix(twice, EDGE), halves(row_matrix(taps, height, groups, 2)),
     )
-    back, to_core, to_chip, obs_weight, weighted, sums = call(
-        adjoint_kernel, [field, edges, edges, plane, plane, (2, 8, LANES)], *parts, precision, covered, members_data
+    back, halo, weighted, sums, increment = call(
+        middle_kernel,
+        [field, (2, groups, height, LANES), plane, (2, 8, LANES), flat],
+        *parts, obs_weight, core, chip, members_data, edge_members, column_twice, row_twice, edge, thin,
     )
-    core, chip = from_core(to_core), from_chip(to_chip)
-    (inside,) = call(second_kernel, [plane], back, column_twice, row_twice, members_data)
-    inside = inside.reshape(flat)
-    (increment,) = call(edge_kernel, [flat], inside, core, chip, edge_members, edge, thin)
     parts = from_all(increment, "mem")
-    core, chip = (x.reshape(groups * height, LANES) for x in (core, chip))
-    (first,) = call(filter_kernel, [field], back, core, chip, column, row, cost=LONG)
+    (first,) = call(wide_filter_kernel, [field], back, halo, column, row, cost=LONG)
     back, to_core, to_chip = call(
         last_kernel,
         [field, (groups * height + 8, LANES), (groups * height, LANES)],

time: 41.6 us -> 39.4 us (0.947)
  waiting for transfers between devices: 15.4 us -> 12.5 us
  starting transfers between devices: 16.2 us -> 17.6 us
  Pallas kernels: 9.07 us -> 8.41 us
    ppermute x5 -> x4, starting transfers between devices: 0.39 us -> 3.28 us  [from_tile(): return lax.ppermute(value, 'tile', [(i, i ^ bit) for i in range(count)])]
    ppermute x3 -> x2, starting transfers between devices: 8.7 us -> 6.52 us  [from_chip(): lax.ppermute(value, 'tile', [(i, (i + 1) % count if i % 2 else (i - 1) %...]
    ppermute x5 -> x4, waiting for transfers between devices: 4.69 us -> 2.8 us  [from_tile(): return lax.ppermute(value, 'tile', [(i, i ^ bit) for i in range(count)])]
    ppermute x6, waiting for transfers between devices: 7.81 us -> 6.83 us  [from_all(): lax.ppermute(value, axis, [(i, i ^ k) for i in range(count)])]
    pallas_call x1, Pallas kernels: 1.56 us -> 0.82 us  [first_increment(): pl.pallas_call(first_kernel, out_shape=[pltpu.VMEM((levels * height + 8,...]
    ppermute x6, starting transfers between devices: 7.11 us -> 7.77 us  [from_all(): lax.ppermute(value, axis, [(i, i ^ k) for i in range(count)])]
    pallas_call x1, Pallas kernels: 1.09 us -> 1.64 us  [held_edges(): pl.pallas_call(edges_kernel, out_shape=[pltpu.VMEM(source.shape, F32), pl...]
    pallas_call x8 -> x6, Pallas kernels: 3.98 us -> 3.6 us  [call(): pl.pallas_call(kernel, out_shape=shapes, in_specs=[vmem] * len(operands),...]
  transfers between devices with their start and end apart: 14 -> 12, of which waited for: 11 -> 10; matrix products, arithmetic and copies ran while one was open for 0% -> 0% of each run, Pallas kernels for 13% -> 10%
where the time goes in v5:
time: 39.4 us; the launch traced here: 39.3 us
  starting transfers between devices  17.6 us (45%)
  waiting for transfers between devices  12.5 us (32%)
  Pallas kernels  8.41 us (21%)
  between operations  0.73 us (2%)
    ppermute x6, starting transfers between devices, from_all(): lax.ppermute(value, axis, [(i, i ^ k) for i in range(count)])  7.77 us
    ppermute x6, waiting for transfers between devices, from_all(): lax.ppermute(value, axis, [(i, i ^ k) for i in range(count)])  6.83 us
    ppermute x2, starting transfers between devices, from_chip(): lax.ppermute(value, 'tile', [(i, (i + 1) % count if i % 2 else (i - 1) %...  6.52 us
    pallas_call x6, Pallas kernels, call(): pl.pallas_call(kernel, out_shape=shapes, in_specs=[vmem] * len(operands),...  3.6 us
    ppermute x4, starting transfers between devices, from_tile(): return lax.ppermute(value, 'tile', [(i, i ^ bit) for i in range(count)])  3.28 us
    ppermute x2, waiting for transfers between devices, from_chip(): lax.ppermute(value, 'tile', [(i, (i + 1) % count if i % 2 else (i - 1) %...  2.91 us
    ppermute x4, waiting for transfers between devices, from_tile(): return lax.ppermute(value, 'tile', [(i, i ^ bit) for i in range(count)])  2.8 us
    pallas_call x1, Pallas kernels, held_edges(): pl.pallas_call(edges_kernel, out_shape=[pltpu.VMEM(source.shape, F32), pl...  1.64 us
  transfers between devices with their start and end apart: 12, of which 10 were waited for; matrix products, arithmetic and copies ran while one was open for 0% of the time, Pallas kernels for 10%

profile of v5, /device:TPU:0, one launch (start us, length us, event | category | flops | bytes accessed | tf_op | source)
XLA Modules:
  0.0 39.3 jit_solution(8141599406211794783)
XLA Ops:
  0.6 1.6 %shard_map.113 = (f32[16,16,256]{2,1,0:T(8,128)S(1)}, bf16[16,6,16,256]{3,2,1,0:T(8,128)(2,1)S(1)}, f32[6,16,256]{2,1,0:T(8,128)S(1)}, f32[2,2,16,128]{3,2,1,0:T...) custom-call(f32[16,16,256]{2,1,0:T(8,128)} %bitcast.7, ...), custom_call_target="tpu_custom_call" | custom-call | tf_op jit(solution)/shard_map/pallas_call | solution.py:427
  2.3 4.6 %collective-permute-start.1 = (f32[272,128]{1,0:T(8,128)S(1)}, f32[272,128]{1,0:T(8,128)S(1)}, u32[]{:S(2)}, u32[]{:S(2)}) collective-permute-start(f32[272,128]{1,0:T(8,128)S(1)} %get-tuple-element.32), channel_id=1, source_target_pairs={{0,28},{4,8},{8,4},{12,16},{16,12},{20,24},{24,20},{28,0},{1,29},{... | collective-permute-start | bytes 417800 | tf_op jit(solution)/shard_map/ppermute | solution.py:513
  6.8 0.8 %shard_map.114 = (f32[104,256]{1,0:T(8,128)S(1)}, bf16[3,2,128,128]{3,2,1,0:T(8,128)(2,1)S(1)}, bf16[2,32,32]{2,1,0:T(8,128)(2,1)S(1)}) custom-call(f32[16,16,256]{2,1,0:T(8,128)S(1)} %get-tuple-element.28.source, f32[272,128]{1,0:T(8,128)S(1)} %get-tuple-element.29.after, bf16[16,6,16,256]{3,2,1,0:T(8,128)(2,1)S(1)} %get-tuple-element.30.members_ref), custom_call_target="tpu_custom_call" | custom-call | flops 1000000000 | bytes 1000000 | tf_op jit(solution)/shard_map/pallas_call | solution.py:453
  7.7 2.6 %collective-permute-done.1.chip = f32[272,128]{1,0:T(8,128)S(1)} collective-permute-done((f32[272,128]{1,0:T(8,128)S(1)}, f32[272,128]{1,0:T(8,128)S(1)}, u32[]{:S(2)}, u32[]{:S(2)}) %collective-permute-start.1) | collective-permute-done | bytes 139296 | tf_op jit(solution)/shard_map/ppermute | solution.py:513
  10.2 0.7 %shard_map.115.refs_0_.i0 = f32[120,256]{1,0:T(8,128)S(1)} custom-call(f32[104,256]{1,0:T(8,128)S(1)} %get-tuple-element.31.inside, f32[272,128]{1,0:T(8,128)S(1)} %collective-permute-done.core, f32[272,128]{1,0:T(8,128)S(1)} %collective-permute-done.1.chip, f32[2,2,16,128]{3,2,1,0:T(8,128)S(1)} %get-tuple-element.33.near, ...), custom_call_target="tpu_custom_call" | custom-call | tf_op jit(solution)/shard_map/pallas_call | solution.py:406
  10.9 3.6 %collective-permute-start.4 = (f32[120,256]{1,0:T(8,128)S(1)}, f32[120,256]{1,0:T(8,128)S(1)}, u32[]{:S(2)}, u32[]{:S(2)}) collective-permute-start(f32[120,256]{1,0:T(8,128)S(1)} %shard_map.115.refs_0_.i0), channel_id=1, source_target_pairs={{0,3},{1,2},{2,1},{3,0},{4,7},{5,6},{6,5},{7,4},{8,11},{9,10},{10,... | collective-permute-start | bytes 368648 | tf_op jit(solution)/shard_map/ppermute | solution.py:518
  14.5 0.5 %collective-permute-start.3 = (f32[120,256]{1,0:T(8,128)S(1)}, f32[120,256]{1,0:T(8,128)S(1)}, u32[]{:S(2)}, u32[]{:S(2)}) collective-permute-start(f32[120,256]{1,0:T(8,128)S(1)} %shard_map.115.refs_0_.i0), channel_id=1, source_target_pairs={{0,2},{1,3},{2,0},{3,1},{4,6},{5,7},{6,4},{7,5},{8,10},{9,11},{10,... | collective-permute-start | bytes 368648 | tf_op jit(solution)/shard_map/ppermute | solution.py:518
  15.1 1.4 %shard_map.116 = (bf16[2,512,256]{2,1,0:T(8,128)(2,1)S(1)}, bf16[2,256,256]{2,1,0:T(8,128)(2,1)S(1)}, bf16[2,256,256]{2,1,0:T(8,128)(2,1)S(1)}, bf16[2,256,256]{...) custom-call(f32[120,256]{1,0:T(8,128)S(1)} %shard_map.115.refs_0_.i0, ...), custom_call_target="tpu_custom_call" | custom-call | bytes 2891776 | tf_op jit(solution)/shard_map/pallas_call | solution.py:471
  16.5 1.4 %collective-permute-done.4.i3 = f32[120,256]{1,0:T(8,128)S(1)} collective-permute-done((f32[120,256]{1,0:T(8,128)S(1)}, f32[120,256]{1,0:T(8,128)S(1)}, u32[]{:S(2)}, u32[]{:S(2)}) %collective-permute-start.4) | collective-permute-done | bytes 122912 | tf_op jit(solution)/shard_map/ppermute | solution.py:518
  17.9 1.5 %collective-permute-done.3.i2 = f32[120,256]{1,0:T(8,128)S(1)} collective-permute-done((f32[120,256]{1,0:T(8,128)S(1)}, f32[120,256]{1,0:T(8,128)S(1)}, u32[]{:S(2)}, u32[]{:S(2)}) %collective-permute-start.3) | collective-permute-done | bytes 122912 | tf_op jit(solution)/shard_map/ppermute | solution.py:518
  19.9 1.1 %shard_map.117 = (f32[16,16,256]{2,1,0:T(8,128)S(1)}, f32[2,2,16,128]{3,2,1,0:T(8,128)S(1)}, f32[6,16,256]{2,1,0:T(8,128)S(1)}, f32[2,8,128]{2,1,0:T(8,128)S(1)}, f32[96,256]{1,0:T(8,128)S(1)}) custom-call(f32[120,256]{1,0:T(8,128)S(1)} %shard_map.115.refs_0_.i0, f32[120,256]{1,0:T(8,128)S(1)} %collective-permute-done.2.i1, ...), custom_call_target="tpu_custom_call" | custom-call | tf_op jit(solution)/shard_map/pallas_call | solution.py:406
  21.0 1.6 %collective-permute-start.7 = (f32[96,256]{1,0:T(8,128)S(1)}, f32[96,256]{1,0:T(8,128)S(1)}, u32[]{:S(2)}, u32[]{:S(2)}) collective-permute-start(f32[96,256]{1,0:T(8,128)S(1)} %get-tuple-element.42.i0), channel_id=1, source_target_pairs={{0,3},{1,2},{2,1},{3,0},{4,7},{5,6},{6,5},{7,4},{8,11},{9,10},{10,... | collective-permute-start | bytes 294920 | tf_op jit(solution)/shard_map/ppermute | solution.py:518
  22.6 0.8 %collective-permute-start.6 = (f32[96,256]{1,0:T(8,128)S(1)}, f32[96,256]{1,0:T(8,128)S(1)}, u32[]{:S(2)}, u32[]{:S(2)}) collective-permute-start(f32[96,256]{1,0:T(8,128)S(1)} %get-tuple-element.42.i0), channel_id=1, source_target_pairs={{0,2},{1,3},{2,0},{3,1},{4,6},{5,7},{6,4},{7,5},{8,10},{9,11},{10,... | collective-permute-start | bytes 294920 | tf_op jit(solution)/shard_map/ppermute | solution.py:518
  23.4 1.2 %collective-permute-start.5 = (f32[96,256]{1,0:T(8,128)S(1)}, f32[96,256]{1,0:T(8,128)S(1)}, u32[]{:S(2)}, u32[]{:S(2)}) collective-permute-start(f32[96,256]{1,0:T(8,128)S(1)} %get-tuple-element.42.i0), channel_id=1, source_target_pairs={{0,1},{1,0},{2,3},{3,2},{4,5},{5,4},{6,7},{7,6},{8,9},{9,8},{10,11... | collective-permute-start | bytes 294920 | tf_op jit(solution)/shard_map/ppermute | solution.py:518
  24.6 2.1 %collective-permute-done.7.i3 = f32[96,256]{1,0:T(8,128)S(1)} collective-permute-done((f32[96,256]{1,0:T(8,128)S(1)}, f32[96,256]{1,0:T(8,128)S(1)}, u32[]{:S(2)}, u32[]{:S(2)}) %collective-permute-start.7) | collective-permute-done | bytes 98336 | tf_op jit(solution)/shard_map/ppermute | solution.py:518
  26.6 1.0 %collective-permute-done.6.i2 = f32[96,256]{1,0:T(8,128)S(1)} collective-permute-done((f32[96,256]{1,0:T(8,128)S(1)}, f32[96,256]{1,0:T(8,128)S(1)}, u32[]{:S(2)}, u32[]{:S(2)}) %collective-permute-start.6) | collective-permute-done | bytes 98336 | tf_op jit(solution)/shard_map/ppermute | solution.py:518
  28.3 1.2 %collective-permute-done.8.core = f32[40,128]{1,0:T(8,128)S(1)} collective-permute-done((f32[40,128]{1,0:T(8,128)S(1)}, f32[40,128]{1,0:T(8,128)S(1)}, u32[]{:S(2)}, u32[]{:S(2)}) %collective-permute-start.8) | collective-permute-done | bytes 20512 | tf_op jit(solution)/shard_map/ppermute | solution.py:504
  29.5 1.4 %collective-permute-start.9 = (f32[8,128]{1,0:T(8,128)S(1)}, f32[8,128]{1,0:T(8,128)S(1)}, u32[]{:S(2)}, u32[]{:S(2)}) collective-permute-start(f32[8,128]{1,0:T(8,128)S(1)} %slice_add_fusion.after), channel_id=1, source_target_pairs={{0,8},{4,12},{8,0},{12,4},{16,24},{20,28},{24,16},{28,20},{1,9},{5... | collective-permute-start | bytes 12296 | tf_op jit(solution)/shard_map/ppermute | solution.py:504
  30.9 2.0 %collective-permute-start.11 = (f32[32,128]{1,0:T(8,128)S(1)}, f32[32,128]{1,0:T(8,128)S(1)}, u32[]{:S(2)}, u32[]{:S(2)}) collective-permute-start(f32[32,128]{1,0:T(8,128)S(1)} %shard_map.120), channel_id=1, source_target_pairs={{0,28},{4,8},{8,4},{12,16},{16,12},{20,24},{24,20},{28,0},{1,29},{... | collective-permute-start | bytes 49160 | tf_op jit(solution)/shard_map/ppermute | solution.py:513
  32.9 0.8 %shard_map.119.first = f32[16,16,256]{2,1,0:T(8,128)S(1)} custom-call(f32[16,16,256]{2,1,0:T(8,128)S(1)} %get-tuple-element.46.back, f32[2,2,16,128]{3,2,1,0:T(8,128)S(1)} %get-tuple-element.47.halo, bf16[2,512,256]{2,1,0:T(8,128)(2,1)S(1)} %get-tuple-element.48.column, bf16[2,256,256]{2,1,0:T(8,128)(2,1)S(1)} %get-tuple-element.49.row), custom_call_target="tpu_custom_call" | custom-call | flops 1000000000 | bytes 1000000 | tf_op jit(solution)/shard_map/pallas_call | solution.py:406
  33.7 1.8 %collective-permute-start.10 = (f32[8,128]{1,0:T(8,128)S(1)}, f32[8,128]{1,0:T(8,128)S(1)}, u32[]{:S(2)}, u32[]{:S(2)}) collective-permute-start(f32[8,128]{1,0:T(8,128)S(1)} %add.7.own), channel_id=1, source_target_pairs={{0,16},{4,20},{8,24},{12,28},{16,0},{20,4},{24,8},{28,12},{1,17},{... | collective-permute-start | bytes 12296 | tf_op jit(solution)/shard_map/ppermute | solution.py:504
  35.8 0.8 %shard_map.121.second = f32[16,16,256]{2,1,0:T(8,128)S(1)} custom-call(f32[16,16,256]{2,1,0:T(8,128)S(1)} %get-tuple-element.50.back, f32[40,128]{1,0:T(8,128)S(1)} %collective-permute-done.8.core, f32[32,128]{1,0:T(8,128)S(1)} %collective-permute-done.11.chip, bf16[2,512,256]{2,1,0:T(8,128)(2,1)S(1)} %get-tuple-element.48.column, ...), custom_call_target="tpu_custom_call" | custom-call | flops 1000000000 | bytes 1000000 | tf_op jit(solution)/shard_map/pallas_call | solution.py:406
  36.6 1.6 %collective-permute-done.10.other = f32[8,128]{1,0:T(8,128)S(1)} collective-permute-done((f32[8,128]{1,0:T(8,128)S(1)}, f32[8,128]{1,0:T(8,128)S(1)}, u32[]{:S(2)}, u32[]{:S(2)}) %collective-permute-start.10) | collective-permute-done | bytes 4128 | tf_op jit(solution)/shard_map/ppermute | solution.py:504
  38.3 1.0 %shard_map.122 = (f32[16,16,256]{2,1,0:T(8,128)}, f32[16,16,256]{2,1,0:T(8,128)}) custom-call(f32[8,128]{1,0:T(8,128)S(1)} %add.7.own, f32[8,128]{1,0:T(8,128)S(1)} %collective-permute-done.10.other, f32[16,16,256]{2,1,0:T(8,128)S(1)} %get-tuple-element.28.source, f32[16,16,256]{2,1,0:T(8,128)S(1)} %shard_map.119.first, f32[16,16,256]{2,1,0:T(8,128)S(1)} %shard_map.121.second), custom_call_target="tpu_custom_call" | custom-call | tf_op jit(solution)/shard_map/pallas_call | solution.py:485
  (12 shorter events, 1.7 us)
Async XLA Ops:
  2.3 8.0 %collective-permute-start.1 = (f32[272,128]{1,0:T(8,128)S(1)}, f32[272,128]{1,0:T(8,128)S(1)}, u32[]{:S(2)}, u32[]{:S(2)}) collective-permute-start(f32[272,128]{1,0:T(8,128)S(1)} %get-tuple-element.32), channel_id=1, source_target_pairs={{0,28},{4,8},{8,4},{12,16},{16,12},{20,24},{24,20},{28,0},{1,29},{... | collective-permute-start | bytes 417800 | tf_op jit(solution)/shard_map/ppermute | solution.py:513
  6.8 3.4 %collective-permute-start = (f32[272,128]{1,0:T(8,128)S(1)}, f32[272,128]{1,0:T(8,128)S(1)}, u32[]{:S(2)}, u32[]{:S(2)}) collective-permute-start(f32[272,128]{1,0:T(8,128)S(1)} %get-tuple-element.29.after), channel_id=1, source_target_pairs={{0,4},{4,0},{8,12},{12,8},{16,20},{20,16},{24,28},{28,24},{1,5},{5... | collective-permute-start | bytes 417800 | tf_op jit(solution)/shard_map/ppermute | solution.py:504
  10.9 7.0 %collective-permute-start.4 = (f32[120,256]{1,0:T(8,128)S(1)}, f32[120,256]{1,0:T(8,128)S(1)}, u32[]{:S(2)}, u32[]{:S(2)}) collective-permute-start(f32[120,256]{1,0:T(8,128)S(1)} %shard_map.115.refs_0_.i0), channel_id=1, source_target_pairs={{0,3},{1,2},{2,1},{3,0},{4,7},{5,6},{6,5},{7,4},{8,11},{9,10},{10,... | collective-permute-start | bytes 368648 | tf_op jit(solution)/shard_map/ppermute | solution.py:518
  14.5 4.9 %collective-permute-start.3 = (f32[120,256]{1,0:T(8,128)S(1)}, f32[120,256]{1,0:T(8,128)S(1)}, u32[]{:S(2)}, u32[]{:S(2)}) collective-permute-start(f32[120,256]{1,0:T(8,128)S(1)} %shard_map.115.refs_0_.i0), channel_id=1, source_target_pairs={{0,2},{1,3},{2,0},{3,1},{4,6},{5,7},{6,4},{7,5},{8,10},{9,11},{10,... | collective-permute-start | bytes 368648 | tf_op jit(solution)/shard_map/ppermute | solution.py:518
  15.0 4.9 %collective-permute-start.2 = (f32[120,256]{1,0:T(8,128)S(1)}, f32[120,256]{1,0:T(8,128)S(1)}, u32[]{:S(2)}, u32[]{:S(2)}) collective-permute-start(f32[120,256]{1,0:T(8,128)S(1)} %shard_map.115.refs_0_.i0), channel_id=1, source_target_pairs={{0,1},{1,0},{2,3},{3,2},{4,5},{5,4},{6,7},{7,6},{8,9},{9,8},{10,11... | collective-permute-start | bytes 368648 | tf_op jit(solution)/shard_map/ppermute | solution.py:518
  21.0 5.6 %collective-permute-start.7 = (f32[96,256]{1,0:T(8,128)S(1)}, f32[96,256]{1,0:T(8,128)S(1)}, u32[]{:S(2)}, u32[]{:S(2)}) collective-permute-start(f32[96,256]{1,0:T(8,128)S(1)} %get-tuple-element.42.i0), channel_id=1, source_target_pairs={{0,3},{1,2},{2,1},{3,0},{4,7},{5,6},{6,5},{7,4},{8,11},{9,10},{10,... | collective-permute-start | bytes 294920 | tf_op jit(solution)/shard_map/ppermute | solution.py:518
  22.6 5.1 %collective-permute-start.6 = (f32[96,256]{1,0:T(8,128)S(1)}, f32[96,256]{1,0:T(8,128)S(1)}, u32[]{:S(2)}, u32[]{:S(2)}) collective-permute-start(f32[96,256]{1,0:T(8,128)S(1)} %get-tuple-element.42.i0), channel_id=1, source_target_pairs={{0,2},{1,3},{2,0},{3,1},{4,6},{5,7},{6,4},{7,5},{8,10},{9,11},{10,... | collective-permute-start | bytes 294920 | tf_op jit(solution)/shard_map/ppermute | solution.py:518
  23.4 4.6 %collective-permute-start.5 = (f32[96,256]{1,0:T(8,128)S(1)}, f32[96,256]{1,0:T(8,128)S(1)}, u32[]{:S(2)}, u32[]{:S(2)}) collective-permute-start(f32[96,256]{1,0:T(8,128)S(1)} %get-tuple-element.42.i0), channel_id=1, source_target_pairs={{0,1},{1,0},{2,3},{3,2},{4,5},{5,4},{6,7},{7,6},{8,9},{9,8},{10,11... | collective-permute-start | bytes 294920 | tf_op jit(solution)/shard_map/ppermute | solution.py:518
  28.2 1.3 %collective-permute-start.8 = (f32[40,128]{1,0:T(8,128)S(1)}, f32[40,128]{1,0:T(8,128)S(1)}, u32[]{:S(2)}, u32[]{:S(2)}) collective-permute-start(f32[40,128]{1,0:T(8,128)S(1)} %get-tuple-element.45), channel_id=1, source_target_pairs={{0,4},{4,0},{8,12},{12,8},{16,20},{20,16},{24,28},{28,24},{1,5},{5... | collective-permute-start | bytes 61448 | tf_op jit(solution)/shard_map/ppermute | solution.py:504
  29.5 4.2 %collective-permute-start.9 = (f32[8,128]{1,0:T(8,128)S(1)}, f32[8,128]{1,0:T(8,128)S(1)}, u32[]{:S(2)}, u32[]{:S(2)}) collective-permute-start(f32[8,128]{1,0:T(8,128)S(1)} %slice_add_fusion.after), channel_id=1, source_target_pairs={{0,8},{4,12},{8,0},{12,4},{16,24},{20,28},{24,16},{28,20},{1,9},{5... | collective-permute-start | bytes 12296 | tf_op jit(solution)/shard_map/ppermute | solution.py:504
  30.9 5.0 %collective-permute-start.11 = (f32[32,128]{1,0:T(8,128)S(1)}, f32[32,128]{1,0:T(8,128)S(1)}, u32[]{:S(2)}, u32[]{:S(2)}) collective-permute-start(f32[32,128]{1,0:T(8,128)S(1)} %shard_map.120), channel_id=1, source_target_pairs={{0,28},{4,8},{8,4},{12,16},{16,12},{20,24},{24,20},{28,0},{1,29},{... | collective-permute-start | bytes 49160 | tf_op jit(solution)/shard_map/ppermute | solution.py:513
  33.7 4.6 %collective-permute-start.10 = (f32[8,128]{1,0:T(8,128)S(1)}, f32[8,128]{1,0:T(8,128)S(1)}, u32[]{:S(2)}, u32[]{:S(2)}) collective-permute-start(f32[8,128]{1,0:T(8,128)S(1)} %add.7.own), channel_id=1, source_target_pairs={{0,16},{4,20},{8,24},{12,28},{16,0},{20,4},{24,8},{28,12},{1,17},{... | collective-permute-start | bytes 12296 | tf_op jit(solution)/shard_map/ppermute | solution.py:504

commit v6 on v5

--- a/solution.py
+++ b/solution.py
@@ -13,6 +13,7 @@
 TCOLS = 8
 REACH = 8
 EDGE = 2 * REACH
+SPARE = 32
 LANES = 128
 F32 = jnp.float32
 BF16 = jnp.bfloat16
@@ -232,7 +233,7 @@
     ref[0], ref[1] = split(matrix)
 
 
-def first_kernel(source, after, members_ref, increment, edge, thin):
+def first_kernel(source, after, members_ref, increment, norm, edge, thin):
     members, levels, height, width = members_ref.shape
     _, _, gap = gaps(width, width)
     column = split(tap_at(gap, True))
@@ -240,8 +241,8 @@
     row = split(tap_at(gap, down // height == across // height))
     lhs = split(source[...].reshape(members * height, width))
     smoothed = dot3(row, split(dot3(lhs, column))).reshape(source.shape)
-    increment[levels * height :] = (source[...] * source[...]).reshape(-1, 8, width).sum(axis=0)
-    increment[: levels * height] = increments(members_ref, smoothed).reshape(levels * height, width)
+    increment[...] = increments(members_ref, smoothed).reshape(levels * height, width)
+    norm[...] = repeated(folded(source[...] * source[...]), SPARE)
     down, across, gap = gaps(LANES, LANES)
     same = down // EDGE == across // EDGE
     for i in range(3):
@@ -272,7 +273,7 @@
     return block[2 * rows : (2 + levels) * rows].reshape(levels, groups, height, LANES)
 
 
-def edge_kernel(inside, core, chip, near, edge_members, edge, thin, out):
+def edge_kernel(inside, norm, core, chip, near, edge_members, edge, thin, out):
     levels, groups, height = edge_members.shape[1:4]
     width = out.shape[-1]
     rows = groups * height
@@ -296,7 +297,10 @@
         for v in range(levels):
             total = jnp.where(level_lanes(total.shape, v), sums[v], total)
         outer.append(total)
+    lane = lane_of(norm.shape)
     out[inside.shape[0] :] = jnp.concatenate(outer, axis=1)
+    top = pl.ds(inside.shape[0], norm.shape[0])
+    out[top, :LANES] = jnp.where(lane >= LANES - SPARE, norm[...], out[top, :LANES])
 
 
 def weight_of(precision, covered):
@@ -321,12 +325,13 @@
     flat = levels * height
     increment = total[:flat].reshape(levels, height, width)
     weighted[...] = obs_weight[...] * increment
-    sums[0] = folded(total[flat : flat + 8])
+    top = total[flat : flat + 8, :LANES]
+    sums[0] = jnp.where(lane_of(top.shape) >= LANES - SPARE, top, 0.0)
     sums[1] = folded(weighted[...] * increment)
     back[...] = adjoint(members_ref, weighted)
     smoothed = own_columns(back, column, row)
     for side, block in enumerate(sides_of(core[...], chip[...])):
-        outer = total[flat + 8 :, side * LANES : (side + 1) * LANES] * block[(2 + levels) * rows :]
+        outer = total[flat:, side * LANES : (side + 1) * LANES] * block[(2 + levels) * rows :]
         members = halo_members(block, rows, groups, levels)
         adjoint_here = jnp.zeros((groups, height, LANES), F32)
         for v in range(levels):
@@ -372,6 +377,10 @@
 
 def copy_kernel(value, after, out):
     out[...] = value[...]
+
+
+def pass_kernel(value, after, out):
+    pass
 
 
 def combine_kernel(own, other, source, first, second, weights, residual, held_weights, held_residual, sems):
@@ -411,6 +420,19 @@
         compiler_params=pltpu.CompilerParams(vmem_limit_bytes=24 * 1024 * 1024),
         cost_estimate=cost,
     )(*operands)
+
+
+def passed(value, after):
+    vmem = pl.BlockSpec(memory_space=pltpu.VMEM)
+    return pl.pallas_call(
+        pass_kernel,
+        out_shape=pltpu.VMEM(value.shape, value.dtype),
+        in_specs=[vmem] * 2,
+        out_specs=vmem,
+        input_output_aliases={0: 0},
+        compiler_params=pltpu.CompilerParams(vmem_limit_bytes=24 * 1024 * 1024),
+        cost_estimate=LONG,
+    )(value, after)
 
 
 def in_hbm(array):
@@ -453,12 +475,13 @@
     return pl.pallas_call(
         first_kernel,
         out_shape=[
-            pltpu.VMEM((levels * height + 8, width), F32),
+            pltpu.VMEM((levels * height, width), F32),
+            pltpu.VMEM((8, LANES), F32),
             pltpu.VMEM((3, 2, LANES, LANES), BF16),
             pltpu.VMEM((2, groups * height, groups * height), BF16),
         ],
         in_specs=[vmem] * 3,
-        out_specs=[vmem] * 3,
+        out_specs=[vmem] * 4,
         compiler_params=pltpu.CompilerParams(vmem_limit_bytes=24 * 1024 * 1024),
         cost_estimate=LONG,
     )(source, after, members_data)
@@ -534,9 +557,9 @@
         source, members_data, precision[0], covered[0]
     )
     core, chip = from_core(to_core), from_chip(to_chip)
-    inside, edge, thin = first_increment(source, to_core, members_data)
+    inside, norm, edge, thin = first_increment(source, to_core, members_data)
     (increment,) = call(
-        edge_kernel, [((levels + 1) * height + 8, width)], inside, core, chip, near, edge_members, edge, thin
+        edge_kernel, [((levels + 1) * height, width)], inside, norm, core, chip, near, edge_members, edge, thin
     )
     parts = from_all(increment, "mem")
     column, row, column_twice, row_twice, edge, thin = fetched(
@@ -551,6 +574,7 @@
     )
     parts = from_all(increment, "mem")
     (first,) = call(wide_filter_kernel, [field], back, halo, column, row, cost=LONG)
+    first, weighted = lax.optimization_barrier((first, weighted))
     back, to_core, to_chip = call(
         last_kernel,
         [field, (groups * height + 8, LANES), (groups * height, LANES)],
@@ -560,6 +584,7 @@
     sums = to_core[groups * height :] + core[groups * height :]
     (to_chip,) = call(copy_kernel, [to_chip.shape], to_chip, sums)
     chip = from_chip(to_chip)
+    first = passed(first, sums)
     sums = sums + from_tile(sums, 2)
     others = from_tile(sums, 4)
     (second,) = call(filter_kernel, [field], back, core, chip, column, row, cost=LONG)

time: 39.4 us -> 38.6 us (0.980)
  waiting for transfers between devices: 12.5 us -> 11.5 us
    ppermute x6, waiting for transfers between devices: 6.83 us -> 5.85 us  [from_all(): lax.ppermute(value, axis, [(i, i ^ k) for i in range(count)])]
    pallas_call x1 -> x2, Pallas kernels: 0.82 us -> 0.82 us  [the longest x1 0.82 us: first_increment(): pl.pallas_call(first_kernel, out_shape=[pltpu.VMEM((levels * height, widt...]
  transfers between devices with their start and end apart: 12 -> 12, of which waited for: 10 -> 11; matrix products, arithmetic and copies ran while one was open for 0% -> 0% of each run, Pallas kernels for 10% -> 10%
where the time goes in v6:
time: 38.6 us; the launch traced here: 38.4 us
  starting transfers between devices  17.8 us (46%)
  waiting for transfers between devices  11.5 us (30%)
  Pallas kernels  8.41 us (22%)
  between operations  0.71 us (2%)
    ppermute x6, starting transfers between devices, from_all(): lax.ppermute(value, axis, [(i, i ^ k) for i in range(count)])  7.77 us
    ppermute x2, starting transfers between devices, from_chip(): lax.ppermute(value, 'tile', [(i, (i + 1) % count if i % 2 else (i - 1) %...  6.52 us
    ppermute x6, waiting for transfers between devices, from_all(): lax.ppermute(value, axis, [(i, i ^ k) for i in range(count)])  5.85 us
    pallas_call x6, Pallas kernels, call(): pl.pallas_call(kernel, out_shape=shapes, in_specs=[vmem] * len(operands),...  3.59 us
    ppermute x4, starting transfers between devices, from_tile(): return lax.ppermute(value, 'tile', [(i, i ^ bit) for i in range(count)])  3.5 us
    ppermute x2, waiting for transfers between devices, from_chip(): lax.ppermute(value, 'tile', [(i, (i + 1) % count if i % 2 else (i - 1) %...  2.9 us
    ppermute x4, waiting for transfers between devices, from_tile(): return lax.ppermute(value, 'tile', [(i, i ^ bit) for i in range(count)])  2.77 us
    pallas_call x1, Pallas kernels, held_edges(): pl.pallas_call(edges_kernel, out_shape=[pltpu.VMEM(source.shape, F32), pl...  1.64 us
  transfers between devices with their start and end apart: 12, of which 11 were waited for; matrix products, arithmetic and copies ran while one was open for 0% of the time, Pallas kernels for 10%

profile of v6, /device:TPU:0, one launch (start us, length us, event | category | flops | bytes accessed | tf_op | source)
XLA Modules:
  0.0 38.4 jit_solution(1707885383960397084)
XLA Ops:
  0.6 1.6 %shard_map.113 = (f32[16,16,256]{2,1,0:T(8,128)S(1)}, bf16[16,6,16,256]{3,2,1,0:T(8,128)(2,1)S(1)}, f32[6,16,256]{2,1,0:T(8,128)S(1)}, f32[2,2,16,128]{3,2,1,0:T...) custom-call(f32[16,16,256]{2,1,0:T(8,128)} %bitcast.7, ...), custom_call_target="tpu_custom_call" | custom-call | tf_op jit(solution)/shard_map/pallas_call | solution.py:449
  2.3 4.6 %collective-permute-start.1 = (f32[272,128]{1,0:T(8,128)S(1)}, f32[272,128]{1,0:T(8,128)S(1)}, u32[]{:S(2)}, u32[]{:S(2)}) collective-permute-start(f32[272,128]{1,0:T(8,128)S(1)} %get-tuple-element.36), channel_id=1, source_target_pairs={{0,28},{4,8},{8,4},{12,16},{16,12},{20,24},{24,20},{28,0},{1,29},{... | collective-permute-start | bytes 417800 | tf_op jit(solution)/shard_map/ppermute | solution.py:536
  6.8 0.8 %shard_map.114 = (f32[96,256]{1,0:T(8,128)S(1)}, f32[8,128]{1,0:T(8,128)S(1)}, bf16[3,2,128,128]{3,2,1,0:T(8,128)(2,1)S(1)}, bf16[2,32,32]{2,1,0:T(8,128)(2,1)S(1)}) custom-call(f32[16,16,256]{2,1,0:T(8,128)S(1)} %get-tuple-element.31.source, f32[272,128]{1,0:T(8,128)S(1)} %get-tuple-element.32.after, bf16[16,6,16,256]{3,2,1,0:T(8,128)(2,1)S(1)} %get-tuple-element.33.members_ref), custom_call_target="tpu_custom_call" | custom-call | flops 1000000000 | bytes 1000000 | tf_op jit(solution)/shard_map/pallas_call | solution.py:475
  7.7 2.6 %collective-permute-done.1.chip = f32[272,128]{1,0:T(8,128)S(1)} collective-permute-done((f32[272,128]{1,0:T(8,128)S(1)}, f32[272,128]{1,0:T(8,128)S(1)}, u32[]{:S(2)}, u32[]{:S(2)}) %collective-permute-start.1) | collective-permute-done | bytes 139296 | tf_op jit(solution)/shard_map/ppermute | solution.py:536
  10.2 0.7 %shard_map.115.refs_0_.i0 = f32[112,256]{1,0:T(8,128)S(1)} custom-call(f32[96,256]{1,0:T(8,128)S(1)} %get-tuple-element.34.inside, f32[8,128]{1,0:T(8,128)S(1)} %get-tuple-element.35.norm, f32[272,128]{1,0:T(8,128)S(1)} %collective-permute-done.core, f32[272,128]{1,0:T(8,128)S(1)} %collective-permute-done.1.chip, ...), custom_call_target="tpu_custom_call" | custom-call | tf_op jit(solution)/shard_map/pallas_call | solution.py:415
  10.9 3.6 %collective-permute-start.4 = (f32[112,256]{1,0:T(8,128)S(1)}, f32[112,256]{1,0:T(8,128)S(1)}, u32[]{:S(2)}, u32[]{:S(2)}) collective-permute-start(f32[112,256]{1,0:T(8,128)S(1)} %shard_map.115.refs_0_.i0), channel_id=1, source_target_pairs={{0,3},{1,2},{2,1},{3,0},{4,7},{5,6},{6,5},{7,4},{8,11},{9,10},{10,... | collective-permute-start | bytes 344072 | tf_op jit(solution)/shard_map/ppermute | solution.py:541
  15.1 1.4 %shard_map.116 = (bf16[2,512,256]{2,1,0:T(8,128)(2,1)S(1)}, bf16[2,256,256]{2,1,0:T(8,128)(2,1)S(1)}, bf16[2,256,256]{2,1,0:T(8,128)(2,1)S(1)}, bf16[2,256,256]{...) custom-call(f32[112,256]{1,0:T(8,128)S(1)} %shard_map.115.refs_0_.i0, ...), custom_call_target="tpu_custom_call" | custom-call | bytes 2891776 | tf_op jit(solution)/shard_map/pallas_call | solution.py:494
  16.5 1.1 %collective-permute-done.4.i3 = f32[112,256]{1,0:T(8,128)S(1)} collective-permute-done((f32[112,256]{1,0:T(8,128)S(1)}, f32[112,256]{1,0:T(8,128)S(1)}, u32[]{:S(2)}, u32[]{:S(2)}) %collective-permute-start.4) | collective-permute-done | bytes 114720 | tf_op jit(solution)/shard_map/ppermute | solution.py:541
  17.6 1.6 %collective-permute-done.3.i2 = f32[112,256]{1,0:T(8,128)S(1)} collective-permute-done((f32[112,256]{1,0:T(8,128)S(1)}, f32[112,256]{1,0:T(8,128)S(1)}, u32[]{:S(2)}, u32[]{:S(2)}) %collective-permute-start.3) | collective-permute-done | bytes 114720 | tf_op jit(solution)/shard_map/ppermute | solution.py:541
  19.3 0.5 %collective-permute-done.2.i1 = f32[112,256]{1,0:T(8,128)S(1)} collective-permute-done((f32[112,256]{1,0:T(8,128)S(1)}, f32[112,256]{1,0:T(8,128)S(1)}, u32[]{:S(2)}, u32[]{:S(2)}) %collective-permute-start.2) | collective-permute-done | bytes 114720 | tf_op jit(solution)/shard_map/ppermute | solution.py:541
  19.8 1.1 %shard_map.117 = (f32[16,16,256]{2,1,0:T(8,128)S(1)}, f32[2,2,16,128]{3,2,1,0:T(8,128)S(1)}, f32[6,16,256]{2,1,0:T(8,128)S(1)}, f32[2,8,128]{2,1,0:T(8,128)S(1)}, f32[96,256]{1,0:T(8,128)S(1)}) custom-call(f32[112,256]{1,0:T(8,128)S(1)} %shard_map.115.refs_0_.i0, f32[112,256]{1,0:T(8,128)S(1)} %collective-permute-done.2.i1, ...), custom_call_target="tpu_custom_call" | custom-call | tf_op jit(solution)/shard_map/pallas_call | solution.py:415
  20.9 1.6 %collective-permute-start.7 = (f32[96,256]{1,0:T(8,128)S(1)}, f32[96,256]{1,0:T(8,128)S(1)}, u32[]{:S(2)}, u32[]{:S(2)}) collective-permute-start(f32[96,256]{1,0:T(8,128)S(1)} %get-tuple-element.46.i0), channel_id=1, source_target_pairs={{0,3},{1,2},{2,1},{3,0},{4,7},{5,6},{6,5},{7,4},{8,11},{9,10},{10,... | collective-permute-start | bytes 294920 | tf_op jit(solution)/shard_map/ppermute | solution.py:541
  22.5 0.7 %collective-permute-start.6 = (f32[96,256]{1,0:T(8,128)S(1)}, f32[96,256]{1,0:T(8,128)S(1)}, u32[]{:S(2)}, u32[]{:S(2)}) collective-permute-start(f32[96,256]{1,0:T(8,128)S(1)} %get-tuple-element.46.i0), channel_id=1, source_target_pairs={{0,2},{1,3},{2,0},{3,1},{4,6},{5,7},{6,4},{7,5},{8,10},{9,11},{10,... | collective-permute-start | bytes 294920 | tf_op jit(solution)/shard_map/ppermute | solution.py:541
  23.2 1.3 %collective-permute-start.5 = (f32[96,256]{1,0:T(8,128)S(1)}, f32[96,256]{1,0:T(8,128)S(1)}, u32[]{:S(2)}, u32[]{:S(2)}) collective-permute-start(f32[96,256]{1,0:T(8,128)S(1)} %get-tuple-element.46.i0), channel_id=1, source_target_pairs={{0,1},{1,0},{2,3},{3,2},{4,5},{5,4},{6,7},{7,6},{8,9},{9,8},{10,11... | collective-permute-start | bytes 294920 | tf_op jit(solution)/shard_map/ppermute | solution.py:541
  24.5 0.8 %shard_map.118.value = f32[16,16,256]{2,1,0:T(8,128)S(1)} custom-call(f32[16,16,256]{2,1,0:T(8,128)S(1)} %get-tuple-element.47.back, f32[2,2,16,128]{3,2,1,0:T(8,128)S(1)} %get-tuple-element.48.halo, bf16[2,512,256]{2,1,0:T(8,128)(2,1)S(1)} %get-tuple-element.49.column, bf16[2,256,256]{2,1,0:T(8,128)(2,1)S(1)} %get-tuple-element.50.row), custom_call_target="tpu_custom_call" | custom-call | flops 1000000000 | bytes 1000000 | tf_op jit(solution)/shard_map/pallas_call | solution.py:415
  25.3 1.3 %collective-permute-done.7.i3 = f32[96,256]{1,0:T(8,128)S(1)} collective-permute-done((f32[96,256]{1,0:T(8,128)S(1)}, f32[96,256]{1,0:T(8,128)S(1)}, u32[]{:S(2)}, u32[]{:S(2)}) %collective-permute-start.7) | collective-permute-done | bytes 98336 | tf_op jit(solution)/shard_map/ppermute | solution.py:541
  26.5 1.0 %collective-permute-done.6.i2 = f32[96,256]{1,0:T(8,128)S(1)} collective-permute-done((f32[96,256]{1,0:T(8,128)S(1)}, f32[96,256]{1,0:T(8,128)S(1)}, u32[]{:S(2)}, u32[]{:S(2)}) %collective-permute-start.6) | collective-permute-done | bytes 98336 | tf_op jit(solution)/shard_map/ppermute | solution.py:541
  28.1 1.2 %collective-permute-done.8.core = f32[40,128]{1,0:T(8,128)S(1)} collective-permute-done((f32[40,128]{1,0:T(8,128)S(1)}, f32[40,128]{1,0:T(8,128)S(1)}, u32[]{:S(2)}, u32[]{:S(2)}) %collective-permute-start.8) | collective-permute-done | bytes 20512 | tf_op jit(solution)/shard_map/ppermute | solution.py:527
  29.3 1.2 %collective-permute-start.9 = (f32[8,128]{1,0:T(8,128)S(1)}, f32[8,128]{1,0:T(8,128)S(1)}, u32[]{:S(2)}, u32[]{:S(2)}) collective-permute-start(f32[8,128]{1,0:T(8,128)S(1)} %slice_add_fusion.after), channel_id=1, source_target_pairs={{0,8},{4,12},{8,0},{12,4},{16,24},{20,28},{24,16},{28,20},{1,9},{5... | collective-permute-start | bytes 12296 | tf_op jit(solution)/shard_map/ppermute | solution.py:527
  30.5 2.0 %collective-permute-start.11 = (f32[32,128]{1,0:T(8,128)S(1)}, f32[32,128]{1,0:T(8,128)S(1)}, u32[]{:S(2)}, u32[]{:S(2)}) collective-permute-start(f32[32,128]{1,0:T(8,128)S(1)} %shard_map.121), channel_id=1, source_target_pairs={{0,28},{4,8},{8,4},{12,16},{16,12},{20,24},{24,20},{28,0},{1,29},{... | collective-permute-start | bytes 49160 | tf_op jit(solution)/shard_map/ppermute | solution.py:536
  32.9 2.2 %collective-permute-start.10 = (f32[8,128]{1,0:T(8,128)S(1)}, f32[8,128]{1,0:T(8,128)S(1)}, u32[]{:S(2)}, u32[]{:S(2)}) collective-permute-start(f32[8,128]{1,0:T(8,128)S(1)} %add.7.own), channel_id=1, source_target_pairs={{0,16},{4,20},{8,24},{12,28},{16,0},{20,4},{24,8},{28,12},{1,17},{... | collective-permute-start | bytes 12296 | tf_op jit(solution)/shard_map/ppermute | solution.py:527
  35.5 0.8 %shard_map.122.second = f32[16,16,256]{2,1,0:T(8,128)S(1)} custom-call(f32[16,16,256]{2,1,0:T(8,128)S(1)} %get-tuple-element.56.back, f32[40,128]{1,0:T(8,128)S(1)} %collective-permute-done.8.core, f32[32,128]{1,0:T(8,128)S(1)} %collective-permute-done.11.chip, bf16[2,512,256]{2,1,0:T(8,128)(2,1)S(1)} %get-tuple-element.49.column, ...), custom_call_target="tpu_custom_call" | custom-call | flops 1000000000 | bytes 1000000 | tf_op jit(solution)/shard_map/pallas_call | solution.py:415
  36.3 1.2 %collective-permute-done.10.other = f32[8,128]{1,0:T(8,128)S(1)} collective-permute-done((f32[8,128]{1,0:T(8,128)S(1)}, f32[8,128]{1,0:T(8,128)S(1)}, u32[]{:S(2)}, u32[]{:S(2)}) %collective-permute-start.10) | collective-permute-done | bytes 4128 | tf_op jit(solution)/shard_map/ppermute | solution.py:527
  37.4 1.0 %shard_map.123 = (f32[16,16,256]{2,1,0:T(8,128)}, f32[16,16,256]{2,1,0:T(8,128)}) custom-call(f32[8,128]{1,0:T(8,128)S(1)} %add.7.own, f32[8,128]{1,0:T(8,128)S(1)} %collective-permute-done.10.other, f32[16,16,256]{2,1,0:T(8,128)S(1)} %get-tuple-element.31.source, f32[16,16,256]{2,1,0:T(8,128)S(1)} %shard_map.120.first, f32[16,16,256]{2,1,0:T(8,128)S(1)} %shard_map.122.second), custom_call_target="tpu_custom_call" | custom-call | tf_op jit(solution)/shard_map/pallas_call | solution.py:508
  (13 shorter events, 2.0 us)
Async XLA Ops:
  2.3 8.0 %collective-permute-start.1 = (f32[272,128]{1,0:T(8,128)S(1)}, f32[272,128]{1,0:T(8,128)S(1)}, u32[]{:S(2)}, u32[]{:S(2)}) collective-permute-start(f32[272,128]{1,0:T(8,128)S(1)} %get-tuple-element.36), channel_id=1, source_target_pairs={{0,28},{4,8},{8,4},{12,16},{16,12},{20,24},{24,20},{28,0},{1,29},{... | collective-permute-start | bytes 417800 | tf_op jit(solution)/shard_map/ppermute | solution.py:536
  6.8 3.4 %collective-permute-start = (f32[272,128]{1,0:T(8,128)S(1)}, f32[272,128]{1,0:T(8,128)S(1)}, u32[]{:S(2)}, u32[]{:S(2)}) collective-permute-start(f32[272,128]{1,0:T(8,128)S(1)} %get-tuple-element.32.after), channel_id=1, source_target_pairs={{0,4},{4,0},{8,12},{12,8},{16,20},{20,16},{24,28},{28,24},{1,5},{5... | collective-permute-start | bytes 417800 | tf_op jit(solution)/shard_map/ppermute | solution.py:527
  10.9 6.7 %collective-permute-start.4 = (f32[112,256]{1,0:T(8,128)S(1)}, f32[112,256]{1,0:T(8,128)S(1)}, u32[]{:S(2)}, u32[]{:S(2)}) collective-permute-start(f32[112,256]{1,0:T(8,128)S(1)} %shard_map.115.refs_0_.i0), channel_id=1, source_target_pairs={{0,3},{1,2},{2,1},{3,0},{4,7},{5,6},{6,5},{7,4},{8,11},{9,10},{10,... | collective-permute-start | bytes 344072 | tf_op jit(solution)/shard_map/ppermute | solution.py:541
  14.5 4.8 %collective-permute-start.3 = (f32[112,256]{1,0:T(8,128)S(1)}, f32[112,256]{1,0:T(8,128)S(1)}, u32[]{:S(2)}, u32[]{:S(2)}) collective-permute-start(f32[112,256]{1,0:T(8,128)S(1)} %shard_map.115.refs_0_.i0), channel_id=1, source_target_pairs={{0,2},{1,3},{2,0},{3,1},{4,6},{5,7},{6,4},{7,5},{8,10},{9,11},{10,... | collective-permute-start | bytes 344072 | tf_op jit(solution)/shard_map/ppermute | solution.py:541
  15.0 4.8 %collective-permute-start.2 = (f32[112,256]{1,0:T(8,128)S(1)}, f32[112,256]{1,0:T(8,128)S(1)}, u32[]{:S(2)}, u32[]{:S(2)}) collective-permute-start(f32[112,256]{1,0:T(8,128)S(1)} %shard_map.115.refs_0_.i0), channel_id=1, source_target_pairs={{0,1},{1,0},{2,3},{3,2},{4,5},{5,4},{6,7},{7,6},{8,9},{9,8},{10,11... | collective-permute-start | bytes 344072 | tf_op jit(solution)/shard_map/ppermute | solution.py:541
  20.9 5.6 %collective-permute-start.7 = (f32[96,256]{1,0:T(8,128)S(1)}, f32[96,256]{1,0:T(8,128)S(1)}, u32[]{:S(2)}, u32[]{:S(2)}) collective-permute-start(f32[96,256]{1,0:T(8,128)S(1)} %get-tuple-element.46.i0), channel_id=1, source_target_pairs={{0,3},{1,2},{2,1},{3,0},{4,7},{5,6},{6,5},{7,4},{8,11},{9,10},{10,... | collective-permute-start | bytes 294920 | tf_op jit(solution)/shard_map/ppermute | solution.py:541
  22.5 5.1 %collective-permute-start.6 = (f32[96,256]{1,0:T(8,128)S(1)}, f32[96,256]{1,0:T(8,128)S(1)}, u32[]{:S(2)}, u32[]{:S(2)}) collective-permute-start(f32[96,256]{1,0:T(8,128)S(1)} %get-tuple-element.46.i0), channel_id=1, source_target_pairs={{0,2},{1,3},{2,0},{3,1},{4,6},{5,7},{6,4},{7,5},{8,10},{9,11},{10,... | collective-permute-start | bytes 294920 | tf_op jit(solution)/shard_map/ppermute | solution.py:541
  23.2 4.6 %collective-permute-start.5 = (f32[96,256]{1,0:T(8,128)S(1)}, f32[96,256]{1,0:T(8,128)S(1)}, u32[]{:S(2)}, u32[]{:S(2)}) collective-permute-start(f32[96,256]{1,0:T(8,128)S(1)} %get-tuple-element.46.i0), channel_id=1, source_target_pairs={{0,1},{1,0},{2,3},{3,2},{4,5},{5,4},{6,7},{7,6},{8,9},{9,8},{10,11... | collective-permute-start | bytes 294920 | tf_op jit(solution)/shard_map/ppermute | solution.py:541
  28.1 1.3 %collective-permute-start.8 = (f32[40,128]{1,0:T(8,128)S(1)}, f32[40,128]{1,0:T(8,128)S(1)}, u32[]{:S(2)}, u32[]{:S(2)}) collective-permute-start(f32[40,128]{1,0:T(8,128)S(1)} %get-tuple-element.54), channel_id=1, source_target_pairs={{0,4},{4,0},{8,12},{12,8},{16,20},{20,16},{24,28},{28,24},{1,5},{5... | collective-permute-start | bytes 61448 | tf_op jit(solution)/shard_map/ppermute | solution.py:527
  29.3 3.6 %collective-permute-start.9 = (f32[8,128]{1,0:T(8,128)S(1)}, f32[8,128]{1,0:T(8,128)S(1)}, u32[]{:S(2)}, u32[]{:S(2)}) collective-permute-start(f32[8,128]{1,0:T(8,128)S(1)} %slice_add_fusion.after), channel_id=1, source_target_pairs={{0,8},{4,12},{8,0},{12,4},{16,24},{20,28},{24,16},{28,20},{1,9},{5... | collective-permute-start | bytes 12296 | tf_op jit(solution)/shard_map/ppermute | solution.py:527
  30.5 5.0 %collective-permute-start.11 = (f32[32,128]{1,0:T(8,128)S(1)}, f32[32,128]{1,0:T(8,128)S(1)}, u32[]{:S(2)}, u32[]{:S(2)}) collective-permute-start(f32[32,128]{1,0:T(8,128)S(1)} %shard_map.121), channel_id=1, source_target_pairs={{0,28},{4,8},{8,4},{12,16},{16,12},{20,24},{24,20},{28,0},{1,29},{... | collective-permute-start | bytes 49160 | tf_op jit(solution)/shard_map/ppermute | solution.py:536
  32.9 4.5 %collective-permute-start.10 = (f32[8,128]{1,0:T(8,128)S(1)}, f32[8,128]{1,0:T(8,128)S(1)}, u32[]{:S(2)}, u32[]{:S(2)}) collective-permute-start(f32[8,128]{1,0:T(8,128)S(1)} %add.7.own), channel_id=1, source_target_pairs={{0,16},{4,20},{8,24},{12,28},{16,0},{20,4},{24,8},{28,12},{1,17},{... | collective-permute-start | bytes 12296 | tf_op jit(solution)/shard_map/ppermute | solution.py:527

commit v7 on v6

--- a/solution.py
+++ b/solution.py
@@ -268,22 +268,30 @@
     out[rows, span] = out[rows, span] + jnp.where(mask, sums, 0.0).reshape(levels * height, LANES)
 
 
+def beside_levels(sums):
+    total = jnp.zeros(sums.shape[1:], F32)
+    for v in range(sums.shape[0]):
+        total = jnp.where(level_lanes(total.shape, v), sums[v], total)
+    return total
+
+
+def apart_levels(packed, levels):
+    return [repeated(jnp.where(level_lanes(packed.shape, v), packed, 0.0), EDGE) for v in range(levels)]
+
+
 def halo_members(block, rows, groups, levels):
     height = rows // groups
     return block[2 * rows : (2 + levels) * rows].reshape(levels, groups, height, LANES)
 
 
-def edge_kernel(inside, norm, core, chip, near, edge_members, edge, thin, out):
+def edge_kernel(norm, core, chip, near, edge_members, edge, thin, out):
     levels, groups, height = edge_members.shape[1:4]
-    width = out.shape[-1]
     rows = groups * height
-    out[: inside.shape[0]] = inside[...]
     sides = sides_of(core[...], chip[...])
     parts = []
     for side, block in enumerate(sides):
         parts += [block[rows : 2 * rows], block[:rows], near[side].reshape(rows, LANES)]
     filtered = split(dot3(both(thin), split(jnp.concatenate(parts, axis=1))))
-    outer = []
     for side, block in enumerate(sides):
         span = slice(3 * side * LANES, 3 * (side + 1) * LANES)
         order = (0, 1, 2) if side == 0 else (2, 1, 0)
@@ -291,15 +299,11 @@
         beyond = dot3(tuple(x[:, span] for x in filtered), matrix)
         middle = slice(span.start + LANES, span.start + 2 * LANES)
         within = dot3(tuple(x[:, middle] for x in filtered), both(edge.at[order[0]]))
-        add_edges(out, edge_sums(edge_members[side], within), side)
-        sums = edge_sums(halo_members(block, rows, groups, levels), beyond)
-        total = jnp.zeros((height, LANES), F32)
-        for v in range(levels):
-            total = jnp.where(level_lanes(total.shape, v), sums[v], total)
-        outer.append(total)
+        lanes = pl.ds(side * LANES, LANES)
+        out[:height, lanes] = beside_levels(edge_sums(edge_members[side], within))
+        out[height:, lanes] = beside_levels(edge_sums(halo_members(block, rows, groups, levels), beyond))
     lane = lane_of(norm.shape)
-    out[inside.shape[0] :] = jnp.concatenate(outer, axis=1)
-    top = pl.ds(inside.shape[0], norm.shape[0])
+    top = pl.ds(0, norm.shape[0])
     out[top, :LANES] = jnp.where(lane >= LANES - SPARE, norm[...], out[top, :LANES])
 
 
@@ -315,27 +319,29 @@
 
 
 def middle_kernel(
-    i0, i1, i2, i3, obs_weight, core, chip, members_ref, edge_members, column, row, edge, thin,
+    i0, i1, i2, i3, e0, e1, e2, e3, obs_weight, core, chip, members_ref, edge_members, column, row, edge, thin,
     back, halo, weighted, sums, out,
 ):
     levels, height, width = obs_weight.shape
     groups = edge_members.shape[2]
     rows = groups * height
-    total = (i0[...] + i1[...]) + (i2[...] + i3[...])
     flat = levels * height
-    increment = total[:flat].reshape(levels, height, width)
+    outer = (e0[...] + e1[...]) + (e2[...] + e3[...])
+    out[...] = (i0[...] + i1[...]) + (i2[...] + i3[...])
+    for side in range(2):
+        add_edges(out, jnp.stack(apart_levels(outer[:height, side * LANES : (side + 1) * LANES], levels)), side)
+    increment = out[...].reshape(levels, height, width)
     weighted[...] = obs_weight[...] * increment
-    top = total[flat : flat + 8, :LANES]
+    top = outer[: sums.shape[1], :LANES]
     sums[0] = jnp.where(lane_of(top.shape) >= LANES - SPARE, top, 0.0)
     sums[1] = folded(weighted[...] * increment)
     back[...] = adjoint(members_ref, weighted)
     smoothed = own_columns(back, column, row)
     for side, block in enumerate(sides_of(core[...], chip[...])):
-        outer = total[flat:, side * LANES : (side + 1) * LANES] * block[(2 + levels) * rows :]
+        here = outer[height:, side * LANES : (side + 1) * LANES] * block[(2 + levels) * rows :]
         members = halo_members(block, rows, groups, levels)
         adjoint_here = jnp.zeros((groups, height, LANES), F32)
-        for v in range(levels):
-            level = repeated(jnp.where(level_lanes(outer.shape, v), outer, 0.0), EDGE)
+        for v, level in enumerate(apart_levels(here, levels)):
             adjoint_here = adjoint_here + members[v] * level
         halo[side] = adjoint_here
     filtered = split(dot3(both(thin), split(jnp.concatenate([halo[i].reshape(rows, LANES) for i in range(2)], axis=1))))
@@ -558,12 +564,11 @@
     )
     core, chip = from_core(to_core), from_chip(to_chip)
     inside, norm, edge, thin = first_increment(source, to_core, members_data)
-    (increment,) = call(
-        edge_kernel, [((levels + 1) * height, width)], inside, norm, core, chip, near, edge_members, edge, thin
-    )
-    parts = from_all(increment, "mem")
+    parts = from_all(inside, "mem")
+    (outer,) = call(edge_kernel, [(2 * height, 2 * LANES)], norm, core, chip, near, edge_members, edge, thin)
+    parts += from_all(outer, "mem")
     column, row, column_twice, row_twice, edge, thin = fetched(
-        increment, halves(column_matrix(taps, width, EDGE)), row,
+        outer, halves(column_matrix(taps, width, EDGE)), row,
         halves(band(twice, own, own)), halves(row_matrix(taps, height, members, 2)),
         edge_matrix(twice, EDGE), halves(row_matrix(taps, height, groups, 2)),
     )

time: 38.6 us -> 37.9 us (0.982)
  waiting for transfers between devices: 11.5 us -> 9.85 us
  starting transfers between devices: 17.8 us -> 18.5 us
    ppermute x6 -> x9, starting transfers between devices: 7.77 us -> 10.9 us  [from_all(): lax.ppermute(value, axis, [(i, i ^ k) for i in range(count)])]
    ppermute x2, waiting for transfers between devices: 2.9 us -> 0.4 us  [from_chip(): lax.ppermute(value, 'tile', [(i, (i + 1) % count if i % 2 else (i - 1) %...]
    ppermute x4, starting transfers between devices: 3.5 us -> 1.12 us  [from_tile(): return lax.ppermute(value, 'tile', [(i, i ^ bit) for i in range(count)])]
    ppermute x4, waiting for transfers between devices: 2.77 us -> 5.1 us  [from_tile(): return lax.ppermute(value, 'tile', [(i, i ^ bit) for i in range(count)])]
    ppermute x6 -> x9, waiting for transfers between devices: 5.85 us -> 4.36 us  [from_all(): lax.ppermute(value, axis, [(i, i ^ k) for i in range(count)])]
  transfers between devices with their start and end apart: 12 -> 15, of which waited for: 11 -> 8; matrix products, arithmetic and copies ran while one was open for 0% -> 0% of each run, Pallas kernels for 10% -> 12%
where the time goes in v7:
time: 37.9 us; the launch traced here: 37.7 us
  starting transfers between devices  18.5 us (49%)
  waiting for transfers between devices  9.85 us (26%)
  Pallas kernels  8.61 us (23%)
  between operations  0.74 us (2%)
    ppermute x9, starting transfers between devices, from_all(): lax.ppermute(value, axis, [(i, i ^ k) for i in range(count)])  10.9 us
    ppermute x2, starting transfers between devices, from_chip(): lax.ppermute(value, 'tile', [(i, (i + 1) % count if i % 2 else (i - 1) %...  6.52 us
    ppermute x4, waiting for transfers between devices, from_tile(): return lax.ppermute(value, 'tile', [(i, i ^ bit) for i in range(count)])  5.1 us
    ppermute x9, waiting for transfers between devices, from_all(): lax.ppermute(value, axis, [(i, i ^ k) for i in range(count)])  4.36 us
    pallas_call x6, Pallas kernels, call(): pl.pallas_call(kernel, out_shape=shapes, in_specs=[vmem] * len(operands),...  3.79 us
    pallas_call x1, Pallas kernels, held_edges(): pl.pallas_call(edges_kernel, out_shape=[pltpu.VMEM(source.shape, F32), pl...  1.64 us
    pallas_call x1, Pallas kernels, fetched(): pl.pallas_call(fetch_kernel, out_shape=[pltpu.VMEM(a.shape, a.dtype) for...  1.35 us
    ppermute x4, starting transfers between devices, from_tile(): return lax.ppermute(value, 'tile', [(i, i ^ bit) for i in range(count)])  1.12 us
  transfers between devices with their start and end apart: 15, of which 8 were waited for; matrix products, arithmetic and copies ran while one was open for 0% of the time, Pallas kernels for 12%

profile of v7, /device:TPU:0, one launch (start us, length us, event | category | flops | bytes accessed | tf_op | source)
XLA Modules:
  0.0 37.7 jit_solution(14062961834831285542)
XLA Ops:
  0.6 1.6 %shard_map.113 = (f32[16,16,256]{2,1,0:T(8,128)S(1)}, bf16[16,6,16,256]{3,2,1,0:T(8,128)(2,1)S(1)}, f32[6,16,256]{2,1,0:T(8,128)S(1)}, f32[2,2,16,128]{3,2,1,0:T...) custom-call(f32[16,16,256]{2,1,0:T(8,128)} %bitcast.7, ...), custom_call_target="tpu_custom_call" | custom-call | tf_op jit(solution)/shard_map/pallas_call | solution.py:455
  2.3 4.6 %collective-permute-start.4 = (f32[272,128]{1,0:T(8,128)S(1)}, f32[272,128]{1,0:T(8,128)S(1)}, u32[]{:S(2)}, u32[]{:S(2)}) collective-permute-start(f32[272,128]{1,0:T(8,128)S(1)} %get-tuple-element.36), channel_id=1, source_target_pairs={{0,28},{4,8},{8,4},{12,16},{16,12},{20,24},{24,20},{28,0},{1,29},{... | collective-permute-start | bytes 417800 | tf_op jit(solution)/shard_map/ppermute | solution.py:542
  6.8 0.8 %shard_map.114 = (f32[96,256]{1,0:T(8,128)S(1)}, f32[8,128]{1,0:T(8,128)S(1)}, bf16[3,2,128,128]{3,2,1,0:T(8,128)(2,1)S(1)}, bf16[2,32,32]{2,1,0:T(8,128)(2,1)S(1)}) custom-call(f32[16,16,256]{2,1,0:T(8,128)S(1)} %get-tuple-element.31.source, f32[272,128]{1,0:T(8,128)S(1)} %get-tuple-element.32.after, bf16[16,6,16,256]{3,2,1,0:T(8,128)(2,1)S(1)} %get-tuple-element.33.members_ref), custom_call_target="tpu_custom_call" | custom-call | flops 1000000000 | bytes 1000000 | tf_op jit(solution)/shard_map/pallas_call | solution.py:481
  7.7 2.5 %collective-permute-start.2 = (f32[96,256]{1,0:T(8,128)S(1)}, f32[96,256]{1,0:T(8,128)S(1)}, u32[]{:S(2)}, u32[]{:S(2)}) collective-permute-start(f32[96,256]{1,0:T(8,128)S(1)} %get-tuple-element.34.i0), channel_id=1, source_target_pairs={{0,3},{1,2},{2,1},{3,0},{4,7},{5,6},{6,5},{7,4},{8,11},{9,10},{10,... | collective-permute-start | bytes 294920 | tf_op jit(solution)/shard_map/ppermute | solution.py:547
  10.7 0.5 %collective-permute-start = (f32[96,256]{1,0:T(8,128)S(1)}, f32[96,256]{1,0:T(8,128)S(1)}, u32[]{:S(2)}, u32[]{:S(2)}) collective-permute-start(f32[96,256]{1,0:T(8,128)S(1)} %get-tuple-element.34.i0), channel_id=1, source_target_pairs={{0,1},{1,0},{2,3},{3,2},{4,5},{5,4},{6,7},{7,6},{8,9},{9,8},{10,11... | collective-permute-start | bytes 294920 | tf_op jit(solution)/shard_map/ppermute | solution.py:547
  11.2 0.7 %shard_map.115.refs_0_.e0 = f32[32,256]{1,0:T(8,128)S(1)} custom-call(f32[8,128]{1,0:T(8,128)S(1)} %get-tuple-element.35.norm, f32[272,128]{1,0:T(8,128)S(1)} %collective-permute-done.3.core, f32[272,128]{1,0:T(8,128)S(1)} %collective-permute-done.4.chip, f32[2,2,16,128]{3,2,1,0:T(8,128)S(1)} %get-tuple-element.37.near, ...), custom_call_target="tpu_custom_call" | custom-call | tf_op jit(solution)/shard_map/pallas_call | solution.py:421
  11.9 2.6 %collective-permute-start.7 = (f32[32,256]{1,0:T(8,128)S(1)}, f32[32,256]{1,0:T(8,128)S(1)}, u32[]{:S(2)}, u32[]{:S(2)}) collective-permute-start(f32[32,256]{1,0:T(8,128)S(1)} %shard_map.115.refs_0_.e0), channel_id=1, source_target_pairs={{0,3},{1,2},{2,1},{3,0},{4,7},{5,6},{6,5},{7,4},{8,11},{9,10},{10,... | collective-permute-start | bytes 98312 | tf_op jit(solution)/shard_map/ppermute | solution.py:547
  15.0 0.7 %collective-permute-start.5 = (f32[32,256]{1,0:T(8,128)S(1)}, f32[32,256]{1,0:T(8,128)S(1)}, u32[]{:S(2)}, u32[]{:S(2)}) collective-permute-start(f32[32,256]{1,0:T(8,128)S(1)} %shard_map.115.refs_0_.e0), channel_id=1, source_target_pairs={{0,1},{1,0},{2,3},{3,2},{4,5},{5,4},{6,7},{7,6},{8,9},{9,8},{10,11... | collective-permute-start | bytes 98312 | tf_op jit(solution)/shard_map/ppermute | solution.py:547
  15.7 1.4 %shard_map.116 = (bf16[2,512,256]{2,1,0:T(8,128)(2,1)S(1)}, bf16[2,256,256]{2,1,0:T(8,128)(2,1)S(1)}, bf16[2,256,256]{2,1,0:T(8,128)(2,1)S(1)}, bf16[2,256,256]{...) custom-call(f32[32,256]{1,0:T(8,128)S(1)} %shard_map.115.refs_0_.e0, ...), custom_call_target="tpu_custom_call" | custom-call | bytes 2891776 | tf_op jit(solution)/shard_map/pallas_call | solution.py:500
  17.1 1.3 %collective-permute-done.6.e2 = f32[32,256]{1,0:T(8,128)S(1)} collective-permute-done((f32[32,256]{1,0:T(8,128)S(1)}, f32[32,256]{1,0:T(8,128)S(1)}, u32[]{:S(2)}, u32[]{:S(2)}) %collective-permute-start.6) | collective-permute-done | bytes 32800 | tf_op jit(solution)/shard_map/ppermute | solution.py:547
  18.4 0.5 %collective-permute-done.5.e1 = f32[32,256]{1,0:T(8,128)S(1)} collective-permute-done((f32[32,256]{1,0:T(8,128)S(1)}, f32[32,256]{1,0:T(8,128)S(1)}, u32[]{:S(2)}, u32[]{:S(2)}) %collective-permute-start.5) | collective-permute-done | bytes 32800 | tf_op jit(solution)/shard_map/ppermute | solution.py:547
  18.9 1.3 %shard_map.117 = (f32[16,16,256]{2,1,0:T(8,128)S(1)}, f32[2,2,16,128]{3,2,1,0:T(8,128)S(1)}, f32[6,16,256]{2,1,0:T(8,128)S(1)}, f32[2,8,128]{2,1,0:T(8,128)S(1)}, f32[96,256]{1,0:T(8,128)S(1)}) custom-call(f32[96,256]{1,0:T(8,128)S(1)} %get-tuple-element.34.i0, f32[96,256]{1,0:T(8,128)S(1)} %collective-permute-done.i1, ...), custom_call_target="tpu_custom_call" | custom-call | tf_op jit(solution)/shard_map/pallas_call | solution.py:421
  20.2 1.8 %collective-permute-start.10 = (f32[96,256]{1,0:T(8,128)S(1)}, f32[96,256]{1,0:T(8,128)S(1)}, u32[]{:S(2)}, u32[]{:S(2)}) collective-permute-start(f32[96,256]{1,0:T(8,128)S(1)} %get-tuple-element.46.i0), channel_id=1, source_target_pairs={{0,3},{1,2},{2,1},{3,0},{4,7},{5,6},{6,5},{7,4},{8,11},{9,10},{10,... | collective-permute-start | bytes 294920 | tf_op jit(solution)/shard_map/ppermute | solution.py:547
  22.5 1.3 %collective-permute-start.8 = (f32[96,256]{1,0:T(8,128)S(1)}, f32[96,256]{1,0:T(8,128)S(1)}, u32[]{:S(2)}, u32[]{:S(2)}) collective-permute-start(f32[96,256]{1,0:T(8,128)S(1)} %get-tuple-element.46.i0), channel_id=1, source_target_pairs={{0,1},{1,0},{2,3},{3,2},{4,5},{5,4},{6,7},{7,6},{8,9},{9,8},{10,11... | collective-permute-start | bytes 294920 | tf_op jit(solution)/shard_map/ppermute | solution.py:547
  23.8 0.8 %shard_map.118.value = f32[16,16,256]{2,1,0:T(8,128)S(1)} custom-call(f32[16,16,256]{2,1,0:T(8,128)S(1)} %get-tuple-element.47.back, f32[2,2,16,128]{3,2,1,0:T(8,128)S(1)} %get-tuple-element.48.halo, bf16[2,512,256]{2,1,0:T(8,128)(2,1)S(1)} %get-tuple-element.49.column, bf16[2,256,256]{2,1,0:T(8,128)(2,1)S(1)} %get-tuple-element.50.row), custom_call_target="tpu_custom_call" | custom-call | flops 1000000000 | bytes 1000000 | tf_op jit(solution)/shard_map/pallas_call | solution.py:421
  24.6 1.5 %collective-permute-done.10.i3 = f32[96,256]{1,0:T(8,128)S(1)} collective-permute-done((f32[96,256]{1,0:T(8,128)S(1)}, f32[96,256]{1,0:T(8,128)S(1)}, u32[]{:S(2)}, u32[]{:S(2)}) %collective-permute-start.10) | collective-permute-done | bytes 98336 | tf_op jit(solution)/shard_map/ppermute | solution.py:547
  26.1 1.0 %collective-permute-done.9.i2 = f32[96,256]{1,0:T(8,128)S(1)} collective-permute-done((f32[96,256]{1,0:T(8,128)S(1)}, f32[96,256]{1,0:T(8,128)S(1)}, u32[]{:S(2)}, u32[]{:S(2)}) %collective-permute-start.9) | collective-permute-done | bytes 98336 | tf_op jit(solution)/shard_map/ppermute | solution.py:547
  27.4 1.2 %collective-permute-done.11.core = f32[40,128]{1,0:T(8,128)S(1)} collective-permute-done((f32[40,128]{1,0:T(8,128)S(1)}, f32[40,128]{1,0:T(8,128)S(1)}, u32[]{:S(2)}, u32[]{:S(2)}) %collective-permute-start.11) | collective-permute-done | bytes 20512 | tf_op jit(solution)/shard_map/ppermute | solution.py:533
  28.6 2.0 %collective-permute-start.14 = (f32[32,128]{1,0:T(8,128)S(1)}, f32[32,128]{1,0:T(8,128)S(1)}, u32[]{:S(2)}, u32[]{:S(2)}) collective-permute-start(f32[32,128]{1,0:T(8,128)S(1)} %shard_map.121), channel_id=1, source_target_pairs={{0,28},{4,8},{8,4},{12,16},{16,12},{20,24},{24,20},{28,0},{1,29},{... | collective-permute-start | bytes 49160 | tf_op jit(solution)/shard_map/ppermute | solution.py:542
  30.6 1.6 %collective-permute-done.12 = f32[8,128]{1,0:T(8,128)S(1)} collective-permute-done((f32[8,128]{1,0:T(8,128)S(1)}, f32[8,128]{1,0:T(8,128)S(1)}, u32[]{:S(2)}, u32[]{:S(2)}) %collective-permute-start.12) | collective-permute-done | bytes 4128 | tf_op jit(solution)/shard_map/ppermute | solution.py:533
  32.2 1.0 %collective-permute-start.13 = (f32[8,128]{1,0:T(8,128)S(1)}, f32[8,128]{1,0:T(8,128)S(1)}, u32[]{:S(2)}, u32[]{:S(2)}) collective-permute-start(f32[8,128]{1,0:T(8,128)S(1)} %add.7.own), channel_id=1, source_target_pairs={{0,16},{4,20},{8,24},{12,28},{16,0},{20,4},{24,8},{28,12},{1,17},{... | collective-permute-start | bytes 12296 | tf_op jit(solution)/shard_map/ppermute | solution.py:533
  33.6 0.8 %shard_map.122.second = f32[16,16,256]{2,1,0:T(8,128)S(1)} custom-call(f32[16,16,256]{2,1,0:T(8,128)S(1)} %get-tuple-element.56.back, f32[40,128]{1,0:T(8,128)S(1)} %collective-permute-done.11.core, f32[32,128]{1,0:T(8,128)S(1)} %collective-permute-done.14.chip, bf16[2,512,256]{2,1,0:T(8,128)(2,1)S(1)} %get-tuple-element.49.column, ...), custom_call_target="tpu_custom_call" | custom-call | flops 1000000000 | bytes 1000000 | tf_op jit(solution)/shard_map/pallas_call | solution.py:421
  34.4 2.3 %collective-permute-done.13.other = f32[8,128]{1,0:T(8,128)S(1)} collective-permute-done((f32[8,128]{1,0:T(8,128)S(1)}, f32[8,128]{1,0:T(8,128)S(1)}, u32[]{:S(2)}, u32[]{:S(2)}) %collective-permute-start.13) | collective-permute-done | bytes 4128 | tf_op jit(solution)/shard_map/ppermute | solution.py:533
  36.7 1.0 %shard_map.123 = (f32[16,16,256]{2,1,0:T(8,128)}, f32[16,16,256]{2,1,0:T(8,128)}) custom-call(f32[8,128]{1,0:T(8,128)S(1)} %add.7.own, f32[8,128]{1,0:T(8,128)S(1)} %collective-permute-done.13.other, f32[16,16,256]{2,1,0:T(8,128)S(1)} %get-tuple-element.31.source, f32[16,16,256]{2,1,0:T(8,128)S(1)} %shard_map.120.first, f32[16,16,256]{2,1,0:T(8,128)S(1)} %shard_map.122.second), custom_call_target="tpu_custom_call" | custom-call | tf_op jit(solution)/shard_map/pallas_call | solution.py:514
  (19 shorter events, 2.2 us)
Async XLA Ops:
  2.3 8.9 %collective-permute-start.4 = (f32[272,128]{1,0:T(8,128)S(1)}, f32[272,128]{1,0:T(8,128)S(1)}, u32[]{:S(2)}, u32[]{:S(2)}) collective-permute-start(f32[272,128]{1,0:T(8,128)S(1)} %get-tuple-element.36), channel_id=1, source_target_pairs={{0,28},{4,8},{8,4},{12,16},{16,12},{20,24},{24,20},{28,0},{1,29},{... | collective-permute-start | bytes 417800 | tf_op jit(solution)/shard_map/ppermute | solution.py:542
  6.8 4.4 %collective-permute-start.3 = (f32[272,128]{1,0:T(8,128)S(1)}, f32[272,128]{1,0:T(8,128)S(1)}, u32[]{:S(2)}, u32[]{:S(2)}) collective-permute-start(f32[272,128]{1,0:T(8,128)S(1)} %get-tuple-element.32.after), channel_id=1, source_target_pairs={{0,4},{4,0},{8,12},{12,8},{16,20},{20,16},{24,28},{28,24},{1,5},{5... | collective-permute-start | bytes 417800 | tf_op jit(solution)/shard_map/ppermute | solution.py:533
  7.7 7.4 %collective-permute-start.2 = (f32[96,256]{1,0:T(8,128)S(1)}, f32[96,256]{1,0:T(8,128)S(1)}, u32[]{:S(2)}, u32[]{:S(2)}) collective-permute-start(f32[96,256]{1,0:T(8,128)S(1)} %get-tuple-element.34.i0), channel_id=1, source_target_pairs={{0,3},{1,2},{2,1},{3,0},{4,7},{5,6},{6,5},{7,4},{8,11},{9,10},{10,... | collective-permute-start | bytes 294920 | tf_op jit(solution)/shard_map/ppermute | solution.py:547
  10.2 6.9 %collective-permute-start.1 = (f32[96,256]{1,0:T(8,128)S(1)}, f32[96,256]{1,0:T(8,128)S(1)}, u32[]{:S(2)}, u32[]{:S(2)}) collective-permute-start(f32[96,256]{1,0:T(8,128)S(1)} %get-tuple-element.34.i0), channel_id=1, source_target_pairs={{0,2},{1,3},{2,0},{3,1},{4,6},{5,7},{6,4},{7,5},{8,10},{9,11},{10,... | collective-permute-start | bytes 294920 | tf_op jit(solution)/shard_map/ppermute | solution.py:547
  10.7 6.4 %collective-permute-start = (f32[96,256]{1,0:T(8,128)S(1)}, f32[96,256]{1,0:T(8,128)S(1)}, u32[]{:S(2)}, u32[]{:S(2)}) collective-permute-start(f32[96,256]{1,0:T(8,128)S(1)} %get-tuple-element.34.i0), channel_id=1, source_target_pairs={{0,1},{1,0},{2,3},{3,2},{4,5},{5,4},{6,7},{7,6},{8,9},{9,8},{10,11... | collective-permute-start | bytes 294920 | tf_op jit(solution)/shard_map/ppermute | solution.py:547
  11.9 5.2 %collective-permute-start.7 = (f32[32,256]{1,0:T(8,128)S(1)}, f32[32,256]{1,0:T(8,128)S(1)}, u32[]{:S(2)}, u32[]{:S(2)}) collective-permute-start(f32[32,256]{1,0:T(8,128)S(1)} %shard_map.115.refs_0_.e0), channel_id=1, source_target_pairs={{0,3},{1,2},{2,1},{3,0},{4,7},{5,6},{6,5},{7,4},{8,11},{9,10},{10,... | collective-permute-start | bytes 98312 | tf_op jit(solution)/shard_map/ppermute | solution.py:547
  14.5 3.9 %collective-permute-start.6 = (f32[32,256]{1,0:T(8,128)S(1)}, f32[32,256]{1,0:T(8,128)S(1)}, u32[]{:S(2)}, u32[]{:S(2)}) collective-permute-start(f32[32,256]{1,0:T(8,128)S(1)} %shard_map.115.refs_0_.e0), channel_id=1, source_target_pairs={{0,2},{1,3},{2,0},{3,1},{4,6},{5,7},{6,4},{7,5},{8,10},{9,11},{10,... | collective-permute-start | bytes 98312 | tf_op jit(solution)/shard_map/ppermute | solution.py:547
  15.0 3.9 %collective-permute-start.5 = (f32[32,256]{1,0:T(8,128)S(1)}, f32[32,256]{1,0:T(8,128)S(1)}, u32[]{:S(2)}, u32[]{:S(2)}) collective-permute-start(f32[32,256]{1,0:T(8,128)S(1)} %shard_map.115.refs_0_.e0), channel_id=1, source_target_pairs={{0,1},{1,0},{2,3},{3,2},{4,5},{5,4},{6,7},{7,6},{8,9},{9,8},{10,11... | collective-permute-start | bytes 98312 | tf_op jit(solution)/shard_map/ppermute | solution.py:547
  20.2 5.9 %collective-permute-start.10 = (f32[96,256]{1,0:T(8,128)S(1)}, f32[96,256]{1,0:T(8,128)S(1)}, u32[]{:S(2)}, u32[]{:S(2)}) collective-permute-start(f32[96,256]{1,0:T(8,128)S(1)} %get-tuple-element.46.i0), channel_id=1, source_target_pairs={{0,3},{1,2},{2,1},{3,0},{4,7},{5,6},{6,5},{7,4},{8,11},{9,10},{10,... | collective-permute-start | bytes 294920 | tf_op jit(solution)/shard_map/ppermute | solution.py:547
  22.0 5.1 %collective-permute-start.9 = (f32[96,256]{1,0:T(8,128)S(1)}, f32[96,256]{1,0:T(8,128)S(1)}, u32[]{:S(2)}, u32[]{:S(2)}) collective-permute-start(f32[96,256]{1,0:T(8,128)S(1)} %get-tuple-element.46.i0), channel_id=1, source_target_pairs={{0,2},{1,3},{2,0},{3,1},{4,6},{5,7},{6,4},{7,5},{8,10},{9,11},{10,... | collective-permute-start | bytes 294920 | tf_op jit(solution)/shard_map/ppermute | solution.py:547
  22.5 4.6 %collective-permute-start.8 = (f32[96,256]{1,0:T(8,128)S(1)}, f32[96,256]{1,0:T(8,128)S(1)}, u32[]{:S(2)}, u32[]{:S(2)}) collective-permute-start(f32[96,256]{1,0:T(8,128)S(1)} %get-tuple-element.46.i0), channel_id=1, source_target_pairs={{0,1},{1,0},{2,3},{3,2},{4,5},{5,4},{6,7},{7,6},{8,9},{9,8},{10,11... | collective-permute-start | bytes 294920 | tf_op jit(solution)/shard_map/ppermute | solution.py:547
  27.4 1.3 %collective-permute-start.11 = (f32[40,128]{1,0:T(8,128)S(1)}, f32[40,128]{1,0:T(8,128)S(1)}, u32[]{:S(2)}, u32[]{:S(2)}) collective-permute-start(f32[40,128]{1,0:T(8,128)S(1)} %get-tuple-element.54), channel_id=1, source_target_pairs={{0,4},{4,0},{8,12},{12,8},{16,20},{20,16},{24,28},{28,24},{1,5},{5... | collective-permute-start | bytes 61448 | tf_op jit(solution)/shard_map/ppermute | solution.py:533
  28.6 3.6 %collective-permute-start.12 = (f32[8,128]{1,0:T(8,128)S(1)}, f32[8,128]{1,0:T(8,128)S(1)}, u32[]{:S(2)}, u32[]{:S(2)}) collective-permute-start(f32[8,128]{1,0:T(8,128)S(1)} %slice_add_fusion.after), channel_id=1, source_target_pairs={{0,8},{4,12},{8,0},{12,4},{16,24},{20,28},{24,16},{28,20},{1,9},{5... | collective-permute-start | bytes 12296 | tf_op jit(solution)/shard_map/ppermute | solution.py:533
  28.6 5.0 %collective-permute-start.14 = (f32[32,128]{1,0:T(8,128)S(1)}, f32[32,128]{1,0:T(8,128)S(1)}, u32[]{:S(2)}, u32[]{:S(2)}) collective-permute-start(f32[32,128]{1,0:T(8,128)S(1)} %shard_map.121), channel_id=1, source_target_pairs={{0,28},{4,8},{8,4},{12,16},{16,12},{20,24},{24,20},{28,0},{1,29},{... | collective-permute-start | bytes 49160 | tf_op jit(solution)/shard_map/ppermute | solution.py:542
  32.2 4.5 %collective-permute-start.13 = (f32[8,128]{1,0:T(8,128)S(1)}, f32[8,128]{1,0:T(8,128)S(1)}, u32[]{:S(2)}, u32[]{:S(2)}) collective-permute-start(f32[8,128]{1,0:T(8,128)S(1)} %add.7.own), channel_id=1, source_target_pairs={{0,16},{4,20},{8,24},{12,28},{16,0},{20,4},{24,8},{28,12},{1,17},{... | collective-permute-start | bytes 12296 | tf_op jit(solution)/shard_map/ppermute | solution.py:533

commit v8 on v7

--- a/solution.py
+++ b/solution.py
@@ -55,8 +55,9 @@
 
 def edge_matrix(taps, edge):
     inner = np.arange(edge)
-    sides = (band(taps, inner - edge, inner), band(taps, inner + edge, inner))
-    return np.stack([halves(np.kron(np.eye(LANES // edge), side)) for side in sides])
+    return np.stack(
+        [halves(np.kron(np.eye(LANES // edge), band(taps, inner + shift * edge, inner))) for shift in (-1, 0, 1)]
+    )
 
 
 def split(x):
@@ -161,13 +162,13 @@
 
 def edges_kernel(
     source_hbm, members_hbm, precision_hbm, covered_hbm,
-    source, members_ref, obs_weight, near, edge_members, to_core, to_chip, precision, covered, sems,
+    source, members_ref, obs_weight, near, near_weight, edge_members, to_core, to_chip, precision, covered, sems,
 ):
+    members, levels, height, width = members_ref.shape
     pairs = ((source_hbm, source), (precision_hbm, precision), (covered_hbm, covered), (members_hbm, members_ref))
     copies = [pltpu.make_async_copy(x, y, sems.at[i]) for i, (x, y) in enumerate(pairs)]
     for copy in copies:
         copy.start()
-    members, levels, height, width = members_ref.shape
     groups = members * EDGE // LANES
     odd = lax.axis_index("tile") % 2 == 1
     rows = groups * height
@@ -185,30 +186,20 @@
     copies[1].wait()
     copies[2].wait()
     obs_weight[...] = weight_of(precision, covered)
-    sides = []
-    for start in (0, width - EDGE):
+    for side, start in enumerate((0, width - EDGE)):
         total = jnp.zeros((height, LANES), F32)
         for v in range(levels):
             origin = start // LANES * LANES
             shift = (v * EDGE - (start - origin)) % LANES
             block = obs_weight[v, :, origin : origin + LANES]
             total = jnp.where(level_lanes(total.shape, v), pltpu.roll(block, shift, 1) if shift else block, total)
-        sides.append(total)
-    send(rows * (2 + levels), *sides)
+        near_weight[side] = total
+    send(rows * (2 + levels), near_weight[0], near_weight[1])
     copies[3].wait()
     for v in range(levels):
         level = members_ref[:, v].astype(F32)
         edge_members[0, v], edge_members[1, v] = pack_edges(level, EDGE, True), pack_edges(level, EDGE, False)
         send(rows * (2 + v), edge_members[0, v], edge_members[1, v])
-
-
-def fetch_kernel(*refs):
-    count = (len(refs) - 2) // 2
-    copies = [pltpu.make_async_copy(refs[1 + i], refs[1 + count + i], refs[-1].at[i]) for i in range(count)]
-    for copy in copies:
-        copy.start()
-    for copy in copies:
-        copy.wait()
 
 
 def own_columns(field, column, row):
@@ -256,16 +247,16 @@
     return repeated(jnp.sum(edge_members * smoothed.reshape(1, groups, height, LANES), axis=1), EDGE)
 
 
-def add_edges(out, sums, side):
-    levels, height, _ = sums.shape
-    width = out.shape[-1]
-    lane = lane_of(sums.shape)
-    if side == 0:
-        span, mask = pl.ds(0, LANES), lane < EDGE
-    else:
-        span, mask = pl.ds(width - LANES, LANES), lane >= LANES - EDGE
-    rows = pl.ds(0, levels * height)
-    out[rows, span] = out[rows, span] + jnp.where(mask, sums, 0.0).reshape(levels * height, LANES)
+def add_columns(out, start, blocks):
+    levels, height, _ = blocks[0].shape
+    origin = start // LANES * LANES
+    lane = lane_of(blocks[0].shape)
+    total = jnp.zeros(lane.shape, F32)
+    for i, block in enumerate(blocks):
+        first = start - origin + i * EDGE
+        total = jnp.where((lane >= first) & (lane < first + EDGE), block, total)
+    rows, span = pl.ds(0, levels * height), pl.ds(origin, LANES)
+    out[rows, span] = out[rows, span] + total.reshape(levels * height, LANES)
 
 
 def beside_levels(sums):
@@ -284,24 +275,24 @@
     return block[2 * rows : (2 + levels) * rows].reshape(levels, groups, height, LANES)
 
 
-def edge_kernel(norm, core, chip, near, edge_members, edge, thin, out):
+def edge_kernel(norm, chip, core, near, edge_members, edge, thin, out):
     levels, groups, height = edge_members.shape[1:4]
     rows = groups * height
     sides = sides_of(core[...], chip[...])
     parts = []
     for side, block in enumerate(sides):
-        parts += [block[rows : 2 * rows], block[:rows], near[side].reshape(rows, LANES)]
-    filtered = split(dot3(both(thin), split(jnp.concatenate(parts, axis=1))))
+        here = [block[rows : 2 * rows], block[:rows], near[side].reshape(rows, LANES)]
+        parts += here if side == 0 else here[::-1]
+    filtered = dot3(both(thin), split(jnp.concatenate(parts, axis=1)))
+    filtered = split(jnp.concatenate([filtered[:, : 3 * LANES], filtered[:, 3 * LANES :]], axis=0))
+    beyond = dot3(filtered, [jnp.concatenate([edge[i, k] for i in range(3)], axis=0) for k in range(2)])
+    middle = tuple(x[:, LANES : 2 * LANES] for x in filtered)
     for side, block in enumerate(sides):
-        span = slice(3 * side * LANES, 3 * (side + 1) * LANES)
-        order = (0, 1, 2) if side == 0 else (2, 1, 0)
-        matrix = [jnp.concatenate([edge[i, k] for i in order], axis=0) for k in range(2)]
-        beyond = dot3(tuple(x[:, span] for x in filtered), matrix)
-        middle = slice(span.start + LANES, span.start + 2 * LANES)
-        within = dot3(tuple(x[:, middle] for x in filtered), both(edge.at[order[0]]))
+        own = slice(side * rows, (side + 1) * rows)
+        within = dot3(tuple(x[own] for x in middle), both(edge.at[2 * side]))
         lanes = pl.ds(side * LANES, LANES)
         out[:height, lanes] = beside_levels(edge_sums(edge_members[side], within))
-        out[height:, lanes] = beside_levels(edge_sums(halo_members(block, rows, groups, levels), beyond))
+        out[height:, lanes] = beside_levels(edge_sums(halo_members(block, rows, groups, levels), beyond[own]))
     lane = lane_of(norm.shape)
     top = pl.ds(0, norm.shape[0])
     out[top, :LANES] = jnp.where(lane >= LANES - SPARE, norm[...], out[top, :LANES])
@@ -318,41 +309,98 @@
     return precision[...] * mask
 
 
-def middle_kernel(
-    i0, i1, i2, i3, e0, e1, e2, e3, obs_weight, core, chip, members_ref, edge_members, column, row, edge, thin,
-    back, halo, weighted, sums, out,
+def packed_adjoint(members, weighted):
+    total = jnp.zeros(members.shape[1:], F32)
+    for v, level in enumerate(apart_levels(weighted, members.shape[0])):
+        total = total + members[v] * level
+    return total
+
+
+def prepare_kernel(
+    after, members_ref, column_hbm, row_hbm, edge_hbm, thin_hbm, next_members, column, row, edge, thin, sems
 ):
+    pairs = ((column_hbm, column), (row_hbm, row), (edge_hbm, edge), (thin_hbm, thin))
+    copies = [pltpu.make_async_copy(x, y, sems.at[i]) for i, (x, y) in enumerate(pairs)]
+    for copy in copies:
+        copy.start()
+    levels, width = members_ref.shape[1], members_ref.shape[-1]
+    for v in range(levels):
+        level = members_ref[:, v].astype(F32)
+        next_members[0, v] = pack_columns(level, EDGE, EDGE)
+        next_members[1, v] = pack_columns(level, width - 2 * EDGE, EDGE)
+    for copy in copies:
+        copy.wait()
+
+
+def main_kernel(i0, i1, i2, i3, obs_weight, members_ref, column, row, first, back, second):
+    first[...] = (i0[...] + i1[...]) + (i2[...] + i3[...])
+    back[...] = adjoint(members_ref, obs_weight[...] * first[...].reshape(obs_weight.shape))
+    second[...] = increments(members_ref, own_columns(back, column, row)).reshape(second.shape)
+
+
+def correction_kernel(
+    e0, e1, e2, e3, main, near_weight, chip, core, edge_members, next_members, edge, thin, outer, own, halo, out
+):
+    levels, groups, height = edge_members.shape[1:4]
+    width = out.shape[-1]
+    rows = groups * height
+    outer[...] = (e0[...] + e1[...]) + (e2[...] + e3[...])
+    out[...] = main[...]
+    for side, block in enumerate(sides_of(core[...], chip[...])):
+        lanes = pl.ds(side * LANES, LANES)
+        own[side] = packed_adjoint(edge_members[side], outer[:height, lanes] * near_weight[side])
+        halo[side] = packed_adjoint(
+            halo_members(block, rows, groups, levels), outer[height:, lanes] * block[(2 + levels) * rows :]
+        )
+    parts = [x[side].reshape(rows, LANES) for side in range(2) for x in (halo, own)]
+    filtered = split(dot3(both(thin), split(jnp.concatenate(parts, axis=1))))
+    for side in range(2):
+        span = slice(2 * side * LANES, 2 * (side + 1) * LANES)
+        matrix = [jnp.concatenate([edge[2 * side, k], edge[1, k]], axis=0) for k in range(2)]
+        outermost = dot3(tuple(x[:, span] for x in filtered), matrix)
+        inner = dot3(tuple(x[:, span.start + LANES : span.stop] for x in filtered), both(edge.at[2 * side]))
+        blocks = [edge_sums(edge_members[side], outermost), edge_sums(next_members[side], inner)]
+        if side == 0:
+            add_columns(out, 0, blocks)
+        else:
+            add_columns(out, width - 2 * EDGE, blocks[::-1])
+
+
+def wide_filter_kernel(
+    main, own, halo, first, outer, obs_weight, column_hbm, row_hbm, weighted, sums, out, column, row, sems
+):
+    copies = [pltpu.make_async_copy(x, y, sems.at[i]) for i, (x, y) in enumerate(((column_hbm, column), (row_hbm, row)))]
+    for copy in copies:
+        copy.start()
     levels, height, width = obs_weight.shape
-    groups = edge_members.shape[2]
-    rows = groups * height
-    flat = levels * height
-    outer = (e0[...] + e1[...]) + (e2[...] + e3[...])
-    out[...] = (i0[...] + i1[...]) + (i2[...] + i3[...])
-    for side in range(2):
-        add_edges(out, jnp.stack(apart_levels(outer[:height, side * LANES : (side + 1) * LANES], levels)), side)
-    increment = out[...].reshape(levels, height, width)
+    weighted[...] = first[...].reshape(obs_weight.shape)
+    for side, start in enumerate((0, width - EDGE)):
+        origin = start // LANES * LANES
+        lane = lane_of((height, LANES))
+        mask = (lane >= start - origin) & (lane < start - origin + EDGE)
+        for v, level in enumerate(apart_levels(outer[:height, pl.ds(side * LANES, LANES)], levels)):
+            span = pl.ds(origin, LANES)
+            weighted[v, :, span] = weighted[v, :, span] + jnp.where(mask, level, 0.0)
+    increment = weighted[...]
     weighted[...] = obs_weight[...] * increment
     top = outer[: sums.shape[1], :LANES]
     sums[0] = jnp.where(lane_of(top.shape) >= LANES - SPARE, top, 0.0)
     sums[1] = folded(weighted[...] * increment)
-    back[...] = adjoint(members_ref, weighted)
-    smoothed = own_columns(back, column, row)
-    for side, block in enumerate(sides_of(core[...], chip[...])):
-        here = outer[height:, side * LANES : (side + 1) * LANES] * block[(2 + levels) * rows :]
-        members = halo_members(block, rows, groups, levels)
-        adjoint_here = jnp.zeros((groups, height, LANES), F32)
-        for v, level in enumerate(apart_levels(here, levels)):
-            adjoint_here = adjoint_here + members[v] * level
-        halo[side] = adjoint_here
-    filtered = split(dot3(both(thin), split(jnp.concatenate([halo[i].reshape(rows, LANES) for i in range(2)], axis=1))))
-    out[...] = increments(members_ref, smoothed).reshape(flat, width)
-    for side in range(2):
-        part = dot3(tuple(x[:, side * LANES : (side + 1) * LANES] for x in filtered), both(edge.at[side]))
-        add_edges(out, edge_sums(edge_members[side], part), side)
-
-
-def wide_filter_kernel(back, halo, column, row, out):
-    lhs = split(beside(back[...], halo[0], halo[1], EDGE))
+    groups = own.shape[1]
+    fields = []
+    for k in range(main.shape[0]):
+        field = main[k]
+        slot, group = k // groups, k % groups
+        ends = []
+        for side, at in enumerate((0, LANES - EDGE)):
+            moved = pltpu.roll(own[side, group], (at - slot * EDGE) % LANES, 1)
+            lane = lane_of(moved.shape)
+            ends.append(jnp.where((lane >= at) & (lane < at + EDGE), moved, 0.0))
+        middle = [jnp.zeros((height, width - 2 * LANES), F32)] if width > 2 * LANES else []
+        fields.append(field + jnp.concatenate([ends[0]] + middle + [ends[1]], axis=1))
+    for copy in copies:
+        copy.wait()
+    lhs = split(beside(jnp.stack(fields), halo[0], halo[1], EDGE))
     out[...] = dot3(both(row), split(dot3(lhs, both(column)))).reshape(out.shape)
 
 
@@ -459,12 +507,13 @@
             pltpu.VMEM(members_data.shape, members_data.dtype),
             pltpu.VMEM(precision.shape, F32),
             pltpu.VMEM((2, groups, height, LANES), F32),
+            pltpu.VMEM((2, height, LANES), F32),
             pltpu.VMEM((2, levels, groups, height, LANES), F32),
             pltpu.VMEM(payload, F32),
             pltpu.VMEM(payload, F32),
         ],
         in_specs=[hbm] * 4,
-        out_specs=[vmem] * 7,
+        out_specs=[vmem] * 8,
         scratch_shapes=[
             pltpu.VMEM(precision.shape, F32),
             pltpu.VMEM(covered.shape, covered.dtype),
@@ -493,19 +542,19 @@
     )(source, after, members_data)
 
 
-def fetched(after, *arrays):
+def call_with_constants(kernel, outs, kept, scratch, operands, constants):
     vmem = pl.BlockSpec(memory_space=pltpu.VMEM)
     hbm = pl.BlockSpec(memory_space=pltpu.HBM)
-    size = sum(a.size * a.dtype.itemsize for a in arrays)
+    held = [pltpu.VMEM(x.shape, x.dtype) for x in kept]
     return pl.pallas_call(
-        fetch_kernel,
-        out_shape=[pltpu.VMEM(a.shape, a.dtype) for a in arrays],
-        in_specs=[vmem] + [hbm] * len(arrays),
-        out_specs=[vmem] * len(arrays),
-        scratch_shapes=[pltpu.SemaphoreType.DMA((len(arrays),))],
+        kernel,
+        out_shape=[pltpu.VMEM(shape, F32) for shape in outs] + held,
+        in_specs=[vmem] * len(operands) + [hbm] * len(constants),
+        out_specs=[vmem] * (len(outs) + len(kept)),
+        scratch_shapes=[pltpu.VMEM(x.shape, x.dtype) for x in scratch] + [pltpu.SemaphoreType.DMA((len(constants),))],
         compiler_params=pltpu.CompilerParams(vmem_limit_bytes=24 * 1024 * 1024),
-        cost_estimate=pl.CostEstimate(flops=0, bytes_accessed=2 * size, transcendentals=0),
-    )(after, *map(in_hbm, arrays))
+        cost_estimate=LONG,
+    )(*operands, *map(in_hbm, constants))
 
 
 def combined(own, other, source, first, second):
@@ -542,9 +591,9 @@
     return lax.ppermute(value, "tile", [(i, (i + 1) % count if i % 2 else (i - 1) % count) for i in range(count)])
 
 
-def from_all(value, axis):
+def from_all(value, axis, order):
     count = lax.axis_size(axis)
-    return [value] + [lax.ppermute(value, axis, [(i, i ^ k) for i in range(count)]) for k in range(1, count)]
+    return [value] + [lax.ppermute(value, axis, [(i, i ^ k) for i in range(count)]) for k in order]
 
 
 def one_tile_row(right_side, perturbations, precision, covered):
@@ -556,30 +605,35 @@
     field = (members, height, width)
     plane = (levels, height, width)
     flat = (levels * height, width)
-    row = halves(row_matrix(taps, height, members, 1))
     own = np.arange(width)
 
-    source, members_data, obs_weight, near, edge_members, to_core, to_chip = held_edges(
+    source, members_data, obs_weight, near, near_weight, edge_members, to_core, to_chip = held_edges(
         source, members_data, precision[0], covered[0]
     )
     core, chip = from_core(to_core), from_chip(to_chip)
-    inside, norm, edge, thin = first_increment(source, to_core, members_data)
-    parts = from_all(inside, "mem")
-    (outer,) = call(edge_kernel, [(2 * height, 2 * LANES)], norm, core, chip, near, edge_members, edge, thin)
-    parts += from_all(outer, "mem")
-    column, row, column_twice, row_twice, edge, thin = fetched(
-        outer, halves(column_matrix(taps, width, EDGE)), row,
-        halves(band(twice, own, own)), halves(row_matrix(taps, height, members, 2)),
-        edge_matrix(twice, EDGE), halves(row_matrix(taps, height, groups, 2)),
-    )
-    back, halo, weighted, sums, increment = call(
-        middle_kernel,
-        [field, (2, groups, height, LANES), plane, (2, 8, LANES), flat],
-        *parts, obs_weight, core, chip, members_data, edge_members, column_twice, row_twice, edge, thin,
-    )
-    parts = from_all(increment, "mem")
-    (first,) = call(wide_filter_kernel, [field], back, halo, column, row, cost=LONG)
-    first, weighted = lax.optimization_barrier((first, weighted))
+    inside, norm, edge, thin = first_increment(source, to_chip, members_data)
+    inside = from_all(inside, "mem", (3, 2, 1))
+    (outer,) = call(edge_kernel, [(2 * height, 2 * LANES)], norm, chip, core, near, edge_members, edge, thin)
+    column_twice, row_twice = halves(band(twice, own, own)), halves(row_matrix(taps, height, members, 2))
+    edge, thin = edge_matrix(twice, EDGE), halves(row_matrix(taps, height, groups, 2))
+    constants = [column_twice, row_twice, edge, thin]
+    next_members, column, row, edge, thin = call_with_constants(
+        prepare_kernel, [edge_members.shape], constants, [], [outer, members_data], constants
+    )
+    increment, main, inside = call(
+        main_kernel, [flat, field, flat], *inside, obs_weight, members_data, column, row
+    )
+    ends = (2, groups, height, LANES)
+    outer, corrected, halo, second = call(
+        correction_kernel, [outer.shape, ends, ends, flat],
+        *from_all(outer, "mem", (3, 2, 1)), inside, near_weight, chip, core, edge_members, next_members, edge, thin,
+    )
+    parts = from_all(second, "mem", (2, 1, 3))
+    column, row = halves(column_matrix(taps, width, EDGE)), halves(row_matrix(taps, height, members, 1))
+    weighted, sums, first, column, row = call_with_constants(
+        wide_filter_kernel, [plane, (2, 8, LANES), field], [column, row], [],
+        [main, corrected, halo, increment, outer, obs_weight], [column, row],
+    )
     back, to_core, to_chip = call(
         last_kernel,
         [field, (groups * height + 8, LANES), (groups * height, LANES)],

time: 37.9 us -> 37.5 us (0.989)
  waiting for transfers between devices: 9.85 us -> 7.91 us
  Pallas kernels: 8.61 us -> 10.1 us
    ppermute x9, waiting for transfers between devices: 4.36 us -> 2.37 us  [from_all(): lax.ppermute(value, axis, [(i, i ^ k) for i in range(count)])]
    pallas_call x1 -> x2, Pallas kernels: 1.35 us -> 3.26 us  [call_with_constants(): pl.pallas_call(kernel, out_shape=[pltpu.VMEM(shape, F32) for shape in out...]
    pallas_call x6, Pallas kernels: 3.79 us -> 3.37 us  [call(): pl.pallas_call(kernel, out_shape=shapes, in_specs=[vmem] * len(operands),...]
  transfers between devices with their start and end apart: 15 -> 15, of which waited for: 8 -> 8; matrix products, arithmetic and copies ran while one was open for 0% -> 0% of each run, Pallas kernels for 12% -> 17%
where the time goes in v8:
time: 37.5 us; the launch traced here: 37.3 us
  starting transfers between devices  18.5 us (49%)
  Pallas kernels  10.1 us (27%)
  waiting for transfers between devices  7.91 us (21%)
  between operations  0.75 us (2%)
    ppermute x9, starting transfers between devices, from_all(): lax.ppermute(value, axis, [(i, i ^ k) for i in range(count)])  10.9 us
    ppermute x2, starting transfers between devices, from_chip(): lax.ppermute(value, 'tile', [(i, (i + 1) % count if i % 2 else (i - 1) %...  6.51 us
    ppermute x4, waiting for transfers between devices, from_tile(): return lax.ppermute(value, 'tile', [(i, i ^ bit) for i in range(count)])  5.12 us
    pallas_call x6, Pallas kernels, call(): pl.pallas_call(kernel, out_shape=shapes, in_specs=[vmem] * len(operands),...  3.37 us
    pallas_call x2, Pallas kernels, call_with_constants(): pl.pallas_call(kernel, out_shape=[pltpu.VMEM(shape, F32) for shape in out...  3.26 us
    ppermute x9, waiting for transfers between devices, from_all(): lax.ppermute(value, axis, [(i, i ^ k) for i in range(count)])  2.37 us
    pallas_call x1, Pallas kernels, held_edges(): pl.pallas_call(edges_kernel, out_shape=[pltpu.VMEM(source.shape, F32), pl...  1.64 us
    ppermute x4, starting transfers between devices, from_tile(): return lax.ppermute(value, 'tile', [(i, i ^ bit) for i in range(count)])  1.08 us
  transfers between devices with their start and end apart: 15, of which 8 were waited for; matrix products, arithmetic and copies ran while one was open for 0% of the time, Pallas kernels for 17%

profile of v8, /device:TPU:0, one launch (start us, length us, event | category | flops | bytes accessed | tf_op | source)
XLA Modules:
  0.0 37.3 jit_solution(10370379709513430298)
XLA Ops:
  0.6 1.6 %shard_map.113 = (f32[16,16,256]{2,1,0:T(8,128)S(1)}, bf16[16,6,16,256]{3,2,1,0:T(8,128)(2,1)S(1)}, f32[6,16,256]{2,1,0:T(8,128)S(1)}, f32[2,2,16,128]{3,2,1,0:T...) custom-call(f32[16,16,256]{2,1,0:T(8,128)} %bitcast.7, ...), custom_call_target="tpu_custom_call" | custom-call | tf_op jit(solution)/shard_map/pallas_call | solution.py:503
  2.3 4.6 %collective-permute-start = (f32[272,128]{1,0:T(8,128)S(1)}, f32[272,128]{1,0:T(8,128)S(1)}, u32[]{:S(2)}, u32[]{:S(2)}) collective-permute-start(f32[272,128]{1,0:T(8,128)S(1)} %get-tuple-element.37.after), channel_id=1, source_target_pairs={{0,28},{4,8},{8,4},{12,16},{16,12},{20,24},{24,20},{28,0},{1,29},{... | collective-permute-start | bytes 417800 | tf_op jit(solution)/shard_map/ppermute | solution.py:591
  6.8 0.8 %shard_map.114 = (f32[96,256]{1,0:T(8,128)S(1)}, f32[8,128]{1,0:T(8,128)S(1)}, bf16[3,2,128,128]{3,2,1,0:T(8,128)(2,1)S(1)}, bf16[2,32,32]{2,1,0:T(8,128)(2,1)S(1)}) custom-call(f32[16,16,256]{2,1,0:T(8,128)S(1)} %get-tuple-element.36.source, f32[272,128]{1,0:T(8,128)S(1)} %get-tuple-element.37.after, bf16[16,6,16,256]{3,2,1,0:T(8,128)(2,1)S(1)} %get-tuple-element.38.members_ref), custom_call_target="tpu_custom_call" | custom-call | flops 1000000000 | bytes 1000000 | tf_op jit(solution)/shard_map/pallas_call | solution.py:530
  7.7 2.5 %collective-permute-start.5 = (f32[96,256]{1,0:T(8,128)S(1)}, f32[96,256]{1,0:T(8,128)S(1)}, u32[]{:S(2)}, u32[]{:S(2)}) collective-permute-start(f32[96,256]{1,0:T(8,128)S(1)} %get-tuple-element.45.i0), channel_id=1, source_target_pairs={{0,3},{1,2},{2,1},{3,0},{4,7},{5,6},{6,5},{7,4},{8,11},{9,10},{10,... | collective-permute-start | bytes 294920 | tf_op jit(solution)/shard_map/ppermute | solution.py:596
  10.2 0.5 %collective-permute-start.6 = (f32[96,256]{1,0:T(8,128)S(1)}, f32[96,256]{1,0:T(8,128)S(1)}, u32[]{:S(2)}, u32[]{:S(2)}) collective-permute-start(f32[96,256]{1,0:T(8,128)S(1)} %get-tuple-element.45.i0), channel_id=1, source_target_pairs={{0,2},{1,3},{2,0},{3,1},{4,6},{5,7},{6,4},{7,5},{8,10},{9,11},{10,... | collective-permute-start | bytes 294920 | tf_op jit(solution)/shard_map/ppermute | solution.py:596
  10.7 0.5 %collective-permute-start.7 = (f32[96,256]{1,0:T(8,128)S(1)}, f32[96,256]{1,0:T(8,128)S(1)}, u32[]{:S(2)}, u32[]{:S(2)}) collective-permute-start(f32[96,256]{1,0:T(8,128)S(1)} %get-tuple-element.45.i0), channel_id=1, source_target_pairs={{0,1},{1,0},{2,3},{3,2},{4,5},{5,4},{6,7},{7,6},{8,9},{9,8},{10,11... | collective-permute-start | bytes 294920 | tf_op jit(solution)/shard_map/ppermute | solution.py:596
  11.2 0.7 %shard_map.115.after.e0 = f32[32,256]{1,0:T(8,128)S(1)} custom-call(f32[8,128]{1,0:T(8,128)S(1)} %get-tuple-element.39.norm, f32[272,128]{1,0:T(8,128)S(1)} %collective-permute-done.chip, f32[272,128]{1,0:T(8,128)S(1)} %collective-permute-done.1.core, f32[2,2,16,128]{3,2,1,0:T(8,128)S(1)} %get-tuple-element.41.near, ...), custom_call_target="tpu_custom_call" | custom-call | tf_op jit(solution)/shard_map/pallas_call | solution.py:469
  11.9 2.6 %collective-permute-start.2 = (f32[32,256]{1,0:T(8,128)S(1)}, f32[32,256]{1,0:T(8,128)S(1)}, u32[]{:S(2)}, u32[]{:S(2)}) collective-permute-start(f32[32,256]{1,0:T(8,128)S(1)} %shard_map.115.after.e0), channel_id=1, source_target_pairs={{0,3},{1,2},{2,1},{3,0},{4,7},{5,6},{6,5},{7,4},{8,11},{9,10},{10,... | collective-permute-start | bytes 98312 | tf_op jit(solution)/shard_map/ppermute | solution.py:596
  15.0 0.7 %collective-permute-start.4 = (f32[32,256]{1,0:T(8,128)S(1)}, f32[32,256]{1,0:T(8,128)S(1)}, u32[]{:S(2)}, u32[]{:S(2)}) collective-permute-start(f32[32,256]{1,0:T(8,128)S(1)} %shard_map.115.after.e0), channel_id=1, source_target_pairs={{0,1},{1,0},{2,3},{3,2},{4,5},{5,4},{6,7},{7,6},{8,9},{9,8},{10,11... | collective-permute-start | bytes 98312 | tf_op jit(solution)/shard_map/ppermute | solution.py:596
  15.7 1.3 %shard_map.116 = (f32[2,6,2,16,128]{4,3,2,1,0:T(8,128)S(1)}, bf16[2,256,256]{2,1,0:T(8,128)(2,1)S(1)}, bf16[2,256,256]{2,1,0:T(8,128)(2,1)S(1)}, bf16[3,2,128,12...) custom-call(f32[32,256]{1,0:T(8,128)S(1)} %shard_map.115.after.e0, ...), custom_call_target="tpu_custom_call" | custom-call | flops 1000000000 | bytes 1000000 | tf_op jit(solution)/shard_map/pallas_call | solution.py:549
  17.0 0.8 %shard_map.117 = (f32[96,256]{1,0:T(8,128)S(1)}, f32[16,16,256]{2,1,0:T(8,128)S(1)}, f32[96,256]{1,0:T(8,128)S(1)}) custom-call(f32[96,256]{1,0:T(8,128)S(1)} %get-tuple-element.45.i0, f32[96,256]{1,0:T(8,128)S(1)} %collective-permute-done.5.i1, f32[96,256]{1,0:T(8,128)S(1)} %collective-permute-done.6.i2, f32[96,256]{1,0:T(8,128)S(1)} %collective-permute-done.7.i3, ...), custom_call_target="tpu_custom_call" | custom-call | tf_op jit(solution)/shard_map/pallas_call | solution.py:469
  18.4 0.5 %collective-permute-done.4.e3 = f32[32,256]{1,0:T(8,128)S(1)} collective-permute-done((f32[32,256]{1,0:T(8,128)S(1)}, f32[32,256]{1,0:T(8,128)S(1)}, u32[]{:S(2)}, u32[]{:S(2)}) %collective-permute-start.4) | collective-permute-done | bytes 32800 | tf_op jit(solution)/shard_map/ppermute | solution.py:596
  18.9 0.9 %shard_map.118 = (f32[32,256]{1,0:T(8,128)S(1)}, f32[2,2,16,128]{3,2,1,0:T(8,128)S(1)}, f32[2,2,16,128]{3,2,1,0:T(8,128)S(1)}, f32[96,256]{1,0:T(8,128)S(1)}) custom-call(f32[32,256]{1,0:T(8,128)S(1)} %shard_map.115.after.e0, f32[32,256]{1,0:T(8,128)S(1)} %collective-permute-done.2.e1, f32[32,256]{1,0:T(8,128)S(1)} %collective-permute-done.3.e2, ...), custom_call_target="tpu_custom_call" | custom-call | tf_op jit(solution)/shard_map/pallas_call | solution.py:469
  19.8 1.8 %collective-permute-start.10 = (f32[96,256]{1,0:T(8,128)S(1)}, f32[96,256]{1,0:T(8,128)S(1)}, u32[]{:S(2)}, u32[]{:S(2)}) collective-permute-start(f32[96,256]{1,0:T(8,128)S(1)} %get-tuple-element.54.i0), channel_id=1, source_target_pairs={{0,3},{1,2},{2,1},{3,0},{4,7},{5,6},{6,5},{7,4},{8,11},{9,10},{10,... | collective-permute-start | bytes 294920 | tf_op jit(solution)/shard_map/ppermute | solution.py:596
  22.0 1.3 %collective-permute-start.9 = (f32[96,256]{1,0:T(8,128)S(1)}, f32[96,256]{1,0:T(8,128)S(1)}, u32[]{:S(2)}, u32[]{:S(2)}) collective-permute-start(f32[96,256]{1,0:T(8,128)S(1)} %get-tuple-element.54.i0), channel_id=1, source_target_pairs={{0,1},{1,0},{2,3},{3,2},{4,5},{5,4},{6,7},{7,6},{8,9},{9,8},{10,11... | collective-permute-start | bytes 294920 | tf_op jit(solution)/shard_map/ppermute | solution.py:596
  23.3 2.0 %shard_map.119 = (f32[6,16,256]{2,1,0:T(8,128)S(1)}, f32[2,8,128]{2,1,0:T(8,128)S(1)}, f32[16,16,256]{2,1,0:T(8,128)S(1)}, bf16[2,512,256]{2,1,0:T(8,128)(2,1)S(1)}, bf16[2,256,256]{2,1,0:T(8,128)(2,1)S(1)}) custom-call(f32[16,16,256]{2,1,0:T(8,128)S(1)} %get-tuple-element.55.main, f32[2,2,16,128]{3,2,1,0:T(8,128)S(1)} %get-tuple-element.56.own, ...), custom_call_target="tpu_custom_call" | custom-call | flops 1000000000 | bytes 1000000 | tf_op jit(solution)/shard_map/pallas_call | solution.py:549
  25.6 1.0 %collective-permute-done.8.i1 = f32[96,256]{1,0:T(8,128)S(1)} collective-permute-done((f32[96,256]{1,0:T(8,128)S(1)}, f32[96,256]{1,0:T(8,128)S(1)}, u32[]{:S(2)}, u32[]{:S(2)}) %collective-permute-start.8) | collective-permute-done | bytes 98336 | tf_op jit(solution)/shard_map/ppermute | solution.py:596
  27.0 1.2 %collective-permute-done.11.core = f32[40,128]{1,0:T(8,128)S(1)} collective-permute-done((f32[40,128]{1,0:T(8,128)S(1)}, f32[40,128]{1,0:T(8,128)S(1)}, u32[]{:S(2)}, u32[]{:S(2)}) %collective-permute-start.11) | collective-permute-done | bytes 20512 | tf_op jit(solution)/shard_map/ppermute | solution.py:582
  28.2 2.0 %collective-permute-start.14 = (f32[32,128]{1,0:T(8,128)S(1)}, f32[32,128]{1,0:T(8,128)S(1)}, u32[]{:S(2)}, u32[]{:S(2)}) collective-permute-start(f32[32,128]{1,0:T(8,128)S(1)} %shard_map.122), channel_id=1, source_target_pairs={{0,28},{4,8},{8,4},{12,16},{16,12},{20,24},{24,20},{28,0},{1,29},{... | collective-permute-start | bytes 49160 | tf_op jit(solution)/shard_map/ppermute | solution.py:591
  30.1 1.6 %collective-permute-done.12 = f32[8,128]{1,0:T(8,128)S(1)} collective-permute-done((f32[8,128]{1,0:T(8,128)S(1)}, f32[8,128]{1,0:T(8,128)S(1)}, u32[]{:S(2)}, u32[]{:S(2)}) %collective-permute-start.12) | collective-permute-done | bytes 4128 | tf_op jit(solution)/shard_map/ppermute | solution.py:582
  31.8 1.0 %collective-permute-start.13 = (f32[8,128]{1,0:T(8,128)S(1)}, f32[8,128]{1,0:T(8,128)S(1)}, u32[]{:S(2)}, u32[]{:S(2)}) collective-permute-start(f32[8,128]{1,0:T(8,128)S(1)} %add.7.own), channel_id=1, source_target_pairs={{0,16},{4,20},{8,24},{12,28},{16,0},{20,4},{24,8},{28,12},{1,17},{... | collective-permute-start | bytes 12296 | tf_op jit(solution)/shard_map/ppermute | solution.py:582
  33.2 0.8 %shard_map.123.second = f32[16,16,256]{2,1,0:T(8,128)S(1)} custom-call(f32[16,16,256]{2,1,0:T(8,128)S(1)} %get-tuple-element.64.back, f32[40,128]{1,0:T(8,128)S(1)} %collective-permute-done.11.core, f32[32,128]{1,0:T(8,128)S(1)} %collective-permute-done.14.chip, bf16[2,512,256]{2,1,0:T(8,128)(2,1)S(1)} %get-tuple-element.66.column, ...), custom_call_target="tpu_custom_call" | custom-call | flops 1000000000 | bytes 1000000 | tf_op jit(solution)/shard_map/pallas_call | solution.py:469
  34.0 2.3 %collective-permute-done.13.other = f32[8,128]{1,0:T(8,128)S(1)} collective-permute-done((f32[8,128]{1,0:T(8,128)S(1)}, f32[8,128]{1,0:T(8,128)S(1)}, u32[]{:S(2)}, u32[]{:S(2)}) %collective-permute-start.13) | collective-permute-done | bytes 4128 | tf_op jit(solution)/shard_map/ppermute | solution.py:582
  36.3 1.0 %shard_map.124 = (f32[16,16,256]{2,1,0:T(8,128)}, f32[16,16,256]{2,1,0:T(8,128)}) custom-call(f32[8,128]{1,0:T(8,128)S(1)} %add.7.own, f32[8,128]{1,0:T(8,128)S(1)} %collective-permute-done.13.other, f32[16,16,256]{2,1,0:T(8,128)S(1)} %get-tuple-element.36.source, f32[16,16,256]{2,1,0:T(8,128)S(1)} %shard_map.121.first, f32[16,16,256]{2,1,0:T(8,128)S(1)} %shard_map.123.second), custom_call_target="tpu_custom_call" | custom-call | tf_op jit(solution)/shard_map/pallas_call | solution.py:563
  (20 shorter events, 2.6 us)
Async XLA Ops:
  2.3 8.9 %collective-permute-start = (f32[272,128]{1,0:T(8,128)S(1)}, f32[272,128]{1,0:T(8,128)S(1)}, u32[]{:S(2)}, u32[]{:S(2)}) collective-permute-start(f32[272,128]{1,0:T(8,128)S(1)} %get-tuple-element.37.after), channel_id=1, source_target_pairs={{0,28},{4,8},{8,4},{12,16},{16,12},{20,24},{24,20},{28,0},{1,29},{... | collective-permute-start | bytes 417800 | tf_op jit(solution)/shard_map/ppermute | solution.py:591
  6.8 4.4 %collective-permute-start.1 = (f32[272,128]{1,0:T(8,128)S(1)}, f32[272,128]{1,0:T(8,128)S(1)}, u32[]{:S(2)}, u32[]{:S(2)}) collective-permute-start(f32[272,128]{1,0:T(8,128)S(1)} %get-tuple-element.40), channel_id=1, source_target_pairs={{0,4},{4,0},{8,12},{12,8},{16,20},{20,16},{24,28},{28,24},{1,5},{5... | collective-permute-start | bytes 417800 | tf_op jit(solution)/shard_map/ppermute | solution.py:582
  7.7 7.3 %collective-permute-start.5 = (f32[96,256]{1,0:T(8,128)S(1)}, f32[96,256]{1,0:T(8,128)S(1)}, u32[]{:S(2)}, u32[]{:S(2)}) collective-permute-start(f32[96,256]{1,0:T(8,128)S(1)} %get-tuple-element.45.i0), channel_id=1, source_target_pairs={{0,3},{1,2},{2,1},{3,0},{4,7},{5,6},{6,5},{7,4},{8,11},{9,10},{10,... | collective-permute-start | bytes 294920 | tf_op jit(solution)/shard_map/ppermute | solution.py:596
  10.2 6.8 %collective-permute-start.6 = (f32[96,256]{1,0:T(8,128)S(1)}, f32[96,256]{1,0:T(8,128)S(1)}, u32[]{:S(2)}, u32[]{:S(2)}) collective-permute-start(f32[96,256]{1,0:T(8,128)S(1)} %get-tuple-element.45.i0), channel_id=1, source_target_pairs={{0,2},{1,3},{2,0},{3,1},{4,6},{5,7},{6,4},{7,5},{8,10},{9,11},{10,... | collective-permute-start | bytes 294920 | tf_op jit(solution)/shard_map/ppermute | solution.py:596
  10.7 6.3 %collective-permute-start.7 = (f32[96,256]{1,0:T(8,128)S(1)}, f32[96,256]{1,0:T(8,128)S(1)}, u32[]{:S(2)}, u32[]{:S(2)}) collective-permute-start(f32[96,256]{1,0:T(8,128)S(1)} %get-tuple-element.45.i0), channel_id=1, source_target_pairs={{0,1},{1,0},{2,3},{3,2},{4,5},{5,4},{6,7},{7,6},{8,9},{9,8},{10,11... | collective-permute-start | bytes 294920 | tf_op jit(solution)/shard_map/ppermute | solution.py:596
  11.9 6.0 %collective-permute-start.2 = (f32[32,256]{1,0:T(8,128)S(1)}, f32[32,256]{1,0:T(8,128)S(1)}, u32[]{:S(2)}, u32[]{:S(2)}) collective-permute-start(f32[32,256]{1,0:T(8,128)S(1)} %shard_map.115.after.e0), channel_id=1, source_target_pairs={{0,3},{1,2},{2,1},{3,0},{4,7},{5,6},{6,5},{7,4},{8,11},{9,10},{10,... | collective-permute-start | bytes 98312 | tf_op jit(solution)/shard_map/ppermute | solution.py:596
  14.5 3.9 %collective-permute-start.3 = (f32[32,256]{1,0:T(8,128)S(1)}, f32[32,256]{1,0:T(8,128)S(1)}, u32[]{:S(2)}, u32[]{:S(2)}) collective-permute-start(f32[32,256]{1,0:T(8,128)S(1)} %shard_map.115.after.e0), channel_id=1, source_target_pairs={{0,2},{1,3},{2,0},{3,1},{4,6},{5,7},{6,4},{7,5},{8,10},{9,11},{10,... | collective-permute-start | bytes 98312 | tf_op jit(solution)/shard_map/ppermute | solution.py:596
  15.0 3.9 %collective-permute-start.4 = (f32[32,256]{1,0:T(8,128)S(1)}, f32[32,256]{1,0:T(8,128)S(1)}, u32[]{:S(2)}, u32[]{:S(2)}) collective-permute-start(f32[32,256]{1,0:T(8,128)S(1)} %shard_map.115.after.e0), channel_id=1, source_target_pairs={{0,1},{1,0},{2,3},{3,2},{4,5},{5,4},{6,7},{7,6},{8,9},{9,8},{10,11... | collective-permute-start | bytes 98312 | tf_op jit(solution)/shard_map/ppermute | solution.py:596
  19.8 5.9 %collective-permute-start.10 = (f32[96,256]{1,0:T(8,128)S(1)}, f32[96,256]{1,0:T(8,128)S(1)}, u32[]{:S(2)}, u32[]{:S(2)}) collective-permute-start(f32[96,256]{1,0:T(8,128)S(1)} %get-tuple-element.54.i0), channel_id=1, source_target_pairs={{0,3},{1,2},{2,1},{3,0},{4,7},{5,6},{6,5},{7,4},{8,11},{9,10},{10,... | collective-permute-start | bytes 294920 | tf_op jit(solution)/shard_map/ppermute | solution.py:596
  21.6 5.1 %collective-permute-start.8 = (f32[96,256]{1,0:T(8,128)S(1)}, f32[96,256]{1,0:T(8,128)S(1)}, u32[]{:S(2)}, u32[]{:S(2)}) collective-permute-start(f32[96,256]{1,0:T(8,128)S(1)} %get-tuple-element.54.i0), channel_id=1, source_target_pairs={{0,2},{1,3},{2,0},{3,1},{4,6},{5,7},{6,4},{7,5},{8,10},{9,11},{10,... | collective-permute-start | bytes 294920 | tf_op jit(solution)/shard_map/ppermute | solution.py:596
  22.0 4.6 %collective-permute-start.9 = (f32[96,256]{1,0:T(8,128)S(1)}, f32[96,256]{1,0:T(8,128)S(1)}, u32[]{:S(2)}, u32[]{:S(2)}) collective-permute-start(f32[96,256]{1,0:T(8,128)S(1)} %get-tuple-element.54.i0), channel_id=1, source_target_pairs={{0,1},{1,0},{2,3},{3,2},{4,5},{5,4},{6,7},{7,6},{8,9},{9,8},{10,11... | collective-permute-start | bytes 294920 | tf_op jit(solution)/shard_map/ppermute | solution.py:596
  26.9 1.3 %collective-permute-start.11 = (f32[40,128]{1,0:T(8,128)S(1)}, f32[40,128]{1,0:T(8,128)S(1)}, u32[]{:S(2)}, u32[]{:S(2)}) collective-permute-start(f32[40,128]{1,0:T(8,128)S(1)} %get-tuple-element.62), channel_id=1, source_target_pairs={{0,4},{4,0},{8,12},{12,8},{16,20},{20,16},{24,28},{28,24},{1,5},{5... | collective-permute-start | bytes 61448 | tf_op jit(solution)/shard_map/ppermute | solution.py:582
  28.2 3.6 %collective-permute-start.12 = (f32[8,128]{1,0:T(8,128)S(1)}, f32[8,128]{1,0:T(8,128)S(1)}, u32[]{:S(2)}, u32[]{:S(2)}) collective-permute-start(f32[8,128]{1,0:T(8,128)S(1)} %slice_add_fusion.after), channel_id=1, source_target_pairs={{0,8},{4,12},{8,0},{12,4},{16,24},{20,28},{24,16},{28,20},{1,9},{5... | collective-permute-start | bytes 12296 | tf_op jit(solution)/shard_map/ppermute | solution.py:582
  28.2 5.0 %collective-permute-start.14 = (f32[32,128]{1,0:T(8,128)S(1)}, f32[32,128]{1,0:T(8,128)S(1)}, u32[]{:S(2)}, u32[]{:S(2)}) collective-permute-start(f32[32,128]{1,0:T(8,128)S(1)} %shard_map.122), channel_id=1, source_target_pairs={{0,28},{4,8},{8,4},{12,16},{16,12},{20,24},{24,20},{28,0},{1,29},{... | collective-permute-start | bytes 49160 | tf_op jit(solution)/shard_map/ppermute | solution.py:591
  31.8 4.5 %collective-permute-start.13 = (f32[8,128]{1,0:T(8,128)S(1)}, f32[8,128]{1,0:T(8,128)S(1)}, u32[]{:S(2)}, u32[]{:S(2)}) collective-permute-start(f32[8,128]{1,0:T(8,128)S(1)} %add.7.own), channel_id=1, source_target_pairs={{0,16},{4,20},{8,24},{12,28},{16,0},{20,4},{24,8},{28,12},{1,17},{... | collective-permute-start | bytes 12296 | tf_op jit(solution)/shard_map/ppermute | solution.py:582

commit v9 on v8

--- a/solution.py
+++ b/solution.py
@@ -644,8 +644,8 @@
     (to_chip,) = call(copy_kernel, [to_chip.shape], to_chip, sums)
     chip = from_chip(to_chip)
     first = passed(first, sums)
-    sums = sums + from_tile(sums, 2)
-    others = from_tile(sums, 4)
+    sums = sums + from_tile(sums, 3)
+    others = from_tile(sums, 5)
     (second,) = call(filter_kernel, [field], back, core, chip, column, row, cost=LONG)
     weights, residual = combined(sums, others, source, first, second)
     return weights[None], residual[None]

time: 37.5 us -> 36.3 us (0.968)
  waiting for transfers between devices: 7.91 us -> 6.77 us
    ppermute x4, waiting for transfers between devices: 5.12 us -> 3.11 us  [from_tile(): return lax.ppermute(value, 'tile', [(i, i ^ bit) for i in range(count)])]
    ppermute x2, waiting for transfers between devices: 0.42 us -> 1.29 us  [from_chip(): lax.ppermute(value, 'tile', [(i, (i + 1) % count if i % 2 else (i - 1) %...]
  transfers between devices with their start and end apart: 15 -> 15, of which waited for: 8 -> 8; matrix products, arithmetic and copies ran while one was open for 0% -> 0% of each run, Pallas kernels for 17% -> 18%
where the time goes in v9:
time: 36.3 us; the launch traced here: 36.1 us
  starting transfers between devices  18.5 us (51%)
  Pallas kernels  10.1 us (28%)
  waiting for transfers between devices  6.77 us (19%)
  between operations  0.75 us (2%)
    ppermute x9, starting transfers between devices, from_all(): lax.ppermute(value, axis, [(i, i ^ k) for i in range(count)])  10.9 us
    ppermute x2, starting transfers between devices, from_chip(): lax.ppermute(value, 'tile', [(i, (i + 1) % count if i % 2 else (i - 1) %...  6.74 us
    pallas_call x6, Pallas kernels, call(): pl.pallas_call(kernel, out_shape=shapes, in_specs=[vmem] * len(operands),...  3.37 us
    pallas_call x2, Pallas kernels, call_with_constants(): pl.pallas_call(kernel, out_shape=[pltpu.VMEM(shape, F32) for shape in out...  3.26 us
    ppermute x4, waiting for transfers between devices, from_tile(): return lax.ppermute(value, 'tile', [(i, i ^ bit) for i in range(count)])  3.11 us
    ppermute x9, waiting for transfers between devices, from_all(): lax.ppermute(value, axis, [(i, i ^ k) for i in range(count)])  2.37 us
    pallas_call x1, Pallas kernels, held_edges(): pl.pallas_call(edges_kernel, out_shape=[pltpu.VMEM(source.shape, F32), pl...  1.64 us
    ppermute x2, waiting for transfers between devices, from_chip(): lax.ppermute(value, 'tile', [(i, (i + 1) % count if i % 2 else (i - 1) %...  1.29 us
  transfers between devices with their start and end apart: 15, of which 8 were waited for; matrix products, arithmetic and copies ran while one was open for 0% of the time, Pallas kernels for 18%

profile of v9, /device:TPU:0, one launch (start us, length us, event | category | flops | bytes accessed | tf_op | source)
XLA Modules:
  0.0 36.1 jit_solution(7039628482223168927)
XLA Ops:
  0.6 1.6 %shard_map.113 = (f32[16,16,256]{2,1,0:T(8,128)S(1)}, bf16[16,6,16,256]{3,2,1,0:T(8,128)(2,1)S(1)}, f32[6,16,256]{2,1,0:T(8,128)S(1)}, f32[2,2,16,128]{3,2,1,0:T...) custom-call(f32[16,16,256]{2,1,0:T(8,128)} %bitcast.7, ...), custom_call_target="tpu_custom_call" | custom-call | tf_op jit(solution)/shard_map/pallas_call | solution.py:503
  2.3 4.6 %collective-permute-start = (f32[272,128]{1,0:T(8,128)S(1)}, f32[272,128]{1,0:T(8,128)S(1)}, u32[]{:S(2)}, u32[]{:S(2)}) collective-permute-start(f32[272,128]{1,0:T(8,128)S(1)} %get-tuple-element.37.after), channel_id=1, source_target_pairs={{0,28},{4,8},{8,4},{12,16},{16,12},{20,24},{24,20},{28,0},{1,29},{... | collective-permute-start | bytes 417800 | tf_op jit(solution)/shard_map/ppermute | solution.py:591
  6.8 0.8 %shard_map.114 = (f32[96,256]{1,0:T(8,128)S(1)}, f32[8,128]{1,0:T(8,128)S(1)}, bf16[3,2,128,128]{3,2,1,0:T(8,128)(2,1)S(1)}, bf16[2,32,32]{2,1,0:T(8,128)(2,1)S(1)}) custom-call(f32[16,16,256]{2,1,0:T(8,128)S(1)} %get-tuple-element.36.source, f32[272,128]{1,0:T(8,128)S(1)} %get-tuple-element.37.after, bf16[16,6,16,256]{3,2,1,0:T(8,128)(2,1)S(1)} %get-tuple-element.38.members_ref), custom_call_target="tpu_custom_call" | custom-call | flops 1000000000 | bytes 1000000 | tf_op jit(solution)/shard_map/pallas_call | solution.py:530
  7.7 2.5 %collective-permute-start.5 = (f32[96,256]{1,0:T(8,128)S(1)}, f32[96,256]{1,0:T(8,128)S(1)}, u32[]{:S(2)}, u32[]{:S(2)}) collective-permute-start(f32[96,256]{1,0:T(8,128)S(1)} %get-tuple-element.45.i0), channel_id=1, source_target_pairs={{0,3},{1,2},{2,1},{3,0},{4,7},{5,6},{6,5},{7,4},{8,11},{9,10},{10,... | collective-permute-start | bytes 294920 | tf_op jit(solution)/shard_map/ppermute | solution.py:596
  10.7 0.5 %collective-permute-start.7 = (f32[96,256]{1,0:T(8,128)S(1)}, f32[96,256]{1,0:T(8,128)S(1)}, u32[]{:S(2)}, u32[]{:S(2)}) collective-permute-start(f32[96,256]{1,0:T(8,128)S(1)} %get-tuple-element.45.i0), channel_id=1, source_target_pairs={{0,1},{1,0},{2,3},{3,2},{4,5},{5,4},{6,7},{7,6},{8,9},{9,8},{10,11... | collective-permute-start | bytes 294920 | tf_op jit(solution)/shard_map/ppermute | solution.py:596
  11.2 0.7 %shard_map.115.after.e0 = f32[32,256]{1,0:T(8,128)S(1)} custom-call(f32[8,128]{1,0:T(8,128)S(1)} %get-tuple-element.39.norm, f32[272,128]{1,0:T(8,128)S(1)} %collective-permute-done.chip, f32[272,128]{1,0:T(8,128)S(1)} %collective-permute-done.1.core, f32[2,2,16,128]{3,2,1,0:T(8,128)S(1)} %get-tuple-element.41.near, ...), custom_call_target="tpu_custom_call" | custom-call | tf_op jit(solution)/shard_map/pallas_call | solution.py:469
  11.9 2.6 %collective-permute-start.2 = (f32[32,256]{1,0:T(8,128)S(1)}, f32[32,256]{1,0:T(8,128)S(1)}, u32[]{:S(2)}, u32[]{:S(2)}) collective-permute-start(f32[32,256]{1,0:T(8,128)S(1)} %shard_map.115.after.e0), channel_id=1, source_target_pairs={{0,3},{1,2},{2,1},{3,0},{4,7},{5,6},{6,5},{7,4},{8,11},{9,10},{10,... | collective-permute-start | bytes 98312 | tf_op jit(solution)/shard_map/ppermute | solution.py:596
  15.0 0.7 %collective-permute-start.4 = (f32[32,256]{1,0:T(8,128)S(1)}, f32[32,256]{1,0:T(8,128)S(1)}, u32[]{:S(2)}, u32[]{:S(2)}) collective-permute-start(f32[32,256]{1,0:T(8,128)S(1)} %shard_map.115.after.e0), channel_id=1, source_target_pairs={{0,1},{1,0},{2,3},{3,2},{4,5},{5,4},{6,7},{7,6},{8,9},{9,8},{10,11... | collective-permute-start | bytes 98312 | tf_op jit(solution)/shard_map/ppermute | solution.py:596
  15.7 1.3 %shard_map.116 = (f32[2,6,2,16,128]{4,3,2,1,0:T(8,128)S(1)}, bf16[2,256,256]{2,1,0:T(8,128)(2,1)S(1)}, bf16[2,256,256]{2,1,0:T(8,128)(2,1)S(1)}, bf16[3,2,128,12...) custom-call(f32[32,256]{1,0:T(8,128)S(1)} %shard_map.115.after.e0, ...), custom_call_target="tpu_custom_call" | custom-call | flops 1000000000 | bytes 1000000 | tf_op jit(solution)/shard_map/pallas_call | solution.py:549
  17.0 0.8 %shard_map.117 = (f32[96,256]{1,0:T(8,128)S(1)}, f32[16,16,256]{2,1,0:T(8,128)S(1)}, f32[96,256]{1,0:T(8,128)S(1)}) custom-call(f32[96,256]{1,0:T(8,128)S(1)} %get-tuple-element.45.i0, f32[96,256]{1,0:T(8,128)S(1)} %collective-permute-done.5.i1, f32[96,256]{1,0:T(8,128)S(1)} %collective-permute-done.6.i2, f32[96,256]{1,0:T(8,128)S(1)} %collective-permute-done.7.i3, ...), custom_call_target="tpu_custom_call" | custom-call | tf_op jit(solution)/shard_map/pallas_call | solution.py:469
  18.4 0.5 %collective-permute-done.4.e3 = f32[32,256]{1,0:T(8,128)S(1)} collective-permute-done((f32[32,256]{1,0:T(8,128)S(1)}, f32[32,256]{1,0:T(8,128)S(1)}, u32[]{:S(2)}, u32[]{:S(2)}) %collective-permute-start.4) | collective-permute-done | bytes 32800 | tf_op jit(solution)/shard_map/ppermute | solution.py:596
  18.9 0.9 %shard_map.118 = (f32[32,256]{1,0:T(8,128)S(1)}, f32[2,2,16,128]{3,2,1,0:T(8,128)S(1)}, f32[2,2,16,128]{3,2,1,0:T(8,128)S(1)}, f32[96,256]{1,0:T(8,128)S(1)}) custom-call(f32[32,256]{1,0:T(8,128)S(1)} %shard_map.115.after.e0, f32[32,256]{1,0:T(8,128)S(1)} %collective-permute-done.2.e1, f32[32,256]{1,0:T(8,128)S(1)} %collective-permute-done.3.e2, ...), custom_call_target="tpu_custom_call" | custom-call | tf_op jit(solution)/shard_map/pallas_call | solution.py:469
  19.8 1.8 %collective-permute-start.10 = (f32[96,256]{1,0:T(8,128)S(1)}, f32[96,256]{1,0:T(8,128)S(1)}, u32[]{:S(2)}, u32[]{:S(2)}) collective-permute-start(f32[96,256]{1,0:T(8,128)S(1)} %get-tuple-element.54.i0), channel_id=1, source_target_pairs={{0,3},{1,2},{2,1},{3,0},{4,7},{5,6},{6,5},{7,4},{8,11},{9,10},{10,... | collective-permute-start | bytes 294920 | tf_op jit(solution)/shard_map/ppermute | solution.py:596
  22.0 1.3 %collective-permute-start.9 = (f32[96,256]{1,0:T(8,128)S(1)}, f32[96,256]{1,0:T(8,128)S(1)}, u32[]{:S(2)}, u32[]{:S(2)}) collective-permute-start(f32[96,256]{1,0:T(8,128)S(1)} %get-tuple-element.54.i0), channel_id=1, source_target_pairs={{0,1},{1,0},{2,3},{3,2},{4,5},{5,4},{6,7},{7,6},{8,9},{9,8},{10,11... | collective-permute-start | bytes 294920 | tf_op jit(solution)/shard_map/ppermute | solution.py:596
  23.3 2.0 %shard_map.119 = (f32[6,16,256]{2,1,0:T(8,128)S(1)}, f32[2,8,128]{2,1,0:T(8,128)S(1)}, f32[16,16,256]{2,1,0:T(8,128)S(1)}, bf16[2,512,256]{2,1,0:T(8,128)(2,1)S(1)}, bf16[2,256,256]{2,1,0:T(8,128)(2,1)S(1)}) custom-call(f32[16,16,256]{2,1,0:T(8,128)S(1)} %get-tuple-element.55.main, f32[2,2,16,128]{3,2,1,0:T(8,128)S(1)} %get-tuple-element.56.own, ...), custom_call_target="tpu_custom_call" | custom-call | flops 1000000000 | bytes 1000000 | tf_op jit(solution)/shard_map/pallas_call | solution.py:549
  25.6 1.0 %collective-permute-done.8.i1 = f32[96,256]{1,0:T(8,128)S(1)} collective-permute-done((f32[96,256]{1,0:T(8,128)S(1)}, f32[96,256]{1,0:T(8,128)S(1)}, u32[]{:S(2)}, u32[]{:S(2)}) %collective-permute-start.8) | collective-permute-done | bytes 98336 | tf_op jit(solution)/shard_map/ppermute | solution.py:596
  27.0 1.2 %collective-permute-done.11.core = f32[40,128]{1,0:T(8,128)S(1)} collective-permute-done((f32[40,128]{1,0:T(8,128)S(1)}, f32[40,128]{1,0:T(8,128)S(1)}, u32[]{:S(2)}, u32[]{:S(2)}) %collective-permute-start.11) | collective-permute-done | bytes 20512 | tf_op jit(solution)/shard_map/ppermute | solution.py:582
  28.2 2.2 %collective-permute-start.14 = (f32[32,128]{1,0:T(8,128)S(1)}, f32[32,128]{1,0:T(8,128)S(1)}, u32[]{:S(2)}, u32[]{:S(2)}) collective-permute-start(f32[32,128]{1,0:T(8,128)S(1)} %shard_map.122), channel_id=1, source_target_pairs={{0,28},{4,8},{8,4},{12,16},{16,12},{20,24},{24,20},{28,0},{1,29},{... | collective-permute-start | bytes 49160 | tf_op jit(solution)/shard_map/ppermute | solution.py:591
  30.3 0.8 %collective-permute-done.12 = f32[8,128]{1,0:T(8,128)S(1)} collective-permute-done((f32[8,128]{1,0:T(8,128)S(1)}, f32[8,128]{1,0:T(8,128)S(1)}, u32[]{:S(2)}, u32[]{:S(2)}) %collective-permute-start.12) | collective-permute-done | bytes 4128 | tf_op jit(solution)/shard_map/ppermute | solution.py:582
  31.2 0.8 %collective-permute-start.13 = (f32[8,128]{1,0:T(8,128)S(1)}, f32[8,128]{1,0:T(8,128)S(1)}, u32[]{:S(2)}, u32[]{:S(2)}) collective-permute-start(f32[8,128]{1,0:T(8,128)S(1)} %add.7.own), channel_id=1, source_target_pairs={{0,20},{4,16},{8,28},{12,24},{16,4},{20,0},{24,12},{28,8},{1,21},{... | collective-permute-start | bytes 12296 | tf_op jit(solution)/shard_map/ppermute | solution.py:582
  32.0 1.3 %collective-permute-done.14.chip = f32[32,128]{1,0:T(8,128)S(1)} collective-permute-done((f32[32,128]{1,0:T(8,128)S(1)}, f32[32,128]{1,0:T(8,128)S(1)}, u32[]{:S(2)}, u32[]{:S(2)}) %collective-permute-start.14) | collective-permute-done | bytes 16416 | tf_op jit(solution)/shard_map/ppermute | solution.py:591
  33.3 0.8 %shard_map.123.second = f32[16,16,256]{2,1,0:T(8,128)S(1)} custom-call(f32[16,16,256]{2,1,0:T(8,128)S(1)} %get-tuple-element.64.back, f32[40,128]{1,0:T(8,128)S(1)} %collective-permute-done.11.core, f32[32,128]{1,0:T(8,128)S(1)} %collective-permute-done.14.chip, bf16[2,512,256]{2,1,0:T(8,128)(2,1)S(1)} %get-tuple-element.66.column, ...), custom_call_target="tpu_custom_call" | custom-call | flops 1000000000 | bytes 1000000 | tf_op jit(solution)/shard_map/pallas_call | solution.py:469
  34.0 1.1 %collective-permute-done.13.other = f32[8,128]{1,0:T(8,128)S(1)} collective-permute-done((f32[8,128]{1,0:T(8,128)S(1)}, f32[8,128]{1,0:T(8,128)S(1)}, u32[]{:S(2)}, u32[]{:S(2)}) %collective-permute-start.13) | collective-permute-done | bytes 4128 | tf_op jit(solution)/shard_map/ppermute | solution.py:582
  35.1 1.0 %shard_map.124 = (f32[16,16,256]{2,1,0:T(8,128)}, f32[16,16,256]{2,1,0:T(8,128)}) custom-call(f32[8,128]{1,0:T(8,128)S(1)} %add.7.own, f32[8,128]{1,0:T(8,128)S(1)} %collective-permute-done.13.other, f32[16,16,256]{2,1,0:T(8,128)S(1)} %get-tuple-element.36.source, f32[16,16,256]{2,1,0:T(8,128)S(1)} %shard_map.121.first, f32[16,16,256]{2,1,0:T(8,128)S(1)} %shard_map.123.second), custom_call_target="tpu_custom_call" | custom-call | tf_op jit(solution)/shard_map/pallas_call | solution.py:563
  (20 shorter events, 2.7 us)
Async XLA Ops:
  2.3 8.9 %collective-permute-start = (f32[272,128]{1,0:T(8,128)S(1)}, f32[272,128]{1,0:T(8,128)S(1)}, u32[]{:S(2)}, u32[]{:S(2)}) collective-permute-start(f32[272,128]{1,0:T(8,128)S(1)} %get-tuple-element.37.after), channel_id=1, source_target_pairs={{0,28},{4,8},{8,4},{12,16},{16,12},{20,24},{24,20},{28,0},{1,29},{... | collective-permute-start | bytes 417800 | tf_op jit(solution)/shard_map/ppermute | solution.py:591
  6.8 4.4 %collective-permute-start.1 = (f32[272,128]{1,0:T(8,128)S(1)}, f32[272,128]{1,0:T(8,128)S(1)}, u32[]{:S(2)}, u32[]{:S(2)}) collective-permute-start(f32[272,128]{1,0:T(8,128)S(1)} %get-tuple-element.40), channel_id=1, source_target_pairs={{0,4},{4,0},{8,12},{12,8},{16,20},{20,16},{24,28},{28,24},{1,5},{5... | collective-permute-start | bytes 417800 | tf_op jit(solution)/shard_map/ppermute | solution.py:582
  7.7 7.3 %collective-permute-start.5 = (f32[96,256]{1,0:T(8,128)S(1)}, f32[96,256]{1,0:T(8,128)S(1)}, u32[]{:S(2)}, u32[]{:S(2)}) collective-permute-start(f32[96,256]{1,0:T(8,128)S(1)} %get-tuple-element.45.i0), channel_id=1, source_target_pairs={{0,3},{1,2},{2,1},{3,0},{4,7},{5,6},{6,5},{7,4},{8,11},{9,10},{10,... | collective-permute-start | bytes 294920 | tf_op jit(solution)/shard_map/ppermute | solution.py:596
  10.2 6.8 %collective-permute-start.6 = (f32[96,256]{1,0:T(8,128)S(1)}, f32[96,256]{1,0:T(8,128)S(1)}, u32[]{:S(2)}, u32[]{:S(2)}) collective-permute-start(f32[96,256]{1,0:T(8,128)S(1)} %get-tuple-element.45.i0), channel_id=1, source_target_pairs={{0,2},{1,3},{2,0},{3,1},{4,6},{5,7},{6,4},{7,5},{8,10},{9,11},{10,... | collective-permute-start | bytes 294920 | tf_op jit(solution)/shard_map/ppermute | solution.py:596
  10.7 6.3 %collective-permute-start.7 = (f32[96,256]{1,0:T(8,128)S(1)}, f32[96,256]{1,0:T(8,128)S(1)}, u32[]{:S(2)}, u32[]{:S(2)}) collective-permute-start(f32[96,256]{1,0:T(8,128)S(1)} %get-tuple-element.45.i0), channel_id=1, source_target_pairs={{0,1},{1,0},{2,3},{3,2},{4,5},{5,4},{6,7},{7,6},{8,9},{9,8},{10,11... | collective-permute-start | bytes 294920 | tf_op jit(solution)/shard_map/ppermute | solution.py:596
  11.9 6.0 %collective-permute-start.2 = (f32[32,256]{1,0:T(8,128)S(1)}, f32[32,256]{1,0:T(8,128)S(1)}, u32[]{:S(2)}, u32[]{:S(2)}) collective-permute-start(f32[32,256]{1,0:T(8,128)S(1)} %shard_map.115.after.e0), channel_id=1, source_target_pairs={{0,3},{1,2},{2,1},{3,0},{4,7},{5,6},{6,5},{7,4},{8,11},{9,10},{10,... | collective-permute-start | bytes 98312 | tf_op jit(solution)/shard_map/ppermute | solution.py:596
  14.5 3.9 %collective-permute-start.3 = (f32[32,256]{1,0:T(8,128)S(1)}, f32[32,256]{1,0:T(8,128)S(1)}, u32[]{:S(2)}, u32[]{:S(2)}) collective-permute-start(f32[32,256]{1,0:T(8,128)S(1)} %shard_map.115.after.e0), channel_id=1, source_target_pairs={{0,2},{1,3},{2,0},{3,1},{4,6},{5,7},{6,4},{7,5},{8,10},{9,11},{10,... | collective-permute-start | bytes 98312 | tf_op jit(solution)/shard_map/ppermute | solution.py:596
  15.0 3.9 %collective-permute-start.4 = (f32[32,256]{1,0:T(8,128)S(1)}, f32[32,256]{1,0:T(8,128)S(1)}, u32[]{:S(2)}, u32[]{:S(2)}) collective-permute-start(f32[32,256]{1,0:T(8,128)S(1)} %shard_map.115.after.e0), channel_id=1, source_target_pairs={{0,1},{1,0},{2,3},{3,2},{4,5},{5,4},{6,7},{7,6},{8,9},{9,8},{10,11... | collective-permute-start | bytes 98312 | tf_op jit(solution)/shard_map/ppermute | solution.py:596
  19.8 5.9 %collective-permute-start.10 = (f32[96,256]{1,0:T(8,128)S(1)}, f32[96,256]{1,0:T(8,128)S(1)}, u32[]{:S(2)}, u32[]{:S(2)}) collective-permute-start(f32[96,256]{1,0:T(8,128)S(1)} %get-tuple-element.54.i0), channel_id=1, source_target_pairs={{0,3},{1,2},{2,1},{3,0},{4,7},{5,6},{6,5},{7,4},{8,11},{9,10},{10,... | collective-permute-start | bytes 294920 | tf_op jit(solution)/shard_map/ppermute | solution.py:596
  21.6 5.1 %collective-permute-start.8 = (f32[96,256]{1,0:T(8,128)S(1)}, f32[96,256]{1,0:T(8,128)S(1)}, u32[]{:S(2)}, u32[]{:S(2)}) collective-permute-start(f32[96,256]{1,0:T(8,128)S(1)} %get-tuple-element.54.i0), channel_id=1, source_target_pairs={{0,2},{1,3},{2,0},{3,1},{4,6},{5,7},{6,4},{7,5},{8,10},{9,11},{10,... | collective-permute-start | bytes 294920 | tf_op jit(solution)/shard_map/ppermute | solution.py:596
  22.0 4.6 %collective-permute-start.9 = (f32[96,256]{1,0:T(8,128)S(1)}, f32[96,256]{1,0:T(8,128)S(1)}, u32[]{:S(2)}, u32[]{:S(2)}) collective-permute-start(f32[96,256]{1,0:T(8,128)S(1)} %get-tuple-element.54.i0), channel_id=1, source_target_pairs={{0,1},{1,0},{2,3},{3,2},{4,5},{5,4},{6,7},{7,6},{8,9},{9,8},{10,11... | collective-permute-start | bytes 294920 | tf_op jit(solution)/shard_map/ppermute | solution.py:596
  26.9 1.3 %collective-permute-start.11 = (f32[40,128]{1,0:T(8,128)S(1)}, f32[40,128]{1,0:T(8,128)S(1)}, u32[]{:S(2)}, u32[]{:S(2)}) collective-permute-start(f32[40,128]{1,0:T(8,128)S(1)} %get-tuple-element.62), channel_id=1, source_target_pairs={{0,4},{4,0},{8,12},{12,8},{16,20},{20,16},{24,28},{28,24},{1,5},{5... | collective-permute-start | bytes 61448 | tf_op jit(solution)/shard_map/ppermute | solution.py:582
  28.2 3.0 %collective-permute-start.12 = (f32[8,128]{1,0:T(8,128)S(1)}, f32[8,128]{1,0:T(8,128)S(1)}, u32[]{:S(2)}, u32[]{:S(2)}) collective-permute-start(f32[8,128]{1,0:T(8,128)S(1)} %slice_add_fusion.after), channel_id=1, source_target_pairs={{0,12},{4,8},{8,4},{12,0},{16,28},{20,24},{24,20},{28,16},{1,13},{... | collective-permute-start | bytes 12296 | tf_op jit(solution)/shard_map/ppermute | solution.py:582
  28.2 5.1 %collective-permute-start.14 = (f32[32,128]{1,0:T(8,128)S(1)}, f32[32,128]{1,0:T(8,128)S(1)}, u32[]{:S(2)}, u32[]{:S(2)}) collective-permute-start(f32[32,128]{1,0:T(8,128)S(1)} %shard_map.122), channel_id=1, source_target_pairs={{0,28},{4,8},{8,4},{12,16},{16,12},{20,24},{24,20},{28,0},{1,29},{... | collective-permute-start | bytes 49160 | tf_op jit(solution)/shard_map/ppermute | solution.py:591
  31.2 3.9 %collective-permute-start.13 = (f32[8,128]{1,0:T(8,128)S(1)}, f32[8,128]{1,0:T(8,128)S(1)}, u32[]{:S(2)}, u32[]{:S(2)}) collective-permute-start(f32[8,128]{1,0:T(8,128)S(1)} %add.7.own), channel_id=1, source_target_pairs={{0,20},{4,16},{8,28},{12,24},{16,4},{20,0},{24,12},{28,8},{1,21},{... | collective-permute-start | bytes 12296 | tf_op jit(solution)/shard_map/ppermute | solution.py:582

commit v10 on v9

--- a/solution.py
+++ b/solution.py
@@ -242,32 +242,63 @@
     kept(thin, tap_at(gap, down // height == across // height))
 
 
-def edge_sums(edge_members, smoothed):
+def edge_terms(edge_members, smoothed):
     groups, height = edge_members.shape[1:3]
-    return repeated(jnp.sum(edge_members * smoothed.reshape(1, groups, height, LANES), axis=1), EDGE)
-
-
-def add_columns(out, start, blocks):
-    levels, height, _ = blocks[0].shape
+    return jnp.sum(edge_members * smoothed.reshape(1, groups, height, LANES), axis=1)
+
+
+def in_slot(shape, slot):
+    lane = lane_of(shape)
+    return (lane >= slot * EDGE) & (lane < (slot + 1) * EDGE)
+
+
+def add_columns(out, start, terms):
+    levels, height, _ = terms[0].shape
     origin = start // LANES * LANES
-    lane = lane_of(blocks[0].shape)
-    total = jnp.zeros(lane.shape, F32)
-    for i, block in enumerate(blocks):
-        first = start - origin + i * EDGE
-        total = jnp.where((lane >= first) & (lane < first + EDGE), block, total)
+    first = (start - origin) // EDGE
+    even, odd = terms if first % 2 == 0 else terms[::-1]
+    even, odd = (x.reshape(levels * height, LANES) for x in (even, odd))
+    lane = lane_of(even.shape)
+    total = jnp.where(
+        lane // EDGE % 2 == 0,
+        even + pltpu.roll(even, LANES - EDGE, 1),
+        odd + pltpu.roll(odd, EDGE, 1),
+    )
+    total = repeated(total, 2 * EDGE)
+    mask = (lane >= start - origin) & (lane < start - origin + 2 * EDGE)
     rows, span = pl.ds(0, levels * height), pl.ds(origin, LANES)
-    out[rows, span] = out[rows, span] + total.reshape(levels * height, LANES)
-
-
-def beside_levels(sums):
-    total = jnp.zeros(sums.shape[1:], F32)
-    for v in range(sums.shape[0]):
-        total = jnp.where(level_lanes(total.shape, v), sums[v], total)
-    return total
+    out[rows, span] = out[rows, span] + jnp.where(mask, total, 0.0)
+
+
+def beside_levels(terms):
+    levels, shape = terms.shape[0], terms.shape[1:]
+    slots = LANES // EDGE
+    moved = []
+    for k in range(slots):
+        part = jnp.zeros(shape, F32)
+        for slot in range(slots):
+            level = (slot + k) % slots
+            if level < levels:
+                part = jnp.where(in_slot(shape, slot), terms[level], part)
+        moved.append(pltpu.roll(part, k * EDGE, 1) if k else part)
+    while len(moved) > 1:
+        moved = [x + y for x, y in zip(moved[::2], moved[1::2])]
+    return moved[0]
 
 
 def apart_levels(packed, levels):
-    return [repeated(jnp.where(level_lanes(packed.shape, v), packed, 0.0), EDGE) for v in range(levels)]
+    slots = LANES // EDGE
+    turned = [packed] + [pltpu.roll(packed, EDGE * k, 1) for k in range(1, slots)]
+    lane = lane_of(packed.shape)
+    out = []
+    for v in range(levels):
+        parts, width = [turned[(slot - v) % slots] for slot in range(slots)], EDGE
+        while len(parts) > 1:
+            left = lane // width % 2 == 0
+            parts = [jnp.where(left, x, y) for x, y in zip(parts[::2], parts[1::2])]
+            width *= 2
+        out.append(parts[0])
+    return out
 
 
 def halo_members(block, rows, groups, levels):
@@ -291,8 +322,8 @@
         own = slice(side * rows, (side + 1) * rows)
         within = dot3(tuple(x[own] for x in middle), both(edge.at[2 * side]))
         lanes = pl.ds(side * LANES, LANES)
-        out[:height, lanes] = beside_levels(edge_sums(edge_members[side], within))
-        out[height:, lanes] = beside_levels(edge_sums(halo_members(block, rows, groups, levels), beyond[own]))
+        out[:height, lanes] = beside_levels(edge_terms(edge_members[side], within))
+        out[height:, lanes] = beside_levels(edge_terms(halo_members(block, rows, groups, levels), beyond[own]))
     lane = lane_of(norm.shape)
     top = pl.ds(0, norm.shape[0])
     out[top, :LANES] = jnp.where(lane >= LANES - SPARE, norm[...], out[top, :LANES])
@@ -359,7 +390,7 @@
         matrix = [jnp.concatenate([edge[2 * side, k], edge[1, k]], axis=0) for k in range(2)]
         outermost = dot3(tuple(x[:, span] for x in filtered), matrix)
         inner = dot3(tuple(x[:, span.start + LANES : span.stop] for x in filtered), both(edge.at[2 * side]))
-        blocks = [edge_sums(edge_members[side], outermost), edge_sums(next_members[side], inner)]
+        blocks = [edge_terms(edge_members[side], outermost), edge_terms(next_members[side], inner)]
         if side == 0:
             add_columns(out, 0, blocks)
         else:
@@ -612,7 +643,7 @@
     )
     core, chip = from_core(to_core), from_chip(to_chip)
     inside, norm, edge, thin = first_increment(source, to_chip, members_data)
-    inside = from_all(inside, "mem", (3, 2, 1))
+    inside = from_all(inside, "mem", (1, 2, 3))
     (outer,) = call(edge_kernel, [(2 * height, 2 * LANES)], norm, chip, core, near, edge_members, edge, thin)
     column_twice, row_twice = halves(band(twice, own, own)), halves(row_matrix(taps, height, members, 2))
     edge, thin = edge_matrix(twice, EDGE), halves(row_matrix(taps, height, groups, 2))

time: 36.3 us -> 35.9 us (0.989)
  transfers between devices with their start and end apart: 15 -> 15, of which waited for: 8 -> 9; matrix products, arithmetic and copies ran while one was open for 0% -> 0% of each run, Pallas kernels for 18% -> 17%
where the time goes in v10:
time: 35.9 us; the launch traced here: 35.7 us
  starting transfers between devices  18.5 us (52%)
  Pallas kernels  9.74 us (27%)
  waiting for transfers between devices  6.74 us (19%)
  between operations  0.74 us (2%)
    ppermute x9, starting transfers between devices, from_all(): lax.ppermute(value, axis, [(i, i ^ k) for i in range(count)])  10.7 us
    ppermute x2, starting transfers between devices, from_chip(): lax.ppermute(value, 'tile', [(i, (i + 1) % count if i % 2 else (i - 1) %...  6.86 us
    pallas_call x2, Pallas kernels, call_with_constants(): pl.pallas_call(kernel, out_shape=[pltpu.VMEM(shape, F32) for shape in out...  3.22 us
    pallas_call x6, Pallas kernels, call(): pl.pallas_call(kernel, out_shape=shapes, in_specs=[vmem] * len(operands),...  3.06 us
    ppermute x4, waiting for transfers between devices, from_tile(): return lax.ppermute(value, 'tile', [(i, i ^ bit) for i in range(count)])  2.99 us
    ppermute x9, waiting for transfers between devices, from_all(): lax.ppermute(value, axis, [(i, i ^ k) for i in range(count)])  2.58 us
    pallas_call x1, Pallas kernels, held_edges(): pl.pallas_call(edges_kernel, out_shape=[pltpu.VMEM(source.shape, F32), pl...  1.64 us
    ppermute x2, waiting for transfers between devices, from_chip(): lax.ppermute(value, 'tile', [(i, (i + 1) % count if i % 2 else (i - 1) %...  1.17 us
  transfers between devices with their start and end apart: 15, of which 9 were waited for; matrix products, arithmetic and copies ran while one was open for 0% of the time, Pallas kernels for 17%

profile of v10, /device:TPU:0, one launch (start us, length us, event | category | flops | bytes accessed | tf_op | source)
XLA Modules:
  0.0 35.7 jit_solution(17953907917382399863)
XLA Ops:
  0.6 1.6 %shard_map.113 = (f32[16,16,256]{2,1,0:T(8,128)S(1)}, bf16[16,6,16,256]{3,2,1,0:T(8,128)(2,1)S(1)}, f32[6,16,256]{2,1,0:T(8,128)S(1)}, f32[2,2,16,128]{3,2,1,0:T...) custom-call(f32[16,16,256]{2,1,0:T(8,128)} %bitcast.7, ...), custom_call_target="tpu_custom_call" | custom-call | tf_op jit(solution)/shard_map/pallas_call | solution.py:534
  2.3 4.6 %collective-permute-start = (f32[272,128]{1,0:T(8,128)S(1)}, f32[272,128]{1,0:T(8,128)S(1)}, u32[]{:S(2)}, u32[]{:S(2)}) collective-permute-start(f32[272,128]{1,0:T(8,128)S(1)} %get-tuple-element.37.after), channel_id=1, source_target_pairs={{0,28},{4,8},{8,4},{12,16},{16,12},{20,24},{24,20},{28,0},{1,29},{... | collective-permute-start | bytes 417800 | tf_op jit(solution)/shard_map/ppermute | solution.py:622
  6.8 0.8 %shard_map.114 = (f32[96,256]{1,0:T(8,128)S(1)}, f32[8,128]{1,0:T(8,128)S(1)}, bf16[3,2,128,128]{3,2,1,0:T(8,128)(2,1)S(1)}, bf16[2,32,32]{2,1,0:T(8,128)(2,1)S(1)}) custom-call(f32[16,16,256]{2,1,0:T(8,128)S(1)} %get-tuple-element.36.source, f32[272,128]{1,0:T(8,128)S(1)} %get-tuple-element.37.after, bf16[16,6,16,256]{3,2,1,0:T(8,128)(2,1)S(1)} %get-tuple-element.38.members_ref), custom_call_target="tpu_custom_call" | custom-call | flops 1000000000 | bytes 1000000 | tf_op jit(solution)/shard_map/pallas_call | solution.py:561
  7.7 1.6 %collective-permute-start.5 = (f32[96,256]{1,0:T(8,128)S(1)}, f32[96,256]{1,0:T(8,128)S(1)}, u32[]{:S(2)}, u32[]{:S(2)}) collective-permute-start(f32[96,256]{1,0:T(8,128)S(1)} %get-tuple-element.45.i0), channel_id=1, source_target_pairs={{0,1},{1,0},{2,3},{3,2},{4,5},{5,4},{6,7},{7,6},{8,9},{9,8},{10,11... | collective-permute-start | bytes 294920 | tf_op jit(solution)/shard_map/ppermute | solution.py:627
  9.2 1.5 %collective-permute-start.6 = (f32[96,256]{1,0:T(8,128)S(1)}, f32[96,256]{1,0:T(8,128)S(1)}, u32[]{:S(2)}, u32[]{:S(2)}) collective-permute-start(f32[96,256]{1,0:T(8,128)S(1)} %get-tuple-element.45.i0), channel_id=1, source_target_pairs={{0,2},{1,3},{2,0},{3,1},{4,6},{5,7},{6,4},{7,5},{8,10},{9,11},{10,... | collective-permute-start | bytes 294920 | tf_op jit(solution)/shard_map/ppermute | solution.py:627
  11.2 0.5 %shard_map.115.after.e0 = f32[32,256]{1,0:T(8,128)S(1)} custom-call(f32[8,128]{1,0:T(8,128)S(1)} %get-tuple-element.39.norm, f32[272,128]{1,0:T(8,128)S(1)} %collective-permute-done.chip, f32[272,128]{1,0:T(8,128)S(1)} %collective-permute-done.1.core, f32[2,2,16,128]{3,2,1,0:T(8,128)S(1)} %get-tuple-element.41.near, ...), custom_call_target="tpu_custom_call" | custom-call | tf_op jit(solution)/shard_map/pallas_call | solution.py:500
  11.7 2.6 %collective-permute-start.2 = (f32[32,256]{1,0:T(8,128)S(1)}, f32[32,256]{1,0:T(8,128)S(1)}, u32[]{:S(2)}, u32[]{:S(2)}) collective-permute-start(f32[32,256]{1,0:T(8,128)S(1)} %shard_map.115.after.e0), channel_id=1, source_target_pairs={{0,3},{1,2},{2,1},{3,0},{4,7},{5,6},{6,5},{7,4},{8,11},{9,10},{10,... | collective-permute-start | bytes 98312 | tf_op jit(solution)/shard_map/ppermute | solution.py:627
  15.3 1.3 %shard_map.116 = (f32[2,6,2,16,128]{4,3,2,1,0:T(8,128)S(1)}, bf16[2,256,256]{2,1,0:T(8,128)(2,1)S(1)}, bf16[2,256,256]{2,1,0:T(8,128)(2,1)S(1)}, bf16[3,2,128,12...) custom-call(f32[32,256]{1,0:T(8,128)S(1)} %shard_map.115.after.e0, ...), custom_call_target="tpu_custom_call" | custom-call | flops 1000000000 | bytes 1000000 | tf_op jit(solution)/shard_map/pallas_call | solution.py:580
  16.7 0.8 %shard_map.117 = (f32[96,256]{1,0:T(8,128)S(1)}, f32[16,16,256]{2,1,0:T(8,128)S(1)}, f32[96,256]{1,0:T(8,128)S(1)}) custom-call(f32[96,256]{1,0:T(8,128)S(1)} %get-tuple-element.45.i0, f32[96,256]{1,0:T(8,128)S(1)} %collective-permute-done.5.i1, f32[96,256]{1,0:T(8,128)S(1)} %collective-permute-done.6.i2, f32[96,256]{1,0:T(8,128)S(1)} %collective-permute-done.7.i3, ...), custom_call_target="tpu_custom_call" | custom-call | tf_op jit(solution)/shard_map/pallas_call | solution.py:500
  17.5 0.7 %collective-permute-done.3.e2 = f32[32,256]{1,0:T(8,128)S(1)} collective-permute-done((f32[32,256]{1,0:T(8,128)S(1)}, f32[32,256]{1,0:T(8,128)S(1)}, u32[]{:S(2)}, u32[]{:S(2)}) %collective-permute-start.3) | collective-permute-done | bytes 32800 | tf_op jit(solution)/shard_map/ppermute | solution.py:627
  18.2 0.5 %collective-permute-done.4.e3 = f32[32,256]{1,0:T(8,128)S(1)} collective-permute-done((f32[32,256]{1,0:T(8,128)S(1)}, f32[32,256]{1,0:T(8,128)S(1)}, u32[]{:S(2)}, u32[]{:S(2)}) %collective-permute-start.4) | collective-permute-done | bytes 32800 | tf_op jit(solution)/shard_map/ppermute | solution.py:627
  18.8 0.7 %shard_map.118 = (f32[32,256]{1,0:T(8,128)S(1)}, f32[2,2,16,128]{3,2,1,0:T(8,128)S(1)}, f32[2,2,16,128]{3,2,1,0:T(8,128)S(1)}, f32[96,256]{1,0:T(8,128)S(1)}) custom-call(f32[32,256]{1,0:T(8,128)S(1)} %shard_map.115.after.e0, f32[32,256]{1,0:T(8,128)S(1)} %collective-permute-done.2.e1, f32[32,256]{1,0:T(8,128)S(1)} %collective-permute-done.3.e2, ...), custom_call_target="tpu_custom_call" | custom-call | tf_op jit(solution)/shard_map/pallas_call | solution.py:500
  19.5 1.6 %collective-permute-start.10 = (f32[96,256]{1,0:T(8,128)S(1)}, f32[96,256]{1,0:T(8,128)S(1)}, u32[]{:S(2)}, u32[]{:S(2)}) collective-permute-start(f32[96,256]{1,0:T(8,128)S(1)} %get-tuple-element.54.i0), channel_id=1, source_target_pairs={{0,3},{1,2},{2,1},{3,0},{4,7},{5,6},{6,5},{7,4},{8,11},{9,10},{10,... | collective-permute-start | bytes 294920 | tf_op jit(solution)/shard_map/ppermute | solution.py:627
  21.5 1.6 %collective-permute-start.9 = (f32[96,256]{1,0:T(8,128)S(1)}, f32[96,256]{1,0:T(8,128)S(1)}, u32[]{:S(2)}, u32[]{:S(2)}) collective-permute-start(f32[96,256]{1,0:T(8,128)S(1)} %get-tuple-element.54.i0), channel_id=1, source_target_pairs={{0,1},{1,0},{2,3},{3,2},{4,5},{5,4},{6,7},{7,6},{8,9},{9,8},{10,11... | collective-permute-start | bytes 294920 | tf_op jit(solution)/shard_map/ppermute | solution.py:627
  23.0 1.9 %shard_map.119 = (f32[6,16,256]{2,1,0:T(8,128)S(1)}, f32[2,8,128]{2,1,0:T(8,128)S(1)}, f32[16,16,256]{2,1,0:T(8,128)S(1)}, bf16[2,512,256]{2,1,0:T(8,128)(2,1)S(1)}, bf16[2,256,256]{2,1,0:T(8,128)(2,1)S(1)}) custom-call(f32[16,16,256]{2,1,0:T(8,128)S(1)} %get-tuple-element.55.main, f32[2,2,16,128]{3,2,1,0:T(8,128)S(1)} %get-tuple-element.56.own, ...), custom_call_target="tpu_custom_call" | custom-call | flops 1000000000 | bytes 1000000 | tf_op jit(solution)/shard_map/pallas_call | solution.py:580
  25.2 1.0 %collective-permute-done.8.i1 = f32[96,256]{1,0:T(8,128)S(1)} collective-permute-done((f32[96,256]{1,0:T(8,128)S(1)}, f32[96,256]{1,0:T(8,128)S(1)}, u32[]{:S(2)}, u32[]{:S(2)}) %collective-permute-start.8) | collective-permute-done | bytes 98336 | tf_op jit(solution)/shard_map/ppermute | solution.py:627
  26.6 1.2 %collective-permute-done.11.core = f32[40,128]{1,0:T(8,128)S(1)} collective-permute-done((f32[40,128]{1,0:T(8,128)S(1)}, f32[40,128]{1,0:T(8,128)S(1)}, u32[]{:S(2)}, u32[]{:S(2)}) %collective-permute-start.11) | collective-permute-done | bytes 20512 | tf_op jit(solution)/shard_map/ppermute | solution.py:613
  27.7 2.3 %collective-permute-start.14 = (f32[32,128]{1,0:T(8,128)S(1)}, f32[32,128]{1,0:T(8,128)S(1)}, u32[]{:S(2)}, u32[]{:S(2)}) collective-permute-start(f32[32,128]{1,0:T(8,128)S(1)} %shard_map.122), channel_id=1, source_target_pairs={{0,28},{4,8},{8,4},{12,16},{16,12},{20,24},{24,20},{28,0},{1,29},{... | collective-permute-start | bytes 49160 | tf_op jit(solution)/shard_map/ppermute | solution.py:622
  30.0 0.7 %collective-permute-done.12 = f32[8,128]{1,0:T(8,128)S(1)} collective-permute-done((f32[8,128]{1,0:T(8,128)S(1)}, f32[8,128]{1,0:T(8,128)S(1)}, u32[]{:S(2)}, u32[]{:S(2)}) %collective-permute-start.12) | collective-permute-done | bytes 4128 | tf_op jit(solution)/shard_map/ppermute | solution.py:613
  30.8 0.9 %collective-permute-start.13 = (f32[8,128]{1,0:T(8,128)S(1)}, f32[8,128]{1,0:T(8,128)S(1)}, u32[]{:S(2)}, u32[]{:S(2)}) collective-permute-start(f32[8,128]{1,0:T(8,128)S(1)} %add.7.own), channel_id=1, source_target_pairs={{0,20},{4,16},{8,28},{12,24},{16,4},{20,0},{24,12},{28,8},{1,21},{... | collective-permute-start | bytes 12296 | tf_op jit(solution)/shard_map/ppermute | solution.py:613
  31.7 1.2 %collective-permute-done.14.chip = f32[32,128]{1,0:T(8,128)S(1)} collective-permute-done((f32[32,128]{1,0:T(8,128)S(1)}, f32[32,128]{1,0:T(8,128)S(1)}, u32[]{:S(2)}, u32[]{:S(2)}) %collective-permute-start.14) | collective-permute-done | bytes 16416 | tf_op jit(solution)/shard_map/ppermute | solution.py:622
  32.8 0.8 %shard_map.123.second = f32[16,16,256]{2,1,0:T(8,128)S(1)} custom-call(f32[16,16,256]{2,1,0:T(8,128)S(1)} %get-tuple-element.64.back, f32[40,128]{1,0:T(8,128)S(1)} %collective-permute-done.11.core, f32[32,128]{1,0:T(8,128)S(1)} %collective-permute-done.14.chip, bf16[2,512,256]{2,1,0:T(8,128)(2,1)S(1)} %get-tuple-element.66.column, ...), custom_call_target="tpu_custom_call" | custom-call | flops 1000000000 | bytes 1000000 | tf_op jit(solution)/shard_map/pallas_call | solution.py:500
  33.6 1.1 %collective-permute-done.13.other = f32[8,128]{1,0:T(8,128)S(1)} collective-permute-done((f32[8,128]{1,0:T(8,128)S(1)}, f32[8,128]{1,0:T(8,128)S(1)}, u32[]{:S(2)}, u32[]{:S(2)}) %collective-permute-start.13) | collective-permute-done | bytes 4128 | tf_op jit(solution)/shard_map/ppermute | solution.py:613
  34.7 1.0 %shard_map.124 = (f32[16,16,256]{2,1,0:T(8,128)}, f32[16,16,256]{2,1,0:T(8,128)}) custom-call(f32[8,128]{1,0:T(8,128)S(1)} %add.7.own, f32[8,128]{1,0:T(8,128)S(1)} %collective-permute-done.13.other, f32[16,16,256]{2,1,0:T(8,128)S(1)} %get-tuple-element.36.source, f32[16,16,256]{2,1,0:T(8,128)S(1)} %shard_map.121.first, f32[16,16,256]{2,1,0:T(8,128)S(1)} %shard_map.123.second), custom_call_target="tpu_custom_call" | custom-call | tf_op jit(solution)/shard_map/pallas_call | solution.py:594
  (20 shorter events, 2.6 us)
Async XLA Ops:
  2.3 8.9 %collective-permute-start = (f32[272,128]{1,0:T(8,128)S(1)}, f32[272,128]{1,0:T(8,128)S(1)}, u32[]{:S(2)}, u32[]{:S(2)}) collective-permute-start(f32[272,128]{1,0:T(8,128)S(1)} %get-tuple-element.37.after), channel_id=1, source_target_pairs={{0,28},{4,8},{8,4},{12,16},{16,12},{20,24},{24,20},{28,0},{1,29},{... | collective-permute-start | bytes 417800 | tf_op jit(solution)/shard_map/ppermute | solution.py:622
  6.8 4.4 %collective-permute-start.1 = (f32[272,128]{1,0:T(8,128)S(1)}, f32[272,128]{1,0:T(8,128)S(1)}, u32[]{:S(2)}, u32[]{:S(2)}) collective-permute-start(f32[272,128]{1,0:T(8,128)S(1)} %get-tuple-element.40), channel_id=1, source_target_pairs={{0,4},{4,0},{8,12},{12,8},{16,20},{20,16},{24,28},{28,24},{1,5},{5... | collective-permute-start | bytes 417800 | tf_op jit(solution)/shard_map/ppermute | solution.py:613
  7.7 7.2 %collective-permute-start.5 = (f32[96,256]{1,0:T(8,128)S(1)}, f32[96,256]{1,0:T(8,128)S(1)}, u32[]{:S(2)}, u32[]{:S(2)}) collective-permute-start(f32[96,256]{1,0:T(8,128)S(1)} %get-tuple-element.45.i0), channel_id=1, source_target_pairs={{0,1},{1,0},{2,3},{3,2},{4,5},{5,4},{6,7},{7,6},{8,9},{9,8},{10,11... | collective-permute-start | bytes 294920 | tf_op jit(solution)/shard_map/ppermute | solution.py:627
  9.2 7.4 %collective-permute-start.6 = (f32[96,256]{1,0:T(8,128)S(1)}, f32[96,256]{1,0:T(8,128)S(1)}, u32[]{:S(2)}, u32[]{:S(2)}) collective-permute-start(f32[96,256]{1,0:T(8,128)S(1)} %get-tuple-element.45.i0), channel_id=1, source_target_pairs={{0,2},{1,3},{2,0},{3,1},{4,6},{5,7},{6,4},{7,5},{8,10},{9,11},{10,... | collective-permute-start | bytes 294920 | tf_op jit(solution)/shard_map/ppermute | solution.py:627
  10.7 5.9 %collective-permute-start.7 = (f32[96,256]{1,0:T(8,128)S(1)}, f32[96,256]{1,0:T(8,128)S(1)}, u32[]{:S(2)}, u32[]{:S(2)}) collective-permute-start(f32[96,256]{1,0:T(8,128)S(1)} %get-tuple-element.45.i0), channel_id=1, source_target_pairs={{0,3},{1,2},{2,1},{3,0},{4,7},{5,6},{6,5},{7,4},{8,11},{9,10},{10,... | collective-permute-start | bytes 294920 | tf_op jit(solution)/shard_map/ppermute | solution.py:627
  11.7 5.8 %collective-permute-start.2 = (f32[32,256]{1,0:T(8,128)S(1)}, f32[32,256]{1,0:T(8,128)S(1)}, u32[]{:S(2)}, u32[]{:S(2)}) collective-permute-start(f32[32,256]{1,0:T(8,128)S(1)} %shard_map.115.after.e0), channel_id=1, source_target_pairs={{0,3},{1,2},{2,1},{3,0},{4,7},{5,6},{6,5},{7,4},{8,11},{9,10},{10,... | collective-permute-start | bytes 98312 | tf_op jit(solution)/shard_map/ppermute | solution.py:627
  14.3 3.9 %collective-permute-start.3 = (f32[32,256]{1,0:T(8,128)S(1)}, f32[32,256]{1,0:T(8,128)S(1)}, u32[]{:S(2)}, u32[]{:S(2)}) collective-permute-start(f32[32,256]{1,0:T(8,128)S(1)} %shard_map.115.after.e0), channel_id=1, source_target_pairs={{0,2},{1,3},{2,0},{3,1},{4,6},{5,7},{6,4},{7,5},{8,10},{9,11},{10,... | collective-permute-start | bytes 98312 | tf_op jit(solution)/shard_map/ppermute | solution.py:627
  14.8 3.9 %collective-permute-start.4 = (f32[32,256]{1,0:T(8,128)S(1)}, f32[32,256]{1,0:T(8,128)S(1)}, u32[]{:S(2)}, u32[]{:S(2)}) collective-permute-start(f32[32,256]{1,0:T(8,128)S(1)} %shard_map.115.after.e0), channel_id=1, source_target_pairs={{0,1},{1,0},{2,3},{3,2},{4,5},{5,4},{6,7},{7,6},{8,9},{9,8},{10,11... | collective-permute-start | bytes 98312 | tf_op jit(solution)/shard_map/ppermute | solution.py:627
  19.5 5.8 %collective-permute-start.10 = (f32[96,256]{1,0:T(8,128)S(1)}, f32[96,256]{1,0:T(8,128)S(1)}, u32[]{:S(2)}, u32[]{:S(2)}) collective-permute-start(f32[96,256]{1,0:T(8,128)S(1)} %get-tuple-element.54.i0), channel_id=1, source_target_pairs={{0,3},{1,2},{2,1},{3,0},{4,7},{5,6},{6,5},{7,4},{8,11},{9,10},{10,... | collective-permute-start | bytes 294920 | tf_op jit(solution)/shard_map/ppermute | solution.py:627
  21.0 5.2 %collective-permute-start.8 = (f32[96,256]{1,0:T(8,128)S(1)}, f32[96,256]{1,0:T(8,128)S(1)}, u32[]{:S(2)}, u32[]{:S(2)}) collective-permute-start(f32[96,256]{1,0:T(8,128)S(1)} %get-tuple-element.54.i0), channel_id=1, source_target_pairs={{0,2},{1,3},{2,0},{3,1},{4,6},{5,7},{6,4},{7,5},{8,10},{9,11},{10,... | collective-permute-start | bytes 294920 | tf_op jit(solution)/shard_map/ppermute | solution.py:627
  21.5 4.8 %collective-permute-start.9 = (f32[96,256]{1,0:T(8,128)S(1)}, f32[96,256]{1,0:T(8,128)S(1)}, u32[]{:S(2)}, u32[]{:S(2)}) collective-permute-start(f32[96,256]{1,0:T(8,128)S(1)} %get-tuple-element.54.i0), channel_id=1, source_target_pairs={{0,1},{1,0},{2,3},{3,2},{4,5},{5,4},{6,7},{7,6},{8,9},{9,8},{10,11... | collective-permute-start | bytes 294920 | tf_op jit(solution)/shard_map/ppermute | solution.py:627
  26.5 1.3 %collective-permute-start.11 = (f32[40,128]{1,0:T(8,128)S(1)}, f32[40,128]{1,0:T(8,128)S(1)}, u32[]{:S(2)}, u32[]{:S(2)}) collective-permute-start(f32[40,128]{1,0:T(8,128)S(1)} %get-tuple-element.62), channel_id=1, source_target_pairs={{0,4},{4,0},{8,12},{12,8},{16,20},{20,16},{24,28},{28,24},{1,5},{5... | collective-permute-start | bytes 61448 | tf_op jit(solution)/shard_map/ppermute | solution.py:613
  27.7 3.0 %collective-permute-start.12 = (f32[8,128]{1,0:T(8,128)S(1)}, f32[8,128]{1,0:T(8,128)S(1)}, u32[]{:S(2)}, u32[]{:S(2)}) collective-permute-start(f32[8,128]{1,0:T(8,128)S(1)} %slice_add_fusion.after), channel_id=1, source_target_pairs={{0,12},{4,8},{8,4},{12,0},{16,28},{20,24},{24,20},{28,16},{1,13},{... | collective-permute-start | bytes 12296 | tf_op jit(solution)/shard_map/ppermute | solution.py:613
  27.7 5.1 %collective-permute-start.14 = (f32[32,128]{1,0:T(8,128)S(1)}, f32[32,128]{1,0:T(8,128)S(1)}, u32[]{:S(2)}, u32[]{:S(2)}) collective-permute-start(f32[32,128]{1,0:T(8,128)S(1)} %shard_map.122), channel_id=1, source_target_pairs={{0,28},{4,8},{8,4},{12,16},{16,12},{20,24},{24,20},{28,0},{1,29},{... | collective-permute-start | bytes 49160 | tf_op jit(solution)/shard_map/ppermute | solution.py:622
  30.8 3.9 %collective-permute-start.13 = (f32[8,128]{1,0:T(8,128)S(1)}, f32[8,128]{1,0:T(8,128)S(1)}, u32[]{:S(2)}, u32[]{:S(2)}) collective-permute-start(f32[8,128]{1,0:T(8,128)S(1)} %add.7.own), channel_id=1, source_target_pairs={{0,20},{4,16},{8,28},{12,24},{16,4},{20,0},{24,12},{28,8},{1,21},{... | collective-permute-start | bytes 12296 | tf_op jit(solution)/shard_map/ppermute | solution.py:613

commit v11 on v10

--- a/solution.py
+++ b/solution.py
@@ -160,9 +160,26 @@
     return sum(x[:, i : i + LANES] for i in range(0, width, LANES))
 
 
+def tap_at(gap, inside):
+    scale = 1.0 / np.sqrt(np.sum(np.exp(-(np.arange(-REACH, REACH + 1.0) ** 2) / 16.0)))
+    square = (gap * gap).astype(F32)
+    return jnp.where(inside & (jnp.abs(gap) <= REACH), jnp.exp(square * (-1.0 / 32.0)) * scale, 0.0)
+
+
+def gaps(rows, columns):
+    shape = (rows, columns)
+    down, across = (lax.broadcasted_iota(jnp.int32, shape, i) for i in range(2))
+    return down, across, down - across
+
+
+def kept(ref, matrix):
+    ref[0], ref[1] = split(matrix)
+
+
 def edges_kernel(
     source_hbm, members_hbm, precision_hbm, covered_hbm,
-    source, members_ref, obs_weight, near, near_weight, edge_members, to_core, to_chip, precision, covered, sems,
+    source, members_ref, obs_weight, near, near_weight, edge_members, to_core, to_chip, column, row, edge, thin,
+    precision, covered, sems,
 ):
     members, levels, height, width = members_ref.shape
     pairs = ((source_hbm, source), (precision_hbm, precision), (covered_hbm, covered), (members_hbm, members_ref))
@@ -172,6 +189,16 @@
     groups = members * EDGE // LANES
     odd = lax.axis_index("tile") % 2 == 1
     rows = groups * height
+    _, _, gap = gaps(width, width)
+    kept(column, tap_at(gap, True))
+    down, across, gap = gaps(members * height, members * height)
+    kept(row, tap_at(gap, down // height == across // height))
+    down, across, gap = gaps(LANES, LANES)
+    same = down // EDGE == across // EDGE
+    for i in range(3):
+        kept(edge.at[i], tap_at(gap + (i - 1) * EDGE, same))
+    down, across, gap = gaps(rows, rows)
+    kept(thin, tap_at(gap, down // height == across // height))
 
     def send(at, first, last):
         first, last = (x.reshape(-1, LANES) for x in (first, last))
@@ -182,7 +209,7 @@
     copies[0].wait()
     near[0], near[1] = pack_columns(source, 0, EDGE), pack_columns(source, width - EDGE, EDGE)
     send(0, near[0], near[1])
-    send(rows, pack_columns(source, EDGE, EDGE), pack_columns(source, width - 2 * EDGE, EDGE))
+    send(rows, pack_columns(source, EDGE, REACH), pack_columns(source, width - EDGE - REACH, REACH))
     copies[1].wait()
     copies[2].wait()
     obs_weight[...] = weight_of(precision, covered)
@@ -194,12 +221,12 @@
             block = obs_weight[v, :, origin : origin + LANES]
             total = jnp.where(level_lanes(total.shape, v), pltpu.roll(block, shift, 1) if shift else block, total)
         near_weight[side] = total
-    send(rows * (2 + levels), near_weight[0], near_weight[1])
+    send(rows + rows // 2 + rows * levels, near_weight[0], near_weight[1])
     copies[3].wait()
     for v in range(levels):
         level = members_ref[:, v].astype(F32)
         edge_members[0, v], edge_members[1, v] = pack_edges(level, EDGE, True), pack_edges(level, EDGE, False)
-        send(rows * (2 + v), edge_members[0, v], edge_members[1, v])
+        send(rows + rows // 2 + rows * v, edge_members[0, v], edge_members[1, v])
 
 
 def own_columns(field, column, row):
@@ -208,38 +235,9 @@
     return dot3(both(row), split(dot3(lhs, both(column)))).reshape(field.shape)
 
 
-def tap_at(gap, inside):
-    scale = 1.0 / np.sqrt(np.sum(np.exp(-(np.arange(-REACH, REACH + 1.0) ** 2) / 16.0)))
-    square = (gap * gap).astype(F32)
-    return jnp.where(inside & (jnp.abs(gap) <= REACH), jnp.exp(square * (-1.0 / 32.0)) * scale, 0.0)
-
-
-def gaps(rows, columns):
-    shape = (rows, columns)
-    down, across = (lax.broadcasted_iota(jnp.int32, shape, i) for i in range(2))
-    return down, across, down - across
-
-
-def kept(ref, matrix):
-    ref[0], ref[1] = split(matrix)
-
-
-def first_kernel(source, after, members_ref, increment, norm, edge, thin):
-    members, levels, height, width = members_ref.shape
-    _, _, gap = gaps(width, width)
-    column = split(tap_at(gap, True))
-    down, across, gap = gaps(members * height, members * height)
-    row = split(tap_at(gap, down // height == across // height))
-    lhs = split(source[...].reshape(members * height, width))
-    smoothed = dot3(row, split(dot3(lhs, column))).reshape(source.shape)
-    increment[...] = increments(members_ref, smoothed).reshape(levels * height, width)
+def first_kernel(source, after, members_ref, column, row, increment, norm):
+    increment[...] = increments(members_ref, own_columns(source, column, row)).reshape(increment.shape)
     norm[...] = repeated(folded(source[...] * source[...]), SPARE)
-    down, across, gap = gaps(LANES, LANES)
-    same = down // EDGE == across // EDGE
-    for i in range(3):
-        kept(edge.at[i], tap_at(gap + (i - 1) * EDGE, same))
-    down, across, gap = gaps(*thin.shape[1:])
-    kept(thin, tap_at(gap, down // height == across // height))
 
 
 def edge_terms(edge_members, smoothed):
@@ -302,8 +300,24 @@
 
 
 def halo_members(block, rows, groups, levels):
-    height = rows // groups
-    return block[2 * rows : (2 + levels) * rows].reshape(levels, groups, height, LANES)
+    start = rows + rows // 2
+    return block[start : start + levels * rows].reshape(levels, groups, rows // groups, LANES)
+
+
+def halo_weight(block, rows, levels):
+    return block[rows + rows // 2 + levels * rows :]
+
+
+def farther_columns(block, rows, side):
+    packed = block[rows : rows + rows // 2]
+    lane = lane_of(packed.shape)
+    if side == 0:
+        halves_of = (pltpu.roll(packed, REACH, 1), packed)
+        mask = lane % EDGE >= REACH
+    else:
+        halves_of = (packed, pltpu.roll(packed, LANES - REACH, 1))
+        mask = lane % EDGE < REACH
+    return jnp.concatenate([jnp.where(mask, x, 0.0) for x in halves_of], axis=0)
 
 
 def edge_kernel(norm, chip, core, near, edge_members, edge, thin, out):
@@ -312,7 +326,7 @@
     sides = sides_of(core[...], chip[...])
     parts = []
     for side, block in enumerate(sides):
-        here = [block[rows : 2 * rows], block[:rows], near[side].reshape(rows, LANES)]
+        here = [farther_columns(block, rows, side), block[:rows], near[side].reshape(rows, LANES)]
         parts += here if side == 0 else here[::-1]
     filtered = dot3(both(thin), split(jnp.concatenate(parts, axis=1)))
     filtered = split(jnp.concatenate([filtered[:, : 3 * LANES], filtered[:, 3 * LANES :]], axis=0))
@@ -381,7 +395,7 @@
         lanes = pl.ds(side * LANES, LANES)
         own[side] = packed_adjoint(edge_members[side], outer[:height, lanes] * near_weight[side])
         halo[side] = packed_adjoint(
-            halo_members(block, rows, groups, levels), outer[height:, lanes] * block[(2 + levels) * rows :]
+            halo_members(block, rows, groups, levels), outer[height:, lanes] * halo_weight(block, rows, levels)
         )
     parts = [x[side].reshape(rows, LANES) for side in range(2) for x in (halo, own)]
     filtered = split(dot3(both(thin), split(jnp.concatenate(parts, axis=1))))
@@ -442,21 +456,24 @@
     out[...] = dot3(both(row), split(dot3(lhs, both(column)))).reshape(out.shape)
 
 
-def last_kernel(i0, i1, i2, i3, obs_weight, before, sums, members_ref, back, to_core, to_chip):
-    levels, height, width = obs_weight.shape
+def norms_kernel(i0, i1, i2, i3, obs_weight, before, sums, weighted, norms):
     increment = ((i0[...] + i1[...]) + (i2[...] + i3[...])).reshape(obs_weight.shape)
-    weighted = obs_weight[...] * increment
-    four = [sums[0], sums[1], folded(before[...] * increment), folded(weighted * increment)]
+    weighted[...] = obs_weight[...] * increment
+    four = [sums[0], sums[1], folded(before[...] * increment), folded(weighted[...] * increment)]
     row = lax.broadcasted_iota(jnp.int32, (8, LANES), 0)
     stacked = jnp.zeros((8, LANES), F32)
     for i, part in enumerate(four):
         stacked = jnp.where(row == i, jnp.sum(part, axis=0, keepdims=True), stacked)
+    norms[...] = stacked
+
+
+def last_kernel(weighted, members_ref, back, to_core, to_chip):
+    height = back.shape[1]
     back[...] = adjoint(members_ref, weighted)
     odd = lax.axis_index("tile") % 2 == 1
     first, last = pack_edges(back, EDGE, True), pack_edges(back, EDGE, False)
     rows = first.shape[0] * height
-    to_core[:rows] = jnp.where(odd, first, last).reshape(rows, LANES)
-    to_core[rows:] = stacked
+    to_core[...] = jnp.where(odd, first, last).reshape(rows, LANES)
     to_chip[...] = jnp.where(odd, last, first).reshape(rows, LANES)
 
 
@@ -527,7 +544,8 @@
 def held_edges(source, members_data, precision, covered):
     members, levels, height, width = members_data.shape
     groups = members * EDGE // LANES
-    payload = ((groups * (2 + levels) + 1) * height, LANES)
+    rows = groups * height
+    payload = (rows + rows // 2 + rows * levels + height, LANES)
     vmem = pl.BlockSpec(memory_space=pltpu.VMEM)
     hbm = pl.BlockSpec(memory_space=pltpu.HBM)
     arrays = (source, members_data, precision, covered)
@@ -542,9 +560,13 @@
             pltpu.VMEM((2, levels, groups, height, LANES), F32),
             pltpu.VMEM(payload, F32),
             pltpu.VMEM(payload, F32),
+            pltpu.VMEM((2, width, width), BF16),
+            pltpu.VMEM((2, members * height, members * height), BF16),
+            pltpu.VMEM((3, 2, LANES, LANES), BF16),
+            pltpu.VMEM((2, groups * height, groups * height), BF16),
         ],
         in_specs=[hbm] * 4,
-        out_specs=[vmem] * 8,
+        out_specs=[vmem] * 12,
         scratch_shapes=[
             pltpu.VMEM(precision.shape, F32),
             pltpu.VMEM(covered.shape, covered.dtype),
@@ -554,23 +576,17 @@
     )(*map(in_hbm, arrays))
 
 
-def first_increment(source, after, members_data):
-    members, levels, height, width = members_data.shape
-    groups = members * EDGE // LANES
+def first_increment(source, after, members_data, column, row):
+    _, levels, height, width = members_data.shape
     vmem = pl.BlockSpec(memory_space=pltpu.VMEM)
     return pl.pallas_call(
         first_kernel,
-        out_shape=[
-            pltpu.VMEM((levels * height, width), F32),
-            pltpu.VMEM((8, LANES), F32),
-            pltpu.VMEM((3, 2, LANES, LANES), BF16),
-            pltpu.VMEM((2, groups * height, groups * height), BF16),
-        ],
-        in_specs=[vmem] * 3,
-        out_specs=[vmem] * 4,
+        out_shape=[pltpu.VMEM((levels * height, width), F32), pltpu.VMEM((8, LANES), F32)],
+        in_specs=[vmem] * 5,
+        out_specs=[vmem] * 2,
         compiler_params=pltpu.CompilerParams(vmem_limit_bytes=24 * 1024 * 1024),
         cost_estimate=LONG,
-    )(source, after, members_data)
+    )(source, after, members_data, column, row)
 
 
 def call_with_constants(kernel, outs, kept, scratch, operands, constants):
@@ -638,11 +654,10 @@
     flat = (levels * height, width)
     own = np.arange(width)
 
-    source, members_data, obs_weight, near, near_weight, edge_members, to_core, to_chip = held_edges(
-        source, members_data, precision[0], covered[0]
-    )
+    held = held_edges(source, members_data, precision[0], covered[0])
+    source, members_data, obs_weight, near, near_weight, edge_members, to_core, to_chip, column, row, edge, thin = held
     core, chip = from_core(to_core), from_chip(to_chip)
-    inside, norm, edge, thin = first_increment(source, to_chip, members_data)
+    inside, norm = first_increment(source, to_chip, members_data, column, row)
     inside = from_all(inside, "mem", (1, 2, 3))
     (outer,) = call(edge_kernel, [(2 * height, 2 * LANES)], norm, chip, core, near, edge_members, edge, thin)
     column_twice, row_twice = halves(band(twice, own, own)), halves(row_matrix(taps, height, members, 2))
@@ -665,18 +680,16 @@
         wide_filter_kernel, [plane, (2, 8, LANES), field], [column, row], [],
         [main, corrected, halo, increment, outer, obs_weight], [column, row],
     )
-    back, to_core, to_chip = call(
-        last_kernel,
-        [field, (groups * height + 8, LANES), (groups * height, LANES)],
-        *parts, obs_weight, weighted, sums, members_data,
-    )
+    weighted, sums = call(norms_kernel, [plane, (8, LANES)], *parts, obs_weight, weighted, sums)
+    ends = (groups * height, LANES)
+    back, to_core, to_chip = call(last_kernel, [field, ends, ends], weighted, members_data)
+    sums = sums + from_core(sums)
     core = from_core(to_core)
-    sums = to_core[groups * height :] + core[groups * height :]
     (to_chip,) = call(copy_kernel, [to_chip.shape], to_chip, sums)
     chip = from_chip(to_chip)
     first = passed(first, sums)
-    sums = sums + from_tile(sums, 3)
-    others = from_tile(sums, 5)
+    sums = sums + from_tile(sums, 5)
+    others = from_tile(sums, 3)
     (second,) = call(filter_kernel, [field], back, core, chip, column, row, cost=LONG)
     weights, residual = combined(sums, others, source, first, second)
     return weights[None], residual[None]

time: 35.9 us -> 35.7 us (level)
  starting transfers between devices: 18.5 us -> 18.1 us
    ppermute x2, starting transfers between devices: 6.86 us -> 5.85 us  [from_chip(): lax.ppermute(value, 'tile', [(i, (i + 1) % count if i % 2 else (i - 1) %...]
    ppermute x2, waiting for transfers between devices: 1.17 us -> 2.06 us  [from_chip(): lax.ppermute(value, 'tile', [(i, (i + 1) % count if i % 2 else (i - 1) %...]
    ppermute x4 -> x5, waiting for transfers between devices: 2.99 us -> 2.3 us  [from_tile(): return lax.ppermute(value, 'tile', [(i, i ^ bit) for i in range(count)])]
    ppermute x4 -> x5, starting transfers between devices: 0.97 us -> 1.55 us  [from_tile(): return lax.ppermute(value, 'tile', [(i, i ^ bit) for i in range(count)])]
    pallas_call x6 -> x7, Pallas kernels: 3.06 us -> 3.14 us  [call(): pl.pallas_call(kernel, out_shape=shapes, in_specs=[vmem] * len(operands),...]
  transfers between devices with their start and end apart: 15 -> 16, of which waited for: 9 -> 8; matrix products, arithmetic and copies ran while one was open for 0% -> 0% of each run, Pallas kernels for 17% -> 18%
where the time goes in v11:
time: 35.7 us; the launch traced here: 35.5 us
  starting transfers between devices  18.1 us (51%)
  Pallas kernels  9.77 us (27%)
  waiting for transfers between devices  6.9 us (19%)
  between operations  0.75 us (2%)
    ppermute x9, starting transfers between devices, from_all(): lax.ppermute(value, axis, [(i, i ^ k) for i in range(count)])  10.7 us
    ppermute x2, starting transfers between devices, from_chip(): lax.ppermute(value, 'tile', [(i, (i + 1) % count if i % 2 else (i - 1) %...  5.85 us
    pallas_call x2, Pallas kernels, call_with_constants(): pl.pallas_call(kernel, out_shape=[pltpu.VMEM(shape, F32) for shape in out...  3.22 us
    pallas_call x7, Pallas kernels, call(): pl.pallas_call(kernel, out_shape=shapes, in_specs=[vmem] * len(operands),...  3.14 us
    ppermute x9, waiting for transfers between devices, from_all(): lax.ppermute(value, axis, [(i, i ^ k) for i in range(count)])  2.54 us
    ppermute x5, waiting for transfers between devices, from_tile(): return lax.ppermute(value, 'tile', [(i, i ^ bit) for i in range(count)])  2.3 us
    ppermute x2, waiting for transfers between devices, from_chip(): lax.ppermute(value, 'tile', [(i, (i + 1) % count if i % 2 else (i - 1) %...  2.06 us
    pallas_call x1, Pallas kernels, held_edges(): pl.pallas_call(edges_kernel, out_shape=[pltpu.VMEM(source.shape, F32), pl...  1.64 us
  transfers between devices with their start and end apart: 16, of which 8 were waited for; matrix products, arithmetic and copies ran while one was open for 0% of the time, Pallas kernels for 18%

profile of v11, /device:TPU:0, one launch (start us, length us, event | category | flops | bytes accessed | tf_op | source)
XLA Modules:
  0.0 35.5 jit_solution(10402047049409918102)
XLA Ops:
  0.6 1.6 %shard_map.113 = (f32[16,16,256]{2,1,0:T(8,128)S(1)}, bf16[16,6,16,256]{3,2,1,0:T(8,128)(2,1)S(1)}, f32[6,16,256]{2,1,0:T(8,128)S(1)}, f32[2,2,16,128]{3,2,1,0:T...) custom-call(f32[16,16,256]{2,1,0:T(8,128)} %bitcast.7, ...), custom_call_target="tpu_custom_call" | custom-call | tf_op jit(solution)/shard_map/pallas_call | solution.py:552
  2.3 4.6 %collective-permute-start = (f32[256,128]{1,0:T(8,128)S(1)}, f32[256,128]{1,0:T(8,128)S(1)}, u32[]{:S(2)}, u32[]{:S(2)}) collective-permute-start(f32[256,128]{1,0:T(8,128)S(1)} %get-tuple-element.41.after), channel_id=1, source_target_pairs={{0,28},{4,8},{8,4},{12,16},{16,12},{20,24},{24,20},{28,0},{1,29},{... | collective-permute-start | bytes 393224 | tf_op jit(solution)/shard_map/ppermute | solution.py:638
  6.8 0.8 %shard_map.114 = (f32[96,256]{1,0:T(8,128)S(1)}, f32[8,128]{1,0:T(8,128)S(1)}) custom-call(f32[16,16,256]{2,1,0:T(8,128)S(1)} %get-tuple-element.40.source, f32[256,128]{1,0:T(8,128)S(1)} %get-tuple-element.41.after, bf16[16,6,16,256]{3,2,1,0:T(8,128)(2,1)S(1)} %get-tuple-element.42.members_ref, bf16[2,256,256]{2,1,0:T(8,128)(2,1)S(1)} %get-tuple-element.43.column, ...), custom_call_target="tpu_custom_call" | custom-call | flops 1000000000 | bytes 1000000 | tf_op jit(solution)/shard_map/pallas_call | solution.py:582
  7.6 1.6 %collective-permute-start.5 = (f32[96,256]{1,0:T(8,128)S(1)}, f32[96,256]{1,0:T(8,128)S(1)}, u32[]{:S(2)}, u32[]{:S(2)}) collective-permute-start(f32[96,256]{1,0:T(8,128)S(1)} %get-tuple-element.51.i0), channel_id=1, source_target_pairs={{0,1},{1,0},{2,3},{3,2},{4,5},{5,4},{6,7},{7,6},{8,9},{9,8},{10,11... | collective-permute-start | bytes 294920 | tf_op jit(solution)/shard_map/ppermute | solution.py:643
  9.2 1.5 %collective-permute-start.6 = (f32[96,256]{1,0:T(8,128)S(1)}, f32[96,256]{1,0:T(8,128)S(1)}, u32[]{:S(2)}, u32[]{:S(2)}) collective-permute-start(f32[96,256]{1,0:T(8,128)S(1)} %get-tuple-element.51.i0), channel_id=1, source_target_pairs={{0,2},{1,3},{2,0},{3,1},{4,6},{5,7},{6,4},{7,5},{8,10},{9,11},{10,... | collective-permute-start | bytes 294920 | tf_op jit(solution)/shard_map/ppermute | solution.py:643
  11.2 0.6 %shard_map.115.after.e0 = f32[32,256]{1,0:T(8,128)S(1)} custom-call(f32[8,128]{1,0:T(8,128)S(1)} %get-tuple-element.45.norm, f32[256,128]{1,0:T(8,128)S(1)} %collective-permute-done.chip, f32[256,128]{1,0:T(8,128)S(1)} %collective-permute-done.1.core, f32[2,2,16,128]{3,2,1,0:T(8,128)S(1)} %get-tuple-element.47.near, ...), custom_call_target="tpu_custom_call" | custom-call | tf_op jit(solution)/shard_map/pallas_call | solution.py:517
  11.7 2.5 %collective-permute-start.2 = (f32[32,256]{1,0:T(8,128)S(1)}, f32[32,256]{1,0:T(8,128)S(1)}, u32[]{:S(2)}, u32[]{:S(2)}) collective-permute-start(f32[32,256]{1,0:T(8,128)S(1)} %shard_map.115.after.e0), channel_id=1, source_target_pairs={{0,3},{1,2},{2,1},{3,0},{4,7},{5,6},{6,5},{7,4},{8,11},{9,10},{10,... | collective-permute-start | bytes 98312 | tf_op jit(solution)/shard_map/ppermute | solution.py:643
  14.8 0.5 %collective-permute-start.4 = (f32[32,256]{1,0:T(8,128)S(1)}, f32[32,256]{1,0:T(8,128)S(1)}, u32[]{:S(2)}, u32[]{:S(2)}) collective-permute-start(f32[32,256]{1,0:T(8,128)S(1)} %shard_map.115.after.e0), channel_id=1, source_target_pairs={{0,1},{1,0},{2,3},{3,2},{4,5},{5,4},{6,7},{7,6},{8,9},{9,8},{10,11... | collective-permute-start | bytes 98312 | tf_op jit(solution)/shard_map/ppermute | solution.py:643
  15.3 1.3 %shard_map.116 = (f32[2,6,2,16,128]{4,3,2,1,0:T(8,128)S(1)}, bf16[2,256,256]{2,1,0:T(8,128)(2,1)S(1)}, bf16[2,256,256]{2,1,0:T(8,128)(2,1)S(1)}, bf16[3,2,128,12...) custom-call(f32[32,256]{1,0:T(8,128)S(1)} %shard_map.115.after.e0, ...), custom_call_target="tpu_custom_call" | custom-call | flops 1000000000 | bytes 1000000 | tf_op jit(solution)/shard_map/pallas_call | solution.py:596
  16.6 0.8 %shard_map.117 = (f32[96,256]{1,0:T(8,128)S(1)}, f32[16,16,256]{2,1,0:T(8,128)S(1)}, f32[96,256]{1,0:T(8,128)S(1)}) custom-call(f32[96,256]{1,0:T(8,128)S(1)} %get-tuple-element.51.i0, f32[96,256]{1,0:T(8,128)S(1)} %collective-permute-done.5.i1, f32[96,256]{1,0:T(8,128)S(1)} %collective-permute-done.6.i2, f32[96,256]{1,0:T(8,128)S(1)} %collective-permute-done.7.i3, ...), custom_call_target="tpu_custom_call" | custom-call | tf_op jit(solution)/shard_map/pallas_call | solution.py:517
  17.5 0.7 %collective-permute-done.3.e2 = f32[32,256]{1,0:T(8,128)S(1)} collective-permute-done((f32[32,256]{1,0:T(8,128)S(1)}, f32[32,256]{1,0:T(8,128)S(1)}, u32[]{:S(2)}, u32[]{:S(2)}) %collective-permute-start.3) | collective-permute-done | bytes 32800 | tf_op jit(solution)/shard_map/ppermute | solution.py:643
  18.2 0.5 %collective-permute-done.4.e3 = f32[32,256]{1,0:T(8,128)S(1)} collective-permute-done((f32[32,256]{1,0:T(8,128)S(1)}, f32[32,256]{1,0:T(8,128)S(1)}, u32[]{:S(2)}, u32[]{:S(2)}) %collective-permute-start.4) | collective-permute-done | bytes 32800 | tf_op jit(solution)/shard_map/ppermute | solution.py:643
  18.7 0.7 %shard_map.118 = (f32[32,256]{1,0:T(8,128)S(1)}, f32[2,2,16,128]{3,2,1,0:T(8,128)S(1)}, f32[2,2,16,128]{3,2,1,0:T(8,128)S(1)}, f32[96,256]{1,0:T(8,128)S(1)}) custom-call(f32[32,256]{1,0:T(8,128)S(1)} %shard_map.115.after.e0, f32[32,256]{1,0:T(8,128)S(1)} %collective-permute-done.2.e1, f32[32,256]{1,0:T(8,128)S(1)} %collective-permute-done.3.e2, ...), custom_call_target="tpu_custom_call" | custom-call | tf_op jit(solution)/shard_map/pallas_call | solution.py:517
  19.4 1.6 %collective-permute-start.10 = (f32[96,256]{1,0:T(8,128)S(1)}, f32[96,256]{1,0:T(8,128)S(1)}, u32[]{:S(2)}, u32[]{:S(2)}) collective-permute-start(f32[96,256]{1,0:T(8,128)S(1)} %get-tuple-element.60.i0), channel_id=1, source_target_pairs={{0,3},{1,2},{2,1},{3,0},{4,7},{5,6},{6,5},{7,4},{8,11},{9,10},{10,... | collective-permute-start | bytes 294920 | tf_op jit(solution)/shard_map/ppermute | solution.py:643
  21.4 1.5 %collective-permute-start.9 = (f32[96,256]{1,0:T(8,128)S(1)}, f32[96,256]{1,0:T(8,128)S(1)}, u32[]{:S(2)}, u32[]{:S(2)}) collective-permute-start(f32[96,256]{1,0:T(8,128)S(1)} %get-tuple-element.60.i0), channel_id=1, source_target_pairs={{0,1},{1,0},{2,3},{3,2},{4,5},{5,4},{6,7},{7,6},{8,9},{9,8},{10,11... | collective-permute-start | bytes 294920 | tf_op jit(solution)/shard_map/ppermute | solution.py:643
  22.9 1.9 %shard_map.119 = (f32[6,16,256]{2,1,0:T(8,128)S(1)}, f32[2,8,128]{2,1,0:T(8,128)S(1)}, f32[16,16,256]{2,1,0:T(8,128)S(1)}, bf16[2,512,256]{2,1,0:T(8,128)(2,1)S(1)}, bf16[2,256,256]{2,1,0:T(8,128)(2,1)S(1)}) custom-call(f32[16,16,256]{2,1,0:T(8,128)S(1)} %get-tuple-element.61.main, f32[2,2,16,128]{3,2,1,0:T(8,128)S(1)} %get-tuple-element.62.own, ...), custom_call_target="tpu_custom_call" | custom-call | flops 1000000000 | bytes 1000000 | tf_op jit(solution)/shard_map/pallas_call | solution.py:596
  25.2 1.0 %collective-permute-done.8.i1 = f32[96,256]{1,0:T(8,128)S(1)} collective-permute-done((f32[96,256]{1,0:T(8,128)S(1)}, f32[96,256]{1,0:T(8,128)S(1)}, u32[]{:S(2)}, u32[]{:S(2)}) %collective-permute-start.8) | collective-permute-done | bytes 98336 | tf_op jit(solution)/shard_map/ppermute | solution.py:643
  26.6 0.6 %collective-permute-start.14 = (f32[32,128]{1,0:T(8,128)S(1)}, f32[32,128]{1,0:T(8,128)S(1)}, u32[]{:S(2)}, u32[]{:S(2)}) collective-permute-start(f32[32,128]{1,0:T(8,128)S(1)} %get-tuple-element.72), channel_id=1, source_target_pairs={{0,4},{4,0},{8,12},{12,8},{16,20},{20,16},{24,28},{28,24},{1,5},{5... | collective-permute-start | bytes 49160 | tf_op jit(solution)/shard_map/ppermute | solution.py:629
  27.5 0.9 %collective-permute-start.12 = (f32[8,128]{1,0:T(8,128)S(1)}, f32[8,128]{1,0:T(8,128)S(1)}, u32[]{:S(2)}, u32[]{:S(2)}) collective-permute-start(f32[8,128]{1,0:T(8,128)S(1)} %add.6.after), channel_id=1, source_target_pairs={{0,20},{4,16},{8,28},{12,24},{16,4},{20,0},{24,12},{28,8},{1,21},{... | collective-permute-start | bytes 12296 | tf_op jit(solution)/shard_map/ppermute | solution.py:629
  28.4 1.3 %collective-permute-start.15 = (f32[32,128]{1,0:T(8,128)S(1)}, f32[32,128]{1,0:T(8,128)S(1)}, u32[]{:S(2)}, u32[]{:S(2)}) collective-permute-start(f32[32,128]{1,0:T(8,128)S(1)} %shard_map.123), channel_id=1, source_target_pairs={{0,28},{4,8},{8,4},{12,16},{16,12},{20,24},{24,20},{28,0},{1,29},{... | collective-permute-start | bytes 49160 | tf_op jit(solution)/shard_map/ppermute | solution.py:638
  29.7 1.7 %collective-permute-done.12 = f32[8,128]{1,0:T(8,128)S(1)} collective-permute-done((f32[8,128]{1,0:T(8,128)S(1)}, f32[8,128]{1,0:T(8,128)S(1)}, u32[]{:S(2)}, u32[]{:S(2)}) %collective-permute-start.12) | collective-permute-done | bytes 4128 | tf_op jit(solution)/shard_map/ppermute | solution.py:629
  31.5 2.1 %collective-permute-done.15.chip = f32[32,128]{1,0:T(8,128)S(1)} collective-permute-done((f32[32,128]{1,0:T(8,128)S(1)}, f32[32,128]{1,0:T(8,128)S(1)}, u32[]{:S(2)}, u32[]{:S(2)}) %collective-permute-start.15) | collective-permute-done | bytes 16416 | tf_op jit(solution)/shard_map/ppermute | solution.py:638
  33.5 0.8 %shard_map.124.second = f32[16,16,256]{2,1,0:T(8,128)S(1)} custom-call(f32[16,16,256]{2,1,0:T(8,128)S(1)} %get-tuple-element.71.back, f32[32,128]{1,0:T(8,128)S(1)} %collective-permute-done.14.core, f32[32,128]{1,0:T(8,128)S(1)} %collective-permute-done.15.chip, bf16[2,512,256]{2,1,0:T(8,128)(2,1)S(1)} %get-tuple-element.74.column, ...), custom_call_target="tpu_custom_call" | custom-call | flops 1000000000 | bytes 1000000 | tf_op jit(solution)/shard_map/pallas_call | solution.py:517
  34.5 1.0 %shard_map.125 = (f32[16,16,256]{2,1,0:T(8,128)}, f32[16,16,256]{2,1,0:T(8,128)}) custom-call(f32[8,128]{1,0:T(8,128)S(1)} %add.7.own, f32[8,128]{1,0:T(8,128)S(1)} %collective-permute-done.13.other, f32[16,16,256]{2,1,0:T(8,128)S(1)} %get-tuple-element.40.source, f32[16,16,256]{2,1,0:T(8,128)S(1)} %shard_map.121.first, f32[16,16,256]{2,1,0:T(8,128)S(1)} %shard_map.124.second), custom_call_target="tpu_custom_call" | custom-call | tf_op jit(solution)/shard_map/pallas_call | solution.py:610
  (23 shorter events, 2.8 us)
Async XLA Ops:
  2.3 8.9 %collective-permute-start = (f32[256,128]{1,0:T(8,128)S(1)}, f32[256,128]{1,0:T(8,128)S(1)}, u32[]{:S(2)}, u32[]{:S(2)}) collective-permute-start(f32[256,128]{1,0:T(8,128)S(1)} %get-tuple-element.41.after), channel_id=1, source_target_pairs={{0,28},{4,8},{8,4},{12,16},{16,12},{20,24},{24,20},{28,0},{1,29},{... | collective-permute-start | bytes 393224 | tf_op jit(solution)/shard_map/ppermute | solution.py:638
  6.8 4.3 %collective-permute-start.1 = (f32[256,128]{1,0:T(8,128)S(1)}, f32[256,128]{1,0:T(8,128)S(1)}, u32[]{:S(2)}, u32[]{:S(2)}) collective-permute-start(f32[256,128]{1,0:T(8,128)S(1)} %get-tuple-element.46), channel_id=1, source_target_pairs={{0,4},{4,0},{8,12},{12,8},{16,20},{20,16},{24,28},{28,24},{1,5},{5... | collective-permute-start | bytes 393224 | tf_op jit(solution)/shard_map/ppermute | solution.py:629
  7.6 7.2 %collective-permute-start.5 = (f32[96,256]{1,0:T(8,128)S(1)}, f32[96,256]{1,0:T(8,128)S(1)}, u32[]{:S(2)}, u32[]{:S(2)}) collective-permute-start(f32[96,256]{1,0:T(8,128)S(1)} %get-tuple-element.51.i0), channel_id=1, source_target_pairs={{0,1},{1,0},{2,3},{3,2},{4,5},{5,4},{6,7},{7,6},{8,9},{9,8},{10,11... | collective-permute-start | bytes 294920 | tf_op jit(solution)/shard_map/ppermute | solution.py:643
  9.2 7.5 %collective-permute-start.6 = (f32[96,256]{1,0:T(8,128)S(1)}, f32[96,256]{1,0:T(8,128)S(1)}, u32[]{:S(2)}, u32[]{:S(2)}) collective-permute-start(f32[96,256]{1,0:T(8,128)S(1)} %get-tuple-element.51.i0), channel_id=1, source_target_pairs={{0,2},{1,3},{2,0},{3,1},{4,6},{5,7},{6,4},{7,5},{8,10},{9,11},{10,... | collective-permute-start | bytes 294920 | tf_op jit(solution)/shard_map/ppermute | solution.py:643
  10.7 5.9 %collective-permute-start.7 = (f32[96,256]{1,0:T(8,128)S(1)}, f32[96,256]{1,0:T(8,128)S(1)}, u32[]{:S(2)}, u32[]{:S(2)}) collective-permute-start(f32[96,256]{1,0:T(8,128)S(1)} %get-tuple-element.51.i0), channel_id=1, source_target_pairs={{0,3},{1,2},{2,1},{3,0},{4,7},{5,6},{6,5},{7,4},{8,11},{9,10},{10,... | collective-permute-start | bytes 294920 | tf_op jit(solution)/shard_map/ppermute | solution.py:643
  11.7 5.7 %collective-permute-start.2 = (f32[32,256]{1,0:T(8,128)S(1)}, f32[32,256]{1,0:T(8,128)S(1)}, u32[]{:S(2)}, u32[]{:S(2)}) collective-permute-start(f32[32,256]{1,0:T(8,128)S(1)} %shard_map.115.after.e0), channel_id=1, source_target_pairs={{0,3},{1,2},{2,1},{3,0},{4,7},{5,6},{6,5},{7,4},{8,11},{9,10},{10,... | collective-permute-start | bytes 98312 | tf_op jit(solution)/shard_map/ppermute | solution.py:643
  14.3 3.9 %collective-permute-start.3 = (f32[32,256]{1,0:T(8,128)S(1)}, f32[32,256]{1,0:T(8,128)S(1)}, u32[]{:S(2)}, u32[]{:S(2)}) collective-permute-start(f32[32,256]{1,0:T(8,128)S(1)} %shard_map.115.after.e0), channel_id=1, source_target_pairs={{0,2},{1,3},{2,0},{3,1},{4,6},{5,7},{6,4},{7,5},{8,10},{9,11},{10,... | collective-permute-start | bytes 98312 | tf_op jit(solution)/shard_map/ppermute | solution.py:643
  14.8 3.9 %collective-permute-start.4 = (f32[32,256]{1,0:T(8,128)S(1)}, f32[32,256]{1,0:T(8,128)S(1)}, u32[]{:S(2)}, u32[]{:S(2)}) collective-permute-start(f32[32,256]{1,0:T(8,128)S(1)} %shard_map.115.after.e0), channel_id=1, source_target_pairs={{0,1},{1,0},{2,3},{3,2},{4,5},{5,4},{6,7},{7,6},{8,9},{9,8},{10,11... | collective-permute-start | bytes 98312 | tf_op jit(solution)/shard_map/ppermute | solution.py:643
  19.4 5.8 %collective-permute-start.10 = (f32[96,256]{1,0:T(8,128)S(1)}, f32[96,256]{1,0:T(8,128)S(1)}, u32[]{:S(2)}, u32[]{:S(2)}) collective-permute-start(f32[96,256]{1,0:T(8,128)S(1)} %get-tuple-element.60.i0), channel_id=1, source_target_pairs={{0,3},{1,2},{2,1},{3,0},{4,7},{5,6},{6,5},{7,4},{8,11},{9,10},{10,... | collective-permute-start | bytes 294920 | tf_op jit(solution)/shard_map/ppermute | solution.py:643
  20.9 5.3 %collective-permute-start.8 = (f32[96,256]{1,0:T(8,128)S(1)}, f32[96,256]{1,0:T(8,128)S(1)}, u32[]{:S(2)}, u32[]{:S(2)}) collective-permute-start(f32[96,256]{1,0:T(8,128)S(1)} %get-tuple-element.60.i0), channel_id=1, source_target_pairs={{0,2},{1,3},{2,0},{3,1},{4,6},{5,7},{6,4},{7,5},{8,10},{9,11},{10,... | collective-permute-start | bytes 294920 | tf_op jit(solution)/shard_map/ppermute | solution.py:643
  21.4 4.8 %collective-permute-start.9 = (f32[96,256]{1,0:T(8,128)S(1)}, f32[96,256]{1,0:T(8,128)S(1)}, u32[]{:S(2)}, u32[]{:S(2)}) collective-permute-start(f32[96,256]{1,0:T(8,128)S(1)} %get-tuple-element.60.i0), channel_id=1, source_target_pairs={{0,1},{1,0},{2,3},{3,2},{4,5},{5,4},{6,7},{7,6},{8,9},{9,8},{10,11... | collective-permute-start | bytes 294920 | tf_op jit(solution)/shard_map/ppermute | solution.py:643
  26.3 1.2 %collective-permute-start.11 = (f32[8,128]{1,0:T(8,128)S(1)}, f32[8,128]{1,0:T(8,128)S(1)}, u32[]{:S(2)}, u32[]{:S(2)}) collective-permute-start(f32[8,128]{1,0:T(8,128)S(1)} %get-tuple-element.68), channel_id=1, source_target_pairs={{0,4},{4,0},{8,12},{12,8},{16,20},{20,16},{24,28},{28,24},{1,5},{5... | collective-permute-start | bytes 12296 | tf_op jit(solution)/shard_map/ppermute | solution.py:629
  26.6 4.9 %collective-permute-start.14 = (f32[32,128]{1,0:T(8,128)S(1)}, f32[32,128]{1,0:T(8,128)S(1)}, u32[]{:S(2)}, u32[]{:S(2)}) collective-permute-start(f32[32,128]{1,0:T(8,128)S(1)} %get-tuple-element.72), channel_id=1, source_target_pairs={{0,4},{4,0},{8,12},{12,8},{16,20},{20,16},{24,28},{28,24},{1,5},{5... | collective-permute-start | bytes 49160 | tf_op jit(solution)/shard_map/ppermute | solution.py:629
  27.5 3.9 %collective-permute-start.12 = (f32[8,128]{1,0:T(8,128)S(1)}, f32[8,128]{1,0:T(8,128)S(1)}, u32[]{:S(2)}, u32[]{:S(2)}) collective-permute-start(f32[8,128]{1,0:T(8,128)S(1)} %add.6.after), channel_id=1, source_target_pairs={{0,20},{4,16},{8,28},{12,24},{16,4},{20,0},{24,12},{28,8},{1,21},{... | collective-permute-start | bytes 12296 | tf_op jit(solution)/shard_map/ppermute | solution.py:629
  28.4 5.1 %collective-permute-start.15 = (f32[32,128]{1,0:T(8,128)S(1)}, f32[32,128]{1,0:T(8,128)S(1)}, u32[]{:S(2)}, u32[]{:S(2)}) collective-permute-start(f32[32,128]{1,0:T(8,128)S(1)} %shard_map.123), channel_id=1, source_target_pairs={{0,28},{4,8},{8,4},{12,16},{16,12},{20,24},{24,20},{28,0},{1,29},{... | collective-permute-start | bytes 49160 | tf_op jit(solution)/shard_map/ppermute | solution.py:638
  31.4 3.0 %collective-permute-start.13 = (f32[8,128]{1,0:T(8,128)S(1)}, f32[8,128]{1,0:T(8,128)S(1)}, u32[]{:S(2)}, u32[]{:S(2)}) collective-permute-start(f32[8,128]{1,0:T(8,128)S(1)} %add.7.own), channel_id=1, source_target_pairs={{0,12},{4,8},{8,4},{12,0},{16,28},{20,24},{24,20},{28,16},{1,13},{... | collective-permute-start | bytes 12296 | tf_op jit(solution)/shard_map/ppermute | solution.py:629

commit v12 on v11

--- a/solution.py
+++ b/solution.py
@@ -68,6 +68,12 @@
 def dot3(left, right):
     mul = functools.partial(jnp.dot, preferred_element_type=F32)
     return mul(left[0], right[0]) + (mul(left[1], right[0]) + mul(left[0], right[1]))
+
+
+def thin3(thin, x):
+    high, low = split(x)
+    left = jnp.concatenate([thin[0], thin[1], thin[0]], axis=1)
+    return jnp.dot(left, jnp.concatenate([high, high, low], axis=0), preferred_element_type=F32)
 
 
 def both(ref):
@@ -328,7 +334,7 @@
     for side, block in enumerate(sides):
         here = [farther_columns(block, rows, side), block[:rows], near[side].reshape(rows, LANES)]
         parts += here if side == 0 else here[::-1]
-    filtered = dot3(both(thin), split(jnp.concatenate(parts, axis=1)))
+    filtered = thin3(thin, jnp.concatenate(parts, axis=1))
     filtered = split(jnp.concatenate([filtered[:, : 3 * LANES], filtered[:, 3 * LANES :]], axis=0))
     beyond = dot3(filtered, [jnp.concatenate([edge[i, k] for i in range(3)], axis=0) for k in range(2)])
     middle = tuple(x[:, LANES : 2 * LANES] for x in filtered)
@@ -398,7 +404,7 @@
             halo_members(block, rows, groups, levels), outer[height:, lanes] * halo_weight(block, rows, levels)
         )
     parts = [x[side].reshape(rows, LANES) for side in range(2) for x in (halo, own)]
-    filtered = split(dot3(both(thin), split(jnp.concatenate(parts, axis=1))))
+    filtered = split(thin3(thin, jnp.concatenate(parts, axis=1)))
     for side in range(2):
         span = slice(2 * side * LANES, 2 * (side + 1) * LANES)
         matrix = [jnp.concatenate([edge[2 * side, k], edge[1, k]], axis=0) for k in range(2)]

time: 35.7 us -> 35.6 us (level)
  no operation moved by 1% of the time
where the time goes in v12:
time: 35.6 us; the launch traced here: 35.4 us
  starting transfers between devices  18 us (51%)
  Pallas kernels  9.69 us (27%)
  waiting for transfers between devices  6.96 us (20%)
  between operations  0.74 us (2%)
    ppermute x9, starting transfers between devices, from_all(): lax.ppermute(value, axis, [(i, i ^ k) for i in range(count)])  10.7 us
    ppermute x2, starting transfers between devices, from_chip(): lax.ppermute(value, 'tile', [(i, (i + 1) % count if i % 2 else (i - 1) %...  5.85 us
    pallas_call x2, Pallas kernels, call_with_constants(): pl.pallas_call(kernel, out_shape=[pltpu.VMEM(shape, F32) for shape in out...  3.22 us
    pallas_call x7, Pallas kernels, call(): pl.pallas_call(kernel, out_shape=shapes, in_specs=[vmem] * len(operands),...  3.07 us
    ppermute x9, waiting for transfers between devices, from_all(): lax.ppermute(value, axis, [(i, i ^ k) for i in range(count)])  2.58 us
    ppermute x5, waiting for transfers between devices, from_tile(): return lax.ppermute(value, 'tile', [(i, i ^ bit) for i in range(count)])  2.32 us
    ppermute x2, waiting for transfers between devices, from_chip(): lax.ppermute(value, 'tile', [(i, (i + 1) % count if i % 2 else (i - 1) %...  2.06 us
    pallas_call x1, Pallas kernels, held_edges(): pl.pallas_call(edges_kernel, out_shape=[pltpu.VMEM(source.shape, F32), pl...  1.64 us
  transfers between devices with their start and end apart: 16, of which 8 were waited for; matrix products, arithmetic and copies ran while one was open for 0% of the time, Pallas kernels for 18%

profile of v12, /device:TPU:0, one launch (start us, length us, event | category | flops | bytes accessed | tf_op | source)
XLA Modules:
  0.0 35.4 jit_solution(5565398551464732135)
XLA Ops:
  0.6 1.6 %shard_map.113 = (f32[16,16,256]{2,1,0:T(8,128)S(1)}, bf16[16,6,16,256]{3,2,1,0:T(8,128)(2,1)S(1)}, f32[6,16,256]{2,1,0:T(8,128)S(1)}, f32[2,2,16,128]{3,2,1,0:T...) custom-call(f32[16,16,256]{2,1,0:T(8,128)} %bitcast.7, ...), custom_call_target="tpu_custom_call" | custom-call | tf_op jit(solution)/shard_map/pallas_call | solution.py:558
  2.3 4.6 %collective-permute-start = (f32[256,128]{1,0:T(8,128)S(1)}, f32[256,128]{1,0:T(8,128)S(1)}, u32[]{:S(2)}, u32[]{:S(2)}) collective-permute-start(f32[256,128]{1,0:T(8,128)S(1)} %get-tuple-element.41.after), channel_id=1, source_target_pairs={{0,28},{4,8},{8,4},{12,16},{16,12},{20,24},{24,20},{28,0},{1,29},{... | collective-permute-start | bytes 393224 | tf_op jit(solution)/shard_map/ppermute | solution.py:644
  6.8 0.8 %shard_map.114 = (f32[96,256]{1,0:T(8,128)S(1)}, f32[8,128]{1,0:T(8,128)S(1)}) custom-call(f32[16,16,256]{2,1,0:T(8,128)S(1)} %get-tuple-element.40.source, f32[256,128]{1,0:T(8,128)S(1)} %get-tuple-element.41.after, bf16[16,6,16,256]{3,2,1,0:T(8,128)(2,1)S(1)} %get-tuple-element.42.members_ref, bf16[2,256,256]{2,1,0:T(8,128)(2,1)S(1)} %get-tuple-element.43.column, ...), custom_call_target="tpu_custom_call" | custom-call | flops 1000000000 | bytes 1000000 | tf_op jit(solution)/shard_map/pallas_call | solution.py:588
  7.6 1.6 %collective-permute-start.5 = (f32[96,256]{1,0:T(8,128)S(1)}, f32[96,256]{1,0:T(8,128)S(1)}, u32[]{:S(2)}, u32[]{:S(2)}) collective-permute-start(f32[96,256]{1,0:T(8,128)S(1)} %get-tuple-element.51.i0), channel_id=1, source_target_pairs={{0,1},{1,0},{2,3},{3,2},{4,5},{5,4},{6,7},{7,6},{8,9},{9,8},{10,11... | collective-permute-start | bytes 294920 | tf_op jit(solution)/shard_map/ppermute | solution.py:649
  9.2 1.5 %collective-permute-start.6 = (f32[96,256]{1,0:T(8,128)S(1)}, f32[96,256]{1,0:T(8,128)S(1)}, u32[]{:S(2)}, u32[]{:S(2)}) collective-permute-start(f32[96,256]{1,0:T(8,128)S(1)} %get-tuple-element.51.i0), channel_id=1, source_target_pairs={{0,2},{1,3},{2,0},{3,1},{4,6},{5,7},{6,4},{7,5},{8,10},{9,11},{10,... | collective-permute-start | bytes 294920 | tf_op jit(solution)/shard_map/ppermute | solution.py:649
  11.2 0.5 %shard_map.115.after.e0 = f32[32,256]{1,0:T(8,128)S(1)} custom-call(f32[8,128]{1,0:T(8,128)S(1)} %get-tuple-element.45.norm, f32[256,128]{1,0:T(8,128)S(1)} %collective-permute-done.chip, f32[256,128]{1,0:T(8,128)S(1)} %collective-permute-done.1.core, f32[2,2,16,128]{3,2,1,0:T(8,128)S(1)} %get-tuple-element.47.near, ...), custom_call_target="tpu_custom_call" | custom-call | tf_op jit(solution)/shard_map/pallas_call | solution.py:523
  11.7 2.5 %collective-permute-start.2 = (f32[32,256]{1,0:T(8,128)S(1)}, f32[32,256]{1,0:T(8,128)S(1)}, u32[]{:S(2)}, u32[]{:S(2)}) collective-permute-start(f32[32,256]{1,0:T(8,128)S(1)} %shard_map.115.after.e0), channel_id=1, source_target_pairs={{0,3},{1,2},{2,1},{3,0},{4,7},{5,6},{6,5},{7,4},{8,11},{9,10},{10,... | collective-permute-start | bytes 98312 | tf_op jit(solution)/shard_map/ppermute | solution.py:649
  14.7 0.5 %collective-permute-start.4 = (f32[32,256]{1,0:T(8,128)S(1)}, f32[32,256]{1,0:T(8,128)S(1)}, u32[]{:S(2)}, u32[]{:S(2)}) collective-permute-start(f32[32,256]{1,0:T(8,128)S(1)} %shard_map.115.after.e0), channel_id=1, source_target_pairs={{0,1},{1,0},{2,3},{3,2},{4,5},{5,4},{6,7},{7,6},{8,9},{9,8},{10,11... | collective-permute-start | bytes 98312 | tf_op jit(solution)/shard_map/ppermute | solution.py:649
  15.3 1.3 %shard_map.116 = (f32[2,6,2,16,128]{4,3,2,1,0:T(8,128)S(1)}, bf16[2,256,256]{2,1,0:T(8,128)(2,1)S(1)}, bf16[2,256,256]{2,1,0:T(8,128)(2,1)S(1)}, bf16[3,2,128,12...) custom-call(f32[32,256]{1,0:T(8,128)S(1)} %shard_map.115.after.e0, ...), custom_call_target="tpu_custom_call" | custom-call | flops 1000000000 | bytes 1000000 | tf_op jit(solution)/shard_map/pallas_call | solution.py:602
  16.6 0.8 %shard_map.117 = (f32[96,256]{1,0:T(8,128)S(1)}, f32[16,16,256]{2,1,0:T(8,128)S(1)}, f32[96,256]{1,0:T(8,128)S(1)}) custom-call(f32[96,256]{1,0:T(8,128)S(1)} %get-tuple-element.51.i0, f32[96,256]{1,0:T(8,128)S(1)} %collective-permute-done.5.i1, f32[96,256]{1,0:T(8,128)S(1)} %collective-permute-done.6.i2, f32[96,256]{1,0:T(8,128)S(1)} %collective-permute-done.7.i3, ...), custom_call_target="tpu_custom_call" | custom-call | tf_op jit(solution)/shard_map/pallas_call | solution.py:523
  17.5 0.6 %collective-permute-done.3.e2 = f32[32,256]{1,0:T(8,128)S(1)} collective-permute-done((f32[32,256]{1,0:T(8,128)S(1)}, f32[32,256]{1,0:T(8,128)S(1)}, u32[]{:S(2)}, u32[]{:S(2)}) %collective-permute-start.3) | collective-permute-done | bytes 32800 | tf_op jit(solution)/shard_map/ppermute | solution.py:649
  18.1 0.5 %collective-permute-done.4.e3 = f32[32,256]{1,0:T(8,128)S(1)} collective-permute-done((f32[32,256]{1,0:T(8,128)S(1)}, f32[32,256]{1,0:T(8,128)S(1)}, u32[]{:S(2)}, u32[]{:S(2)}) %collective-permute-start.4) | collective-permute-done | bytes 32800 | tf_op jit(solution)/shard_map/ppermute | solution.py:649
  18.6 0.7 %shard_map.118 = (f32[32,256]{1,0:T(8,128)S(1)}, f32[2,2,16,128]{3,2,1,0:T(8,128)S(1)}, f32[2,2,16,128]{3,2,1,0:T(8,128)S(1)}, f32[96,256]{1,0:T(8,128)S(1)}) custom-call(f32[32,256]{1,0:T(8,128)S(1)} %shard_map.115.after.e0, f32[32,256]{1,0:T(8,128)S(1)} %collective-permute-done.2.e1, f32[32,256]{1,0:T(8,128)S(1)} %collective-permute-done.3.e2, ...), custom_call_target="tpu_custom_call" | custom-call | tf_op jit(solution)/shard_map/pallas_call | solution.py:523
  19.3 1.6 %collective-permute-start.10 = (f32[96,256]{1,0:T(8,128)S(1)}, f32[96,256]{1,0:T(8,128)S(1)}, u32[]{:S(2)}, u32[]{:S(2)}) collective-permute-start(f32[96,256]{1,0:T(8,128)S(1)} %get-tuple-element.60.i0), channel_id=1, source_target_pairs={{0,3},{1,2},{2,1},{3,0},{4,7},{5,6},{6,5},{7,4},{8,11},{9,10},{10,... | collective-permute-start | bytes 294920 | tf_op jit(solution)/shard_map/ppermute | solution.py:649
  21.4 1.5 %collective-permute-start.9 = (f32[96,256]{1,0:T(8,128)S(1)}, f32[96,256]{1,0:T(8,128)S(1)}, u32[]{:S(2)}, u32[]{:S(2)}) collective-permute-start(f32[96,256]{1,0:T(8,128)S(1)} %get-tuple-element.60.i0), channel_id=1, source_target_pairs={{0,1},{1,0},{2,3},{3,2},{4,5},{5,4},{6,7},{7,6},{8,9},{9,8},{10,11... | collective-permute-start | bytes 294920 | tf_op jit(solution)/shard_map/ppermute | solution.py:649
  22.9 1.9 %shard_map.119 = (f32[6,16,256]{2,1,0:T(8,128)S(1)}, f32[2,8,128]{2,1,0:T(8,128)S(1)}, f32[16,16,256]{2,1,0:T(8,128)S(1)}, bf16[2,512,256]{2,1,0:T(8,128)(2,1)S(1)}, bf16[2,256,256]{2,1,0:T(8,128)(2,1)S(1)}) custom-call(f32[16,16,256]{2,1,0:T(8,128)S(1)} %get-tuple-element.61.main, f32[2,2,16,128]{3,2,1,0:T(8,128)S(1)} %get-tuple-element.62.own, ...), custom_call_target="tpu_custom_call" | custom-call | flops 1000000000 | bytes 1000000 | tf_op jit(solution)/shard_map/pallas_call | solution.py:602
  25.2 1.0 %collective-permute-done.8.i1 = f32[96,256]{1,0:T(8,128)S(1)} collective-permute-done((f32[96,256]{1,0:T(8,128)S(1)}, f32[96,256]{1,0:T(8,128)S(1)}, u32[]{:S(2)}, u32[]{:S(2)}) %collective-permute-start.8) | collective-permute-done | bytes 98336 | tf_op jit(solution)/shard_map/ppermute | solution.py:649
  26.5 0.6 %collective-permute-start.14 = (f32[32,128]{1,0:T(8,128)S(1)}, f32[32,128]{1,0:T(8,128)S(1)}, u32[]{:S(2)}, u32[]{:S(2)}) collective-permute-start(f32[32,128]{1,0:T(8,128)S(1)} %get-tuple-element.72), channel_id=1, source_target_pairs={{0,4},{4,0},{8,12},{12,8},{16,20},{20,16},{24,28},{28,24},{1,5},{5... | collective-permute-start | bytes 49160 | tf_op jit(solution)/shard_map/ppermute | solution.py:635
  27.5 0.9 %collective-permute-start.12 = (f32[8,128]{1,0:T(8,128)S(1)}, f32[8,128]{1,0:T(8,128)S(1)}, u32[]{:S(2)}, u32[]{:S(2)}) collective-permute-start(f32[8,128]{1,0:T(8,128)S(1)} %add.6.after), channel_id=1, source_target_pairs={{0,20},{4,16},{8,28},{12,24},{16,4},{20,0},{24,12},{28,8},{1,21},{... | collective-permute-start | bytes 12296 | tf_op jit(solution)/shard_map/ppermute | solution.py:635
  28.4 1.3 %collective-permute-start.15 = (f32[32,128]{1,0:T(8,128)S(1)}, f32[32,128]{1,0:T(8,128)S(1)}, u32[]{:S(2)}, u32[]{:S(2)}) collective-permute-start(f32[32,128]{1,0:T(8,128)S(1)} %shard_map.123), channel_id=1, source_target_pairs={{0,28},{4,8},{8,4},{12,16},{16,12},{20,24},{24,20},{28,0},{1,29},{... | collective-permute-start | bytes 49160 | tf_op jit(solution)/shard_map/ppermute | solution.py:644
  29.7 1.7 %collective-permute-done.12 = f32[8,128]{1,0:T(8,128)S(1)} collective-permute-done((f32[8,128]{1,0:T(8,128)S(1)}, f32[8,128]{1,0:T(8,128)S(1)}, u32[]{:S(2)}, u32[]{:S(2)}) %collective-permute-start.12) | collective-permute-done | bytes 4128 | tf_op jit(solution)/shard_map/ppermute | solution.py:635
  31.4 2.1 %collective-permute-done.15.chip = f32[32,128]{1,0:T(8,128)S(1)} collective-permute-done((f32[32,128]{1,0:T(8,128)S(1)}, f32[32,128]{1,0:T(8,128)S(1)}, u32[]{:S(2)}, u32[]{:S(2)}) %collective-permute-start.15) | collective-permute-done | bytes 16416 | tf_op jit(solution)/shard_map/ppermute | solution.py:644
  33.5 0.8 %shard_map.124.second = f32[16,16,256]{2,1,0:T(8,128)S(1)} custom-call(f32[16,16,256]{2,1,0:T(8,128)S(1)} %get-tuple-element.71.back, f32[32,128]{1,0:T(8,128)S(1)} %collective-permute-done.14.core, f32[32,128]{1,0:T(8,128)S(1)} %collective-permute-done.15.chip, bf16[2,512,256]{2,1,0:T(8,128)(2,1)S(1)} %get-tuple-element.74.column, ...), custom_call_target="tpu_custom_call" | custom-call | flops 1000000000 | bytes 1000000 | tf_op jit(solution)/shard_map/pallas_call | solution.py:523
  34.4 1.0 %shard_map.125 = (f32[16,16,256]{2,1,0:T(8,128)}, f32[16,16,256]{2,1,0:T(8,128)}) custom-call(f32[8,128]{1,0:T(8,128)S(1)} %add.7.own, f32[8,128]{1,0:T(8,128)S(1)} %collective-permute-done.13.other, f32[16,16,256]{2,1,0:T(8,128)S(1)} %get-tuple-element.40.source, f32[16,16,256]{2,1,0:T(8,128)S(1)} %shard_map.121.first, f32[16,16,256]{2,1,0:T(8,128)S(1)} %shard_map.124.second), custom_call_target="tpu_custom_call" | custom-call | tf_op jit(solution)/shard_map/pallas_call | solution.py:616
  (23 shorter events, 2.9 us)
Async XLA Ops:
  2.3 8.9 %collective-permute-start = (f32[256,128]{1,0:T(8,128)S(1)}, f32[256,128]{1,0:T(8,128)S(1)}, u32[]{:S(2)}, u32[]{:S(2)}) collective-permute-start(f32[256,128]{1,0:T(8,128)S(1)} %get-tuple-element.41.after), channel_id=1, source_target_pairs={{0,28},{4,8},{8,4},{12,16},{16,12},{20,24},{24,20},{28,0},{1,29},{... | collective-permute-start | bytes 393224 | tf_op jit(solution)/shard_map/ppermute | solution.py:644
  6.8 4.3 %collective-permute-start.1 = (f32[256,128]{1,0:T(8,128)S(1)}, f32[256,128]{1,0:T(8,128)S(1)}, u32[]{:S(2)}, u32[]{:S(2)}) collective-permute-start(f32[256,128]{1,0:T(8,128)S(1)} %get-tuple-element.46), channel_id=1, source_target_pairs={{0,4},{4,0},{8,12},{12,8},{16,20},{20,16},{24,28},{28,24},{1,5},{5... | collective-permute-start | bytes 393224 | tf_op jit(solution)/shard_map/ppermute | solution.py:635
  7.6 7.1 %collective-permute-start.5 = (f32[96,256]{1,0:T(8,128)S(1)}, f32[96,256]{1,0:T(8,128)S(1)}, u32[]{:S(2)}, u32[]{:S(2)}) collective-permute-start(f32[96,256]{1,0:T(8,128)S(1)} %get-tuple-element.51.i0), channel_id=1, source_target_pairs={{0,1},{1,0},{2,3},{3,2},{4,5},{5,4},{6,7},{7,6},{8,9},{9,8},{10,11... | collective-permute-start | bytes 294920 | tf_op jit(solution)/shard_map/ppermute | solution.py:649
  9.2 7.4 %collective-permute-start.6 = (f32[96,256]{1,0:T(8,128)S(1)}, f32[96,256]{1,0:T(8,128)S(1)}, u32[]{:S(2)}, u32[]{:S(2)}) collective-permute-start(f32[96,256]{1,0:T(8,128)S(1)} %get-tuple-element.51.i0), channel_id=1, source_target_pairs={{0,2},{1,3},{2,0},{3,1},{4,6},{5,7},{6,4},{7,5},{8,10},{9,11},{10,... | collective-permute-start | bytes 294920 | tf_op jit(solution)/shard_map/ppermute | solution.py:649
  10.7 5.9 %collective-permute-start.7 = (f32[96,256]{1,0:T(8,128)S(1)}, f32[96,256]{1,0:T(8,128)S(1)}, u32[]{:S(2)}, u32[]{:S(2)}) collective-permute-start(f32[96,256]{1,0:T(8,128)S(1)} %get-tuple-element.51.i0), channel_id=1, source_target_pairs={{0,3},{1,2},{2,1},{3,0},{4,7},{5,6},{6,5},{7,4},{8,11},{9,10},{10,... | collective-permute-start | bytes 294920 | tf_op jit(solution)/shard_map/ppermute | solution.py:649
  11.7 5.8 %collective-permute-start.2 = (f32[32,256]{1,0:T(8,128)S(1)}, f32[32,256]{1,0:T(8,128)S(1)}, u32[]{:S(2)}, u32[]{:S(2)}) collective-permute-start(f32[32,256]{1,0:T(8,128)S(1)} %shard_map.115.after.e0), channel_id=1, source_target_pairs={{0,3},{1,2},{2,1},{3,0},{4,7},{5,6},{6,5},{7,4},{8,11},{9,10},{10,... | collective-permute-start | bytes 98312 | tf_op jit(solution)/shard_map/ppermute | solution.py:649
  14.2 3.9 %collective-permute-start.3 = (f32[32,256]{1,0:T(8,128)S(1)}, f32[32,256]{1,0:T(8,128)S(1)}, u32[]{:S(2)}, u32[]{:S(2)}) collective-permute-start(f32[32,256]{1,0:T(8,128)S(1)} %shard_map.115.after.e0), channel_id=1, source_target_pairs={{0,2},{1,3},{2,0},{3,1},{4,6},{5,7},{6,4},{7,5},{8,10},{9,11},{10,... | collective-permute-start | bytes 98312 | tf_op jit(solution)/shard_map/ppermute | solution.py:649
  14.7 3.9 %collective-permute-start.4 = (f32[32,256]{1,0:T(8,128)S(1)}, f32[32,256]{1,0:T(8,128)S(1)}, u32[]{:S(2)}, u32[]{:S(2)}) collective-permute-start(f32[32,256]{1,0:T(8,128)S(1)} %shard_map.115.after.e0), channel_id=1, source_target_pairs={{0,1},{1,0},{2,3},{3,2},{4,5},{5,4},{6,7},{7,6},{8,9},{9,8},{10,11... | collective-permute-start | bytes 98312 | tf_op jit(solution)/shard_map/ppermute | solution.py:649
  19.3 5.8 %collective-permute-start.10 = (f32[96,256]{1,0:T(8,128)S(1)}, f32[96,256]{1,0:T(8,128)S(1)}, u32[]{:S(2)}, u32[]{:S(2)}) collective-permute-start(f32[96,256]{1,0:T(8,128)S(1)} %get-tuple-element.60.i0), channel_id=1, source_target_pairs={{0,3},{1,2},{2,1},{3,0},{4,7},{5,6},{6,5},{7,4},{8,11},{9,10},{10,... | collective-permute-start | bytes 294920 | tf_op jit(solution)/shard_map/ppermute | solution.py:649
  20.9 5.3 %collective-permute-start.8 = (f32[96,256]{1,0:T(8,128)S(1)}, f32[96,256]{1,0:T(8,128)S(1)}, u32[]{:S(2)}, u32[]{:S(2)}) collective-permute-start(f32[96,256]{1,0:T(8,128)S(1)} %get-tuple-element.60.i0), channel_id=1, source_target_pairs={{0,2},{1,3},{2,0},{3,1},{4,6},{5,7},{6,4},{7,5},{8,10},{9,11},{10,... | collective-permute-start | bytes 294920 | tf_op jit(solution)/shard_map/ppermute | solution.py:649
  21.4 4.8 %collective-permute-start.9 = (f32[96,256]{1,0:T(8,128)S(1)}, f32[96,256]{1,0:T(8,128)S(1)}, u32[]{:S(2)}, u32[]{:S(2)}) collective-permute-start(f32[96,256]{1,0:T(8,128)S(1)} %get-tuple-element.60.i0), channel_id=1, source_target_pairs={{0,1},{1,0},{2,3},{3,2},{4,5},{5,4},{6,7},{7,6},{8,9},{9,8},{10,11... | collective-permute-start | bytes 294920 | tf_op jit(solution)/shard_map/ppermute | solution.py:649
  26.2 1.2 %collective-permute-start.11 = (f32[8,128]{1,0:T(8,128)S(1)}, f32[8,128]{1,0:T(8,128)S(1)}, u32[]{:S(2)}, u32[]{:S(2)}) collective-permute-start(f32[8,128]{1,0:T(8,128)S(1)} %get-tuple-element.68), channel_id=1, source_target_pairs={{0,4},{4,0},{8,12},{12,8},{16,20},{20,16},{24,28},{28,24},{1,5},{5... | collective-permute-start | bytes 12296 | tf_op jit(solution)/shard_map/ppermute | solution.py:635
  26.5 4.9 %collective-permute-start.14 = (f32[32,128]{1,0:T(8,128)S(1)}, f32[32,128]{1,0:T(8,128)S(1)}, u32[]{:S(2)}, u32[]{:S(2)}) collective-permute-start(f32[32,128]{1,0:T(8,128)S(1)} %get-tuple-element.72), channel_id=1, source_target_pairs={{0,4},{4,0},{8,12},{12,8},{16,20},{20,16},{24,28},{28,24},{1,5},{5... | collective-permute-start | bytes 49160 | tf_op jit(solution)/shard_map/ppermute | solution.py:635
  27.5 3.9 %collective-permute-start.12 = (f32[8,128]{1,0:T(8,128)S(1)}, f32[8,128]{1,0:T(8,128)S(1)}, u32[]{:S(2)}, u32[]{:S(2)}) collective-permute-start(f32[8,128]{1,0:T(8,128)S(1)} %add.6.after), channel_id=1, source_target_pairs={{0,20},{4,16},{8,28},{12,24},{16,4},{20,0},{24,12},{28,8},{1,21},{... | collective-permute-start | bytes 12296 | tf_op jit(solution)/shard_map/ppermute | solution.py:635
  28.4 5.1 %collective-permute-start.15 = (f32[32,128]{1,0:T(8,128)S(1)}, f32[32,128]{1,0:T(8,128)S(1)}, u32[]{:S(2)}, u32[]{:S(2)}) collective-permute-start(f32[32,128]{1,0:T(8,128)S(1)} %shard_map.123), channel_id=1, source_target_pairs={{0,28},{4,8},{8,4},{12,16},{16,12},{20,24},{24,20},{28,0},{1,29},{... | collective-permute-start | bytes 49160 | tf_op jit(solution)/shard_map/ppermute | solution.py:644
  31.4 3.0 %collective-permute-start.13 = (f32[8,128]{1,0:T(8,128)S(1)}, f32[8,128]{1,0:T(8,128)S(1)}, u32[]{:S(2)}, u32[]{:S(2)}) collective-permute-start(f32[8,128]{1,0:T(8,128)S(1)} %add.7.own), channel_id=1, source_target_pairs={{0,12},{4,8},{8,4},{12,0},{16,28},{20,24},{24,20},{28,16},{1,13},{... | collective-permute-start | bytes 12296 | tf_op jit(solution)/shard_map/ppermute | solution.py:635

commit v13 on v12

--- a/solution.py
+++ b/solution.py
@@ -67,6 +67,10 @@
 
 def dot3(left, right):
     mul = functools.partial(jnp.dot, preferred_element_type=F32)
+    if left[0].shape[1] == LANES:
+        return mul(
+            jnp.concatenate([left[0], left[1], left[0]], axis=1), jnp.concatenate([right[0], right[0], right[1]], axis=0)
+        )
     return mul(left[0], right[0]) + (mul(left[1], right[0]) + mul(left[0], right[1]))
 
 

time: 35.6 us -> 35.6 us (level)
  no operation moved by 1% of the time
where the time goes in v13:
time: 35.6 us; the launch traced here: 35.4 us
  starting transfers between devices  18 us (51%)
  Pallas kernels  9.68 us (27%)
  waiting for transfers between devices  6.96 us (20%)
  between operations  0.75 us (2%)
    ppermute x9, starting transfers between devices, from_all(): lax.ppermute(value, axis, [(i, i ^ k) for i in range(count)])  10.7 us
    ppermute x2, starting transfers between devices, from_chip(): lax.ppermute(value, 'tile', [(i, (i + 1) % count if i % 2 else (i - 1) %...  5.85 us
    pallas_call x2, Pallas kernels, call_with_constants(): pl.pallas_call(kernel, out_shape=[pltpu.VMEM(shape, F32) for shape in out...  3.22 us
    pallas_call x7, Pallas kernels, call(): pl.pallas_call(kernel, out_shape=shapes, in_specs=[vmem] * len(operands),...  3.06 us
    ppermute x9, waiting for transfers between devices, from_all(): lax.ppermute(value, axis, [(i, i ^ k) for i in range(count)])  2.58 us
    ppermute x5, waiting for transfers between devices, from_tile(): return lax.ppermute(value, 'tile', [(i, i ^ bit) for i in range(count)])  2.32 us
    ppermute x2, waiting for transfers between devices, from_chip(): lax.ppermute(value, 'tile', [(i, (i + 1) % count if i % 2 else (i - 1) %...  2.06 us
    pallas_call x1, Pallas kernels, held_edges(): pl.pallas_call(edges_kernel, out_shape=[pltpu.VMEM(source.shape, F32), pl...  1.64 us
  transfers between devices with their start and end apart: 16, of which 8 were waited for; matrix products, arithmetic and copies ran while one was open for 0% of the time, Pallas kernels for 18%

profile of v13, /device:TPU:0, one launch (start us, length us, event | category | flops | bytes accessed | tf_op | source)
XLA Modules:
  0.0 35.4 jit_solution(8302542038411701630)
XLA Ops:
  0.6 1.6 %shard_map.113 = (f32[16,16,256]{2,1,0:T(8,128)S(1)}, bf16[16,6,16,256]{3,2,1,0:T(8,128)(2,1)S(1)}, f32[6,16,256]{2,1,0:T(8,128)S(1)}, f32[2,2,16,128]{3,2,1,0:T...) custom-call(f32[16,16,256]{2,1,0:T(8,128)} %bitcast.7, ...), custom_call_target="tpu_custom_call" | custom-call | tf_op jit(solution)/shard_map/pallas_call | solution.py:562
  2.3 4.6 %collective-permute-start = (f32[256,128]{1,0:T(8,128)S(1)}, f32[256,128]{1,0:T(8,128)S(1)}, u32[]{:S(2)}, u32[]{:S(2)}) collective-permute-start(f32[256,128]{1,0:T(8,128)S(1)} %get-tuple-element.41.after), channel_id=1, source_target_pairs={{0,28},{4,8},{8,4},{12,16},{16,12},{20,24},{24,20},{28,0},{1,29},{... | collective-permute-start | bytes 393224 | tf_op jit(solution)/shard_map/ppermute | solution.py:648
  6.8 0.8 %shard_map.114 = (f32[96,256]{1,0:T(8,128)S(1)}, f32[8,128]{1,0:T(8,128)S(1)}) custom-call(f32[16,16,256]{2,1,0:T(8,128)S(1)} %get-tuple-element.40.source, f32[256,128]{1,0:T(8,128)S(1)} %get-tuple-element.41.after, bf16[16,6,16,256]{3,2,1,0:T(8,128)(2,1)S(1)} %get-tuple-element.42.members_ref, bf16[2,256,256]{2,1,0:T(8,128)(2,1)S(1)} %get-tuple-element.43.column, ...), custom_call_target="tpu_custom_call" | custom-call | flops 1000000000 | bytes 1000000 | tf_op jit(solution)/shard_map/pallas_call | solution.py:592
  7.6 1.6 %collective-permute-start.5 = (f32[96,256]{1,0:T(8,128)S(1)}, f32[96,256]{1,0:T(8,128)S(1)}, u32[]{:S(2)}, u32[]{:S(2)}) collective-permute-start(f32[96,256]{1,0:T(8,128)S(1)} %get-tuple-element.51.i0), channel_id=1, source_target_pairs={{0,1},{1,0},{2,3},{3,2},{4,5},{5,4},{6,7},{7,6},{8,9},{9,8},{10,11... | collective-permute-start | bytes 294920 | tf_op jit(solution)/shard_map/ppermute | solution.py:653
  9.2 1.5 %collective-permute-start.6 = (f32[96,256]{1,0:T(8,128)S(1)}, f32[96,256]{1,0:T(8,128)S(1)}, u32[]{:S(2)}, u32[]{:S(2)}) collective-permute-start(f32[96,256]{1,0:T(8,128)S(1)} %get-tuple-element.51.i0), channel_id=1, source_target_pairs={{0,2},{1,3},{2,0},{3,1},{4,6},{5,7},{6,4},{7,5},{8,10},{9,11},{10,... | collective-permute-start | bytes 294920 | tf_op jit(solution)/shard_map/ppermute | solution.py:653
  11.2 0.5 %shard_map.115.after.e0 = f32[32,256]{1,0:T(8,128)S(1)} custom-call(f32[8,128]{1,0:T(8,128)S(1)} %get-tuple-element.45.norm, f32[256,128]{1,0:T(8,128)S(1)} %collective-permute-done.chip, f32[256,128]{1,0:T(8,128)S(1)} %collective-permute-done.1.core, f32[2,2,16,128]{3,2,1,0:T(8,128)S(1)} %get-tuple-element.47.near, ...), custom_call_target="tpu_custom_call" | custom-call | tf_op jit(solution)/shard_map/pallas_call | solution.py:527
  11.7 2.5 %collective-permute-start.2 = (f32[32,256]{1,0:T(8,128)S(1)}, f32[32,256]{1,0:T(8,128)S(1)}, u32[]{:S(2)}, u32[]{:S(2)}) collective-permute-start(f32[32,256]{1,0:T(8,128)S(1)} %shard_map.115.after.e0), channel_id=1, source_target_pairs={{0,3},{1,2},{2,1},{3,0},{4,7},{5,6},{6,5},{7,4},{8,11},{9,10},{10,... | collective-permute-start | bytes 98312 | tf_op jit(solution)/shard_map/ppermute | solution.py:653
  14.7 0.5 %collective-permute-start.4 = (f32[32,256]{1,0:T(8,128)S(1)}, f32[32,256]{1,0:T(8,128)S(1)}, u32[]{:S(2)}, u32[]{:S(2)}) collective-permute-start(f32[32,256]{1,0:T(8,128)S(1)} %shard_map.115.after.e0), channel_id=1, source_target_pairs={{0,1},{1,0},{2,3},{3,2},{4,5},{5,4},{6,7},{7,6},{8,9},{9,8},{10,11... | collective-permute-start | bytes 98312 | tf_op jit(solution)/shard_map/ppermute | solution.py:653
  15.3 1.3 %shard_map.116 = (f32[2,6,2,16,128]{4,3,2,1,0:T(8,128)S(1)}, bf16[2,256,256]{2,1,0:T(8,128)(2,1)S(1)}, bf16[2,256,256]{2,1,0:T(8,128)(2,1)S(1)}, bf16[3,2,128,12...) custom-call(f32[32,256]{1,0:T(8,128)S(1)} %shard_map.115.after.e0, ...), custom_call_target="tpu_custom_call" | custom-call | flops 1000000000 | bytes 1000000 | tf_op jit(solution)/shard_map/pallas_call | solution.py:606
  16.6 0.8 %shard_map.117 = (f32[96,256]{1,0:T(8,128)S(1)}, f32[16,16,256]{2,1,0:T(8,128)S(1)}, f32[96,256]{1,0:T(8,128)S(1)}) custom-call(f32[96,256]{1,0:T(8,128)S(1)} %get-tuple-element.51.i0, f32[96,256]{1,0:T(8,128)S(1)} %collective-permute-done.5.i1, f32[96,256]{1,0:T(8,128)S(1)} %collective-permute-done.6.i2, f32[96,256]{1,0:T(8,128)S(1)} %collective-permute-done.7.i3, ...), custom_call_target="tpu_custom_call" | custom-call | tf_op jit(solution)/shard_map/pallas_call | solution.py:527
  17.5 0.7 %collective-permute-done.3.e2 = f32[32,256]{1,0:T(8,128)S(1)} collective-permute-done((f32[32,256]{1,0:T(8,128)S(1)}, f32[32,256]{1,0:T(8,128)S(1)}, u32[]{:S(2)}, u32[]{:S(2)}) %collective-permute-start.3) | collective-permute-done | bytes 32800 | tf_op jit(solution)/shard_map/ppermute | solution.py:653
  18.1 0.5 %collective-permute-done.4.e3 = f32[32,256]{1,0:T(8,128)S(1)} collective-permute-done((f32[32,256]{1,0:T(8,128)S(1)}, f32[32,256]{1,0:T(8,128)S(1)}, u32[]{:S(2)}, u32[]{:S(2)}) %collective-permute-start.4) | collective-permute-done | bytes 32800 | tf_op jit(solution)/shard_map/ppermute | solution.py:653
  18.6 0.7 %shard_map.118 = (f32[32,256]{1,0:T(8,128)S(1)}, f32[2,2,16,128]{3,2,1,0:T(8,128)S(1)}, f32[2,2,16,128]{3,2,1,0:T(8,128)S(1)}, f32[96,256]{1,0:T(8,128)S(1)}) custom-call(f32[32,256]{1,0:T(8,128)S(1)} %shard_map.115.after.e0, f32[32,256]{1,0:T(8,128)S(1)} %collective-permute-done.2.e1, f32[32,256]{1,0:T(8,128)S(1)} %collective-permute-done.3.e2, ...), custom_call_target="tpu_custom_call" | custom-call | tf_op jit(solution)/shard_map/pallas_call | solution.py:527
  19.3 1.6 %collective-permute-start.10 = (f32[96,256]{1,0:T(8,128)S(1)}, f32[96,256]{1,0:T(8,128)S(1)}, u32[]{:S(2)}, u32[]{:S(2)}) collective-permute-start(f32[96,256]{1,0:T(8,128)S(1)} %get-tuple-element.60.i0), channel_id=1, source_target_pairs={{0,3},{1,2},{2,1},{3,0},{4,7},{5,6},{6,5},{7,4},{8,11},{9,10},{10,... | collective-permute-start | bytes 294920 | tf_op jit(solution)/shard_map/ppermute | solution.py:653
  21.4 1.5 %collective-permute-start.9 = (f32[96,256]{1,0:T(8,128)S(1)}, f32[96,256]{1,0:T(8,128)S(1)}, u32[]{:S(2)}, u32[]{:S(2)}) collective-permute-start(f32[96,256]{1,0:T(8,128)S(1)} %get-tuple-element.60.i0), channel_id=1, source_target_pairs={{0,1},{1,0},{2,3},{3,2},{4,5},{5,4},{6,7},{7,6},{8,9},{9,8},{10,11... | collective-permute-start | bytes 294920 | tf_op jit(solution)/shard_map/ppermute | solution.py:653
  22.9 1.9 %shard_map.119 = (f32[6,16,256]{2,1,0:T(8,128)S(1)}, f32[2,8,128]{2,1,0:T(8,128)S(1)}, f32[16,16,256]{2,1,0:T(8,128)S(1)}, bf16[2,512,256]{2,1,0:T(8,128)(2,1)S(1)}, bf16[2,256,256]{2,1,0:T(8,128)(2,1)S(1)}) custom-call(f32[16,16,256]{2,1,0:T(8,128)S(1)} %get-tuple-element.61.main, f32[2,2,16,128]{3,2,1,0:T(8,128)S(1)} %get-tuple-element.62.own, ...), custom_call_target="tpu_custom_call" | custom-call | flops 1000000000 | bytes 1000000 | tf_op jit(solution)/shard_map/pallas_call | solution.py:606
  25.2 1.0 %collective-permute-done.8.i1 = f32[96,256]{1,0:T(8,128)S(1)} collective-permute-done((f32[96,256]{1,0:T(8,128)S(1)}, f32[96,256]{1,0:T(8,128)S(1)}, u32[]{:S(2)}, u32[]{:S(2)}) %collective-permute-start.8) | collective-permute-done | bytes 98336 | tf_op jit(solution)/shard_map/ppermute | solution.py:653
  26.5 0.6 %collective-permute-start.14 = (f32[32,128]{1,0:T(8,128)S(1)}, f32[32,128]{1,0:T(8,128)S(1)}, u32[]{:S(2)}, u32[]{:S(2)}) collective-permute-start(f32[32,128]{1,0:T(8,128)S(1)} %get-tuple-element.72), channel_id=1, source_target_pairs={{0,4},{4,0},{8,12},{12,8},{16,20},{20,16},{24,28},{28,24},{1,5},{5... | collective-permute-start | bytes 49160 | tf_op jit(solution)/shard_map/ppermute | solution.py:639
  27.5 0.9 %collective-permute-start.12 = (f32[8,128]{1,0:T(8,128)S(1)}, f32[8,128]{1,0:T(8,128)S(1)}, u32[]{:S(2)}, u32[]{:S(2)}) collective-permute-start(f32[8,128]{1,0:T(8,128)S(1)} %add.6.after), channel_id=1, source_target_pairs={{0,20},{4,16},{8,28},{12,24},{16,4},{20,0},{24,12},{28,8},{1,21},{... | collective-permute-start | bytes 12296 | tf_op jit(solution)/shard_map/ppermute | solution.py:639
  28.3 1.3 %collective-permute-start.15 = (f32[32,128]{1,0:T(8,128)S(1)}, f32[32,128]{1,0:T(8,128)S(1)}, u32[]{:S(2)}, u32[]{:S(2)}) collective-permute-start(f32[32,128]{1,0:T(8,128)S(1)} %shard_map.123), channel_id=1, source_target_pairs={{0,28},{4,8},{8,4},{12,16},{16,12},{20,24},{24,20},{28,0},{1,29},{... | collective-permute-start | bytes 49160 | tf_op jit(solution)/shard_map/ppermute | solution.py:648
  29.6 1.7 %collective-permute-done.12 = f32[8,128]{1,0:T(8,128)S(1)} collective-permute-done((f32[8,128]{1,0:T(8,128)S(1)}, f32[8,128]{1,0:T(8,128)S(1)}, u32[]{:S(2)}, u32[]{:S(2)}) %collective-permute-start.12) | collective-permute-done | bytes 4128 | tf_op jit(solution)/shard_map/ppermute | solution.py:639
  31.4 2.1 %collective-permute-done.15.chip = f32[32,128]{1,0:T(8,128)S(1)} collective-permute-done((f32[32,128]{1,0:T(8,128)S(1)}, f32[32,128]{1,0:T(8,128)S(1)}, u32[]{:S(2)}, u32[]{:S(2)}) %collective-permute-start.15) | collective-permute-done | bytes 16416 | tf_op jit(solution)/shard_map/ppermute | solution.py:648
  33.5 0.8 %shard_map.124.second = f32[16,16,256]{2,1,0:T(8,128)S(1)} custom-call(f32[16,16,256]{2,1,0:T(8,128)S(1)} %get-tuple-element.71.back, f32[32,128]{1,0:T(8,128)S(1)} %collective-permute-done.14.core, f32[32,128]{1,0:T(8,128)S(1)} %collective-permute-done.15.chip, bf16[2,512,256]{2,1,0:T(8,128)(2,1)S(1)} %get-tuple-element.74.column, ...), custom_call_target="tpu_custom_call" | custom-call | flops 1000000000 | bytes 1000000 | tf_op jit(solution)/shard_map/pallas_call | solution.py:527
  34.4 1.0 %shard_map.125 = (f32[16,16,256]{2,1,0:T(8,128)}, f32[16,16,256]{2,1,0:T(8,128)}) custom-call(f32[8,128]{1,0:T(8,128)S(1)} %add.7.own, f32[8,128]{1,0:T(8,128)S(1)} %collective-permute-done.13.other, f32[16,16,256]{2,1,0:T(8,128)S(1)} %get-tuple-element.40.source, f32[16,16,256]{2,1,0:T(8,128)S(1)} %shard_map.121.first, f32[16,16,256]{2,1,0:T(8,128)S(1)} %shard_map.124.second), custom_call_target="tpu_custom_call" | custom-call | tf_op jit(solution)/shard_map/pallas_call | solution.py:620
  (23 shorter events, 2.8 us)
Async XLA Ops:
  2.3 8.9 %collective-permute-start = (f32[256,128]{1,0:T(8,128)S(1)}, f32[256,128]{1,0:T(8,128)S(1)}, u32[]{:S(2)}, u32[]{:S(2)}) collective-permute-start(f32[256,128]{1,0:T(8,128)S(1)} %get-tuple-element.41.after), channel_id=1, source_target_pairs={{0,28},{4,8},{8,4},{12,16},{16,12},{20,24},{24,20},{28,0},{1,29},{... | collective-permute-start | bytes 393224 | tf_op jit(solution)/shard_map/ppermute | solution.py:648
  6.8 4.3 %collective-permute-start.1 = (f32[256,128]{1,0:T(8,128)S(1)}, f32[256,128]{1,0:T(8,128)S(1)}, u32[]{:S(2)}, u32[]{:S(2)}) collective-permute-start(f32[256,128]{1,0:T(8,128)S(1)} %get-tuple-element.46), channel_id=1, source_target_pairs={{0,4},{4,0},{8,12},{12,8},{16,20},{20,16},{24,28},{28,24},{1,5},{5... | collective-permute-start | bytes 393224 | tf_op jit(solution)/shard_map/ppermute | solution.py:639
  7.6 7.1 %collective-permute-start.5 = (f32[96,256]{1,0:T(8,128)S(1)}, f32[96,256]{1,0:T(8,128)S(1)}, u32[]{:S(2)}, u32[]{:S(2)}) collective-permute-start(f32[96,256]{1,0:T(8,128)S(1)} %get-tuple-element.51.i0), channel_id=1, source_target_pairs={{0,1},{1,0},{2,3},{3,2},{4,5},{5,4},{6,7},{7,6},{8,9},{9,8},{10,11... | collective-permute-start | bytes 294920 | tf_op jit(solution)/shard_map/ppermute | solution.py:653
  9.2 7.4 %collective-permute-start.6 = (f32[96,256]{1,0:T(8,128)S(1)}, f32[96,256]{1,0:T(8,128)S(1)}, u32[]{:S(2)}, u32[]{:S(2)}) collective-permute-start(f32[96,256]{1,0:T(8,128)S(1)} %get-tuple-element.51.i0), channel_id=1, source_target_pairs={{0,2},{1,3},{2,0},{3,1},{4,6},{5,7},{6,4},{7,5},{8,10},{9,11},{10,... | collective-permute-start | bytes 294920 | tf_op jit(solution)/shard_map/ppermute | solution.py:653
  10.7 5.9 %collective-permute-start.7 = (f32[96,256]{1,0:T(8,128)S(1)}, f32[96,256]{1,0:T(8,128)S(1)}, u32[]{:S(2)}, u32[]{:S(2)}) collective-permute-start(f32[96,256]{1,0:T(8,128)S(1)} %get-tuple-element.51.i0), channel_id=1, source_target_pairs={{0,3},{1,2},{2,1},{3,0},{4,7},{5,6},{6,5},{7,4},{8,11},{9,10},{10,... | collective-permute-start | bytes 294920 | tf_op jit(solution)/shard_map/ppermute | solution.py:653
  11.7 5.8 %collective-permute-start.2 = (f32[32,256]{1,0:T(8,128)S(1)}, f32[32,256]{1,0:T(8,128)S(1)}, u32[]{:S(2)}, u32[]{:S(2)}) collective-permute-start(f32[32,256]{1,0:T(8,128)S(1)} %shard_map.115.after.e0), channel_id=1, source_target_pairs={{0,3},{1,2},{2,1},{3,0},{4,7},{5,6},{6,5},{7,4},{8,11},{9,10},{10,... | collective-permute-start | bytes 98312 | tf_op jit(solution)/shard_map/ppermute | solution.py:653
  14.2 3.9 %collective-permute-start.3 = (f32[32,256]{1,0:T(8,128)S(1)}, f32[32,256]{1,0:T(8,128)S(1)}, u32[]{:S(2)}, u32[]{:S(2)}) collective-permute-start(f32[32,256]{1,0:T(8,128)S(1)} %shard_map.115.after.e0), channel_id=1, source_target_pairs={{0,2},{1,3},{2,0},{3,1},{4,6},{5,7},{6,4},{7,5},{8,10},{9,11},{10,... | collective-permute-start | bytes 98312 | tf_op jit(solution)/shard_map/ppermute | solution.py:653
  14.7 3.9 %collective-permute-start.4 = (f32[32,256]{1,0:T(8,128)S(1)}, f32[32,256]{1,0:T(8,128)S(1)}, u32[]{:S(2)}, u32[]{:S(2)}) collective-permute-start(f32[32,256]{1,0:T(8,128)S(1)} %shard_map.115.after.e0), channel_id=1, source_target_pairs={{0,1},{1,0},{2,3},{3,2},{4,5},{5,4},{6,7},{7,6},{8,9},{9,8},{10,11... | collective-permute-start | bytes 98312 | tf_op jit(solution)/shard_map/ppermute | solution.py:653
  19.3 5.8 %collective-permute-start.10 = (f32[96,256]{1,0:T(8,128)S(1)}, f32[96,256]{1,0:T(8,128)S(1)}, u32[]{:S(2)}, u32[]{:S(2)}) collective-permute-start(f32[96,256]{1,0:T(8,128)S(1)} %get-tuple-element.60.i0), channel_id=1, source_target_pairs={{0,3},{1,2},{2,1},{3,0},{4,7},{5,6},{6,5},{7,4},{8,11},{9,10},{10,... | collective-permute-start | bytes 294920 | tf_op jit(solution)/shard_map/ppermute | solution.py:653
  20.9 5.3 %collective-permute-start.8 = (f32[96,256]{1,0:T(8,128)S(1)}, f32[96,256]{1,0:T(8,128)S(1)}, u32[]{:S(2)}, u32[]{:S(2)}) collective-permute-start(f32[96,256]{1,0:T(8,128)S(1)} %get-tuple-element.60.i0), channel_id=1, source_target_pairs={{0,2},{1,3},{2,0},{3,1},{4,6},{5,7},{6,4},{7,5},{8,10},{9,11},{10,... | collective-permute-start | bytes 294920 | tf_op jit(solution)/shard_map/ppermute | solution.py:653
  21.4 4.8 %collective-permute-start.9 = (f32[96,256]{1,0:T(8,128)S(1)}, f32[96,256]{1,0:T(8,128)S(1)}, u32[]{:S(2)}, u32[]{:S(2)}) collective-permute-start(f32[96,256]{1,0:T(8,128)S(1)} %get-tuple-element.60.i0), channel_id=1, source_target_pairs={{0,1},{1,0},{2,3},{3,2},{4,5},{5,4},{6,7},{7,6},{8,9},{9,8},{10,11... | collective-permute-start | bytes 294920 | tf_op jit(solution)/shard_map/ppermute | solution.py:653
  26.2 1.2 %collective-permute-start.11 = (f32[8,128]{1,0:T(8,128)S(1)}, f32[8,128]{1,0:T(8,128)S(1)}, u32[]{:S(2)}, u32[]{:S(2)}) collective-permute-start(f32[8,128]{1,0:T(8,128)S(1)} %get-tuple-element.68), channel_id=1, source_target_pairs={{0,4},{4,0},{8,12},{12,8},{16,20},{20,16},{24,28},{28,24},{1,5},{5... | collective-permute-start | bytes 12296 | tf_op jit(solution)/shard_map/ppermute | solution.py:639
  26.5 4.9 %collective-permute-start.14 = (f32[32,128]{1,0:T(8,128)S(1)}, f32[32,128]{1,0:T(8,128)S(1)}, u32[]{:S(2)}, u32[]{:S(2)}) collective-permute-start(f32[32,128]{1,0:T(8,128)S(1)} %get-tuple-element.72), channel_id=1, source_target_pairs={{0,4},{4,0},{8,12},{12,8},{16,20},{20,16},{24,28},{28,24},{1,5},{5... | collective-permute-start | bytes 49160 | tf_op jit(solution)/shard_map/ppermute | solution.py:639
  27.5 3.9 %collective-permute-start.12 = (f32[8,128]{1,0:T(8,128)S(1)}, f32[8,128]{1,0:T(8,128)S(1)}, u32[]{:S(2)}, u32[]{:S(2)}) collective-permute-start(f32[8,128]{1,0:T(8,128)S(1)} %add.6.after), channel_id=1, source_target_pairs={{0,20},{4,16},{8,28},{12,24},{16,4},{20,0},{24,12},{28,8},{1,21},{... | collective-permute-start | bytes 12296 | tf_op jit(solution)/shard_map/ppermute | solution.py:639
  28.3 5.1 %collective-permute-start.15 = (f32[32,128]{1,0:T(8,128)S(1)}, f32[32,128]{1,0:T(8,128)S(1)}, u32[]{:S(2)}, u32[]{:S(2)}) collective-permute-start(f32[32,128]{1,0:T(8,128)S(1)} %shard_map.123), channel_id=1, source_target_pairs={{0,28},{4,8},{8,4},{12,16},{16,12},{20,24},{24,20},{28,0},{1,29},{... | collective-permute-start | bytes 49160 | tf_op jit(solution)/shard_map/ppermute | solution.py:648
  31.4 3.0 %collective-permute-start.13 = (f32[8,128]{1,0:T(8,128)S(1)}, f32[8,128]{1,0:T(8,128)S(1)}, u32[]{:S(2)}, u32[]{:S(2)}) collective-permute-start(f32[8,128]{1,0:T(8,128)S(1)} %add.7.own), channel_id=1, source_target_pairs={{0,12},{4,8},{8,4},{12,0},{16,28},{20,24},{24,20},{28,16},{1,13},{... | collective-permute-start | bytes 12296 | tf_op jit(solution)/shard_map/ppermute | solution.py:639
